TPU v7x, 32 devices: a whole 2x2x4 slice. The times are simulated.
32 devices in a mesh: row: 8 (over z, y), col: 4 (over x, core).
Axes of the slice: x: 2, y: 2, z: 4, core: 2. Of those that a mesh axis runs over, the one named last changes fastest.
Arguments:
- right_sides: bfloat16 [32, 4, 384, 256], P('row', 'col'), may hold values from -120 to 120
- stiff_diag: bfloat16 [32, 4, 384, 384], P('row', 'col'), may hold values from -0.85 to 7.85
- stiff_upper: bfloat16 [32, 4, 384, 384], P('row', 'col'), may hold values from -0.635 to 0.635
- local_diag: bfloat16 [48, 4, 384, 384], P('row', 'col'), may hold values from -0.089 to 0.79
- local_upper: bfloat16 [40, 4, 384, 384], P('row', 'col'), may hold values from -0.034 to 0.034
- coarse_basis: bfloat16 [8, 4, 6, 1536], P('row', 'col'), may hold values from -0.21875 to 0.21875
- coarse_factor: bfloat16 [192, 192], replicated, may hold values from -0.4375 to 0.4375
Outputs:
- solution: float32 [32, 4, 384, 256], P('row', 'col')
All inputs are finite; a program needn't handle non-finite values.
Results may differ from a plain program's by a relative error of at most 0.0018.
Values may be sent and summed in bfloat16 or wider, within the bound.
No kernel may reach another device: no remote copies, remote signals or barrier semaphores. Data moves between devices by JAX's collectives and lax.ppermute only.
A program may use at most 64 MiB of HBM per device.

v0:
```python
import jax
import jax.numpy as jnp
from jax import lax
from jax.sharding import PartitionSpec as P

ITERS = 2


def with_halo(cells, sides, width):
    for axis, dim in sides:
        count = lax.axis_size(axis)
        ends = count - 1
        head = lax.slice_in_dim(cells, 0, width, axis=dim)
        tail = lax.slice_in_dim(cells, cells.shape[dim] - width, cells.shape[dim], axis=dim)
        cells = jnp.concatenate(
            [
                lax.ppermute(tail, axis, [(i, (i + 1) % count) for i in range(ends)]),
                cells,
                lax.ppermute(head, axis, [((i + 1) % count, i) for i in range(ends)]),
            ],
            axis=dim,
        )
    return cells


def apply_blocks(blocks, vectors):
    return jnp.einsum("nij,njr->nir", blocks, vectors, preferred_element_type=jnp.float32)


def apply_transposed(blocks, vectors):
    return jnp.einsum("nji,njr->nir", blocks, vectors, preferred_element_type=jnp.float32)


def times_transposed(matrix, vectors):
    return lax.dot_general(
        matrix, vectors, (((0,), (0,)), ((), ())), preferred_element_type=jnp.float32
    )


def times_plain(matrix, vectors):
    return jnp.dot(matrix, vectors, preferred_element_type=jnp.float32)


def column_dots(left_vec, right_vec):
    return jnp.sum(left_vec * right_vec, axis=(0, 1))


def global_sums(values):
    return lax.psum(values, ("row", "col"))


def operate(vector, s_diag, s_upper):
    vec_bf = vector.astype(jnp.bfloat16)
    downward = apply_transposed(s_upper, vec_bf)
    edge_rows = jnp.stack([vec_bf[0].astype(jnp.float32), downward[-1]])
    padded = with_halo(edge_rows, (("row", 0),), 1)
    above_layer = padded[3].astype(jnp.bfloat16)
    raised = jnp.concatenate([vec_bf[1:], above_layer[None]], axis=0)
    result = apply_blocks(s_diag, vec_bf) + apply_blocks(s_upper, raised)
    lowered = jnp.concatenate([padded[0][None], downward[:-1]], axis=0)
    return result + lowered


def precondition(residual, l_diag, l_upper, basis_rows, factor, own_start):
    res_bf = residual.astype(jnp.bfloat16)
    extended = with_halo(res_bf, (("row", 0),), 1)
    local_part = apply_blocks(l_diag[1:-1], extended[1:-1])
    local_part = local_part + apply_blocks(l_upper[1:], extended[2:])
    local_part = local_part + apply_transposed(l_upper[:-1], extended[:-2])
    bottom = times_plain(l_diag[0], extended[0]) + times_plain(l_upper[0], extended[1])
    upper_end = times_plain(l_diag[-1], extended[-1]) + times_transposed(l_upper[-1], extended[-2])
    arrivals = with_halo(jnp.stack([bottom, upper_end]), (("row", 0),), 1)
    from_below = arrivals[0]
    from_above = arrivals[3]
    local_part = local_part.at[0].add(from_below).at[-1].add(from_above)
    flat_res = res_bf.reshape(-1, res_bf.shape[-1])
    coarse_rhs = times_plain(basis_rows, flat_res).astype(jnp.bfloat16)
    own_cols = lax.dynamic_slice_in_dim(factor, own_start, basis_rows.shape[0], 1)
    solved = times_plain(factor, lax.all_gather(coarse_rhs, ("row", "col"), axis=0, tiled=True))
    coarse_sol = times_transposed(own_cols, solved.astype(jnp.bfloat16)).astype(jnp.bfloat16)
    spread = times_transposed(basis_rows, coarse_sol)
    return local_part + spread.reshape(local_part.shape)


def on_device(
    right_sides, stiff_diag, stiff_upper, local_diag, local_upper, coarse_basis, coarse_factor
):
    s_diag = stiff_diag[:, 0]
    s_upper = stiff_upper[:, 0]
    l_diag = local_diag[:, 0]
    l_upper = local_upper[:, 0]
    basis_rows = coarse_basis[0, 0]
    own_start = (
        lax.axis_index("row") * lax.axis_size("col") + lax.axis_index("col")
    ) * basis_rows.shape[0]
    residual = right_sides[:, 0].astype(jnp.float32)
    solution = jnp.zeros_like(residual)
    direction = residual
    image_vec = residual
    gamma_before = None
    step_len = None
    for iteration in range(ITERS):
        precond = precondition(residual, l_diag, l_upper, basis_rows, coarse_factor, own_start)
        image_pre = operate(precond, s_diag, s_upper)
        both_sums = global_sums(
            jnp.stack([column_dots(residual, precond), column_dots(precond, image_pre)])
        )
        if iteration == 0:
            step_len = both_sums[0] / both_sums[1]
            direction = precond
            image_vec = image_pre
        else:
            beta_coef = both_sums[0] / gamma_before
            step_len = both_sums[0] / (both_sums[1] - beta_coef * both_sums[0] / step_len)
            direction = precond + beta_coef * direction
            image_vec = image_pre + beta_coef * image_vec
        solution = solution + step_len * direction
        if iteration + 1 < ITERS:
            residual = residual - step_len * image_vec
        gamma_before = both_sums[0]
    return solution[:, None]


def solution(mesh):
    in_specs = (
        P("row", "col", None, None),
        P("row", "col", None, None),
        P("row", "col", None, None),
        P("row", "col", None, None),
        P("row", "col", None, None),
        P("row", "col", None, None),
        P(),
    )
    out_specs = P("row", "col", None, None)
    return jax.shard_map(
        on_device, mesh=mesh, in_specs=in_specs, out_specs=out_specs, check_vma=False
    )
```

profile of v0, /device:TPU:0, one launch (start us, length us, event | category | flops | bytes accessed | tf_op | source)
XLA Modules:
  0.0 287.4 jit_solution(17813687727485483265)
XLA Ops:
  0.0 1.9 slice_bitcast_fusion.9
  1.9 1.3 collective-permute-start
  3.2 6.2 %collective-permute-start.1 = (bf16[1,384,256]{2,1,0:T(8,128)(2,1)}, bf16[1,384,256]{2,1,0:T(8,128)(2,1)}, u32[]{:S(2)}, u32[]{:S(2)}) collective-permute-start(bf16[1,384,256]{2,1,0:T(8,128)(2,1)} %get-tuple-element.63), channel_id=1, source_target_pairs={{0,4},{4,8},{8,12},{12,16},{16,20},{20,24},{24,28},{1,5},{5,9},{9,... | collective-permute-start | bytes 589832 | tf_op jit(solution)/shard_map/ppermute | solution.py:17
  9.4 3.4 %fusion.22 = f32[4,384,256]{2,1,0:T(8,128)} fusion(bf16[6,1,384,384]{3,2,0,1:T(8,128)(2,1)} %bitcast.167, bf16[4,1,384,256]{3,2,1,0:T(8,128)(2,1)} %param.15), kind=kOutput, calls=%fused_computation.47 | convolution fusion | flops 301989888 | bytes 3538944 | tf_op jit(solution)/shard_map/nij,njr->nir/dot_general | solution.py:27
  12.7 1.0 fusion.52
  14.0 43.1 %all-gather = bf16[32,6,256]{2,1,0:T(8,128)(2,1)} all-gather(bf16[1,6,256]{2,1,0:T(8,128)(2,1)S(1)} %fusion.19), channel_id=1, replica_groups=mesh['row'=8,'col'=4] {'row','col'}, dimensions={0}, use_global_device_ids=true | all-gather | bytes 101376 | tf_op jit(solution)/shard_map/all_gather | solution.py:79
  57.2 1.6 reshape.191
  58.7 1.3 fusion.18
  60.0 1.6 convolution_bitcast_fusion.1
  61.6 1.0 fusion.46
  62.6 3.0 %copy.79 = f32[1536,256]{1,0:T(8,128)} copy(f32[1536,256]{0,1:T(8,128)} %convolution_bitcast_fusion.1) | data formatting | bytes 3145728 | tf_op jit(solution)/shard_map/dot_general | solution.py:35
  65.6 1.4 fusion.6
  67.1 1.3 collective-permute-start.2
  68.4 1.4 fusion.5
  69.8 1.3 collective-permute-start.3
  71.2 1.6 fusion.23
  72.8 1.6 bitcast_add_fusion
  74.4 11.5 %collective-permute-done.2 = f32[1,384,256]{2,1,0:T(8,128)S(1)} collective-permute-done((f32[1,384,256]{2,1,0:T(8,128)S(1)}, f32[1,384,256]{2,1,0:T(8,128)S(1)}, u32[]{:S(2)}, u32[]{:S(2)}) %collective-permute-start.2) | collective-permute-done | bytes 393248 | tf_op jit(solution)/shard_map/ppermute | solution.py:17
  86.4 1.3 collective-permute-start.4
  88.4 5.0 %collective-permute-start.5 = (f32[1,384,256]{2,1,0:T(8,128)S(1)}, f32[1,384,256]{2,1,0:T(8,128)S(1)}, u32[]{:S(2)}, u32[]{:S(2)}) collective-permute-start(f32[1,384,256]{2,1,0:T(8,128)S(1)} %slice.249), channel_id=1, source_target_pairs={{0,4},{4,8},{8,12},{12,16},{16,20},{20,24},{24,28},{1,5},{5,9},{9,... | collective-permute-start | bytes 1179656 | tf_op jit(solution)/shard_map/ppermute | solution.py:17
  93.5 2.2 collective-permute-done.4
  96.3 8.0 %collective-permute-done.5 = f32[1,384,256]{2,1,0:T(8,128)S(1)} collective-permute-done((f32[1,384,256]{2,1,0:T(8,128)S(1)}, f32[1,384,256]{2,1,0:T(8,128)S(1)}, u32[]{:S(2)}, u32[]{:S(2)}) %collective-permute-start.5) | collective-permute-done | bytes 393248 | tf_op jit(solution)/shard_map/ppermute | solution.py:17
  104.3 1.8 fusion
  106.1 39.8 %psum.14 = f32[2,256]{1,0:T(2,128)S(1)} all-reduce(f32[2,256]{1,0:T(2,128)S(1)} %pad_maximum_fusion.4), channel_id=1, replica_groups=mesh['row'=8,'col'=4] {'row','col'}, use_global_device_ids=true, to_apply=%region_2.0 | all-reduce | flops 512 | bytes 4096 | tf_op jit(solution)/shard_map/psum | solution.py:49
  145.9 1.7 fusion.25
  147.9 1.7 fusion.21
  149.6 0.8 fusion.92
  150.4 1.3 fusion.50
  151.7 1.3 collective-permute-start.6
  153.0 5.5 %collective-permute-start.7 = (bf16[1,384,256]{2,1,0:T(8,128)(2,1)}, bf16[1,384,256]{2,1,0:T(8,128)(2,1)}, u32[]{:S(2)}, u32[]{:S(2)}) collective-permute-start(bf16[1,384,256]{2,1,0:T(8,128)(2,1)} %get-tuple-element.61), channel_id=1, source_target_pairs={{0,4},{4,8},{8,12},{12,16},{16,20},{20,24},{24,28},{1,5},{5,9},{9,... | collective-permute-start | bytes 589832 | tf_op jit(solution)/shard_map/ppermute | solution.py:17
  158.6 38.6 %all-gather.1 = bf16[32,6,256]{2,1,0:T(8,128)(2,1)S(1)} all-gather(bf16[1,6,256]{2,1,0:T(8,128)(2,1)S(1)} %fusion.20), channel_id=1, replica_groups=mesh['row'=8,'col'=4] {'row','col'}, dimensions={0}, use_global_device_ids=true | all-gather | bytes 101376 | tf_op jit(solution)/shard_map/all_gather | solution.py:79
  198.0 1.2 fusion.17
  199.1 1.6 convolution_bitcast_fusion
  200.8 1.2 fusion.44
  202.0 3.0 %copy.96 = f32[1536,256]{1,0:T(8,128)} copy(f32[1536,256]{0,1:T(8,128)} %convolution_bitcast_fusion) | data formatting | bytes 3145728 | tf_op jit(solution)/shard_map/dot_general | solution.py:35
  205.0 1.4 fusion.4
  206.4 1.3 collective-permute-start.8
  207.7 1.3 fusion.3
  209.0 1.6 collective-permute-start.9
  210.7 1.5 fusion.24
  212.2 1.7 add_bitcast_fusion.1
  213.9 11.4 %collective-permute-done.8 = f32[1,384,256]{2,1,0:T(8,128)S(1)} collective-permute-done((f32[1,384,256]{2,1,0:T(8,128)S(1)}, f32[1,384,256]{2,1,0:T(8,128)S(1)}, u32[]{:S(2)}, u32[]{:S(2)}) %collective-permute-start.8) | collective-permute-done | bytes 393248 | tf_op jit(solution)/shard_map/ppermute | solution.py:17
  226.1 1.3 collective-permute-start.10
  228.1 5.0 %collective-permute-start.11 = (f32[1,384,256]{2,1,0:T(8,128)S(1)}, f32[1,384,256]{2,1,0:T(8,128)S(1)}, u32[]{:S(2)}, u32[]{:S(2)}) collective-permute-start(f32[1,384,256]{2,1,0:T(8,128)S(1)} %slice.259), channel_id=1, source_target_pairs={{0,4},{4,8},{8,12},{12,16},{16,20},{20,24},{24,28},{1,5},{5,9},{9,... | collective-permute-start | bytes 1179656 | tf_op jit(solution)/shard_map/ppermute | solution.py:17
  233.2 2.2 collective-permute-done.10
  236.0 8.0 %collective-permute-done.11 = f32[1,384,256]{2,1,0:T(8,128)S(1)} collective-permute-done((f32[1,384,256]{2,1,0:T(8,128)S(1)}, f32[1,384,256]{2,1,0:T(8,128)S(1)}, u32[]{:S(2)}, u32[]{:S(2)}) %collective-permute-start.11) | collective-permute-done | bytes 393248 | tf_op jit(solution)/shard_map/ppermute | solution.py:17
  244.8 39.8 %psum.15 = f32[2,256]{1,0:T(2,128)S(1)} all-reduce(f32[2,256]{1,0:T(2,128)S(1)} %pad_maximum_fusion.5), channel_id=1, replica_groups=mesh['row'=8,'col'=4] {'row','col'}, use_global_device_ids=true, to_apply=%region_5.0 | all-reduce | flops 512 | bytes 4096 | tf_op jit(solution)/shard_map/psum | solution.py:49
  284.6 2.8 add_bitcast_fusion
  (71 shorter events, 5.9 us)
Async XLA Ops:
  0.0 87.7 %copy-start = (bf16[4,1,384,384]{3,2,1,0:T(8,128)(2,1)S(1)}, bf16[4,1,384,384]{3,2,1,0:T(8,128)(2,1)}, u32[]{:S(2)}) copy-start(bf16[4,1,384,384]{3,2,1,0:T(8,128)(2,1)} %param.17) | copy-start | bytes 3538948
  1.9 63.7 %collective-permute-start = (bf16[1,384,256]{2,1,0:T(8,128)(2,1)}, bf16[1,384,256]{2,1,0:T(8,128)(2,1)}, u32[]{:S(2)}, u32[]{:S(2)}) collective-permute-start(bf16[1,384,256]{2,1,0:T(8,128)(2,1)} %get-tuple-element.64), channel_id=1, source_target_pairs={{4,0},{8,4},{12,8},{16,12},{20,16},{24,20},{28,24},{5,1},{9,5},{13... | collective-permute-start | bytes 589832 | tf_op jit(solution)/shard_map/ppermute | solution.py:19
  3.2 65.2 %collective-permute-start.1 = (bf16[1,384,256]{2,1,0:T(8,128)(2,1)}, bf16[1,384,256]{2,1,0:T(8,128)(2,1)}, u32[]{:S(2)}, u32[]{:S(2)}) collective-permute-start(bf16[1,384,256]{2,1,0:T(8,128)(2,1)} %get-tuple-element.63), channel_id=1, source_target_pairs={{0,4},{4,8},{8,12},{12,16},{16,20},{20,24},{24,28},{1,5},{5,9},{9,... | collective-permute-start | bytes 589832 | tf_op jit(solution)/shard_map/ppermute | solution.py:17
  9.4 3.4 %copy-start.1 = (bf16[4,1,384,256]{3,2,1,0:T(8,128)(2,1)S(1)}, bf16[4,1,384,256]{3,2,1,0:T(8,128)(2,1)}, u32[]{:S(2)}) copy-start(bf16[4,1,384,256]{3,2,1,0:T(8,128)(2,1)} %param.15) | copy-start | bytes 2359300
  9.4 3.4 %copy-start.4 = (bf16[5,1,384,384]{3,2,1,0:T(8,128)(2,1)S(1)}, bf16[5,1,384,384]{3,2,1,0:T(8,128)(2,1)}, u32[]{:S(2)}) copy-start(bf16[5,1,384,384]{3,2,1,0:T(8,128)(2,1)} %param.19) | copy-start | bytes 4423684
  9.4 4.4 %copy-start.15 = (bf16[1,1,6,1536]{3,2,1,0:T(8,128)(2,1)S(1)}, bf16[1,1,6,1536]{3,2,1,0:T(8,128)(2,1)}, u32[]{:S(2)}) copy-start(bf16[1,1,6,1536]{3,2,1,0:T(8,128)(2,1)} %param.20) | copy-start | bytes 55300
  67.1 18.9 %collective-permute-start.2 = (f32[1,384,256]{2,1,0:T(8,128)S(1)}, f32[1,384,256]{2,1,0:T(8,128)S(1)}, u32[]{:S(2)}, u32[]{:S(2)}) collective-permute-start(f32[1,384,256]{2,1,0:T(8,128)S(1)} %fusion.6), channel_id=1, source_target_pairs={{0,4},{4,8},{8,12},{12,16},{16,20},{20,24},{24,28},{1,5},{5,9},{9,... | collective-permute-start | bytes 1179656 | tf_op jit(solution)/shard_map/ppermute | solution.py:17
  69.8 16.2 %collective-permute-start.3 = (f32[1,384,256]{2,1,0:T(8,128)S(1)}, f32[1,384,256]{2,1,0:T(8,128)S(1)}, u32[]{:S(2)}, u32[]{:S(2)}) collective-permute-start(f32[1,384,256]{2,1,0:T(8,128)S(1)} %fusion.5), channel_id=1, source_target_pairs={{4,0},{8,4},{12,8},{16,12},{20,16},{24,20},{28,24},{5,1},{9,5},{13... | collective-permute-start | bytes 1179656 | tf_op jit(solution)/shard_map/ppermute | solution.py:19
  71.1 1.6 copy-start.13
  74.4 11.7 %copy-start.9 = (f32[1536,256]{1,0:T(8,128)S(1)}, f32[1536,256]{1,0:T(8,128)}, u32[]{:S(2)}) copy-start(f32[1536,256]{1,0:T(8,128)} %copy.79) | copy-start | bytes 4718596
  86.4 17.9 %copy-start.2 = (f32[4,384,256]{2,1,0:T(8,128)}, f32[4,384,256]{2,1,0:T(8,128)S(1)}, u32[]{:S(2)}) copy-start(f32[4,384,256]{2,1,0:T(8,128)S(1)} %get-tuple-element.60) | copy-start | bytes 4718596
  86.4 9.3 %collective-permute-start.4 = (bf16[1,384,256]{2,1,0:T(8,128)(2,1)S(1)}, bf16[1,384,256]{2,1,0:T(8,128)(2,1)S(1)}, u32[]{:S(2)}, u32[]{:S(2)}) collective-permute-start(bf16[1,384,256]{2,1,0:T(8,128)(2,1)S(1)} %slice.337), channel_id=1, source_target_pairs={{4,0},{8,4},{12,8},{16,12},{20,16},{24,20},{28,24},{5,1},{9,5},{13... | collective-permute-start | bytes 589832 | tf_op jit(solution)/shard_map/ppermute | solution.py:19
  88.4 5.1 %copy-start.7 = (f32[4,384,256]{2,1,0:T(8,128)}, f32[4,384,256]{2,1,0:T(8,128)S(1)}, u32[]{:S(2)}) copy-start(f32[4,384,256]{2,1,0:T(8,128)S(1)} %convolution_bitcast_fusion.3) | copy-start | bytes 4718596
  88.4 15.9 %collective-permute-start.5 = (f32[1,384,256]{2,1,0:T(8,128)S(1)}, f32[1,384,256]{2,1,0:T(8,128)S(1)}, u32[]{:S(2)}, u32[]{:S(2)}) collective-permute-start(f32[1,384,256]{2,1,0:T(8,128)S(1)} %slice.249), channel_id=1, source_target_pairs={{0,4},{4,8},{8,12},{12,16},{16,20},{20,24},{24,28},{1,5},{5,9},{9,... | collective-permute-start | bytes 1179656 | tf_op jit(solution)/shard_map/ppermute | solution.py:17
  93.5 10.8 %slice-start = ((f32[4,384,256]{2,1,0:T(8,128)}), f32[3,384,256]{2,1,0:T(8,128)S(1)}, s32[]{:S(2)}) async-start(f32[4,384,256]{2,1,0:T(8,128)} %copy-done.7), calls=%async_computation | async-start | bytes 2359296 | tf_op jit(solution)/shard_map/slice | solution.py:60
  93.5 10.8 %copy-start.11 = (bf16[4,1,384,384]{3,2,1,0:T(8,128)(2,1)S(1)}, bf16[4,1,384,384]{3,2,1,0:T(8,128)(2,1)}, u32[]{:S(2)}) copy-start(bf16[4,1,384,384]{3,2,1,0:T(8,128)(2,1)} %param.16) | copy-start | bytes 3538948
  145.9 2.0 copy-start.6
  149.6 48.4 %copy-start.16 = (bf16[192,192]{1,0:T(8,128)(2,1)S(1)}, bf16[192,192]{1,0:T(8,128)(2,1)}, u32[]{:S(2)}) copy-start(bf16[192,192]{1,0:T(8,128)(2,1)} %param.21) | copy-start | bytes 221188
  151.7 53.4 %collective-permute-start.6 = (bf16[1,384,256]{2,1,0:T(8,128)(2,1)}, bf16[1,384,256]{2,1,0:T(8,128)(2,1)}, u32[]{:S(2)}, u32[]{:S(2)}) collective-permute-start(bf16[1,384,256]{2,1,0:T(8,128)(2,1)} %get-tuple-element.62), channel_id=1, source_target_pairs={{4,0},{8,4},{12,8},{16,12},{20,16},{24,20},{28,24},{5,1},{9,5},{13... | collective-permute-start | bytes 589832 | tf_op jit(solution)/shard_map/ppermute | solution.py:19
  153.0 54.8 %collective-permute-start.7 = (bf16[1,384,256]{2,1,0:T(8,128)(2,1)}, bf16[1,384,256]{2,1,0:T(8,128)(2,1)}, u32[]{:S(2)}, u32[]{:S(2)}) collective-permute-start(bf16[1,384,256]{2,1,0:T(8,128)(2,1)} %get-tuple-element.61), channel_id=1, source_target_pairs={{0,4},{4,8},{8,12},{12,16},{16,20},{20,24},{24,28},{1,5},{5,9},{9,... | collective-permute-start | bytes 589832 | tf_op jit(solution)/shard_map/ppermute | solution.py:17
  205.0 5.6 %copy-start.5 = (bf16[5,1,384,384]{3,2,1,0:T(8,128)(2,1)S(1)}, bf16[5,1,384,384]{3,2,1,0:T(8,128)(2,1)}, u32[]{:S(2)}) copy-start(bf16[5,1,384,384]{3,2,1,0:T(8,128)(2,1)} %param.19) | copy-start | bytes 4423684
  206.4 18.9 %collective-permute-start.8 = (f32[1,384,256]{2,1,0:T(8,128)S(1)}, f32[1,384,256]{2,1,0:T(8,128)S(1)}, u32[]{:S(2)}, u32[]{:S(2)}) collective-permute-start(f32[1,384,256]{2,1,0:T(8,128)S(1)} %fusion.4), channel_id=1, source_target_pairs={{0,4},{4,8},{8,12},{12,16},{16,20},{20,24},{24,28},{1,5},{5,9},{9,... | collective-permute-start | bytes 1179656 | tf_op jit(solution)/shard_map/ppermute | solution.py:17
  209.0 3.1 %copy-start.14 = (f32[4,256,384]{1,2,0:T(8,128)S(1)}, f32[4,256,384]{1,2,0:T(8,128)}, u32[]{:S(2)}) copy-start(f32[4,256,384]{1,2,0:T(8,128)} %fusion.21) | copy-start | bytes 4718596
  209.0 16.3 %collective-permute-start.9 = (f32[1,384,256]{2,1,0:T(8,128)S(1)}, f32[1,384,256]{2,1,0:T(8,128)S(1)}, u32[]{:S(2)}, u32[]{:S(2)}) collective-permute-start(f32[1,384,256]{2,1,0:T(8,128)S(1)} %fusion.3), channel_id=1, source_target_pairs={{4,0},{8,4},{12,8},{16,12},{20,16},{24,20},{28,24},{5,1},{9,5},{13... | collective-permute-start | bytes 1179656 | tf_op jit(solution)/shard_map/ppermute | solution.py:19
  212.2 13.3 %copy-start.10 = (f32[1536,256]{1,0:T(8,128)S(1)}, f32[1536,256]{1,0:T(8,128)}, u32[]{:S(2)}) copy-start(f32[1536,256]{1,0:T(8,128)} %copy.96) | copy-start | bytes 4718596
  213.9 11.6 %copy-start.3 = (f32[4,384,256]{2,1,0:T(8,128)S(1)}, f32[4,384,256]{2,1,0:T(8,128)}, u32[]{:S(2)}) copy-start(f32[4,384,256]{2,1,0:T(8,128)} %get-tuple-element.69) | copy-start | bytes 4718596
  226.1 9.3 %collective-permute-start.10 = (bf16[1,384,256]{2,1,0:T(8,128)(2,1)S(1)}, bf16[1,384,256]{2,1,0:T(8,128)(2,1)S(1)}, u32[]{:S(2)}, u32[]{:S(2)}) collective-permute-start(bf16[1,384,256]{2,1,0:T(8,128)(2,1)S(1)} %slice.336), channel_id=1, source_target_pairs={{4,0},{8,4},{12,8},{16,12},{20,16},{24,20},{28,24},{5,1},{9,5},{13... | collective-permute-start | bytes 589832 | tf_op jit(solution)/shard_map/ppermute | solution.py:19
  228.0 5.1 %copy-start.8 = (f32[4,384,256]{2,1,0:T(8,128)}, f32[4,384,256]{2,1,0:T(8,128)S(1)}, u32[]{:S(2)}) copy-start(f32[4,384,256]{2,1,0:T(8,128)S(1)} %convolution_bitcast_fusion.2) | copy-start | bytes 4718596
  228.1 15.9 %collective-permute-start.11 = (f32[1,384,256]{2,1,0:T(8,128)S(1)}, f32[1,384,256]{2,1,0:T(8,128)S(1)}, u32[]{:S(2)}, u32[]{:S(2)}) collective-permute-start(f32[1,384,256]{2,1,0:T(8,128)S(1)} %slice.259), channel_id=1, source_target_pairs={{0,4},{4,8},{8,12},{12,16},{16,20},{20,24},{24,28},{1,5},{5,9},{9,... | collective-permute-start | bytes 1179656 | tf_op jit(solution)/shard_map/ppermute | solution.py:17
  233.2 10.8 %slice-start.1 = ((f32[4,384,256]{2,1,0:T(8,128)}), f32[3,384,256]{2,1,0:T(8,128)S(1)}, s32[]{:S(2)}) async-start(f32[4,384,256]{2,1,0:T(8,128)} %copy-done.8), calls=%async_computation.1 | async-start | bytes 2359296 | tf_op jit(solution)/shard_map/slice | solution.py:60
  233.2 10.8 %copy-start.12 = (bf16[4,1,384,384]{3,2,1,0:T(8,128)(2,1)S(1)}, bf16[4,1,384,384]{3,2,1,0:T(8,128)(2,1)}, u32[]{:S(2)}) copy-start(bf16[4,1,384,384]{3,2,1,0:T(8,128)(2,1)} %param.16) | copy-start | bytes 3538948
where the time goes:
time: 288 us; the launch traced here: 287 us
  blocking collectives  161 us (56%)
  waiting for transfers between devices  43.3 us (15%)
  matrix products  32.6 us (11%)
  starting transfers between devices  32.4 us (11%)
  local copies, waits for them, and re-layouts  11.5 us (4%)
  other arithmetic  5.72 us (2%)
    all_gather x2, blocking collectives, precondition(): lax.all_gather(coarse_rhs, ('row', 'col'), axis=0, tiled=True)  81.8 us
    psum x2, blocking collectives, global_sums(): return lax.psum(values, ('row', 'col'))  79.6 us
    ppermute x6, waiting for transfers between devices, with_halo(): lax.ppermute(tail, axis, [(i, (i + 1) % count) for i in range(ends)])  38.9 us
    ppermute x6, starting transfers between devices, with_halo(): lax.ppermute(tail, axis, [(i, (i + 1) % count) for i in range(ends)])  24.4 us
    dot_general x8, matrix products, apply_blocks(): jnp.einsum('nij,njr->nir', blocks, vectors, preferred_element_type=jnp.fl...  11.9 us
    dot_general x8, matrix products, times_plain(): return jnp.dot(matrix, vectors, preferred_element_type=jnp.float32)  8.16 us
    ppermute x6, starting transfers between devices, with_halo(): lax.ppermute(head, axis, [((i + 1) % count, i) for i in range(ends)])  8.05 us
    dot_general x6, matrix products, times_transposed(): lax.dot_general(matrix, vectors, (((0,), (0,)), ((), ())), preferred_elem...  7.94 us
  transfers between devices with their start and end apart: 12, of which 6 were waited for; matrix products, arithmetic and copies ran while one was open for 12% of the time, Pallas kernels for 0%

commit v1 on v0

v1 whole, which is shorter than its diff:
```python
import functools

import jax
import jax.numpy as jnp
from jax import lax
from jax.experimental import pallas as pl
from jax.experimental.pallas import tpu as pltpu
from jax.sharding import PartitionSpec as P

BF = jnp.bfloat16
F32 = jnp.float32
ALL = ("row", "col")
PAD = 8


def mm(a, b):
    return lax.dot_general(a, b, (((1,), (0,)), ((), ())), preferred_element_type=F32)


def mmt(a, b):
    return lax.dot_general(a, b, (((0,), (0,)), ((), ())), preferred_element_type=F32)


def is_even():
    return lax.rem(lax.axis_index("row"), 2) == 0


def call(body, outs, args, name, flops=0):
    shapes = [jax.ShapeDtypeStruct(s, d) for s, d in outs]
    total = sum(a.size * a.dtype.itemsize for a in list(args) + shapes)
    return pl.pallas_call(
        body,
        out_shape=shapes,
        in_specs=[pl.BlockSpec(memory_space=pltpu.VMEM)] * len(args),
        out_specs=[pl.BlockSpec(memory_space=pltpu.VMEM)] * len(outs),
        compiler_params=pltpu.CompilerParams(vmem_limit_bytes=24 * 1024 * 1024),
        cost_estimate=pl.CostEstimate(flops=flops, bytes_accessed=total, transcendentals=0),
        name=name,
    )(*args)


def inner_solve(e, ld, lu, y, y0, y5):
    e1, e2, e3, e4 = e[0], e[1], e[2], e[3]
    y0[...] = mm(lu[0], e1)
    y5[...] = mmt(lu[4], e4)
    y[0] = mm(ld[1], e1) + mm(lu[1], e2)
    y[1] = mm(ld[2], e2) + mm(lu[2], e3) + mmt(lu[1], e1)
    y[2] = mm(ld[3], e3) + mm(lu[3], e4) + mmt(lu[2], e2)
    y[3] = mm(ld[4], e4) + mmt(lu[3], e3)


def margin_solve(h2, h1, y0, y5, ld0, ld5, s2, s1):
    even = is_even()
    e0 = jnp.where(even, h2[...], h1[...])
    e5 = jnp.where(even, h1[...], h2[...])
    low = (y0[...] + mm(ld0[0], e0)).astype(BF)
    high = (y5[...] + mm(ld5[0], e5)).astype(BF)
    s2[...] = jnp.where(even, low, high)
    s1[...] = jnp.where(even, high, low)


def add_coarse(h2, h1, y, lu0, lu4, gathered, fpad, fown, basis, p):
    even = is_even()
    e0 = jnp.where(even, h2[...], h1[...])
    e5 = jnp.where(even, h1[...], h2[...])
    g = gathered[...].reshape(-1, gathered.shape[-1])
    v = mm(fpad[...], g).astype(BF)
    u = mmt(fown[...], v).astype(BF)
    size = p.shape[1]
    for k in range(4):
        part = y[k] + mmt(basis[:, k * size : (k + 1) * size], u)
        if k == 0:
            part = part + mmt(lu0[0], e0)
        if k == 3:
            part = part + mm(lu4[0], e5)
        p[k] = part


def join_margins(m2, m1, p, su3, zb, z, s2, s1):
    even = is_even()
    below = jnp.where(even, m2[...], m1[...]).astype(F32)
    above = jnp.where(even, m1[...], m2[...]).astype(F32)
    first = p[0] + below
    last = p[3] + above
    z[0] = first
    z[1] = p[1]
    z[2] = p[2]
    z[3] = last
    fb = first.astype(BF)
    lb = last.astype(BF)
    zb[0] = fb
    zb[1] = p[1].astype(BF)
    zb[2] = p[2].astype(BF)
    zb[3] = lb
    lift = mmt(su3[0], lb).astype(BF)
    s2[...] = jnp.where(even, fb, lift)
    s1[...] = jnp.where(even, lift, fb)


def colsum(x):
    return jnp.sum(x, axis=0, keepdims=True)


def inner_operate(zb, z, r, sd, su, w, wt, rho):
    acc = jnp.zeros_like(rho)
    for k in range(4):
        if k == 0:
            w[k] = mm(su[k], zb[k + 1])
        elif k < 3:
            w[k] = mm(su[k], zb[k + 1]) + mmt(su[k - 1], zb[k - 1])
        else:
            w[k] = mmt(su[k - 1], zb[k - 1])
        own = mm(sd[k], zb[k])
        wt[k] = mmt(sd[k], zb[k]) - own
        w[k] = w[k] + own
        acc = acc + colsum(r[k].astype(F32) * z[k])
    rho[...] = acc


def join_operate(n2, n1, w, su3, basis, wf, wb, g, s2, s1):
    even = is_even()
    below = jnp.where(even, n2[...], n1[...]).astype(F32)
    above = jnp.where(even, n1[...], n2[...])
    first = w[0] + below
    last = w[3] + mm(su3[0], above)
    fb = first.astype(BF)
    lb = last.astype(BF)
    s2[...] = jnp.where(even, fb, lb)
    s1[...] = jnp.where(even, lb, fb)
    wf[0] = first
    wf[1] = w[1]
    wf[2] = w[2]
    wf[3] = last
    wb[0] = fb
    wb[1] = w[1].astype(BF)
    wb[2] = w[2].astype(BF)
    wb[3] = lb
    flat = wb[...].reshape(-1, wb.shape[-1])
    out = mm(basis[...], flat).astype(BF)
    for k in range(g.shape[0]):
        g[k] = out


def coarse_rhs(e, basis, g):
    out = mm(basis[...], e[...].reshape(-1, e.shape[-1])).astype(BF)
    for k in range(g.shape[0]):
        g[k] = out


def join_second(m2, m1, p, q, s):
    even = is_even()
    below = jnp.where(even, m2[...], m1[...]).astype(F32)
    above = jnp.where(even, m1[...], m2[...]).astype(F32)
    first = p[0] + below
    q[0] = first
    q[1] = p[1]
    q[2] = p[2]
    q[3] = p[3] + above
    s[...] = first.astype(BF)


def inner_products(q, z, r, w, wt, sd, su, sums, edge):
    d0 = s1 = s2 = s3 = s5 = jnp.zeros((1, q.shape[-1]), F32)
    for k in range(4):
        qk = q[k]
        qb = qk.astype(BF)
        wk = w[k]
        part = mm(sd[k], qb)
        if k < 3:
            part = part + 2.0 * mm(su[k], q[k + 1].astype(BF))
        else:
            edge[...] = 2.0 * mmt(su[k], qb)
        d0 = d0 + colsum(z[k] * wk)
        s1 = s1 + colsum(r[k].astype(F32) * qk)
        s2 = s2 + colsum(wk * qk)
        s3 = s3 + colsum((wk + wt[k]) * qk)
        s5 = s5 + colsum(qk * part)
    sums[0:1] = d0
    sums[1:2] = s1
    sums[2:3] = s2
    sums[3:4] = s3
    sums[4:5] = s5


def join_sums(t, edge, sums, rho, out):
    s5 = sums[4:5] + colsum(edge[...] * t[...].astype(F32))
    full = jnp.concatenate([rho[...], sums[0:4], s5, rho[...], rho[...]], axis=0)
    for k in range(out.shape[0]):
        out[k] = full


def finish(parts, z, q, x):
    total = parts[0]
    for k in range(1, parts.shape[0]):
        total = total + parts[k]
    rho0, d0, s1, s2, s3, s5 = (total[k : k + 1] for k in range(6))
    a0 = rho0 / d0
    rho1 = a0 * (a0 * s2 - s1)
    grow = 1.0 + rho1 / rho0
    a1 = rho1 / (grow * grow * d0 - grow * a0 * (s3 + s2) + a0 * a0 * s5)
    cz = a0 + a1 * grow
    cq = a1 * a0
    for k in range(4):
        x[k] = cz * z[k] - cq * q[k]


def swap_pairs(count):
    first = [(i, i + 1) for i in range(1, count - 1, 2)]
    second = [(i, i + 1) for i in range(0, count - 1, 2)]
    both = lambda pairs: pairs + [(b, a) for a, b in pairs]
    return both(first), both(second)


def swap(s2, s1):
    odd_even, even_odd = swap_pairs(lax.axis_size("row"))
    return lax.ppermute(s2, "row", odd_even), lax.ppermute(s1, "row", even_odd)


def gather(copies):
    return lax.all_to_all(copies, ALL, 0, 0)


def on_device(rhs, stiff_diag, stiff_upper, local_diag, local_upper, coarse_basis, coarse_factor):
    r = rhs[:, 0]
    sd, su, ld, lu = stiff_diag[:, 0], stiff_upper[:, 0], local_diag[:, 0], local_upper[:, 0]
    layers, size, cols = r.shape
    devices = lax.axis_size("row") * lax.axis_size("col")
    rows = lax.axis_size("row")
    ncb = coarse_basis.shape[2]
    layer = (size, cols)
    own = lax.axis_index("row") * lax.axis_size("col") + lax.axis_index("col")

    even = lax.rem(lax.axis_index("row"), 2) == 0
    low, high = r[0], r[-1]
    h2, h1 = swap(jnp.where(even, low, high), jnp.where(even, high, low))

    basis = jnp.pad(coarse_basis[0, 0], ((0, PAD - ncb), (0, 0)))
    nco = coarse_factor.shape[0]
    wide = lax.broadcasted_iota(jnp.int32, (nco, devices * PAD), 1)
    narrow = lax.broadcasted_iota(jnp.int32, (nco, devices * PAD), 0)
    spread = ((wide // PAD == narrow // ncb) & (wide % PAD == narrow % ncb)).astype(BF)
    fpad = jnp.dot(coarse_factor, spread, preferred_element_type=F32).astype(BF)
    fown = lax.dynamic_slice_in_dim(fpad, own * PAD, PAD, 1)

    ld0, ld5, lu0, lu4, su3 = ld[0:1], ld[-1:], lu[0:1], lu[-1:], su[-1:]
    block = 2 * size * size * cols

    def precondition(e, halo, copies):
        h2, h1 = halo
        gathered = gather(copies)
        y, y0, y5 = call(inner_solve, [((layers,) + layer, F32), (layer, F32), (layer, F32)], (e, ld, lu), "inner_solve", 12 * block)
        sends = call(margin_solve, [(layer, BF)] * 2, (h2, h1, y0, y5, ld0, ld5), "margin_solve", 2 * block)
        margins = swap(*sends)
        (p,) = call(add_coarse, [((layers,) + layer, F32)], (h2, h1, y, lu0, lu4, gathered, fpad, fown, basis), "add_coarse", 3 * block)
        return margins, p

    (copies0,) = call(coarse_rhs, [((devices, PAD, cols), BF)], (r, basis), "coarse_rhs", block // 32)
    (m2, m1), p = precondition(r, (h2, h1), copies0)
    zb, z, s2, s1 = call(
        join_margins, [((layers,) + layer, BF), ((layers,) + layer, F32), (layer, BF), (layer, BF)], (m2, m1, p, su3), "join_margins", block
    )
    n2, n1 = swap(s2, s1)
    w, wt, rho = call(
        inner_operate, [((layers,) + layer, F32)] * 2 + [((1, cols), F32)], (zb, z, r, sd, su), "inner_operate", 14 * block
    )
    wf, wb, copies1, s2, s1 = call(
        join_operate,
        [((layers,) + layer, F32), ((layers,) + layer, BF), ((devices, PAD, cols), BF), (layer, BF), (layer, BF)],
        (n2, n1, w, su3, basis),
        "join_operate",
        block,
    )
    (m2, m1), p = precondition(wb, swap(s2, s1), copies1)
    q, low = call(join_second, [((layers,) + layer, F32), (layer, BF)], (m2, m1, p), "join_second")
    t = lax.ppermute(low, "row", [(i + 1, i) for i in range(rows - 1)])
    sums, edge = call(
        inner_products, [((PAD, cols), F32), (layer, F32)], (q, z, r, wf, wt, sd, su), "inner_products", 8 * block
    )
    (copies,) = call(join_sums, [((devices, PAD, cols), F32)], (t, edge, sums, rho), "join_sums")
    (x,) = call(finish, [((layers,) + layer, F32)], (gather(copies), z, q), "finish")
    return x[:, None]


def solution(mesh):
    split = P("row", "col", None, None)
    return jax.shard_map(on_device, mesh=mesh, in_specs=(split,) * 6 + (P(),), out_specs=split, check_vma=False)
```

time: 288 us -> 118 us (0.41)
  blocking collectives: 161 us -> 16.1 us
  matrix products: 32.6 us -> 0.37 us
  waiting for transfers between devices: 43.3 us -> 20.3 us
  Pallas kernels: 0 us -> 16.8 us
  local copies, waits for them, and re-layouts: 11.5 us -> 23.3 us
  starting transfers between devices: 32.4 us -> 38.2 us
  other arithmetic: 5.72 us -> 1.24 us
    all_gather x2 -> x0, blocking collectives: 81.8 us -> none  [precondition(): lax.all_gather(coarse_rhs, ('row', 'col'), axis=0, tiled=True)]
    psum x2 -> x0, blocking collectives: 79.6 us -> none  [global_sums(): return lax.psum(values, ('row', 'col'))]
    dot_general x26 -> x1, matrix products: 32.6 us -> 0.37 us  [on_device(): fpad = jnp.dot(coarse_factor, spread, preferred_element_type=F32).astype(BF)]
    ppermute x12 -> x11, waiting for transfers between devices: 43.3 us -> 20.3 us  [the longest x5 13.3 us: swap(): lax.ppermute(s1, 'row', even_odd)]
    unnamed x36 -> x80, local copies, waits for them, and re-layouts: 2.54 us -> 19.8 us
    pallas_call x0 -> x14, Pallas kernels: none -> 16.8 us  [call(): pl.pallas_call(body, out_shape=shapes, in_specs=[pl.BlockSpec(memory_spac...]
    all_to_all x0 -> x1, blocking collectives: none -> 16.1 us  [gather(): return lax.all_to_all(copies, ALL, 0, 0)]
    all_to_all x0 -> x2, starting transfers between devices: none -> 10.7 us  [gather(): return lax.all_to_all(copies, ALL, 0, 0)]
  transfers between devices with their start and end apart: 12 -> 13, of which waited for: 6 -> 5; matrix products, arithmetic and copies ran while one was open for 12% -> 4% of each run, Pallas kernels for 0% -> 10%
where the time goes in v1:
time: 118 us; the launch traced here: 117 us
  starting transfers between devices  38.2 us (32%)
  local copies, waits for them, and re-layouts  23.3 us (20%)
  waiting for transfers between devices  20.3 us (17%)
  Pallas kernels  16.8 us (14%)
  blocking collectives  16.1 us (14%)
  other arithmetic  1.24 us (1%)
    ppermute x5, starting transfers between devices, swap(): lax.ppermute(s1, 'row', even_odd)  22.9 us
    unnamed x80, local copies, waits for them, and re-layouts  19.8 us
    pallas_call x14, Pallas kernels, call(): pl.pallas_call(body, out_shape=shapes, in_specs=[pl.BlockSpec(memory_spac...  16.8 us
    all_to_all x1, blocking collectives, gather(): return lax.all_to_all(copies, ALL, 0, 0)  16.1 us
    ppermute x5, waiting for transfers between devices, swap(): lax.ppermute(s1, 'row', even_odd)  13.3 us
    all_to_all x2, starting transfers between devices, gather(): return lax.all_to_all(copies, ALL, 0, 0)  10.7 us
    ppermute x1, waiting for transfers between devices, on_device(): t = lax.ppermute(low, 'row', [(i + 1, i) for i in range(rows - 1)])  7.03 us
    ppermute x5, starting transfers between devices, swap(): lax.ppermute(s2, 'row', odd_even)  3.32 us
  transfers between devices with their start and end apart: 13, of which 5 were waited for; matrix products, arithmetic and copies ran while one was open for 4% of the time, Pallas kernels for 10%

profile of v1, /device:TPU:0, one launch (start us, length us, event | category | flops | bytes accessed | tf_op | source)
XLA Modules:
  0.0 116.9 jit_solution(13113744284400779574)
XLA Ops:
  0.0 0.8 pad.4.basis
  0.8 1.1 copy-done.1
  1.9 0.9 coarse_rhs.1
  3.4 7.4 %all-to-all-start = ((bf16[32,8,256]{2,1,0:T(8,128)(2,1)}), bf16[32,8,256]{2,1,0:T(8,128)(2,1)}, u32[]{:S(2)}, u32[]{:S(2)}) async-start(bf16[32,8,256]{2,1,0:T(8,128)(2,1)} %coarse_rhs.1), calls=%async_computation | async-start | bytes 262144 | tf_op jit(solution)/shard_map/all_to_all | solution.py:220
  10.9 1.2 %select_bitcast_fusion = (bf16[384,256]{1,0:T(8,128)(2,1)S(1)}, bf16[384,256]{1,0:T(8,128)(2,1)S(1)}) fusion(pred[]{:T(512)S(6)} %eq.12, bf16[4,1,384,256]{3,2,1,0:T(8,128)(2,1)} %param.7), kind=kLoop, calls=%fused_computation.8 | loop fusion | flops 196608 | bytes 786433 | tf_op jit(solution)/shard_map/jit(_where)/select_n | solution.py:235
  12.1 1.8 %collective-permute-start.1 = (bf16[384,256]{1,0:T(8,128)(2,1)S(1)}, bf16[384,256]{1,0:T(8,128)(2,1)S(1)}, u32[]{:S(2)}, u32[]{:S(2)}) collective-permute-start(bf16[384,256]{1,0:T(8,128)(2,1)S(1)} %get-tuple-element.61), channel_id=1, source_target_pairs={{0,4},{8,12},{16,20},{24,28},{4,0},{12,8},{20,16},{28,24},{1,5},{9... | collective-permute-start | bytes 589832 | tf_op jit(solution)/shard_map/ppermute | solution.py:216
  14.7 1.3 %slice_bitcast_fusion.1 = (bf16[1,384,384]{2,1,0:T(8,128)(2,1)S(1)}, bf16[1,384,384]{2,1,0:T(8,128)(2,1)S(1)}) fusion(bf16[5,1,384,384]{3,2,1,0:T(8,128)(2,1)} %param.11), kind=kLoop, calls=%fused_computation.2 | loop fusion | bytes 1179648 | tf_op jit(solution)/shard_map/slice | solution.py:245
  16.0 1.4 %inner_solve.2 = (f32[4,384,256]{2,1,0:T(8,128)S(1)}, f32[384,256]{1,0:T(8,128)S(1)}, f32[384,256]{1,0:T(8,128)S(1)}) custom-call(bf16[4,384,256]{2,1,0:T(8,128)(2,1)S(1)} %bitcast.28, bf16[6,384,384]{2,1,0:T(8,128)(2,1)S(1)} %bitcast.31, bf16[5,384,384]{2,1,0:T(8,128)(2,1)S(1)} %bitcast.33), custom_call_target="tpu_custom_call" | custom-call | flops 905969664 | bytes 6389760 | tf_op jit(solution)/shard_map/inner_solve/pallas_call | solution.py:31
  17.4 1.2 %slice_bitcast_fusion.su3 = bf16[1,384,384]{2,1,0:T(8,128)(2,1)S(1)} fusion(bf16[4,1,384,384]{3,2,1,0:T(8,128)(2,1)} %param.9), kind=kLoop, calls=%fused_computation.1 | loop fusion | bytes 589824 | tf_op jit(solution)/shard_map/slice | solution.py:245
  18.7 4.5 %collective-permute-done.1.h1 = bf16[384,256]{1,0:T(8,128)(2,1)S(1)} collective-permute-done((bf16[384,256]{1,0:T(8,128)(2,1)S(1)}, bf16[384,256]{1,0:T(8,128)(2,1)S(1)}, u32[]{:S(2)}, u32[]{:S(2)}) %collective-permute-start.1) | collective-permute-done | bytes 196640 | tf_op jit(solution)/shard_map/ppermute | solution.py:216
  24.6 5.4 %collective-permute-start.3 = (bf16[384,256]{1,0:T(8,128)(2,1)S(1)}, bf16[384,256]{1,0:T(8,128)(2,1)S(1)}, u32[]{:S(2)}, u32[]{:S(2)}) collective-permute-start(bf16[384,256]{1,0:T(8,128)(2,1)S(1)} %get-tuple-element.34), channel_id=1, source_target_pairs={{0,4},{8,12},{16,20},{24,28},{4,0},{12,8},{20,16},{28,24},{1,5},{9... | collective-permute-start | bytes 589832 | tf_op jit(solution)/shard_map/ppermute | solution.py:216
  30.5 1.4 %copy-done.20 = f32[4,384,256]{2,1,0:T(8,128)S(1)} copy-done((f32[4,384,256]{2,1,0:T(8,128)S(1)}, f32[4,384,256]{2,1,0:T(8,128)}, u32[]{:S(2)}) %copy-start.20) | copy-done | bytes 1572888
  31.9 0.9 copy-done.24
  32.8 1.9 %add_coarse.2.p = f32[4,384,256]{2,1,0:T(8,128)S(1)} custom-call(bf16[384,256]{1,0:T(8,128)(2,1)S(1)} %copy-done.24, bf16[384,256]{1,0:T(8,128)(2,1)S(1)} %collective-permute-done.1.h1, f32[4,384,256]{2,1,0:T(8,128)S(1)} %copy-done.20, bf16[1,384,384]{2,1,0:T(8,128)(2,1)S(1)} %get-tuple-element.60.lu0, bf16[1,384,384]{2,1,0:T(8,128)(2,1)S(1)} %get-tuple-element.59.lu4, ...), custom_call_target="tpu_custom_call" | custom-call | flops 226492416 | bytes 4385792 | tf_op jit(solution)/shard_map/add_coarse/pallas_call | solution.py:31
  34.8 0.7 copy-done.35
  35.4 1.9 %collective-permute-done.3.m1 = bf16[384,256]{1,0:T(8,128)(2,1)S(1)} collective-permute-done((bf16[384,256]{1,0:T(8,128)(2,1)S(1)}, bf16[384,256]{1,0:T(8,128)(2,1)S(1)}, u32[]{:S(2)}, u32[]{:S(2)}) %collective-permute-start.3) | collective-permute-done | bytes 196640 | tf_op jit(solution)/shard_map/ppermute | solution.py:216
  37.3 0.7 copy-done.37
  38.0 0.9 copy-done.36
  38.9 0.9 copy-done.38
  40.2 0.7 collective-permute-start.4
  40.9 5.4 %collective-permute-start.5 = (bf16[384,256]{1,0:T(8,128)(2,1)S(1)}, bf16[384,256]{1,0:T(8,128)(2,1)S(1)}, u32[]{:S(2)}, u32[]{:S(2)}) collective-permute-start(bf16[384,256]{1,0:T(8,128)(2,1)S(1)} %get-tuple-element.37), channel_id=1, source_target_pairs={{0,4},{8,12},{16,20},{24,28},{4,0},{12,8},{20,16},{28,24},{1,5},{9... | collective-permute-start | bytes 589832 | tf_op jit(solution)/shard_map/ppermute | solution.py:216
  46.3 1.6 %inner_operate.1 = (f32[4,384,256]{2,1,0:T(8,128)S(1)}, f32[4,384,256]{2,1,0:T(8,128)S(1)}, f32[1,256]{1,0:T(1,128)S(1)}) custom-call(bf16[4,384,256]{2,1,0:T(8,128)(2,1)S(1)} %get-tuple-element.38.zb, f32[4,384,256]{2,1,0:T(8,128)S(1)} %get-tuple-element.39.z, bf16[4,384,256]{2,1,0:T(8,128)(2,1)S(1)} %bitcast.29, bf16[4,384,384]{2,1,0:T(8,128)(2,1)S(1)} %bitcast.37, ...), custom_call_target="tpu_custom_call" | custom-call | flops 1056964608 | bytes 8651776 | tf_op jit(solution)/shard_map/inner_operate/pallas_call | solution.py:31
  47.9 1.2 %copy-done.15 = f32[4,384,256]{2,1,0:T(8,128)} copy-done((f32[4,384,256]{2,1,0:T(8,128)}, f32[4,384,256]{2,1,0:T(8,128)S(1)}, u32[]{:S(2)}) %copy-start.15) | copy-done | bytes 1572888
  49.1 4.9 %collective-permute-done.5.n1 = bf16[384,256]{1,0:T(8,128)(2,1)S(1)} collective-permute-done((bf16[384,256]{1,0:T(8,128)(2,1)S(1)}, bf16[384,256]{1,0:T(8,128)(2,1)S(1)}, u32[]{:S(2)}, u32[]{:S(2)}) %collective-permute-start.5) | collective-permute-done | bytes 196640 | tf_op jit(solution)/shard_map/ppermute | solution.py:216
  54.0 1.2 %join_operate.1 = (f32[4,384,256]{2,1,0:T(8,128)S(1)}, bf16[4,384,256]{2,1,0:T(8,128)(2,1)S(1)}, bf16[32,8,256]{2,1,0:T(8,128)(2,1)S(1)}, bf16[384,256]{1,0:T(8,128)(2,1)}, bf16[384,256]{1,0:T(8,128)(2,1)}) custom-call(bf16[384,256]{1,0:T(8,128)(2,1)S(1)} %collective-permute-done.4.n2, bf16[384,256]{1,0:T(8,128)(2,1)S(1)} %collective-permute-done.5.n1, ...), custom_call_target="tpu_custom_call" | custom-call | flops 75497472 | bytes 5169152 | tf_op jit(solution)/shard_map/join_operate/pallas_call | solution.py:31
  55.2 1.1 copy-done.17
  56.3 0.9 copy-done.25
  57.9 5.4 %collective-permute-start.7 = (bf16[384,256]{1,0:T(8,128)(2,1)}, bf16[384,256]{1,0:T(8,128)(2,1)}, u32[]{:S(2)}, u32[]{:S(2)}) collective-permute-start(bf16[384,256]{1,0:T(8,128)(2,1)} %get-tuple-element.42), channel_id=1, source_target_pairs={{0,4},{8,12},{16,20},{24,28},{4,0},{12,8},{20,16},{28,24},{1,5},{9... | collective-permute-start | bytes 589832 | tf_op jit(solution)/shard_map/ppermute | solution.py:216
  63.3 3.3 %all-to-all-start.1 = ((bf16[32,8,256]{2,1,0:T(8,128)(2,1)}), bf16[32,8,256]{2,1,0:T(8,128)(2,1)}, u32[]{:S(2)}, u32[]{:S(2)}) async-start(bf16[32,8,256]{2,1,0:T(8,128)(2,1)} %copy-done.39), calls=%async_computation.1 | async-start | bytes 262144 | tf_op jit(solution)/shard_map/all_to_all | solution.py:220
  66.6 1.5 %copy-done.4 = bf16[6,1,384,384]{3,2,1,0:T(8,128)(2,1)S(1)} copy-done((bf16[6,1,384,384]{3,2,1,0:T(8,128)(2,1)S(1)}, bf16[6,1,384,384]{3,2,1,0:T(8,128)(2,1)}, u32[]{:S(2)}) %copy-start.4) | copy-done | bytes 1769496
  68.1 1.4 %copy-done.6 = bf16[5,1,384,384]{3,2,1,0:T(8,128)(2,1)S(1)} copy-done((bf16[5,1,384,384]{3,2,1,0:T(8,128)(2,1)S(1)}, bf16[5,1,384,384]{3,2,1,0:T(8,128)(2,1)}, u32[]{:S(2)}) %copy-start.6) | copy-done | bytes 1474584
  69.5 1.1 copy-done.26
  70.6 1.4 %inner_solve.3 = (f32[4,384,256]{2,1,0:T(8,128)S(1)}, f32[384,256]{1,0:T(8,128)S(1)}, f32[384,256]{1,0:T(8,128)S(1)}) custom-call(bf16[4,384,256]{2,1,0:T(8,128)(2,1)S(1)} %copy-done.26, bf16[6,384,384]{2,1,0:T(8,128)(2,1)S(1)} %bitcast.32, bf16[5,384,384]{2,1,0:T(8,128)(2,1)S(1)} %bitcast.34), custom_call_target="tpu_custom_call" | custom-call | flops 905969664 | bytes 6389760 | tf_op jit(solution)/shard_map/inner_solve/pallas_call | solution.py:31
  72.0 1.1 copy-done.21
  73.2 2.0 %margin_solve.3 = (bf16[384,256]{1,0:T(8,128)(2,1)}, bf16[384,256]{1,0:T(8,128)(2,1)}) custom-call(bf16[384,256]{1,0:T(8,128)(2,1)S(1)} %collective-permute-done.6.h2, bf16[384,256]{1,0:T(8,128)(2,1)} %collective-permute-done.7.h1, f32[384,256]{1,0:T(8,128)S(1)} %get-tuple-element.44.y0, f32[384,256]{1,0:T(8,128)S(1)} %get-tuple-element.45.y5, ...), custom_call_target="tpu_custom_call" | custom-call | flops 150994944 | bytes 2162688 | tf_op jit(solution)/shard_map/margin_solve/pallas_call | solution.py:31
  75.9 4.9 %collective-permute-start.9 = (bf16[384,256]{1,0:T(8,128)(2,1)}, bf16[384,256]{1,0:T(8,128)(2,1)}, u32[]{:S(2)}, u32[]{:S(2)}) collective-permute-start(bf16[384,256]{1,0:T(8,128)(2,1)} %get-tuple-element.47), channel_id=1, source_target_pairs={{0,4},{8,12},{16,20},{24,28},{4,0},{12,8},{20,16},{28,24},{1,5},{9... | collective-permute-start | bytes 589832 | tf_op jit(solution)/shard_map/ppermute | solution.py:216
  80.8 1.4 %copy-done.22 = f32[4,384,256]{2,1,0:T(8,128)S(1)} copy-done((f32[4,384,256]{2,1,0:T(8,128)S(1)}, f32[4,384,256]{2,1,0:T(8,128)}, u32[]{:S(2)}) %copy-start.22) | copy-done | bytes 1572888
  82.2 0.7 copy-done.30
  82.9 0.9 copy-done.32
  83.8 0.8 copy-done.34
  84.6 2.0 %add_coarse.3.p = f32[4,384,256]{2,1,0:T(8,128)S(1)} custom-call(bf16[384,256]{1,0:T(8,128)(2,1)S(1)} %collective-permute-done.6.h2, bf16[384,256]{1,0:T(8,128)(2,1)} %collective-permute-done.7.h1, f32[4,384,256]{2,1,0:T(8,128)S(1)} %copy-done.22, bf16[1,384,384]{2,1,0:T(8,128)(2,1)S(1)} %get-tuple-element.60.lu0, ...), custom_call_target="tpu_custom_call" | custom-call | flops 226492416 | bytes 4385792 | tf_op jit(solution)/shard_map/add_coarse/pallas_call | solution.py:31
  86.7 2.0 %collective-permute-done.9.m1 = bf16[384,256]{1,0:T(8,128)(2,1)} collective-permute-done((bf16[384,256]{1,0:T(8,128)(2,1)}, bf16[384,256]{1,0:T(8,128)(2,1)}, u32[]{:S(2)}, u32[]{:S(2)}) %collective-permute-start.9) | collective-permute-done | bytes 196640 | tf_op jit(solution)/shard_map/ppermute | solution.py:216
  88.7 1.1 join_second.1
  89.8 1.3 %collective-permute-start.10 = (bf16[384,256]{1,0:T(8,128)(2,1)S(1)}, bf16[384,256]{1,0:T(8,128)(2,1)S(1)}, u32[]{:S(2)}, u32[]{:S(2)}) collective-permute-start(bf16[384,256]{1,0:T(8,128)(2,1)S(1)} %get-tuple-element.50), channel_id=1, source_target_pairs={{4,0},{8,4},{12,8},{16,12},{20,16},{24,20},{28,24},{5,1},{9,5},{13... | collective-permute-start | bytes 589832 | tf_op jit(solution)/shard_map/ppermute | solution.py:275
  91.2 1.1 inner_products.1
  92.2 7.0 %collective-permute-done.10.t = bf16[384,256]{1,0:T(8,128)(2,1)S(1)} collective-permute-done((bf16[384,256]{1,0:T(8,128)(2,1)S(1)}, bf16[384,256]{1,0:T(8,128)(2,1)S(1)}, u32[]{:S(2)}, u32[]{:S(2)}) %collective-permute-start.10) | collective-permute-done | bytes 196640 | tf_op jit(solution)/shard_map/ppermute | solution.py:275
  99.4 16.1 %all_to_all.15.parts = f32[32,8,256]{2,1,0:T(8,128)S(1)} all-to-all(f32[32,8,256]{2,1,0:T(8,128)S(1)} %join_sums.1), channel_id=1, replica_groups=mesh['row'=8,'col'=4] {'row','col'}, dimensions={0} | all-to-all | bytes 524288 | tf_op jit(solution)/shard_map/all_to_all | solution.py:220
  115.5 1.4 %finish.1 = f32[4,384,256]{2,1,0:T(8,128)} custom-call(f32[32,8,256]{2,1,0:T(8,128)S(1)} %all_to_all.15.parts, f32[4,384,256]{2,1,0:T(8,128)S(1)} %get-tuple-element.39.z, f32[4,384,256]{2,1,0:T(8,128)S(1)} %get-tuple-element.51.q), custom_call_target="tpu_custom_call" | custom-call | bytes 4980736 | tf_op jit(solution)/shard_map/finish/pallas_call | solution.py:31
  (86 shorter events, 5.1 us)
Async XLA Ops:
  0.0 29.9 %copy-start = (bf16[192,192]{1,0:T(8,128)(2,1)S(1)}, bf16[192,192]{1,0:T(8,128)(2,1)}, u32[]{:S(2)}) copy-start(bf16[192,192]{1,0:T(8,128)(2,1)} %param.13) | copy-start | bytes 221188
  0.8 1.1 copy-start.1
  1.9 12.7 %copy-start.3 = (bf16[6,1,384,384]{3,2,1,0:T(8,128)(2,1)S(1)}, bf16[6,1,384,384]{3,2,1,0:T(8,128)(2,1)}, u32[]{:S(2)}) copy-start(bf16[6,1,384,384]{3,2,1,0:T(8,128)(2,1)} %param.10) | copy-start | bytes 5308420
  3.4 27.0 %all-to-all-start = ((bf16[32,8,256]{2,1,0:T(8,128)(2,1)}), bf16[32,8,256]{2,1,0:T(8,128)(2,1)}, u32[]{:S(2)}, u32[]{:S(2)}) async-start(bf16[32,8,256]{2,1,0:T(8,128)(2,1)} %coarse_rhs.1), calls=%async_computation | async-start | bytes 262144 | tf_op jit(solution)/shard_map/all_to_all | solution.py:220
  10.8 5.2 %copy-start.2 = (bf16[4,1,384,256]{3,2,1,0:T(8,128)(2,1)S(1)}, bf16[4,1,384,256]{3,2,1,0:T(8,128)(2,1)}, u32[]{:S(2)}) copy-start(bf16[4,1,384,256]{3,2,1,0:T(8,128)(2,1)} %param.7) | copy-start | bytes 2359300
  10.8 5.2 %copy-start.5 = (bf16[5,1,384,384]{3,2,1,0:T(8,128)(2,1)S(1)}, bf16[5,1,384,384]{3,2,1,0:T(8,128)(2,1)}, u32[]{:S(2)}) copy-start(bf16[5,1,384,384]{3,2,1,0:T(8,128)(2,1)} %param.11) | copy-start | bytes 4423684
  12.1 11.1 %collective-permute-start.1 = (bf16[384,256]{1,0:T(8,128)(2,1)S(1)}, bf16[384,256]{1,0:T(8,128)(2,1)S(1)}, u32[]{:S(2)}, u32[]{:S(2)}) collective-permute-start(bf16[384,256]{1,0:T(8,128)(2,1)S(1)} %get-tuple-element.61), channel_id=1, source_target_pairs={{0,4},{8,12},{16,20},{24,28},{4,0},{12,8},{20,16},{28,24},{1,5},{9... | collective-permute-start | bytes 589832 | tf_op jit(solution)/shard_map/ppermute | solution.py:216
  13.8 9.4 %collective-permute-start = (bf16[384,256]{1,0:T(8,128)(2,1)S(1)}, bf16[384,256]{1,0:T(8,128)(2,1)S(1)}, u32[]{:S(2)}, u32[]{:S(2)}) collective-permute-start(bf16[384,256]{1,0:T(8,128)(2,1)S(1)} %get-tuple-element.62), channel_id=1, source_target_pairs={{4,8},{12,16},{20,24},{8,4},{16,12},{24,20},{5,9},{13,17},{21,25},... | collective-permute-start | bytes 589832 | tf_op jit(solution)/shard_map/ppermute | solution.py:216
  14.7 8.6 %copy-start.11 = (bf16[1,384,384]{2,1,0:T(8,128)(2,1)}, bf16[1,384,384]{2,1,0:T(8,128)(2,1)S(1)}, u32[]{:S(2)}) copy-start(bf16[1,384,384]{2,1,0:T(8,128)(2,1)S(1)} %get-tuple-element.57.ld5) | copy-start | bytes 884740
  14.7 8.6 %copy-start.13 = (bf16[1,384,384]{2,1,0:T(8,128)(2,1)}, bf16[1,384,384]{2,1,0:T(8,128)(2,1)S(1)}, u32[]{:S(2)}) copy-start(bf16[1,384,384]{2,1,0:T(8,128)(2,1)S(1)} %get-tuple-element.58.ld0) | copy-start | bytes 884740
  17.4 6.2 %copy-start.19 = (f32[4,384,256]{2,1,0:T(8,128)}, f32[4,384,256]{2,1,0:T(8,128)S(1)}, u32[]{:S(2)}) copy-start(f32[4,384,256]{2,1,0:T(8,128)S(1)} %get-tuple-element.35.y) | copy-start | bytes 4718596
  17.4 13.0 %copy-start.28 = (bf16[8,1536]{1,0:T(8,128)(2,1)S(1)}, bf16[8,1536]{1,0:T(8,128)(2,1)}, u32[]{:S(2)}) copy-start(bf16[8,1536]{1,0:T(8,128)(2,1)} %copy-done.27) | copy-start | bytes 73732
  23.9 10.9 %collective-permute-start.2 = (bf16[384,256]{1,0:T(8,128)(2,1)S(1)}, bf16[384,256]{1,0:T(8,128)(2,1)S(1)}, u32[]{:S(2)}, u32[]{:S(2)}) collective-permute-start(bf16[384,256]{1,0:T(8,128)(2,1)S(1)} %get-tuple-element.33), channel_id=1, source_target_pairs={{4,8},{12,16},{20,24},{8,4},{16,12},{24,20},{5,9},{13,17},{21,25},... | collective-permute-start | bytes 589832 | tf_op jit(solution)/shard_map/ppermute | solution.py:216
  24.6 12.7 %collective-permute-start.3 = (bf16[384,256]{1,0:T(8,128)(2,1)S(1)}, bf16[384,256]{1,0:T(8,128)(2,1)S(1)}, u32[]{:S(2)}, u32[]{:S(2)}) collective-permute-start(bf16[384,256]{1,0:T(8,128)(2,1)S(1)} %get-tuple-element.34), channel_id=1, source_target_pairs={{0,4},{8,12},{16,20},{24,28},{4,0},{12,8},{20,16},{28,24},{1,5},{9... | collective-permute-start | bytes 589832 | tf_op jit(solution)/shard_map/ppermute | solution.py:216
  30.3 4.4 %copy-start.31 = (bf16[256,192]{0,1:T(8,128)(2,1)}, bf16[256,192]{0,1:T(8,128)(2,1)S(1)}, u32[]{:S(2)}) copy-start(bf16[256,192]{0,1:T(8,128)(2,1)S(1)} %convolution_convert_fusion) | copy-start | bytes 294916
  30.4 4.3 %copy-start.33 = (bf16[192,8]{1,0:T(8,128)(2,1)}, bf16[192,8]{1,0:T(8,128)(2,1)S(1)}, u32[]{:S(2)}) copy-start(bf16[192,8]{1,0:T(8,128)(2,1)S(1)} %dynamic-slice_bitcast_fusion.fown) | copy-start | bytes 9220
  30.5 1.4 %copy-start.20 = (f32[4,384,256]{2,1,0:T(8,128)S(1)}, f32[4,384,256]{2,1,0:T(8,128)}, u32[]{:S(2)}) copy-start(f32[4,384,256]{2,1,0:T(8,128)} %copy-done.19) | copy-start | bytes 4718596
  31.9 0.9 copy-start.24
  32.8 13.5 %copy-start.9 = (bf16[4,1,384,384]{3,2,1,0:T(8,128)(2,1)S(1)}, bf16[4,1,384,384]{3,2,1,0:T(8,128)(2,1)}, u32[]{:S(2)}) copy-start(bf16[4,1,384,384]{3,2,1,0:T(8,128)(2,1)} %param.8) | copy-start | bytes 3538948
  34.7 11.6 %copy-start.7 = (bf16[4,1,384,384]{3,2,1,0:T(8,128)(2,1)S(1)}, bf16[4,1,384,384]{3,2,1,0:T(8,128)(2,1)}, u32[]{:S(2)}) copy-start(bf16[4,1,384,384]{3,2,1,0:T(8,128)(2,1)} %param.9) | copy-start | bytes 3538948
  38.0 0.9 copy-start.36
  38.9 0.9 copy-start.38
  40.2 8.9 %collective-permute-start.4 = (bf16[384,256]{1,0:T(8,128)(2,1)S(1)}, bf16[384,256]{1,0:T(8,128)(2,1)S(1)}, u32[]{:S(2)}, u32[]{:S(2)}) collective-permute-start(bf16[384,256]{1,0:T(8,128)(2,1)S(1)} %get-tuple-element.36), channel_id=1, source_target_pairs={{4,8},{12,16},{20,24},{8,4},{16,12},{24,20},{5,9},{13,17},{21,25},... | collective-permute-start | bytes 589832 | tf_op jit(solution)/shard_map/ppermute | solution.py:216
  40.9 13.1 %collective-permute-start.5 = (bf16[384,256]{1,0:T(8,128)(2,1)S(1)}, bf16[384,256]{1,0:T(8,128)(2,1)S(1)}, u32[]{:S(2)}, u32[]{:S(2)}) collective-permute-start(bf16[384,256]{1,0:T(8,128)(2,1)S(1)} %get-tuple-element.37), channel_id=1, source_target_pairs={{0,4},{8,12},{16,20},{24,28},{4,0},{12,8},{20,16},{28,24},{1,5},{9... | collective-permute-start | bytes 589832 | tf_op jit(solution)/shard_map/ppermute | solution.py:216
  46.3 7.7 %copy-start.29 = (bf16[8,1536]{1,0:T(8,128)(2,1)S(1)}, bf16[8,1536]{1,0:T(8,128)(2,1)}, u32[]{:S(2)}) copy-start(bf16[8,1536]{1,0:T(8,128)(2,1)} %copy-done.27) | copy-start | bytes 73732
  47.9 1.2 %copy-start.15 = (f32[4,384,256]{2,1,0:T(8,128)}, f32[4,384,256]{2,1,0:T(8,128)S(1)}, u32[]{:S(2)}) copy-start(f32[4,384,256]{2,1,0:T(8,128)S(1)} %get-tuple-element.53.wt) | copy-start | bytes 4718596
  55.2 1.1 copy-start.17
  56.3 0.9 copy-start.25
  57.2 6.1 %copy-start.39 = (bf16[32,8,256]{2,1,0:T(8,128)(2,1)}, bf16[32,8,256]{2,1,0:T(8,128)(2,1)S(1)}, u32[]{:S(2)}) copy-start(bf16[32,8,256]{2,1,0:T(8,128)(2,1)S(1)} %get-tuple-element.49) | copy-start | bytes 393220
  57.2 15.9 %collective-permute-start.6 = (bf16[384,256]{1,0:T(8,128)(2,1)}, bf16[384,256]{1,0:T(8,128)(2,1)S(1)}, u32[]{:S(2)}, u32[]{:S(2)}) collective-permute-start(bf16[384,256]{1,0:T(8,128)(2,1)} %get-tuple-element.41), channel_id=1, source_target_pairs={{4,8},{12,16},{20,24},{8,4},{16,12},{24,20},{5,9},{13,17},{21,25},... | collective-permute-start | bytes 589832 | tf_op jit(solution)/shard_map/ppermute | solution.py:216
  57.9 15.3 %collective-permute-start.7 = (bf16[384,256]{1,0:T(8,128)(2,1)}, bf16[384,256]{1,0:T(8,128)(2,1)}, u32[]{:S(2)}, u32[]{:S(2)}) collective-permute-start(bf16[384,256]{1,0:T(8,128)(2,1)} %get-tuple-element.42), channel_id=1, source_target_pairs={{0,4},{8,12},{16,20},{24,28},{4,0},{12,8},{20,16},{28,24},{1,5},{9... | collective-permute-start | bytes 589832 | tf_op jit(solution)/shard_map/ppermute | solution.py:216
  63.3 17.5 %all-to-all-start.1 = ((bf16[32,8,256]{2,1,0:T(8,128)(2,1)}), bf16[32,8,256]{2,1,0:T(8,128)(2,1)}, u32[]{:S(2)}, u32[]{:S(2)}) async-start(bf16[32,8,256]{2,1,0:T(8,128)(2,1)} %copy-done.39), calls=%async_computation.1 | async-start | bytes 262144 | tf_op jit(solution)/shard_map/all_to_all | solution.py:220
  66.6 1.5 %copy-start.4 = (bf16[6,1,384,384]{3,2,1,0:T(8,128)(2,1)S(1)}, bf16[6,1,384,384]{3,2,1,0:T(8,128)(2,1)}, u32[]{:S(2)}) copy-start(bf16[6,1,384,384]{3,2,1,0:T(8,128)(2,1)} %param.10) | copy-start | bytes 5308420
  68.1 1.4 %copy-start.6 = (bf16[5,1,384,384]{3,2,1,0:T(8,128)(2,1)S(1)}, bf16[5,1,384,384]{3,2,1,0:T(8,128)(2,1)}, u32[]{:S(2)}) copy-start(bf16[5,1,384,384]{3,2,1,0:T(8,128)(2,1)} %param.11) | copy-start | bytes 4423684
  69.5 1.1 copy-start.26
  70.6 2.6 %copy-start.12 = (bf16[1,384,384]{2,1,0:T(8,128)(2,1)S(1)}, bf16[1,384,384]{2,1,0:T(8,128)(2,1)}, u32[]{:S(2)}) copy-start(bf16[1,384,384]{2,1,0:T(8,128)(2,1)} %copy-done.11) | copy-start | bytes 884740
  70.6 2.6 %copy-start.14 = (bf16[1,384,384]{2,1,0:T(8,128)(2,1)S(1)}, bf16[1,384,384]{2,1,0:T(8,128)(2,1)}, u32[]{:S(2)}) copy-start(bf16[1,384,384]{2,1,0:T(8,128)(2,1)} %copy-done.13) | copy-start | bytes 884740
  72.0 1.1 copy-start.21
  75.2 11.5 %collective-permute-start.8 = (bf16[384,256]{1,0:T(8,128)(2,1)}, bf16[384,256]{1,0:T(8,128)(2,1)S(1)}, u32[]{:S(2)}, u32[]{:S(2)}) collective-permute-start(bf16[384,256]{1,0:T(8,128)(2,1)} %get-tuple-element.46), channel_id=1, source_target_pairs={{4,8},{12,16},{20,24},{8,4},{16,12},{24,20},{5,9},{13,17},{21,25},... | collective-permute-start | bytes 589832 | tf_op jit(solution)/shard_map/ppermute | solution.py:216
  75.9 12.8 %collective-permute-start.9 = (bf16[384,256]{1,0:T(8,128)(2,1)}, bf16[384,256]{1,0:T(8,128)(2,1)}, u32[]{:S(2)}, u32[]{:S(2)}) collective-permute-start(bf16[384,256]{1,0:T(8,128)(2,1)} %get-tuple-element.47), channel_id=1, source_target_pairs={{0,4},{8,12},{16,20},{24,28},{4,0},{12,8},{20,16},{28,24},{1,5},{9... | collective-permute-start | bytes 589832 | tf_op jit(solution)/shard_map/ppermute | solution.py:216
  80.8 1.4 %copy-start.22 = (f32[4,384,256]{2,1,0:T(8,128)S(1)}, f32[4,384,256]{2,1,0:T(8,128)}, u32[]{:S(2)}) copy-start(f32[4,384,256]{2,1,0:T(8,128)} %copy-done.21) | copy-start | bytes 4718596
  82.9 0.9 copy-start.32
  83.8 0.8 copy-start.34
  84.6 6.5 %copy-start.10 = (bf16[4,1,384,384]{3,2,1,0:T(8,128)(2,1)S(1)}, bf16[4,1,384,384]{3,2,1,0:T(8,128)(2,1)}, u32[]{:S(2)}) copy-start(bf16[4,1,384,384]{3,2,1,0:T(8,128)(2,1)} %param.8) | copy-start | bytes 3538948
  84.6 6.5 %copy-start.16 = (f32[4,384,256]{2,1,0:T(8,128)S(1)}, f32[4,384,256]{2,1,0:T(8,128)}, u32[]{:S(2)}) copy-start(f32[4,384,256]{2,1,0:T(8,128)} %copy-done.15) | copy-start | bytes 4718596
  84.6 6.5 %copy-start.18 = (f32[4,384,256]{2,1,0:T(8,128)S(1)}, f32[4,384,256]{2,1,0:T(8,128)}, u32[]{:S(2)}) copy-start(f32[4,384,256]{2,1,0:T(8,128)} %copy-done.17) | copy-start | bytes 4718596
  86.7 4.5 %copy-start.8 = (bf16[4,1,384,384]{3,2,1,0:T(8,128)(2,1)S(1)}, bf16[4,1,384,384]{3,2,1,0:T(8,128)(2,1)}, u32[]{:S(2)}) copy-start(bf16[4,1,384,384]{3,2,1,0:T(8,128)(2,1)} %param.9) | copy-start | bytes 3538948
  89.8 9.5 %collective-permute-start.10 = (bf16[384,256]{1,0:T(8,128)(2,1)S(1)}, bf16[384,256]{1,0:T(8,128)(2,1)S(1)}, u32[]{:S(2)}, u32[]{:S(2)}) collective-permute-start(bf16[384,256]{1,0:T(8,128)(2,1)S(1)} %get-tuple-element.50), channel_id=1, source_target_pairs={{4,0},{8,4},{12,8},{16,12},{20,16},{24,20},{28,24},{5,1},{9,5},{13... | collective-permute-start | bytes 589832 | tf_op jit(solution)/shard_map/ppermute | solution.py:275
  (5 other events, 3.4 us)

commit v2 on v1

v2 whole, which is shorter than its diff:
```python
import jax
import jax.numpy as jnp
from jax import lax
from jax.experimental import pallas as pl
from jax.experimental.pallas import tpu as pltpu
from jax.sharding import PartitionSpec as P

BF = jnp.bfloat16
F32 = jnp.float32
ALL = ("row", "col")
PAD = 16
LIMIT = 16 * 1024 * 1024
SOLVE_COST = 1200


def mm(a, b):
    return lax.dot_general(a, b, (((1,), (0,)), ((), ())), preferred_element_type=F32)


def mmt(a, b):
    return lax.dot_general(a, b, (((0,), (0,)), ((), ())), preferred_element_type=F32)


def colsum(x):
    return jnp.sum(x, axis=0, keepdims=True)


def is_lower(chain):
    return lax.rem(lax.axis_index("row"), 2) == (0 if chain == 2 else 1)


def pick(from2, from1):
    low2 = is_lower(2)
    return jnp.where(low2, from2, from1), jnp.where(low2, from1, from2)


def call(body, outs, args, name, flops=0, after=None, scratch=(), hbm=()):
    shapes = [jax.ShapeDtypeStruct(d, t) for d, t in outs]
    total = sum(a.size * a.dtype.itemsize for a in list(args) + shapes)
    specs = [pl.BlockSpec(memory_space=pltpu.HBM if i in hbm else pltpu.VMEM) for i in range(len(args))]
    kernel, count = body, len(args)
    if after is not None:
        args = tuple(args) + (after,)
        specs = specs + [pl.BlockSpec(memory_space=pl.ANY)]
        kernel = lambda *refs: body(*refs[:count], *refs[count + 1 :])
    return pl.pallas_call(
        kernel,
        out_shape=shapes,
        in_specs=specs,
        out_specs=[pl.BlockSpec(memory_space=pltpu.VMEM)] * len(outs),
        scratch_shapes=list(scratch),
        compiler_params=pltpu.CompilerParams(vmem_limit_bytes=LIMIT),
        cost_estimate=pl.CostEstimate(flops=flops, bytes_accessed=total, transcendentals=0),
        name=name,
    )(*args)


def load_edges(r, s2, s1, sems):
    last = r.shape[0] - 1
    at = jnp.where(is_lower(2), 0, last)
    copies = [pltpu.make_async_copy(r.at[at], s2, sems.at[0]), pltpu.make_async_copy(r.at[last - at], s1, sems.at[1])]
    for c in copies:
        c.start()
    for c in copies:
        c.wait()


def inner_solve(e, ld, lu, y, ye):
    e1, e2, e3, e4 = e[0], e[1], e[2], e[3]
    ye[0] = mm(lu[0], e1)
    ye[1] = mmt(lu[4], e4)
    y[0] = mm(ld[1], e1) + mm(lu[1], e2)
    y[1] = mm(ld[2], e2) + mm(lu[2], e3) + mmt(lu[1], e1)
    y[2] = mm(ld[3], e3) + mm(lu[3], e4) + mmt(lu[2], e2)
    y[3] = mm(ld[4], e4) + mmt(lu[3], e3)


def margin_solve(chain):
    def body(h, ye, ld, s):
        side = jnp.where(is_lower(chain), 0, 1)
        s[...] = (ye[side] + mm(ld[side * (ld.shape[0] - 1)], h[...])).astype(BF)

    return body


def add_coarse(h2, h1, y, lu, gathered, fpad, fown, basis, p):
    e0, e5 = pick(h2[...], h1[...])
    g = gathered[...].reshape(-1, gathered.shape[-1])
    v = mm(fpad[...], g).astype(BF)
    u = mmt(fown[...], v).astype(BF)
    size = p.shape[1]
    for k in range(4):
        part = y[k] + mmt(basis[:, k * size : (k + 1) * size], u)
        if k == 0:
            part = part + mmt(lu[0], e0)
        if k == 3:
            part = part + mm(lu[4], e5)
        p[k] = part


def join_margin(chain):
    def body(m, p, su, z, s):
        lower = is_lower(chain)

        @pl.when(lower)
        def _():
            edge = p[0] + m[...].astype(F32)
            z[...] = edge
            s[...] = edge.astype(BF)

        @pl.when(jnp.logical_not(lower))
        def _():
            edge = p[3] + m[...].astype(F32)
            z[...] = edge
            s[...] = mmt(su[3], edge.astype(BF)).astype(BF)

    return body


def inner_operate(z2, z1, p, r, sd, su, z, w, wt, rho):
    z[0], z[3] = pick(z2[...], z1[...])
    z[1] = p[1]
    z[2] = p[2]
    acc = jnp.zeros(rho.shape, F32)
    for k in range(4):
        zk = z[k]
        zb = zk.astype(BF)
        if k == 0:
            w[k] = mm(su[k], z[k + 1].astype(BF))
        elif k < 3:
            w[k] = mm(su[k], z[k + 1].astype(BF)) + mmt(su[k - 1], z[k - 1].astype(BF))
        else:
            w[k] = mmt(su[k - 1], z[k - 1].astype(BF))
        own = mm(sd[k], zb)
        wt[k] = mmt(sd[k], zb) - own
        w[k] = w[k] + own
        acc = acc + colsum(r[k].astype(F32) * zk)
    rho[...] = acc


def join_operate(chain):
    def body(n, w, su, edge, s):
        lower = is_lower(chain)

        @pl.when(lower)
        def _():
            out = w[0] + n[...].astype(F32)
            edge[...] = out
            s[...] = out.astype(BF)

        @pl.when(jnp.logical_not(lower))
        def _():
            out = w[3] + mm(su[3], n[...])
            edge[...] = out
            s[...] = out.astype(BF)

    return body


def coarse_rhs(ncb):
    def body(e, basis, g):
        out = mm(basis[...], e[...].reshape(-1, e.shape[-1]))
        out = jnp.concatenate([out, jnp.zeros((PAD - ncb, out.shape[1]), F32)], axis=0).astype(BF)
        for k in range(g.shape[0]):
            g[k] = out

    return body


def prepare(ncb):
    def body(basis, factor, padded, fpad, fown):
        rows = basis[...].astype(F32)
        padded[...] = jnp.concatenate([rows, jnp.zeros((PAD - ncb, rows.shape[1]), F32)], axis=0).astype(BF)
        nco = factor.shape[0]
        own = lax.axis_index("row") * lax.axis_size("col") + lax.axis_index("col")

        def columns(first, width):
            source = lax.broadcasted_iota(jnp.int32, (nco, width), 0)
            target = lax.broadcasted_iota(jnp.int32, (nco, width), 1)
            at = lax.rem(target, PAD)
            match = (source == (first + target // PAD) * ncb + at) & (at < ncb)
            chosen = jnp.where(match, 1.0, 0.0).astype(BF)
            return mm(factor[...], chosen).astype(BF)

        fown[...] = columns(own, PAD)
        width = 128

        def step(i, carry):
            fpad[:, pl.ds(pl.multiple_of(i * width, width), width)] = columns(i * (width // PAD), width)
            return carry

        lax.fori_loop(0, fpad.shape[1] // width, step, 0)

    return body


def three(x):
    parts = []
    for _ in range(3):
        top = x.astype(BF).astype(F32)
        parts.append(top)
        x = x - top
    return parts


def coarse_rhs_sums(w2, w1, w, z, rho, basis, wf, wb, g):
    wf[0], wf[3] = pick(w2[...], w1[...])
    wf[1] = w[1]
    wf[2] = w[2]
    acc = jnp.zeros(rho.shape, F32)
    for k in range(4):
        wk = wf[k]
        wb[k] = wk.astype(BF)
        acc = acc + colsum(wk * z[k])
    out = mm(basis[...], wb[...].reshape(-1, wb.shape[-1]))
    zero = jnp.zeros(rho.shape, F32)
    out = jnp.concatenate([out[:8]] + three(rho[...]) + three(acc) + [zero, zero], axis=0).astype(BF)
    for k in range(g.shape[0]):
        g[k] = out


def join_second(chain):
    def body(m, p, q, s):
        at = jnp.where(is_lower(chain), 0, 3)
        edge = p[at] + m[...].astype(F32)
        q[...] = edge
        s[...] = edge.astype(BF)

    return body


def inner_products(q2, q1, p, z, r, w, wt, sd, su, q, sums, edge):
    q[0], q[3] = pick(q2[...], q1[...])
    q[1] = p[1]
    q[2] = p[2]
    s1 = s2 = s4 = s5 = jnp.zeros((1, q.shape[-1]), F32)
    for k in range(4):
        qk = q[k]
        qb = qk.astype(BF)
        wk = w[k]
        part = mm(sd[k], qb)
        if k < 3:
            part = part + 2.0 * mm(su[k], q[k + 1].astype(BF))
        else:
            edge[...] = 2.0 * mmt(su[k], qb)
        s1 = s1 + colsum(r[k].astype(F32) * qk)
        s2 = s2 + colsum(wk * qk)
        s4 = s4 + colsum((wk + wk + wt[k]) * qk)
        s5 = s5 + colsum(qk * part)
    sums[...] = jnp.concatenate([s1, s2, s4, s5], axis=0)


def join_sums(t2, t1, edge, sums, out):
    _, t = pick(t2[...], t1[...])
    s5 = sums[3:4] + colsum(edge[...] * t.astype(F32))
    full = jnp.concatenate([sums[0:3], s5], axis=0)
    for k in range(out.shape[0]):
        out[k] = full


def finish(parts, early, z, q, x):
    total = parts[0]
    first = early[0].astype(F32)
    for k in range(1, parts.shape[0]):
        total = total + parts[k]
        first = first + early[k].astype(F32)
    rho0 = first[8:9] + first[9:10] + first[10:11]
    d0 = first[11:12] + first[12:13] + first[13:14]
    s1, s2, s4, s5 = (total[k : k + 1] for k in range(4))
    a0 = rho0 / d0
    rho1 = a0 * (a0 * s2 - s1)
    grow = 1.0 + rho1 / rho0
    a1 = rho1 / (grow * grow * d0 - grow * a0 * s4 + a0 * a0 * s5)
    cz = a0 + a1 * grow
    cq = a1 * a0
    for k in range(4):
        x[k] = cz * z[k] - cq * q[k]


def pairs(chain, count):
    return [(i, i + 1) for i in range(1 if chain == 2 else 0, count - 1, 2)]


def swap(chain, x):
    each = pairs(chain, lax.axis_size("row"))
    return lax.ppermute(x, "row", each + [(b, a) for a, b in each])


def send_down(chain, x):
    return lax.ppermute(x, "row", [(b, a) for a, b in pairs(chain, lax.axis_size("row"))])


def gather(copies):
    return lax.all_to_all(copies, ALL, 0, 0)


def on_device(rhs, stiff_diag, stiff_upper, local_diag, local_upper, coarse_basis, coarse_factor):
    layers, _, size, cols = rhs.shape
    devices = lax.axis_size("row") * lax.axis_size("col")
    ncb = coarse_basis.shape[2]
    layer, whole, row = (size, cols), (layers, size, cols), (1, cols)
    block = 2 * size * size * cols
    nco = coarse_factor.shape[0]

    r, sd, su, ld, lu = rhs[:, 0], stiff_diag[:, 0], stiff_upper[:, 0], local_diag[:, 0], local_upper[:, 0]
    s2, s1 = call(load_edges, [(layer, BF), (layer, BF)], (r,), "load_edges", 0, None, [pltpu.SemaphoreType.DMA((2,))], (0,))
    h2, h1 = swap(2, s2), swap(1, s1)
    copies = ((devices, PAD, cols), BF)

    def solve(e, h2, h1, gathered):
        y, ye = call(inner_solve, [(whole, F32), ((2,) + layer, F32)], (e, ld, lu), "inner_solve", SOLVE_COST * block)
        m = []
        for chain, h in ((2, h2), (1, h1)):
            (s,) = call(margin_solve(chain), [(layer, BF)], (h, ye, ld), "margin_solve", block)
            m.append(swap(chain, s))
        (p,) = call(add_coarse, [(whole, F32)], (h2, h1, y, lu, gathered, fpad, fown, basis), "add_coarse", 3 * block)
        return m, p

    raw_basis = coarse_basis[0, 0]
    (g,) = call(coarse_rhs(ncb), [copies], (r, raw_basis), "coarse_rhs", block // 32, s1)
    basis, fpad, fown = call(
        prepare(ncb),
        [((PAD, layers * size), BF), ((nco, devices * PAD), BF), ((nco, PAD), BF)],
        (raw_basis, coarse_factor),
        "prepare",
        block // 8,
        g,
    )
    (m2, m1), p = solve(r, h2, h1, gather(g))
    z2, s2 = call(join_margin(2), [(layer, F32), (layer, BF)], (m2, p, su), "join_margin", block)
    n2 = swap(2, s2)
    z1, s1 = call(join_margin(1), [(layer, F32), (layer, BF)], (m1, p, su), "join_margin", block)
    n1 = swap(1, s1)
    z, wi, wt, rho = call(inner_operate, [(whole, F32)] * 3 + [(row, F32)], (z2, z1, p, r, sd, su), "inner_operate", 14 * block)
    w2, s2 = call(join_operate(2), [(layer, F32), (layer, BF)], (n2, wi, su), "join_operate", block)
    h2 = swap(2, s2)
    w1, s1 = call(join_operate(1), [(layer, F32), (layer, BF)], (n1, wi, su), "join_operate", block)
    h1 = swap(1, s1)
    w, wb, g = call(
        coarse_rhs_sums, [(whole, F32), (whole, BF), copies], (w2, w1, wi, z, rho, basis), "coarse_rhs_sums", block // 32
    )
    early = gather(g)
    (m2, m1), p = solve(wb, h2, h1, early)
    q2, s2 = call(join_second(2), [(layer, F32), (layer, BF)], (m2, p), "join_second")
    t2 = send_down(2, s2)
    q1, s1 = call(join_second(1), [(layer, F32), (layer, BF)], (m1, p), "join_second")
    t1 = send_down(1, s1)
    q, sums, edge = call(
        inner_products, [(whole, F32), ((4, cols), F32), (layer, F32)], (q2, q1, p, z, r, w, wt, sd, su), "inner_products", 8 * block
    )
    (g,) = call(join_sums, [((devices, 4, cols), F32)], (t2, t1, edge, sums), "join_sums")
    x = pl.pallas_call(
        finish,
        out_shape=jax.ShapeDtypeStruct(whole, F32),
        in_specs=[pl.BlockSpec(memory_space=pltpu.VMEM)] * 4,
        out_specs=pl.BlockSpec(memory_space=pltpu.VMEM),
        compiler_params=pltpu.CompilerParams(vmem_limit_bytes=LIMIT),
        name="finish",
    )(gather(g), early, z, q)
    return x[:, None]


def solution(mesh):
    split = P("row", "col", None, None)
    return jax.shard_map(on_device, mesh=mesh, in_specs=(split,) * 6 + (P(),), out_specs=split, check_vma=False)
```

time: 118 us -> 102 us (0.86)
  waiting for transfers between devices: 20.3 us -> 8.73 us
  Pallas kernels: 16.8 us -> 25.6 us
  local copies, waits for them, and re-layouts: 23.3 us -> 16.4 us
  starting transfers between devices: 38.2 us -> 33.4 us
  other arithmetic: 1.24 us -> 0 us
    ppermute x11 -> x12, waiting for transfers between devices: 20.3 us -> 7.13 us  [the longest x2 5.38 us: send_down(): lax.ppermute(x, 'row', [(b, a) for a, b in pairs(chain, lax.axis_size('ro...]
    pallas_call x14 -> x22, Pallas kernels: 16.8 us -> 25.6 us  [the longest x21 24.2 us: call(): pl.pallas_call(kernel, out_shape=shapes, in_specs=specs, out_specs=[pl.Bl...]
    ppermute x11 -> x12, starting transfers between devices: 27.5 us -> 20.8 us  [the longest x10 18.8 us: swap(): return lax.ppermute(x, 'row', each + [(b, a) for a, b in each])]
    unnamed x80 -> x64, local copies, waits for them, and re-layouts: 19.8 us -> 16.4 us
    slice x3 -> x0, local copies, waits for them, and re-layouts: 2.62 us -> none  [on_device(): ld0, ld5, lu0, lu4, su3 = (ld[0:1], ld[-1:], lu[0:1], lu[-1:], su[-1:])]
    all_to_all x2, starting transfers between devices: 10.7 us -> 12.6 us  [gather(): return lax.all_to_all(copies, ALL, 0, 0)]
    all_to_all x2, waiting for transfers between devices: 0.01 us -> 1.59 us  [gather(): return lax.all_to_all(copies, ALL, 0, 0)]
    select_n x1 -> x0, other arithmetic: 1.2 us -> none  [on_device(): h2, h1 = swap(jnp.where(even, low, high), jnp.where(even, high, low))]
  transfers between devices with their start and end apart: 13 -> 14, of which waited for: 5 -> 3; matrix products, arithmetic and copies ran while one was open for 4% -> 0% of each run, Pallas kernels for 10% -> 23%
where the time goes in v2:
time: 102 us; the launch traced here: 101 us
  starting transfers between devices  33.4 us (33%)
  Pallas kernels  25.6 us (25%)
  blocking collectives  16.7 us (16%)
  local copies, waits for them, and re-layouts  16.4 us (16%)
  waiting for transfers between devices  8.73 us (9%)
    pallas_call x21, Pallas kernels, call(): pl.pallas_call(kernel, out_shape=shapes, in_specs=specs, out_specs=[pl.Bl...  24.2 us
    ppermute x10, starting transfers between devices, swap(): return lax.ppermute(x, 'row', each + [(b, a) for a, b in each])  18.8 us
    all_to_all x1, blocking collectives, gather(): return lax.all_to_all(copies, ALL, 0, 0)  16.7 us
    unnamed x64, local copies, waits for them, and re-layouts  16.4 us
    all_to_all x2, starting transfers between devices, gather(): return lax.all_to_all(copies, ALL, 0, 0)  12.6 us
    ppermute x2, waiting for transfers between devices, send_down(): lax.ppermute(x, 'row', [(b, a) for a, b in pairs(chain, lax.axis_size('ro...  5.38 us
  transfers between devices with their start and end apart: 14, of which 3 were waited for; matrix products, arithmetic and copies ran while one was open for 0% of the time, Pallas kernels for 23%

profile of v2, /device:TPU:0, one launch (start us, length us, event | category | flops | bytes accessed | tf_op | source)
XLA Modules:
  0.0 101.2 jit_solution(3248010421123591368)
XLA Ops:
  0.0 1.3 %copy-done.4 = bf16[4,1,384,256]{3,2,1,0:T(8,128)(2,1)S(1)} copy-done((bf16[4,1,384,256]{3,2,1,0:T(8,128)(2,1)S(1)}, bf16[4,1,384,256]{3,2,1,0:T(8,128)(2,1)}, u32[]{:S(2)}) %copy-start.4) | copy-done | bytes 786456
  1.3 1.3 %load_edges.1 = (bf16[384,256]{1,0:T(8,128)(2,1)}, bf16[384,256]{1,0:T(8,128)(2,1)}) custom-call(bf16[4,384,256]{2,1,0:T(8,128)(2,1)S(1)} %bitcast.21), custom_call_target="tpu_custom_call" | custom-call | bytes 1179648 | tf_op jit(solution)/shard_map/load_edges/pallas_call | solution.py:46
  3.2 5.8 %collective-permute-start.2 = (bf16[384,256]{1,0:T(8,128)(2,1)}, bf16[384,256]{1,0:T(8,128)(2,1)S(1)}, u32[]{:S(2)}, u32[]{:S(2)}) collective-permute-start(bf16[384,256]{1,0:T(8,128)(2,1)} %get-tuple-element.38.refs_2_), channel_id=1, source_target_pairs={{0,4},{8,12},{16,20},{24,28},{4,0},{12,8},{20,16},{28,24},{1,5},{9... | collective-permute-start | bytes 589832 | tf_op jit(solution)/shard_map/ppermute | solution.py:286
  9.0 0.7 copy-done.28
  9.7 0.9 coarse_rhs.1.refs_2_
  10.7 4.7 %all-to-all-start = ((bf16[32,16,256]{2,1,0:T(8,128)(2,1)}), bf16[32,16,256]{2,1,0:T(8,128)(2,1)S(1)}, u32[]{:S(2)}, u32[]{:S(2)}) async-start(bf16[32,16,256]{2,1,0:T(8,128)(2,1)} %coarse_rhs.1.refs_2_), calls=%async_computation | async-start | bytes 524288 | tf_op jit(solution)/shard_map/all_to_all | solution.py:294
  15.5 1.4 %copy-done.8 = bf16[5,1,384,384]{3,2,1,0:T(8,128)(2,1)S(1)} copy-done((bf16[5,1,384,384]{3,2,1,0:T(8,128)(2,1)S(1)}, bf16[5,1,384,384]{3,2,1,0:T(8,128)(2,1)}, u32[]{:S(2)}) %copy-start.8) | copy-done | bytes 1474584
  16.8 1.4 %inner_solve.2 = (f32[4,384,256]{2,1,0:T(8,128)S(1)}, f32[2,384,256]{2,1,0:T(8,128)S(1)}) custom-call(bf16[4,384,256]{2,1,0:T(8,128)(2,1)S(1)} %bitcast.23, bf16[6,384,384]{2,1,0:T(8,128)(2,1)S(1)} %bitcast.15, bf16[5,384,384]{2,1,0:T(8,128)(2,1)S(1)} %bitcast.26), custom_call_target="tpu_custom_call" | custom-call | flops 90596966400 | bytes 6389760 | tf_op jit(solution)/shard_map/inner_solve/pallas_call | solution.py:46
  18.2 1.2 %margin_solve.5 = bf16[384,256]{1,0:T(8,128)(2,1)} custom-call(bf16[384,256]{1,0:T(8,128)(2,1)S(1)} %collective-permute-done.2.h1.h, f32[2,384,256]{2,1,0:T(8,128)S(1)} %get-tuple-element.37.ye, bf16[6,384,384]{2,1,0:T(8,128)(2,1)S(1)} %bitcast.16), custom_call_target="tpu_custom_call" | custom-call | flops 75497472 | bytes 2949120 | tf_op jit(solution)/shard_map/margin_solve/pallas_call | solution.py:46
  19.4 1.8 %collective-permute-start.4 = (bf16[384,256]{1,0:T(8,128)(2,1)}, bf16[384,256]{1,0:T(8,128)(2,1)}, u32[]{:S(2)}, u32[]{:S(2)}) collective-permute-start(bf16[384,256]{1,0:T(8,128)(2,1)} %margin_solve.5), channel_id=1, source_target_pairs={{0,4},{8,12},{16,20},{24,28},{4,0},{12,8},{20,16},{28,24},{1,5},{9... | collective-permute-start | bytes 589832 | tf_op jit(solution)/shard_map/ppermute | solution.py:286
  21.2 0.9 margin_solve.4
  22.2 1.4 %collective-permute-start.1 = (bf16[384,256]{1,0:T(8,128)(2,1)}, bf16[384,256]{1,0:T(8,128)(2,1)}, u32[]{:S(2)}, u32[]{:S(2)}) collective-permute-start(bf16[384,256]{1,0:T(8,128)(2,1)} %margin_solve.4), channel_id=1, source_target_pairs={{4,8},{12,16},{20,24},{8,4},{16,12},{24,20},{5,9},{13,17},{21,25},... | collective-permute-start | bytes 589832 | tf_op jit(solution)/shard_map/ppermute | solution.py:286
  23.5 0.9 prepare.1
  24.4 1.6 %all-to-all-done.gathered = bf16[32,16,256]{2,1,0:T(8,128)(2,1)S(1)} async-done(((bf16[32,16,256]{2,1,0:T(8,128)(2,1)}), bf16[32,16,256]{2,1,0:T(8,128)(2,1)S(1)}, u32[]{:S(2)}, u32[]{:S(2)}) %all-to-all-start) | async-done | bytes 262176 | tf_op jit(solution)/shard_map/all_to_all | solution.py:294
  26.0 1.4 %copy-done.9 = bf16[5,1,384,384]{3,2,1,0:T(8,128)(2,1)S(1)} copy-done((bf16[5,1,384,384]{3,2,1,0:T(8,128)(2,1)S(1)}, bf16[5,1,384,384]{3,2,1,0:T(8,128)(2,1)}, u32[]{:S(2)}) %copy-start.9) | copy-done | bytes 1474584
  27.4 1.4 %copy-done.19 = f32[4,384,256]{2,1,0:T(8,128)S(1)} copy-done((f32[4,384,256]{2,1,0:T(8,128)S(1)}, f32[4,384,256]{2,1,0:T(8,128)}, u32[]{:S(2)}) %copy-start.19) | copy-done | bytes 1572888
  28.8 0.9 copy-done.23
  29.7 0.9 copy-done.25
  30.7 1.0 add_coarse.2.p
  31.9 1.2 %join_margin.3 = (f32[384,256]{1,0:T(8,128)S(1)}, bf16[384,256]{1,0:T(8,128)(2,1)S(1)}) custom-call(bf16[384,256]{1,0:T(8,128)(2,1)} %collective-permute-done.4.m, f32[4,384,256]{2,1,0:T(8,128)S(1)} %add_coarse.2.p, bf16[4,384,384]{2,1,0:T(8,128)(2,1)S(1)} %bitcast.9), custom_call_target="tpu_custom_call" | custom-call | flops 75497472 | bytes 3538944 | tf_op jit(solution)/shard_map/join_margin/pallas_call | solution.py:46
  33.2 1.7 %collective-permute-start.6 = (bf16[384,256]{1,0:T(8,128)(2,1)S(1)}, bf16[384,256]{1,0:T(8,128)(2,1)S(1)}, u32[]{:S(2)}, u32[]{:S(2)}) collective-permute-start(bf16[384,256]{1,0:T(8,128)(2,1)S(1)} %get-tuple-element.49), channel_id=1, source_target_pairs={{0,4},{8,12},{16,20},{24,28},{4,0},{12,8},{20,16},{28,24},{1,5},{9... | collective-permute-start | bytes 589832 | tf_op jit(solution)/shard_map/ppermute | solution.py:286
  34.9 1.0 join_margin.2
  36.6 1.6 %inner_operate.1 = (f32[4,384,256]{2,1,0:T(8,128)S(1)}, f32[4,384,256]{2,1,0:T(8,128)S(1)}, f32[4,384,256]{2,1,0:T(8,128)S(1)}, f32[1,256]{1,0:T(1,128)S(1)}) custom-call(f32[384,256]{1,0:T(8,128)S(1)} %get-tuple-element.44.z2, f32[384,256]{1,0:T(8,128)S(1)} %get-tuple-element.45.z1, f32[4,384,256]{2,1,0:T(8,128)S(1)} %add_coarse.2.p, ...), custom_call_target="tpu_custom_call" | custom-call | flops 1056964608 | bytes 10224640 | tf_op jit(solution)/shard_map/inner_operate/pallas_call | solution.py:46
  38.2 1.7 %collective-permute-done.6.n = bf16[384,256]{1,0:T(8,128)(2,1)S(1)} collective-permute-done((bf16[384,256]{1,0:T(8,128)(2,1)S(1)}, bf16[384,256]{1,0:T(8,128)(2,1)S(1)}, u32[]{:S(2)}, u32[]{:S(2)}) %collective-permute-start.6) | collective-permute-done | bytes 196640 | tf_op jit(solution)/shard_map/ppermute | solution.py:286
  40.0 0.9 join_operate.3
  40.9 2.4 %collective-permute-start.8 = (bf16[384,256]{1,0:T(8,128)(2,1)}, bf16[384,256]{1,0:T(8,128)(2,1)}, u32[]{:S(2)}, u32[]{:S(2)}) collective-permute-start(bf16[384,256]{1,0:T(8,128)(2,1)} %get-tuple-element.55), channel_id=1, source_target_pairs={{0,4},{8,12},{16,20},{24,28},{4,0},{12,8},{20,16},{28,24},{1,5},{9... | collective-permute-start | bytes 589832 | tf_op jit(solution)/shard_map/ppermute | solution.py:286
  43.3 0.7 join_operate.2
  44.1 1.3 %collective-permute-start.5 = (bf16[384,256]{1,0:T(8,128)(2,1)}, bf16[384,256]{1,0:T(8,128)(2,1)}, u32[]{:S(2)}, u32[]{:S(2)}) collective-permute-start(bf16[384,256]{1,0:T(8,128)(2,1)} %get-tuple-element.47), channel_id=1, source_target_pairs={{4,8},{12,16},{20,24},{8,4},{16,12},{24,20},{5,9},{13,17},{21,25},... | collective-permute-start | bytes 589832 | tf_op jit(solution)/shard_map/ppermute | solution.py:286
  45.8 1.2 %copy-done.16 = f32[4,384,256]{2,1,0:T(8,128)} copy-done((f32[4,384,256]{2,1,0:T(8,128)}, f32[4,384,256]{2,1,0:T(8,128)S(1)}, u32[]{:S(2)}) %copy-start.16) | copy-done | bytes 1572888
  47.7 0.9 copy-done.30
  48.5 7.9 %all-to-all-start.1 = ((bf16[32,16,256]{2,1,0:T(8,128)(2,1)}), bf16[32,16,256]{2,1,0:T(8,128)(2,1)S(1)}, u32[]{:S(2)}, u32[]{:S(2)}) async-start(bf16[32,16,256]{2,1,0:T(8,128)(2,1)} %copy-done.26), calls=%async_computation.1 | async-start | bytes 524288 | tf_op jit(solution)/shard_map/all_to_all | solution.py:294
  56.4 1.4 %copy-done.10 = bf16[5,1,384,384]{3,2,1,0:T(8,128)(2,1)S(1)} copy-done((bf16[5,1,384,384]{3,2,1,0:T(8,128)(2,1)S(1)}, bf16[5,1,384,384]{3,2,1,0:T(8,128)(2,1)}, u32[]{:S(2)}) %copy-start.10) | copy-done | bytes 1474584
  57.8 1.1 %copy-done.31 = bf16[4,384,256]{2,1,0:T(8,128)(2,1)S(1)} copy-done((bf16[4,384,256]{2,1,0:T(8,128)(2,1)S(1)}, bf16[4,384,256]{2,1,0:T(8,128)(2,1)}, u32[]{:S(2)}) %copy-start.31) | copy-done | bytes 786456
  58.9 1.4 %inner_solve.3 = (f32[4,384,256]{2,1,0:T(8,128)S(1)}, f32[2,384,256]{2,1,0:T(8,128)S(1)}) custom-call(bf16[4,384,256]{2,1,0:T(8,128)(2,1)S(1)} %copy-done.31, bf16[6,384,384]{2,1,0:T(8,128)(2,1)S(1)} %bitcast.18, bf16[5,384,384]{2,1,0:T(8,128)(2,1)S(1)} %bitcast.28), custom_call_target="tpu_custom_call" | custom-call | flops 90596966400 | bytes 6389760 | tf_op jit(solution)/shard_map/inner_solve/pallas_call | solution.py:46
  60.3 2.1 %margin_solve.7 = bf16[384,256]{1,0:T(8,128)(2,1)} custom-call(bf16[384,256]{1,0:T(8,128)(2,1)} %collective-permute-done.8.h1.h, f32[2,384,256]{2,1,0:T(8,128)S(1)} %get-tuple-element.54.ye, bf16[6,384,384]{2,1,0:T(8,128)(2,1)S(1)} %bitcast.19), custom_call_target="tpu_custom_call" | custom-call | flops 75497472 | bytes 2949120 | tf_op jit(solution)/shard_map/margin_solve/pallas_call | solution.py:46
  62.5 1.8 %collective-permute-start.10 = (bf16[384,256]{1,0:T(8,128)(2,1)}, bf16[384,256]{1,0:T(8,128)(2,1)}, u32[]{:S(2)}, u32[]{:S(2)}) collective-permute-start(bf16[384,256]{1,0:T(8,128)(2,1)} %margin_solve.7), channel_id=1, source_target_pairs={{0,4},{8,12},{16,20},{24,28},{4,0},{12,8},{20,16},{28,24},{1,5},{9... | collective-permute-start | bytes 589832 | tf_op jit(solution)/shard_map/ppermute | solution.py:286
  64.2 1.9 %margin_solve.6 = bf16[384,256]{1,0:T(8,128)(2,1)} custom-call(bf16[384,256]{1,0:T(8,128)(2,1)} %collective-permute-done.5.h.h2, f32[2,384,256]{2,1,0:T(8,128)S(1)} %get-tuple-element.54.ye, bf16[6,384,384]{2,1,0:T(8,128)(2,1)S(1)} %bitcast.20), custom_call_target="tpu_custom_call" | custom-call | flops 75497472 | bytes 2949120 | tf_op jit(solution)/shard_map/margin_solve/pallas_call | solution.py:46
  66.1 1.3 %collective-permute-start.7 = (bf16[384,256]{1,0:T(8,128)(2,1)}, bf16[384,256]{1,0:T(8,128)(2,1)}, u32[]{:S(2)}, u32[]{:S(2)}) collective-permute-start(bf16[384,256]{1,0:T(8,128)(2,1)} %margin_solve.6), channel_id=1, source_target_pairs={{4,8},{12,16},{20,24},{8,4},{16,12},{24,20},{5,9},{13,17},{21,25},... | collective-permute-start | bytes 589832 | tf_op jit(solution)/shard_map/ppermute | solution.py:286
  67.4 1.4 %copy-done.11 = bf16[5,1,384,384]{3,2,1,0:T(8,128)(2,1)S(1)} copy-done((bf16[5,1,384,384]{3,2,1,0:T(8,128)(2,1)S(1)}, bf16[5,1,384,384]{3,2,1,0:T(8,128)(2,1)}, u32[]{:S(2)}) %copy-start.11) | copy-done | bytes 1474584
  68.8 1.4 %copy-done.21 = f32[4,384,256]{2,1,0:T(8,128)S(1)} copy-done((f32[4,384,256]{2,1,0:T(8,128)S(1)}, f32[4,384,256]{2,1,0:T(8,128)}, u32[]{:S(2)}) %copy-start.21) | copy-done | bytes 1572888
  70.2 2.1 %add_coarse.3.p = f32[4,384,256]{2,1,0:T(8,128)S(1)} custom-call(bf16[384,256]{1,0:T(8,128)(2,1)} %collective-permute-done.5.h.h2, bf16[384,256]{1,0:T(8,128)(2,1)} %collective-permute-done.8.h1.h, f32[4,384,256]{2,1,0:T(8,128)S(1)} %copy-done.21, bf16[5,384,384]{2,1,0:T(8,128)(2,1)S(1)} %bitcast.29, bf16[32,16,256]{2,1,0:T(8,128)(2,1)S(1)} %all-to-all-done.1.gathered.early, ...), custom_call_target="tpu_custom_call" | custom-call | flops 226492416 | bytes 5527552 | tf_op jit(solution)/shard_map/add_coarse/pallas_call | solution.py:46
  72.4 1.1 %join_second.3 = (f32[384,256]{1,0:T(8,128)S(1)}, bf16[384,256]{1,0:T(8,128)(2,1)S(1)}) custom-call(bf16[384,256]{1,0:T(8,128)(2,1)} %collective-permute-done.10.m, f32[4,384,256]{2,1,0:T(8,128)S(1)} %add_coarse.3.p), custom_call_target="tpu_custom_call" | custom-call | bytes 2359296 | tf_op jit(solution)/shard_map/join_second/pallas_call | solution.py:46
  73.5 1.3 %collective-permute-start.11 = (bf16[384,256]{1,0:T(8,128)(2,1)S(1)}, bf16[384,256]{1,0:T(8,128)(2,1)S(1)}, u32[]{:S(2)}, u32[]{:S(2)}) collective-permute-start(bf16[384,256]{1,0:T(8,128)(2,1)S(1)} %get-tuple-element.59), channel_id=1, source_target_pairs={{4,0},{12,8},{20,16},{28,24},{5,1},{13,9},{21,17},{29,25},{6,2},{1... | collective-permute-start | bytes 589832 | tf_op jit(solution)/shard_map/ppermute | solution.py:290
  74.8 1.0 join_second.2
  76.6 1.0 %inner_products.1 = (f32[4,384,256]{2,1,0:T(8,128)S(1)}, f32[4,256]{1,0:T(4,128)S(1)}, f32[384,256]{1,0:T(8,128)S(1)}) custom-call(f32[384,256]{1,0:T(8,128)S(1)} %get-tuple-element.60.q2, f32[384,256]{1,0:T(8,128)S(1)} %get-tuple-element.61.q1, f32[4,384,256]{2,1,0:T(8,128)S(1)} %add_coarse.3.p, f32[4,384,256]{2,1,0:T(8,128)S(1)} %copy-done.3, ...), custom_call_target="tpu_custom_call" | custom-call | flops 603979776 | bytes 12193792 | tf_op jit(solution)/shard_map/inner_products/pallas_call | solution.py:46
  77.6 5.4 %collective-permute-done.11.t1 = bf16[384,256]{1,0:T(8,128)(2,1)S(1)} collective-permute-done((bf16[384,256]{1,0:T(8,128)(2,1)S(1)}, bf16[384,256]{1,0:T(8,128)(2,1)S(1)}, u32[]{:S(2)}, u32[]{:S(2)}) %collective-permute-start.11) | collective-permute-done | bytes 196640 | tf_op jit(solution)/shard_map/ppermute | solution.py:290
  83.1 16.7 %all_to_all.15.parts = f32[32,4,256]{2,1,0:T(4,128)S(1)} all-to-all(f32[32,4,256]{2,1,0:T(4,128)S(1)} %join_sums.1), channel_id=1, replica_groups=mesh['row'=8,'col'=4] {'row','col'}, dimensions={0} | all-to-all | bytes 262144 | tf_op jit(solution)/shard_map/all_to_all | solution.py:294
  99.8 1.4 %finish.1 = f32[4,384,256]{2,1,0:T(8,128)} custom-call(f32[32,4,256]{2,1,0:T(4,128)S(1)} %all_to_all.15.parts, bf16[32,16,256]{2,1,0:T(8,128)(2,1)S(1)} %all-to-all-done.1.gathered.early, f32[4,384,256]{2,1,0:T(8,128)S(1)} %copy-done.3, f32[4,384,256]{2,1,0:T(8,128)S(1)} %get-tuple-element.66.q), custom_call_target="tpu_custom_call" | custom-call | tf_op jit(solution)/shard_map/finish/pallas_call | solution.py:352
  (67 shorter events, 3.6 us)
Async XLA Ops:
  0.0 15.4 %copy-start.1 = (bf16[6,1,384,384]{3,2,1,0:T(8,128)(2,1)S(1)}, bf16[6,1,384,384]{3,2,1,0:T(8,128)(2,1)}, u32[]{:S(2)}) copy-start(bf16[6,1,384,384]{3,2,1,0:T(8,128)(2,1)} %param.10) | copy-start | bytes 5308420
  0.0 1.3 %copy-start.4 = (bf16[4,1,384,256]{3,2,1,0:T(8,128)(2,1)S(1)}, bf16[4,1,384,256]{3,2,1,0:T(8,128)(2,1)}, u32[]{:S(2)}) copy-start(bf16[4,1,384,256]{3,2,1,0:T(8,128)(2,1)} %param.7) | copy-start | bytes 2359300
  1.3 14.2 %copy-start.5 = (bf16[4,1,384,256]{3,2,1,0:T(8,128)(2,1)S(1)}, bf16[4,1,384,256]{3,2,1,0:T(8,128)(2,1)}, u32[]{:S(2)}) copy-start(bf16[4,1,384,256]{3,2,1,0:T(8,128)(2,1)} %param.7) | copy-start | bytes 2359300
  2.5 18.7 %collective-permute-start = (bf16[384,256]{1,0:T(8,128)(2,1)}, bf16[384,256]{1,0:T(8,128)(2,1)S(1)}, u32[]{:S(2)}, u32[]{:S(2)}) collective-permute-start(bf16[384,256]{1,0:T(8,128)(2,1)} %get-tuple-element.36), channel_id=1, source_target_pairs={{4,8},{12,16},{20,24},{8,4},{16,12},{24,20},{5,9},{13,17},{21,25},... | collective-permute-start | bytes 589832 | tf_op jit(solution)/shard_map/ppermute | solution.py:286
  3.2 15.0 %collective-permute-start.2 = (bf16[384,256]{1,0:T(8,128)(2,1)}, bf16[384,256]{1,0:T(8,128)(2,1)S(1)}, u32[]{:S(2)}, u32[]{:S(2)}) collective-permute-start(bf16[384,256]{1,0:T(8,128)(2,1)} %get-tuple-element.38.refs_2_), channel_id=1, source_target_pairs={{0,4},{8,12},{16,20},{24,28},{4,0},{12,8},{20,16},{28,24},{1,5},{9... | collective-permute-start | bytes 589832 | tf_op jit(solution)/shard_map/ppermute | solution.py:286
  9.0 0.7 copy-start.28
  10.7 15.3 %all-to-all-start = ((bf16[32,16,256]{2,1,0:T(8,128)(2,1)}), bf16[32,16,256]{2,1,0:T(8,128)(2,1)S(1)}, u32[]{:S(2)}, u32[]{:S(2)}) async-start(bf16[32,16,256]{2,1,0:T(8,128)(2,1)} %coarse_rhs.1.refs_2_), calls=%async_computation | async-start | bytes 524288 | tf_op jit(solution)/shard_map/all_to_all | solution.py:294
  15.4 1.4 %copy-start.8 = (bf16[5,1,384,384]{3,2,1,0:T(8,128)(2,1)S(1)}, bf16[5,1,384,384]{3,2,1,0:T(8,128)(2,1)}, u32[]{:S(2)}) copy-start(bf16[5,1,384,384]{3,2,1,0:T(8,128)(2,1)} %param.11) | copy-start | bytes 4423684
  18.2 4.0 %copy-start.18 = (f32[4,384,256]{2,1,0:T(8,128)}, f32[4,384,256]{2,1,0:T(8,128)S(1)}, u32[]{:S(2)}) copy-start(f32[4,384,256]{2,1,0:T(8,128)S(1)} %get-tuple-element.39.y) | copy-start | bytes 4718596
  18.2 3.9 %copy-start.24 = (bf16[384,256]{1,0:T(8,128)(2,1)}, bf16[384,256]{1,0:T(8,128)(2,1)S(1)}, u32[]{:S(2)}) copy-start(bf16[384,256]{1,0:T(8,128)(2,1)S(1)} %collective-permute-done.2.h1.h) | copy-start | bytes 589828
  19.4 4.1 %copy-start.27 = (bf16[192,192]{1,0:T(8,128)(2,1)S(1)}, bf16[192,192]{1,0:T(8,128)(2,1)}, u32[]{:S(2)}) copy-start(bf16[192,192]{1,0:T(8,128)(2,1)} %refs_1_.1) | copy-start | bytes 221188
  19.4 4.1 %copy-start.29 = (bf16[1,1,6,1536]{3,2,1,0:T(8,128)(2,1)S(1)}, bf16[1,1,6,1536]{3,2,1,0:T(8,128)(2,1)}, u32[]{:S(2)}) copy-start(bf16[1,1,6,1536]{3,2,1,0:T(8,128)(2,1)} %param.12) | copy-start | bytes 55300
  19.4 12.2 %collective-permute-start.4 = (bf16[384,256]{1,0:T(8,128)(2,1)}, bf16[384,256]{1,0:T(8,128)(2,1)}, u32[]{:S(2)}, u32[]{:S(2)}) collective-permute-start(bf16[384,256]{1,0:T(8,128)(2,1)} %margin_solve.5), channel_id=1, source_target_pairs={{0,4},{8,12},{16,20},{24,28},{4,0},{12,8},{20,16},{28,24},{1,5},{9... | collective-permute-start | bytes 589832 | tf_op jit(solution)/shard_map/ppermute | solution.py:286
  21.2 3.2 %copy-start.22 = (bf16[384,256]{1,0:T(8,128)(2,1)}, bf16[384,256]{1,0:T(8,128)(2,1)S(1)}, u32[]{:S(2)}) copy-start(bf16[384,256]{1,0:T(8,128)(2,1)S(1)} %collective-permute-done.h.h2) | copy-start | bytes 589828
  22.2 12.7 %collective-permute-start.1 = (bf16[384,256]{1,0:T(8,128)(2,1)}, bf16[384,256]{1,0:T(8,128)(2,1)}, u32[]{:S(2)}, u32[]{:S(2)}) collective-permute-start(bf16[384,256]{1,0:T(8,128)(2,1)} %margin_solve.4), channel_id=1, source_target_pairs={{4,8},{12,16},{20,24},{8,4},{16,12},{24,20},{5,9},{13,17},{21,25},... | collective-permute-start | bytes 589832 | tf_op jit(solution)/shard_map/ppermute | solution.py:286
  26.0 1.4 %copy-start.9 = (bf16[5,1,384,384]{3,2,1,0:T(8,128)(2,1)S(1)}, bf16[5,1,384,384]{3,2,1,0:T(8,128)(2,1)}, u32[]{:S(2)}) copy-start(bf16[5,1,384,384]{3,2,1,0:T(8,128)(2,1)} %param.11) | copy-start | bytes 4423684
  27.4 1.4 %copy-start.19 = (f32[4,384,256]{2,1,0:T(8,128)S(1)}, f32[4,384,256]{2,1,0:T(8,128)}, u32[]{:S(2)}) copy-start(f32[4,384,256]{2,1,0:T(8,128)} %copy-done.18) | copy-start | bytes 4718596
  28.8 0.9 copy-start.23
  29.7 0.9 copy-start.25
  30.7 1.3 %copy-start = (bf16[4,1,384,384]{3,2,1,0:T(8,128)(2,1)S(1)}, bf16[4,1,384,384]{3,2,1,0:T(8,128)(2,1)}, u32[]{:S(2)}) copy-start(bf16[4,1,384,384]{3,2,1,0:T(8,128)(2,1)} %param.9) | copy-start | bytes 3538948
  33.2 3.4 %copy-start.6 = (bf16[4,1,384,256]{3,2,1,0:T(8,128)(2,1)S(1)}, bf16[4,1,384,256]{3,2,1,0:T(8,128)(2,1)}, u32[]{:S(2)}) copy-start(bf16[4,1,384,256]{3,2,1,0:T(8,128)(2,1)} %param.7) | copy-start | bytes 2359300
  33.2 3.4 %copy-start.12 = (bf16[4,1,384,384]{3,2,1,0:T(8,128)(2,1)S(1)}, bf16[4,1,384,384]{3,2,1,0:T(8,128)(2,1)}, u32[]{:S(2)}) copy-start(bf16[4,1,384,384]{3,2,1,0:T(8,128)(2,1)} %param.8) | copy-start | bytes 3538948
  33.2 6.8 %collective-permute-start.6 = (bf16[384,256]{1,0:T(8,128)(2,1)S(1)}, bf16[384,256]{1,0:T(8,128)(2,1)S(1)}, u32[]{:S(2)}, u32[]{:S(2)}) collective-permute-start(bf16[384,256]{1,0:T(8,128)(2,1)S(1)} %get-tuple-element.49), channel_id=1, source_target_pairs={{0,4},{8,12},{16,20},{24,28},{4,0},{12,8},{20,16},{28,24},{1,5},{9... | collective-permute-start | bytes 589832 | tf_op jit(solution)/shard_map/ppermute | solution.py:286
  35.9 7.4 %collective-permute-start.3 = (bf16[384,256]{1,0:T(8,128)(2,1)S(1)}, bf16[384,256]{1,0:T(8,128)(2,1)S(1)}, u32[]{:S(2)}, u32[]{:S(2)}) collective-permute-start(bf16[384,256]{1,0:T(8,128)(2,1)S(1)} %get-tuple-element.43), channel_id=1, source_target_pairs={{4,8},{12,16},{20,24},{8,4},{16,12},{24,20},{5,9},{13,17},{21,25},... | collective-permute-start | bytes 589832 | tf_op jit(solution)/shard_map/ppermute | solution.py:286
  38.2 5.9 %copy-start.14 = (f32[4,384,256]{2,1,0:T(8,128)}, f32[4,384,256]{2,1,0:T(8,128)S(1)}, u32[]{:S(2)}) copy-start(f32[4,384,256]{2,1,0:T(8,128)S(1)} %get-tuple-element.63.wt) | copy-start | bytes 4718596
  38.2 7.2 %copy-start.2 = (f32[4,384,256]{2,1,0:T(8,128)}, f32[4,384,256]{2,1,0:T(8,128)S(1)}, u32[]{:S(2)}) copy-start(f32[4,384,256]{2,1,0:T(8,128)S(1)} %get-tuple-element.51.z) | copy-start | bytes 4718596
  40.9 19.4 %collective-permute-start.8 = (bf16[384,256]{1,0:T(8,128)(2,1)}, bf16[384,256]{1,0:T(8,128)(2,1)}, u32[]{:S(2)}, u32[]{:S(2)}) collective-permute-start(bf16[384,256]{1,0:T(8,128)(2,1)} %get-tuple-element.55), channel_id=1, source_target_pairs={{0,4},{8,12},{16,20},{24,28},{4,0},{12,8},{20,16},{28,24},{1,5},{9... | collective-permute-start | bytes 589832 | tf_op jit(solution)/shard_map/ppermute | solution.py:286
  44.1 20.1 %collective-permute-start.5 = (bf16[384,256]{1,0:T(8,128)(2,1)}, bf16[384,256]{1,0:T(8,128)(2,1)}, u32[]{:S(2)}, u32[]{:S(2)}) collective-permute-start(bf16[384,256]{1,0:T(8,128)(2,1)} %get-tuple-element.47), channel_id=1, source_target_pairs={{4,8},{12,16},{20,24},{8,4},{16,12},{24,20},{5,9},{13,17},{21,25},... | collective-permute-start | bytes 589832 | tf_op jit(solution)/shard_map/ppermute | solution.py:286
  45.8 1.2 %copy-start.16 = (f32[4,384,256]{2,1,0:T(8,128)}, f32[4,384,256]{2,1,0:T(8,128)S(1)}, u32[]{:S(2)}) copy-start(f32[4,384,256]{2,1,0:T(8,128)S(1)} %get-tuple-element.62.w) | copy-start | bytes 4718596
  46.9 0.7 copy-start.26
  47.7 0.9 copy-start.30
  48.5 18.9 %all-to-all-start.1 = ((bf16[32,16,256]{2,1,0:T(8,128)(2,1)}), bf16[32,16,256]{2,1,0:T(8,128)(2,1)S(1)}, u32[]{:S(2)}, u32[]{:S(2)}) async-start(bf16[32,16,256]{2,1,0:T(8,128)(2,1)} %copy-done.26), calls=%async_computation.1 | async-start | bytes 524288 | tf_op jit(solution)/shard_map/all_to_all | solution.py:294
  56.4 1.4 %copy-start.10 = (bf16[5,1,384,384]{3,2,1,0:T(8,128)(2,1)S(1)}, bf16[5,1,384,384]{3,2,1,0:T(8,128)(2,1)}, u32[]{:S(2)}) copy-start(bf16[5,1,384,384]{3,2,1,0:T(8,128)(2,1)} %param.11) | copy-start | bytes 4423684
  57.8 1.1 %copy-start.31 = (bf16[4,384,256]{2,1,0:T(8,128)(2,1)S(1)}, bf16[4,384,256]{2,1,0:T(8,128)(2,1)}, u32[]{:S(2)}) copy-start(bf16[4,384,256]{2,1,0:T(8,128)(2,1)} %copy-done.30) | copy-start | bytes 2359300
  60.3 5.8 %copy-start.20 = (f32[4,384,256]{2,1,0:T(8,128)}, f32[4,384,256]{2,1,0:T(8,128)S(1)}, u32[]{:S(2)}) copy-start(f32[4,384,256]{2,1,0:T(8,128)S(1)} %get-tuple-element.56.y) | copy-start | bytes 4718596
  62.5 9.9 %collective-permute-start.10 = (bf16[384,256]{1,0:T(8,128)(2,1)}, bf16[384,256]{1,0:T(8,128)(2,1)}, u32[]{:S(2)}, u32[]{:S(2)}) collective-permute-start(bf16[384,256]{1,0:T(8,128)(2,1)} %margin_solve.7), channel_id=1, source_target_pairs={{0,4},{8,12},{16,20},{24,28},{4,0},{12,8},{20,16},{28,24},{1,5},{9... | collective-permute-start | bytes 589832 | tf_op jit(solution)/shard_map/ppermute | solution.py:286
  66.1 8.8 %collective-permute-start.7 = (bf16[384,256]{1,0:T(8,128)(2,1)}, bf16[384,256]{1,0:T(8,128)(2,1)}, u32[]{:S(2)}, u32[]{:S(2)}) collective-permute-start(bf16[384,256]{1,0:T(8,128)(2,1)} %margin_solve.6), channel_id=1, source_target_pairs={{4,8},{12,16},{20,24},{8,4},{16,12},{24,20},{5,9},{13,17},{21,25},... | collective-permute-start | bytes 589832 | tf_op jit(solution)/shard_map/ppermute | solution.py:286
  67.4 1.4 %copy-start.11 = (bf16[5,1,384,384]{3,2,1,0:T(8,128)(2,1)S(1)}, bf16[5,1,384,384]{3,2,1,0:T(8,128)(2,1)}, u32[]{:S(2)}) copy-start(bf16[5,1,384,384]{3,2,1,0:T(8,128)(2,1)} %param.11) | copy-start | bytes 4423684
  68.8 1.4 %copy-start.21 = (f32[4,384,256]{2,1,0:T(8,128)S(1)}, f32[4,384,256]{2,1,0:T(8,128)}, u32[]{:S(2)}) copy-start(f32[4,384,256]{2,1,0:T(8,128)} %copy-done.20) | copy-start | bytes 4718596
  70.2 6.3 %copy-start.15 = (f32[4,384,256]{2,1,0:T(8,128)S(1)}, f32[4,384,256]{2,1,0:T(8,128)}, u32[]{:S(2)}) copy-start(f32[4,384,256]{2,1,0:T(8,128)} %copy-done.14) | copy-start | bytes 4718596
  70.2 6.3 %copy-start.17 = (f32[4,384,256]{2,1,0:T(8,128)S(1)}, f32[4,384,256]{2,1,0:T(8,128)}, u32[]{:S(2)}) copy-start(f32[4,384,256]{2,1,0:T(8,128)} %copy-done.16) | copy-start | bytes 4718596
  72.4 4.2 %copy-start.3 = (f32[4,384,256]{2,1,0:T(8,128)S(1)}, f32[4,384,256]{2,1,0:T(8,128)}, u32[]{:S(2)}) copy-start(f32[4,384,256]{2,1,0:T(8,128)} %copy-done.2) | copy-start | bytes 4718596
  72.4 4.2 %copy-start.7 = (bf16[4,1,384,256]{3,2,1,0:T(8,128)(2,1)S(1)}, bf16[4,1,384,256]{3,2,1,0:T(8,128)(2,1)}, u32[]{:S(2)}) copy-start(bf16[4,1,384,256]{3,2,1,0:T(8,128)(2,1)} %param.7) | copy-start | bytes 2359300
  72.4 4.2 %copy-start.13 = (bf16[4,1,384,384]{3,2,1,0:T(8,128)(2,1)S(1)}, bf16[4,1,384,384]{3,2,1,0:T(8,128)(2,1)}, u32[]{:S(2)}) copy-start(bf16[4,1,384,384]{3,2,1,0:T(8,128)(2,1)} %param.8) | copy-start | bytes 3538948
  73.5 9.4 %collective-permute-start.11 = (bf16[384,256]{1,0:T(8,128)(2,1)S(1)}, bf16[384,256]{1,0:T(8,128)(2,1)S(1)}, u32[]{:S(2)}, u32[]{:S(2)}) collective-permute-start(bf16[384,256]{1,0:T(8,128)(2,1)S(1)} %get-tuple-element.59), channel_id=1, source_target_pairs={{4,0},{12,8},{20,16},{28,24},{5,1},{13,9},{21,17},{29,25},{6,2},{1... | collective-permute-start | bytes 589832 | tf_op jit(solution)/shard_map/ppermute | solution.py:290
  75.8 7.2 %collective-permute-start.9 = (bf16[384,256]{1,0:T(8,128)(2,1)S(1)}, bf16[384,256]{1,0:T(8,128)(2,1)S(1)}, u32[]{:S(2)}, u32[]{:S(2)}) collective-permute-start(bf16[384,256]{1,0:T(8,128)(2,1)S(1)} %get-tuple-element.58), channel_id=1, source_target_pairs={{8,4},{16,12},{24,20},{9,5},{17,13},{25,21},{10,6},{18,14},{26,22}... | collective-permute-start | bytes 589832 | tf_op jit(solution)/shard_map/ppermute | solution.py:290

commit v3 on v2

v3 whole, which is shorter than its diff:
```python
import jax
import jax.numpy as jnp
from jax import lax
from jax.experimental import pallas as pl
from jax.experimental.pallas import tpu as pltpu
from jax.sharding import PartitionSpec as P

BF = jnp.bfloat16
F32 = jnp.float32
ALL = ("row", "col")
PAD = 16
LIMIT = 16 * 1024 * 1024
SCHEDULE_COST = 1200


def mm(a, b):
    return lax.dot_general(a, b, (((1,), (0,)), ((), ())), preferred_element_type=F32)


def mmt(a, b):
    return lax.dot_general(a, b, (((0,), (0,)), ((), ())), preferred_element_type=F32)


def colsum(x):
    return jnp.sum(x, axis=0, keepdims=True)


def is_lower(chain):
    return lax.rem(lax.axis_index("row"), 2) == (0 if chain == 2 else 1)


def goes_on(lower):
    row = lax.axis_index("row")
    return jnp.where(lower, row > 0, row < lax.axis_size("row") - 1)


def kept(x, lower):
    return jnp.where(goes_on(lower), x, jnp.zeros_like(x))


def pick(from2, from1):
    low2 = is_lower(2)
    return jnp.where(low2, from2, from1), jnp.where(low2, from1, from2)


def run_copies(pairs, sems):
    copies = [pltpu.make_async_copy(a, b, sems.at[i]) for i, (a, b) in enumerate(pairs)]
    for c in copies:
        c.start()
    for c in copies:
        c.wait()


def call(body, outs, args, name, flops=0, after=None, scratch=(), hbm=()):
    shapes = [jax.ShapeDtypeStruct(d, t) for d, t in outs]
    total = sum(a.size * a.dtype.itemsize for a in list(args) + shapes)
    count = len(args)
    late = [] if after is None else list(after)
    specs = [pl.BlockSpec(memory_space=pltpu.HBM if i in hbm else pltpu.VMEM) for i in range(count)]

    def kernel(*refs):
        body(*refs[:count], *refs[count + len(late) :])

    return pl.pallas_call(
        kernel,
        out_shape=shapes,
        in_specs=specs + [pl.BlockSpec(memory_space=pl.ANY)] * len(late),
        out_specs=[pl.BlockSpec(memory_space=pltpu.VMEM)] * len(outs),
        scratch_shapes=list(scratch),
        compiler_params=pltpu.CompilerParams(vmem_limit_bytes=LIMIT),
        cost_estimate=pl.CostEstimate(flops=flops, bytes_accessed=total, transcendentals=0),
        name=name,
    )(*args, *late)


def mark(out):
    out[...] = jnp.zeros(out.shape, F32)


def load_edge(chain):
    def body(r, s, sems):
        run_copies([(r.at[jnp.where(is_lower(chain), 0, r.shape[0] - 1)], s)], sems)

    return body


def margin_solve(chain):
    def body(h, e, ld, lu, s, diag, upper, sems):
        lower = is_lower(chain)
        at = [jnp.where(lower, 0, m.shape[0] - 1) for m in (ld, lu)]
        run_copies([(ld.at[at[0]], diag), (lu.at[at[1]], upper)], sems)

        @pl.when(lower)
        def _():
            s[...] = (mm(diag[...], h[...]) + mm(upper[...], e[...])).astype(BF)

        @pl.when(jnp.logical_not(lower))
        def _():
            s[...] = (mm(diag[...], h[...]) + mmt(upper[...], e[...])).astype(BF)

    return body


def solve_layers(h2, h1, o2, o1, e, ld, lu, gathered, fpad, fown, basis, p):
    e0, e5 = pick(h2[...], h1[...])
    e0, e5 = kept(e0, True), kept(e5, False)
    e1, e4 = pick(o2[...], o1[...])
    e2, e3 = e[1], e[2]
    g = gathered[...].reshape(-1, gathered.shape[-1])
    v = mm(fpad[...], g).astype(BF)
    u = mmt(fown[...], v).astype(BF)
    size = p.shape[1]
    p[0] = mm(ld[1], e1) + mm(lu[1], e2) + mmt(lu[0], e0)
    p[1] = mm(ld[2], e2) + mm(lu[2], e3) + mmt(lu[1], e1)
    p[2] = mm(ld[3], e3) + mm(lu[3], e4) + mmt(lu[2], e2)
    p[3] = mm(ld[4], e4) + mm(lu[4], e5) + mmt(lu[3], e3)
    for k in range(4):
        p[k] = p[k] + mmt(basis[:, k * size : (k + 1) * size], u)


def join_margin(chain):
    def body(m, p, su, z, s):
        lower = is_lower(chain)
        edge = p[jnp.where(lower, 0, 3)] + kept(m[...], lower).astype(F32)
        z[...] = edge
        s[...] = edge.astype(BF)

        @pl.when(jnp.logical_not(lower))
        def _():
            s[...] = mmt(su[3], edge.astype(BF)).astype(BF)

    return body


def inner_operate(z2, z1, p, r, sd, su, z, w, wb, rho):
    z[0], z[3] = pick(z2[...], z1[...])
    z[1] = p[1]
    z[2] = p[2]
    acc = jnp.zeros(rho.shape, F32)
    for k in range(4):
        zk = z[k]
        acc = acc + colsum(r[k].astype(F32) * zk)
        w[k] = mm(sd[k], zk.astype(BF))
        if k < 3:
            w[k] = w[k] + mm(su[k], z[k + 1].astype(BF))
        if k > 0:
            w[k] = w[k] + mmt(su[k - 1], z[k - 1].astype(BF))
        wb[k] = w[k].astype(BF)
    rho[...] = acc


def join_operate(chain):
    def body(n, w, su, edge, s):
        lower = is_lower(chain)
        term = kept(n[...], lower)

        @pl.when(lower)
        def _():
            edge[...] = w[0] + term.astype(F32)

        @pl.when(jnp.logical_not(lower))
        def _():
            edge[...] = w[3] + mm(su[3], term)

        s[...] = edge[...].astype(BF)

    return body


def coarse_rhs(ncb):
    def body(e, basis, g, held, sems):
        run_copies([(e, held)], sems)
        out = mm(basis[...], held[...].reshape(-1, e.shape[-1]))
        out = jnp.concatenate([out, jnp.zeros((PAD - ncb, out.shape[1]), F32)], axis=0).astype(BF)
        for k in range(g.shape[0]):
            g[k] = out

    return body


def prepare(ncb):
    def body(basis, factor, padded, fpad, fown):
        rows = basis[...].astype(F32)
        padded[...] = jnp.concatenate([rows, jnp.zeros((PAD - ncb, rows.shape[1]), F32)], axis=0).astype(BF)
        nco = factor.shape[0]
        own = lax.axis_index("row") * lax.axis_size("col") + lax.axis_index("col")

        def columns(first, width):
            source = lax.broadcasted_iota(jnp.int32, (nco, width), 0)
            target = lax.broadcasted_iota(jnp.int32, (nco, width), 1)
            at = lax.rem(target, PAD)
            match = (source == (first + target // PAD) * ncb + at) & (at < ncb)
            chosen = jnp.where(match, 1.0, 0.0).astype(BF)
            return mm(factor[...], chosen).astype(BF)

        fown[...] = columns(own, PAD)
        width = 128

        def step(i, carry):
            fpad[:, pl.ds(pl.multiple_of(i * width, width), width)] = columns(i * (width // PAD), width)
            return carry

        lax.fori_loop(0, fpad.shape[1] // width, step, 0)

    return body


def three(x):
    parts = []
    for _ in range(3):
        top = x.astype(BF).astype(F32)
        parts.append(top)
        x = x - top
    return parts


def coarse_rhs_sums(ncb):
    def body(w2, w1, w, z2, z1, p, rho, basis, g):
        ends = [pick(w2[...], w1[...]), pick(z2[...], z1[...])]
        acc = jnp.zeros(rho.shape, F32)
        out = jnp.zeros((ncb, rho.shape[1]), F32)
        size = w.shape[1]
        for k in range(4):
            wk, zk = (w[k], p[k]) if 0 < k < 3 else (pair[k // 3] for pair in ends)
            out = out + mm(basis[:, k * size : (k + 1) * size], wk.astype(BF))
            acc = acc + colsum(wk * zk)
        rows = [out, jnp.zeros((8 - ncb, out.shape[1]), F32)] + three(rho[...]) + three(acc)
        out = jnp.concatenate(rows + [jnp.zeros((2, out.shape[1]), F32)], axis=0).astype(BF)
        for k in range(g.shape[0]):
            g[k] = out

    return body


def join_second(chain):
    def body(m, p, su, q, s, product):
        lower = is_lower(chain)
        half = s.shape[1]
        edge = p[jnp.where(lower, 0, 3)] + kept(m[...], lower).astype(F32)
        q[...] = edge
        product[...] = edge

        @pl.when(lower)
        def _():
            s[...] = edge[:, :half].astype(BF)

        @pl.when(jnp.logical_not(lower))
        def _():
            out = 2.0 * mmt(su[3], edge.astype(BF))
            product[...] = out
            s[...] = out[:, half:].astype(BF)

    return body


def inner_products(q2, q1, o2, o1, p, z, r, w, sd, su, q, sums):
    q[0], q[3] = pick(q2[...], q1[...])
    q[1] = p[1]
    q[2] = p[2]
    ends = pick(o2[...], o1[...])
    s1 = s2 = s4 = s5 = jnp.zeros((1, q.shape[-1]), F32)
    for k in range(4):
        qk = q[k]
        qb = qk.astype(BF)
        wk = (w[k] if 0 < k < 3 else ends[k // 3]).astype(F32)
        zk = z[k]
        own = mm(sd[k], qb)
        s5 = s5 + colsum(qk * own)
        s4 = s4 + colsum(zk * own)
        s4 = s4 + colsum((wk + wk - mm(sd[k], zk.astype(BF))) * qk)
        if k < 3:
            s5 = s5 + 2.0 * colsum(qk * mm(su[k], q[k + 1].astype(BF)))
        s1 = s1 + colsum(r[k].astype(F32) * qk)
        s2 = s2 + colsum(wk * qk)
    sums[...] = jnp.concatenate([s1, s2, s4, s5], axis=0)


def join_sums(t2, t1, c2, c1, sums, out):
    low_in, high_in = pick(t2[...], t1[...])
    low, high = pick(c2[...], c1[...])
    half = low_in.shape[1]
    above = colsum(high[:, :half] * kept(high_in, False).astype(F32))
    below = colsum(low[:, half:] * kept(low_in, True).astype(F32))
    s5 = sums[3:4] + jnp.concatenate([above, below], axis=1)
    full = jnp.concatenate([sums[0:3], s5], axis=0)
    for k in range(out.shape[0]):
        out[k] = full


def finish(parts, early, z, q, x):
    total = parts[0]
    first = early[0].astype(F32)
    for k in range(1, parts.shape[0]):
        total = total + parts[k]
        first = first + early[k].astype(F32)
    rho0 = first[8:9] + first[9:10] + first[10:11]
    d0 = first[11:12] + first[12:13] + first[13:14]
    s1, s2, s4, s5 = (total[k : k + 1] for k in range(4))
    a0 = rho0 / d0
    rho1 = a0 * (a0 * s2 - s1)
    grow = 1.0 + rho1 / rho0
    a1 = rho1 / (grow * grow * d0 - grow * a0 * s4 + a0 * a0 * s5)
    cz = a0 + a1 * grow
    cq = a1 * a0
    for k in range(4):
        x[k] = cz * z[k] - cq * q[k]


def swap(chain, x):
    rows, cols = lax.axis_size("row"), lax.axis_size("col")
    moves = []
    for row in range(rows):
        other = row + 1 if (row % 2 == 0) == (chain == 1) else row - 1
        for col in range(cols):
            inside = 0 <= other < rows
            to = (other, col) if inside else (row, min(col ^ 1, cols - 1))
            moves.append((row * cols + col, to[0] * cols + to[1]))
    return lax.ppermute(x, ALL, moves)


def gather(copies):
    return lax.all_to_all(copies, ALL, 0, 0)


def on_device(rhs, stiff_diag, stiff_upper, local_diag, local_upper, coarse_basis, coarse_factor):
    layers, _, size, cols = rhs.shape
    devices = lax.axis_size("row") * lax.axis_size("col")
    ncb, nco = coarse_basis.shape[2], coarse_factor.shape[0]
    layer, whole, row = (size, cols), (layers, size, cols), (1, cols)
    copies = ((devices, PAD, cols), BF)
    edge = [(layer, F32), (layer, BF)]
    block = 2 * size * size * cols
    dma = lambda n: pltpu.SemaphoreType.DMA((n,))
    r, sd, su, ld, lu = rhs[:, 0], stiff_diag[:, 0], stiff_upper[:, 0], local_diag[:, 0], local_upper[:, 0]
    raw_basis = coarse_basis[0, 0]

    def margins(h2, h1, o2, o1, order):
        blocks = [pltpu.VMEM((size, size), BF)] * 2 + [dma(2)]
        take = lambda chain, h, o, after: call(
            margin_solve(chain), [(layer, BF)], (h, o, ld, lu), "margin_solve", 2 * block, after, blocks, (2, 3)
        )[0]
        s2 = take(2, h2, o2, order)
        s1 = take(1, h1, o1, [s2])
        return swap(2, s2), swap(1, s1)

    def beside(g):
        return call(mark, [((8, 128), F32)], (), "beside", SCHEDULE_COST * block, [g])[0]

    def solve(h2, h1, o2, o1, e, gathered):
        args = (h2, h1, o2, o1, e, ld, lu, gathered, fpad, fown, basis)
        return call(solve_layers, [(whole, F32)], args, "solve_layers", 12 * block)[0]

    (s2,) = call(load_edge(2), [(layer, BF)], (r,), "load_edge", 0, None, [dma(1)], (0,))
    h2 = swap(2, s2)
    (s1,) = call(load_edge(1), [(layer, BF)], (r,), "load_edge", 0, [s2], [dma(1)], (0,))
    h1 = swap(1, s1)
    (g,) = call(coarse_rhs(ncb), [copies], (r, raw_basis), "coarse_rhs", block // 32, [s1], [pltpu.VMEM(whole, BF), dma(1)], (0,))
    gathered = gather(g)
    m2, m1 = margins(h2, h1, s2, s1, [beside(g)])
    basis, fpad, fown = call(
        prepare(ncb),
        [((PAD, layers * size), BF), ((nco, devices * PAD), BF), ((nco, PAD), BF)],
        (raw_basis, coarse_factor),
        "prepare",
        block // 8,
        [gathered],
    )
    p = solve(h2, h1, s2, s1, r, gathered)
    z2, s2 = call(join_margin(2), edge, (m2, p, su), "join_margin", block)
    z1, s1 = call(join_margin(1), edge, (m1, p, su), "join_margin", block, [s2])
    n2, n1 = swap(2, s2), swap(1, s1)
    z, wi, w, rho = call(
        inner_operate, [(whole, F32)] * 2 + [(whole, BF), (row, F32)], (z2, z1, p, r, sd, su), "inner_operate", 10 * block
    )
    w2, o2 = call(join_operate(2), edge, (n2, wi, su), "join_operate", block)
    w1, o1 = call(join_operate(1), edge, (n1, wi, su), "join_operate", block, [o2])
    h2, h1 = swap(2, o2), swap(1, o1)
    (g,) = call(coarse_rhs_sums(ncb), [copies], (w2, w1, wi, z2, z1, p, rho, raw_basis), "coarse_rhs_sums", block // 32)
    early = gather(g)
    m2, m1 = margins(h2, h1, o2, o1, [beside(g)])
    p = solve(h2, h1, o2, o1, w, early)
    half = [(layer, F32), ((size, cols // 2), BF), (layer, F32)]
    q2, s2, c2 = call(join_second(2), half, (m2, p, su), "join_second", block)
    q1, s1, c1 = call(join_second(1), half, (m1, p, su), "join_second", block, [s2])
    t2, t1 = swap(2, s2), swap(1, s1)
    q, sums = call(
        inner_products,
        [(whole, F32), ((4, cols), F32)],
        (q2, q1, o2, o1, p, z, r, w, sd, su),
        "inner_products",
        12 * block,
    )
    (g,) = call(join_sums, [((devices, 4, cols), F32)], (t2, t1, c2, c1, sums), "join_sums")
    (x,) = call(finish, [(whole, F32)], (gather(g), early, z, q), "finish")
    return x[:, None]


def solution(mesh):
    split = P("row", "col", None, None)
    return jax.shard_map(on_device, mesh=mesh, in_specs=(split,) * 6 + (P(),), out_specs=split, check_vma=False)
```

time: 102 us -> 93.8 us (0.920)
  starting transfers between devices: 33.4 us -> 24.6 us
  waiting for transfers between devices: 8.73 us -> 14.6 us
  blocking collectives: 16.7 us -> 13.7 us
  local copies, waits for them, and re-layouts: 16.4 us -> 15 us
    all_to_all x2, starting transfers between devices: 12.6 us -> 7.57 us  [gather(): return lax.all_to_all(copies, ALL, 0, 0)]
    ppermute x12, starting transfers between devices: 20.8 us -> 17.1 us  [swap(): return lax.ppermute(x, ALL, moves)]
    ppermute x12, waiting for transfers between devices: 7.13 us -> 10.5 us  [swap(): return lax.ppermute(x, ALL, moves)]
    all_to_all x1, blocking collectives: 16.7 us -> 13.7 us  [gather(): return lax.all_to_all(copies, ALL, 0, 0)]
    all_to_all x2, waiting for transfers between devices: 1.59 us -> 4.06 us  [gather(): return lax.all_to_all(copies, ALL, 0, 0)]
    unnamed x64 -> x66, local copies, waits for them, and re-layouts: 16.4 us -> 15 us
    pallas_call x22 -> x23, Pallas kernels: 25.6 us -> 24.6 us  [call(): pl.pallas_call(kernel, out_shape=shapes, in_specs=specs + [pl.BlockSpec(m...]
  transfers between devices with their start and end apart: 14 -> 14, of which waited for: 3 -> 4; matrix products, arithmetic and copies ran while one was open for 0% -> 0% of each run, Pallas kernels for 23% -> 23%
where the time goes in v3:
time: 93.8 us; the launch traced here: 93 us
  Pallas kernels  24.6 us (26%)
  starting transfers between devices  24.6 us (26%)
  local copies, waits for them, and re-layouts  15 us (16%)
  waiting for transfers between devices  14.6 us (16%)
  blocking collectives  13.7 us (15%)
    pallas_call x23, Pallas kernels, call(): pl.pallas_call(kernel, out_shape=shapes, in_specs=specs + [pl.BlockSpec(m...  24.6 us
    ppermute x12, starting transfers between devices, swap(): return lax.ppermute(x, ALL, moves)  17.1 us
    unnamed x66, local copies, waits for them, and re-layouts  15 us
    all_to_all x1, blocking collectives, gather(): return lax.all_to_all(copies, ALL, 0, 0)  13.7 us
    ppermute x12, waiting for transfers between devices, swap(): return lax.ppermute(x, ALL, moves)  10.5 us
    all_to_all x2, starting transfers between devices, gather(): return lax.all_to_all(copies, ALL, 0, 0)  7.57 us
    all_to_all x2, waiting for transfers between devices, gather(): return lax.all_to_all(copies, ALL, 0, 0)  4.06 us
  transfers between devices with their start and end apart: 14, of which 4 were waited for; matrix products, arithmetic and copies ran while one was open for 0% of the time, Pallas kernels for 23%

profile of v3, /device:TPU:0, one launch (start us, length us, event | category | flops | bytes accessed | tf_op | source)
XLA Modules:
  0.0 93.0 jit_solution(4848235506297725613)
XLA Ops:
  0.0 1.1 %copy-done.6 = bf16[4,1,384,256]{3,2,1,0:T(8,128)(2,1)S(1)} copy-done((bf16[4,1,384,256]{3,2,1,0:T(8,128)(2,1)S(1)}, bf16[4,1,384,256]{3,2,1,0:T(8,128)(2,1)}, u32[]{:S(2)}) %copy-start.6) | copy-done | bytes 786456
  1.1 0.2 load_edge.2.refs_1_.refs_2_
  1.4 0.5 collective-permute-start
  2.1 4.1 %collective-permute-start.2 = (bf16[384,256]{1,0:T(8,128)(2,1)S(1)}, bf16[384,256]{1,0:T(8,128)(2,1)S(1)}, u32[]{:S(2)}, u32[]{:S(2)}) collective-permute-start(bf16[384,256]{1,0:T(8,128)(2,1)S(1)} %load_edge.3.refs_2_.refs_3_.refs_1_), channel_id=1, source_target_pairs={{0,4},{1,5},{2,6},{3,7},{4,0},{5,1},{6,2},{7,3},{8,12},{9,13},{10,... | collective-permute-start | bytes 589832 | tf_op jit(solution)/shard_map/ppermute | solution.py:318
  6.2 1.0 %coarse_rhs.1.refs_0_ = bf16[32,16,256]{2,1,0:T(8,128)(2,1)} custom-call(bf16[4,384,256]{2,1,0:T(8,128)(2,1)S(1)} %bitcast.31, bf16[6,1536]{1,0:T(8,128)(2,1)S(1)} %bitcast.37, bf16[384,256]{1,0:T(8,128)(2,1)S(1)} %load_edge.3.refs_2_.refs_3_.refs_1_), custom_call_target="tpu_custom_call" | custom-call | flops 2359296 | bytes 1067008 | tf_op jit(solution)/shard_map/coarse_rhs/pallas_call | solution.py:64
  7.2 4.7 %all-to-all-start = ((bf16[32,16,256]{2,1,0:T(8,128)(2,1)}), bf16[32,16,256]{2,1,0:T(8,128)(2,1)S(1)}, u32[]{:S(2)}, u32[]{:S(2)}) async-start(bf16[32,16,256]{2,1,0:T(8,128)(2,1)} %coarse_rhs.1.refs_0_), calls=%async_computation | async-start | bytes 524288 | tf_op jit(solution)/shard_map/all_to_all | solution.py:322
  12.0 1.5 %copy-done.1 = bf16[6,1,384,384]{3,2,1,0:T(8,128)(2,1)S(1)} copy-done((bf16[6,1,384,384]{3,2,1,0:T(8,128)(2,1)S(1)}, bf16[6,1,384,384]{3,2,1,0:T(8,128)(2,1)}, u32[]{:S(2)}) %copy-start.1) | copy-done | bytes 1769496
  13.5 0.4 copy-done.2
  14.0 0.5 margin_solve.4.refs_4_
  14.5 0.3 collective-permute-start.1
  14.8 1.2 %margin_solve.5 = bf16[384,256]{1,0:T(8,128)(2,1)} custom-call(bf16[384,256]{1,0:T(8,128)(2,1)S(1)} %collective-permute-done.2.refs_1_.refs_0_, bf16[384,256]{1,0:T(8,128)(2,1)S(1)} %load_edge.3.refs_2_.refs_3_.refs_1_, bf16[6,384,384]{2,1,0:T(8,128)(2,1)S(1)} %bitcast.18, bf16[5,384,384]{2,1,0:T(8,128)(2,1)S(1)} %bitcast.24, ...), custom_call_target="tpu_custom_call" | custom-call | flops 150994944 | bytes 3833856 | tf_op jit(solution)/shard_map/margin_solve/pallas_call | solution.py:64
  16.1 3.0 %collective-permute-start.4 = (bf16[384,256]{1,0:T(8,128)(2,1)}, bf16[384,256]{1,0:T(8,128)(2,1)}, u32[]{:S(2)}, u32[]{:S(2)}) collective-permute-start(bf16[384,256]{1,0:T(8,128)(2,1)} %margin_solve.5), channel_id=1, source_target_pairs={{0,4},{1,5},{2,6},{3,7},{4,0},{5,1},{6,2},{7,3},{8,12},{9,13},{10,... | collective-permute-start | bytes 589832 | tf_op jit(solution)/shard_map/ppermute | solution.py:318
  19.1 3.5 %all-to-all-done.refs_2_.refs_7_ = bf16[32,16,256]{2,1,0:T(8,128)(2,1)S(1)} async-done(((bf16[32,16,256]{2,1,0:T(8,128)(2,1)}), bf16[32,16,256]{2,1,0:T(8,128)(2,1)S(1)}, u32[]{:S(2)}, u32[]{:S(2)}) %all-to-all-start) | async-done | bytes 262176 | tf_op jit(solution)/shard_map/all_to_all | solution.py:322
  22.6 0.9 prepare.1
  23.5 1.5 %copy-done.3 = bf16[5,1,384,384]{3,2,1,0:T(8,128)(2,1)S(1)} copy-done((bf16[5,1,384,384]{3,2,1,0:T(8,128)(2,1)S(1)}, bf16[5,1,384,384]{3,2,1,0:T(8,128)(2,1)}, u32[]{:S(2)}) %copy-start.3) | copy-done | bytes 1474584
  25.0 1.1 %copy-done.7 = bf16[4,1,384,256]{3,2,1,0:T(8,128)(2,1)S(1)} copy-done((bf16[4,1,384,256]{3,2,1,0:T(8,128)(2,1)S(1)}, bf16[4,1,384,256]{3,2,1,0:T(8,128)(2,1)}, u32[]{:S(2)}) %copy-start.7) | copy-done | bytes 786456
  26.1 0.9 %copy-done.17 = bf16[32,16,256]{2,1,0:T(8,128)(2,1)S(1)} copy-done((bf16[32,16,256]{2,1,0:T(8,128)(2,1)S(1)}, bf16[32,16,256]{2,1,0:T(8,128)(2,1)}, u32[]{:S(2)}) %copy-start.17) | copy-done | bytes 262168
  27.1 0.9 copy-done.21
  28.0 0.9 copy-done.23
  28.9 1.9 %solve_layers.2.refs_1_.refs_2_.refs_5_ = f32[4,384,256]{2,1,0:T(8,128)S(1)} custom-call(bf16[384,256]{1,0:T(8,128)(2,1)S(1)} %copy-done.21, bf16[384,256]{1,0:T(8,128)(2,1)S(1)} %copy-done.23, bf16[384,256]{1,0:T(8,128)(2,1)S(1)} %load_edge.2.refs_1_.refs_2_, bf16[384,256]{1,0:T(8,128)(2,1)S(1)} %load_edge.3.refs_2_.refs_3_.refs_1_, ...), custom_call_target="tpu_custom_call" | custom-call | flops 905969664 | bytes 6903808 | tf_op jit(solution)/shard_map/solve_layers/pallas_call | solution.py:64
  30.8 1.0 %join_margin.2 = (f32[384,256]{1,0:T(8,128)S(1)}, bf16[384,256]{1,0:T(8,128)(2,1)S(1)}) custom-call(bf16[384,256]{1,0:T(8,128)(2,1)} %collective-permute-done.1.refs_0_, f32[4,384,256]{2,1,0:T(8,128)S(1)} %solve_layers.2.refs_1_.refs_2_.refs_5_, bf16[4,384,384]{2,1,0:T(8,128)(2,1)S(1)} %bitcast.9), custom_call_target="tpu_custom_call" | custom-call | flops 75497472 | bytes 3538944 | tf_op jit(solution)/shard_map/join_margin/pallas_call | solution.py:64
  31.9 1.4 %join_margin.3 = (f32[384,256]{1,0:T(8,128)S(1)}, bf16[384,256]{1,0:T(8,128)(2,1)S(1)}) custom-call(bf16[384,256]{1,0:T(8,128)(2,1)} %collective-permute-done.4.refs_0_, f32[4,384,256]{2,1,0:T(8,128)S(1)} %solve_layers.2.refs_1_.refs_2_.refs_5_, bf16[4,384,384]{2,1,0:T(8,128)(2,1)S(1)} %bitcast.10, bf16[384,256]{1,0:T(8,128)(2,1)S(1)} %get-tuple-element.31.refs_3_), custom_call_target="tpu_custom_call" | custom-call | flops 75497472 | bytes 3538944 | tf_op jit(solution)/shard_map/join_margin/pallas_call | solution.py:64
  33.3 2.4 %collective-permute-start.6 = (bf16[384,256]{1,0:T(8,128)(2,1)S(1)}, bf16[384,256]{1,0:T(8,128)(2,1)S(1)}, u32[]{:S(2)}, u32[]{:S(2)}) collective-permute-start(bf16[384,256]{1,0:T(8,128)(2,1)S(1)} %get-tuple-element.37), channel_id=1, source_target_pairs={{0,4},{1,5},{2,6},{3,7},{4,0},{5,1},{6,2},{7,3},{8,12},{9,13},{10,... | collective-permute-start | bytes 589832 | tf_op jit(solution)/shard_map/ppermute | solution.py:318
  35.7 1.2 %inner_operate.1 = (f32[4,384,256]{2,1,0:T(8,128)S(1)}, f32[4,384,256]{2,1,0:T(8,128)S(1)}, bf16[4,384,256]{2,1,0:T(8,128)(2,1)S(1)}, f32[1,256]{1,0:T(1,128)S(1)}) custom-call(f32[384,256]{1,0:T(8,128)S(1)} %get-tuple-element.32.refs_0_.refs_3_, f32[384,256]{1,0:T(8,128)S(1)} %get-tuple-element.33.refs_1_.refs_4_, ...), custom_call_target="tpu_custom_call" | custom-call | flops 754974720 | bytes 9438208 | tf_op jit(solution)/shard_map/inner_operate/pallas_call | solution.py:64
  37.1 9.2 %collective-permute-done.6.refs_0_ = bf16[384,256]{1,0:T(8,128)(2,1)S(1)} collective-permute-done((bf16[384,256]{1,0:T(8,128)(2,1)S(1)}, bf16[384,256]{1,0:T(8,128)(2,1)S(1)}, u32[]{:S(2)}, u32[]{:S(2)}) %collective-permute-start.6) | collective-permute-done | bytes 196640 | tf_op jit(solution)/shard_map/ppermute | solution.py:318
  46.3 1.0 %join_operate.3 = (f32[384,256]{1,0:T(8,128)S(1)}, bf16[384,256]{1,0:T(8,128)(2,1)}) custom-call(bf16[384,256]{1,0:T(8,128)(2,1)S(1)} %collective-permute-done.6.refs_0_, f32[4,384,256]{2,1,0:T(8,128)S(1)} %get-tuple-element.34.refs_1_.refs_2_, bf16[4,384,384]{2,1,0:T(8,128)(2,1)S(1)} %bitcast.13, bf16[384,256]{1,0:T(8,128)(2,1)S(1)} %get-tuple-element.35.refs_3_.refs_1_.refs_2_), custom_call_target="tpu_custom_call" | custom-call | flops 75497472 | bytes 3538944 | tf_op jit(solution)/shard_map/join_operate/pallas_call | solution.py:64
  47.3 2.2 %collective-permute-start.8 = (bf16[384,256]{1,0:T(8,128)(2,1)}, bf16[384,256]{1,0:T(8,128)(2,1)}, u32[]{:S(2)}, u32[]{:S(2)}) collective-permute-start(bf16[384,256]{1,0:T(8,128)(2,1)} %get-tuple-element.40.refs_3_.refs_1_), channel_id=1, source_target_pairs={{0,4},{1,5},{2,6},{3,7},{4,0},{5,1},{6,2},{7,3},{8,12},{9,13},{10,... | collective-permute-start | bytes 589832 | tf_op jit(solution)/shard_map/ppermute | solution.py:318
  49.5 0.3 coarse_rhs_sums.1.refs_0_
  49.9 0.7 copy-done.18
  50.5 2.8 %all-to-all-start.1 = ((bf16[32,16,256]{2,1,0:T(8,128)(2,1)}), bf16[32,16,256]{2,1,0:T(8,128)(2,1)S(1)}, u32[]{:S(2)}, u32[]{:S(2)}) async-start(bf16[32,16,256]{2,1,0:T(8,128)(2,1)} %copy-done.18), calls=%async_computation.1 | async-start | bytes 524288 | tf_op jit(solution)/shard_map/all_to_all | solution.py:322
  53.4 1.0 %copy-done.19 = bf16[32,16,256]{2,1,0:T(8,128)(2,1)S(1)} copy-done((bf16[32,16,256]{2,1,0:T(8,128)(2,1)S(1)}, bf16[32,16,256]{2,1,0:T(8,128)(2,1)}, u32[]{:S(2)}) %copy-start.19) | copy-done | bytes 262168
  54.4 1.4 %copy-done.4 = bf16[5,1,384,384]{3,2,1,0:T(8,128)(2,1)S(1)} copy-done((bf16[5,1,384,384]{3,2,1,0:T(8,128)(2,1)S(1)}, bf16[5,1,384,384]{3,2,1,0:T(8,128)(2,1)}, u32[]{:S(2)}) %copy-start.4) | copy-done | bytes 1474584
  55.8 2.1 %margin_solve.6.refs_4_ = bf16[384,256]{1,0:T(8,128)(2,1)} custom-call(bf16[384,256]{1,0:T(8,128)(2,1)} %collective-permute-done.5.refs_0_, bf16[384,256]{1,0:T(8,128)(2,1)S(1)} %get-tuple-element.35.refs_3_.refs_1_.refs_2_, bf16[6,384,384]{2,1,0:T(8,128)(2,1)S(1)} %bitcast.20, bf16[5,384,384]{2,1,0:T(8,128)(2,1)S(1)} %bitcast.26, f32[8,128]{1,0:T(8,128)S(1)} %beside.3.refs_4_), custom_call_target="tpu_custom_call" | custom-call | flops 150994944 | bytes 3833856 | tf_op jit(solution)/shard_map/margin_solve/pallas_call | solution.py:64
  57.9 0.3 collective-permute-start.7
  58.2 2.2 %margin_solve.7 = bf16[384,256]{1,0:T(8,128)(2,1)} custom-call(bf16[384,256]{1,0:T(8,128)(2,1)} %collective-permute-done.8.refs_1_.refs_0_, bf16[384,256]{1,0:T(8,128)(2,1)} %get-tuple-element.40.refs_3_.refs_1_, bf16[6,384,384]{2,1,0:T(8,128)(2,1)S(1)} %bitcast.21, bf16[5,384,384]{2,1,0:T(8,128)(2,1)S(1)} %bitcast.27, bf16[384,256]{1,0:T(8,128)(2,1)} %margin_solve.6.refs_4_), custom_call_target="tpu_custom_call" | custom-call | flops 150994944 | bytes 3833856 | tf_op jit(solution)/shard_map/margin_solve/pallas_call | solution.py:64
  60.4 3.0 %collective-permute-start.10 = (bf16[384,256]{1,0:T(8,128)(2,1)}, bf16[384,256]{1,0:T(8,128)(2,1)}, u32[]{:S(2)}, u32[]{:S(2)}) collective-permute-start(bf16[384,256]{1,0:T(8,128)(2,1)} %margin_solve.7), channel_id=1, source_target_pairs={{0,4},{1,5},{2,6},{3,7},{4,0},{5,1},{6,2},{7,3},{8,12},{9,13},{10,... | collective-permute-start | bytes 589832 | tf_op jit(solution)/shard_map/ppermute | solution.py:318
  63.5 0.5 all-to-all-done.1.refs_7_.refs_1_
  64.0 1.4 %copy-done.5 = bf16[5,1,384,384]{3,2,1,0:T(8,128)(2,1)S(1)} copy-done((bf16[5,1,384,384]{3,2,1,0:T(8,128)(2,1)S(1)}, bf16[5,1,384,384]{3,2,1,0:T(8,128)(2,1)}, u32[]{:S(2)}) %copy-start.5) | copy-done | bytes 1474584
  65.4 1.1 %copy-done.14 = bf16[4,384,256]{2,1,0:T(8,128)(2,1)S(1)} copy-done((bf16[4,384,256]{2,1,0:T(8,128)(2,1)S(1)}, bf16[4,384,256]{2,1,0:T(8,128)(2,1)}, u32[]{:S(2)}) %copy-start.14) | copy-done | bytes 786456
  66.5 0.9 copy-done.25
  67.4 3.0 %solve_layers.3.refs_1_.refs_4_ = f32[4,384,256]{2,1,0:T(8,128)S(1)} custom-call(bf16[384,256]{1,0:T(8,128)(2,1)} %collective-permute-done.5.refs_0_, bf16[384,256]{1,0:T(8,128)(2,1)} %collective-permute-done.8.refs_1_.refs_0_, bf16[384,256]{1,0:T(8,128)(2,1)S(1)} %get-tuple-element.35.refs_3_.refs_1_.refs_2_, ...), custom_call_target="tpu_custom_call" | custom-call | flops 905969664 | bytes 6903808 | tf_op jit(solution)/shard_map/solve_layers/pallas_call | solution.py:64
  70.4 1.1 %join_second.2 = (f32[384,256]{1,0:T(8,128)S(1)}, bf16[384,128]{1,0:T(8,128)(2,1)S(1)}, f32[384,256]{1,0:T(8,128)S(1)}) custom-call(bf16[384,256]{1,0:T(8,128)(2,1)} %collective-permute-done.7.refs_0_, f32[4,384,256]{2,1,0:T(8,128)S(1)} %solve_layers.3.refs_1_.refs_4_, bf16[4,384,384]{2,1,0:T(8,128)(2,1)S(1)} %bitcast.14), custom_call_target="tpu_custom_call" | custom-call | flops 75497472 | bytes 3833856 | tf_op jit(solution)/shard_map/join_second/pallas_call | solution.py:64
  71.6 1.4 %join_second.3 = (f32[384,256]{1,0:T(8,128)S(1)}, bf16[384,128]{1,0:T(8,128)(2,1)S(1)}, f32[384,256]{1,0:T(8,128)S(1)}) custom-call(bf16[384,256]{1,0:T(8,128)(2,1)} %collective-permute-done.10.refs_0_, f32[4,384,256]{2,1,0:T(8,128)S(1)} %solve_layers.3.refs_1_.refs_4_, bf16[4,384,384]{2,1,0:T(8,128)(2,1)S(1)} %bitcast.15, ...), custom_call_target="tpu_custom_call" | custom-call | flops 75497472 | bytes 3833856 | tf_op jit(solution)/shard_map/join_second/pallas_call | solution.py:64
  73.1 1.0 %collective-permute-start.11 = (bf16[384,128]{1,0:T(8,128)(2,1)S(1)}, bf16[384,128]{1,0:T(8,128)(2,1)S(1)}, u32[]{:S(2)}, u32[]{:S(2)}) collective-permute-start(bf16[384,128]{1,0:T(8,128)(2,1)S(1)} %get-tuple-element.43), channel_id=1, source_target_pairs={{0,4},{1,5},{2,6},{3,7},{4,0},{5,1},{6,2},{7,3},{8,12},{9,13},{10,... | collective-permute-start | bytes 294920 | tf_op jit(solution)/shard_map/ppermute | solution.py:318
  74.2 2.3 %inner_products.1 = (f32[4,384,256]{2,1,0:T(8,128)S(1)}, f32[4,256]{1,0:T(4,128)S(1)}) custom-call(f32[384,256]{1,0:T(8,128)S(1)} %get-tuple-element.46.refs_0_, f32[384,256]{1,0:T(8,128)S(1)} %get-tuple-element.47.refs_1_, bf16[384,256]{1,0:T(8,128)(2,1)S(1)} %get-tuple-element.35.refs_3_.refs_1_.refs_2_, ...), custom_call_target="tpu_custom_call" | custom-call | flops 905969664 | bytes 9834496 | tf_op jit(solution)/shard_map/inner_products/pallas_call | solution.py:64
  76.4 1.3 %collective-permute-done.11.refs_1_ = bf16[384,128]{1,0:T(8,128)(2,1)S(1)} collective-permute-done((bf16[384,128]{1,0:T(8,128)(2,1)S(1)}, bf16[384,128]{1,0:T(8,128)(2,1)S(1)}, u32[]{:S(2)}, u32[]{:S(2)}) %collective-permute-start.11) | collective-permute-done | bytes 98336 | tf_op jit(solution)/shard_map/ppermute | solution.py:318
  78.0 13.7 %all_to_all.15.refs_0_ = f32[32,4,256]{2,1,0:T(4,128)S(1)} all-to-all(f32[32,4,256]{2,1,0:T(4,128)S(1)} %join_sums.1), channel_id=1, replica_groups=mesh['row'=8,'col'=4] {'row','col'}, dimensions={0} | all-to-all | bytes 262144 | tf_op jit(solution)/shard_map/all_to_all | solution.py:322
  91.7 1.4 %finish.1 = f32[4,384,256]{2,1,0:T(8,128)} custom-call(f32[32,4,256]{2,1,0:T(4,128)S(1)} %all_to_all.15.refs_0_, bf16[32,16,256]{2,1,0:T(8,128)(2,1)S(1)} %all-to-all-done.1.refs_7_.refs_1_, f32[4,384,256]{2,1,0:T(8,128)S(1)} %copy-done.10, f32[4,384,256]{2,1,0:T(8,128)S(1)} %get-tuple-element.50.refs_3_), custom_call_target="tpu_custom_call" | custom-call | bytes 5111808 | tf_op jit(solution)/shard_map/finish/pallas_call | solution.py:64
  (70 shorter events, 0.8 us)
Async XLA Ops:
  0.0 1.1 %copy-start.6 = (bf16[4,1,384,256]{3,2,1,0:T(8,128)(2,1)S(1)}, bf16[4,1,384,256]{3,2,1,0:T(8,128)(2,1)}, u32[]{:S(2)}) copy-start(bf16[4,1,384,256]{3,2,1,0:T(8,128)(2,1)} %param.7) | copy-start | bytes 2359300
  1.1 5.1 %copy-start.26 = (bf16[1,1,6,1536]{3,2,1,0:T(8,128)(2,1)S(1)}, bf16[1,1,6,1536]{3,2,1,0:T(8,128)(2,1)}, u32[]{:S(2)}) copy-start(bf16[1,1,6,1536]{3,2,1,0:T(8,128)(2,1)} %param.12) | copy-start | bytes 55300
  1.4 10.6 %collective-permute-start = (bf16[384,256]{1,0:T(8,128)(2,1)S(1)}, bf16[384,256]{1,0:T(8,128)(2,1)S(1)}, u32[]{:S(2)}, u32[]{:S(2)}) collective-permute-start(bf16[384,256]{1,0:T(8,128)(2,1)S(1)} %load_edge.2.refs_1_.refs_2_), channel_id=1, source_target_pairs={{0,1},{1,0},{2,3},{3,2},{4,8},{5,9},{6,10},{7,11},{8,4},{9,5},{10,... | collective-permute-start | bytes 589832 | tf_op jit(solution)/shard_map/ppermute | solution.py:318
  2.1 12.7 %collective-permute-start.2 = (bf16[384,256]{1,0:T(8,128)(2,1)S(1)}, bf16[384,256]{1,0:T(8,128)(2,1)S(1)}, u32[]{:S(2)}, u32[]{:S(2)}) collective-permute-start(bf16[384,256]{1,0:T(8,128)(2,1)S(1)} %load_edge.3.refs_2_.refs_3_.refs_1_), channel_id=1, source_target_pairs={{0,4},{1,5},{2,6},{3,7},{4,0},{5,1},{6,2},{7,3},{8,12},{9,13},{10,... | collective-permute-start | bytes 589832 | tf_op jit(solution)/shard_map/ppermute | solution.py:318
  7.2 15.3 %all-to-all-start = ((bf16[32,16,256]{2,1,0:T(8,128)(2,1)}), bf16[32,16,256]{2,1,0:T(8,128)(2,1)S(1)}, u32[]{:S(2)}, u32[]{:S(2)}) async-start(bf16[32,16,256]{2,1,0:T(8,128)(2,1)} %coarse_rhs.1.refs_0_), calls=%async_computation | async-start | bytes 524288 | tf_op jit(solution)/shard_map/all_to_all | solution.py:322
  12.0 1.6 %copy-start.1 = (bf16[6,1,384,384]{3,2,1,0:T(8,128)(2,1)S(1)}, bf16[6,1,384,384]{3,2,1,0:T(8,128)(2,1)}, u32[]{:S(2)}) copy-start(bf16[6,1,384,384]{3,2,1,0:T(8,128)(2,1)} %param.10) | copy-start | bytes 5308420
  12.0 2.0 %copy-start.2 = (bf16[5,1,384,384]{3,2,1,0:T(8,128)(2,1)S(1)}, bf16[5,1,384,384]{3,2,1,0:T(8,128)(2,1)}, u32[]{:S(2)}) copy-start(bf16[5,1,384,384]{3,2,1,0:T(8,128)(2,1)} %param.11) | copy-start | bytes 4423684
  12.0 2.4 %copy-start.20 = (bf16[384,256]{1,0:T(8,128)(2,1)}, bf16[384,256]{1,0:T(8,128)(2,1)S(1)}, u32[]{:S(2)}) copy-start(bf16[384,256]{1,0:T(8,128)(2,1)S(1)} %collective-permute-done.refs_0_) | copy-start | bytes 589828
  14.5 8.1 %copy-start.32 = (bf16[192,192]{1,0:T(8,128)(2,1)S(1)}, bf16[192,192]{1,0:T(8,128)(2,1)}, u32[]{:S(2)}) copy-start(bf16[192,192]{1,0:T(8,128)(2,1)} %refs_1_.1) | copy-start | bytes 221188
  14.5 16.3 %collective-permute-start.1 = (bf16[384,256]{1,0:T(8,128)(2,1)S(1)}, bf16[384,256]{1,0:T(8,128)(2,1)}, u32[]{:S(2)}, u32[]{:S(2)}) collective-permute-start(bf16[384,256]{1,0:T(8,128)(2,1)S(1)} %margin_solve.4.refs_4_), channel_id=1, source_target_pairs={{0,1},{1,0},{2,3},{3,2},{4,8},{5,9},{6,10},{7,11},{8,4},{9,5},{10,... | collective-permute-start | bytes 589832 | tf_op jit(solution)/shard_map/ppermute | solution.py:318
  14.8 1.2 %copy-start.22 = (bf16[384,256]{1,0:T(8,128)(2,1)}, bf16[384,256]{1,0:T(8,128)(2,1)S(1)}, u32[]{:S(2)}) copy-start(bf16[384,256]{1,0:T(8,128)(2,1)S(1)} %collective-permute-done.2.refs_1_.refs_0_) | copy-start | bytes 589828
  16.1 15.9 %collective-permute-start.4 = (bf16[384,256]{1,0:T(8,128)(2,1)}, bf16[384,256]{1,0:T(8,128)(2,1)}, u32[]{:S(2)}, u32[]{:S(2)}) collective-permute-start(bf16[384,256]{1,0:T(8,128)(2,1)} %margin_solve.5), channel_id=1, source_target_pairs={{0,4},{1,5},{2,6},{3,7},{4,0},{5,1},{6,2},{7,3},{8,12},{9,13},{10,... | collective-permute-start | bytes 589832 | tf_op jit(solution)/shard_map/ppermute | solution.py:318
  22.6 0.9 copy-start.16
  23.5 7.3 %copy-start.24 = (bf16[192,512]{1,0:T(8,128)(2,1)}, bf16[192,512]{1,0:T(8,128)(2,1)S(1)}, u32[]{:S(2)}) copy-start(bf16[192,512]{1,0:T(8,128)(2,1)S(1)} %get-tuple-element.28.refs_8_) | copy-start | bytes 589828
  23.5 7.3 %copy-start.28 = (bf16[16,1536]{1,0:T(8,128)(2,1)}, bf16[16,1536]{1,0:T(8,128)(2,1)S(1)}, u32[]{:S(2)}) copy-start(bf16[16,1536]{1,0:T(8,128)(2,1)S(1)} %get-tuple-element.30.refs_10_) | copy-start | bytes 147460
  23.5 7.3 %copy-start.30 = (bf16[192,16]{1,0:T(8,128)(2,1)}, bf16[192,16]{1,0:T(8,128)(2,1)S(1)}, u32[]{:S(2)}) copy-start(bf16[192,16]{1,0:T(8,128)(2,1)S(1)} %get-tuple-element.29.refs_9_) | copy-start | bytes 18436
  23.5 1.5 %copy-start.3 = (bf16[5,1,384,384]{3,2,1,0:T(8,128)(2,1)S(1)}, bf16[5,1,384,384]{3,2,1,0:T(8,128)(2,1)}, u32[]{:S(2)}) copy-start(bf16[5,1,384,384]{3,2,1,0:T(8,128)(2,1)} %param.11) | copy-start | bytes 4423684
  25.0 1.1 %copy-start.7 = (bf16[4,1,384,256]{3,2,1,0:T(8,128)(2,1)S(1)}, bf16[4,1,384,256]{3,2,1,0:T(8,128)(2,1)}, u32[]{:S(2)}) copy-start(bf16[4,1,384,256]{3,2,1,0:T(8,128)(2,1)} %param.7) | copy-start | bytes 2359300
  26.1 0.9 %copy-start.17 = (bf16[32,16,256]{2,1,0:T(8,128)(2,1)S(1)}, bf16[32,16,256]{2,1,0:T(8,128)(2,1)}, u32[]{:S(2)}) copy-start(bf16[32,16,256]{2,1,0:T(8,128)(2,1)} %copy-done.16) | copy-start | bytes 786436
  27.1 0.9 copy-start.21
  28.0 0.9 copy-start.23
  28.9 1.9 %copy-start = (bf16[4,1,384,384]{3,2,1,0:T(8,128)(2,1)S(1)}, bf16[4,1,384,384]{3,2,1,0:T(8,128)(2,1)}, u32[]{:S(2)}) copy-start(bf16[4,1,384,384]{3,2,1,0:T(8,128)(2,1)} %param.9) | copy-start | bytes 3538948
  31.8 3.8 %copy-start.11 = (bf16[4,1,384,384]{3,2,1,0:T(8,128)(2,1)S(1)}, bf16[4,1,384,384]{3,2,1,0:T(8,128)(2,1)}, u32[]{:S(2)}) copy-start(bf16[4,1,384,384]{3,2,1,0:T(8,128)(2,1)} %param.8) | copy-start | bytes 3538948
  31.8 5.1 %collective-permute-start.3 = (bf16[384,256]{1,0:T(8,128)(2,1)S(1)}, bf16[384,256]{1,0:T(8,128)(2,1)S(1)}, u32[]{:S(2)}, u32[]{:S(2)}) collective-permute-start(bf16[384,256]{1,0:T(8,128)(2,1)S(1)} %get-tuple-element.31.refs_3_), channel_id=1, source_target_pairs={{0,1},{1,0},{2,3},{3,2},{4,8},{5,9},{6,10},{7,11},{8,4},{9,5},{10,... | collective-permute-start | bytes 589832 | tf_op jit(solution)/shard_map/ppermute | solution.py:318
  33.3 13.0 %collective-permute-start.6 = (bf16[384,256]{1,0:T(8,128)(2,1)S(1)}, bf16[384,256]{1,0:T(8,128)(2,1)S(1)}, u32[]{:S(2)}, u32[]{:S(2)}) collective-permute-start(bf16[384,256]{1,0:T(8,128)(2,1)S(1)} %get-tuple-element.37), channel_id=1, source_target_pairs={{0,4},{1,5},{2,6},{3,7},{4,0},{5,1},{6,2},{7,3},{8,12},{9,13},{10,... | collective-permute-start | bytes 589832 | tf_op jit(solution)/shard_map/ppermute | solution.py:318
  36.9 10.4 %copy-start.9 = (f32[4,384,256]{2,1,0:T(8,128)}, f32[4,384,256]{2,1,0:T(8,128)S(1)}, u32[]{:S(2)}) copy-start(f32[4,384,256]{2,1,0:T(8,128)S(1)} %get-tuple-element.48.refs_5_.refs_2_) | copy-start | bytes 4718596
  36.9 10.4 %copy-start.13 = (bf16[4,384,256]{2,1,0:T(8,128)(2,1)}, bf16[4,384,256]{2,1,0:T(8,128)(2,1)S(1)}, u32[]{:S(2)}) copy-start(bf16[4,384,256]{2,1,0:T(8,128)(2,1)S(1)} %get-tuple-element.41.refs_4_.refs_7_) | copy-start | bytes 2359300
  37.0 12.5 %copy-start.27 = (bf16[1,1,6,1536]{3,2,1,0:T(8,128)(2,1)S(1)}, bf16[1,1,6,1536]{3,2,1,0:T(8,128)(2,1)}, u32[]{:S(2)}) copy-start(bf16[1,1,6,1536]{3,2,1,0:T(8,128)(2,1)} %param.12) | copy-start | bytes 55300
  37.0 17.4 %collective-permute-start.5 = (bf16[384,256]{1,0:T(8,128)(2,1)S(1)}, bf16[384,256]{1,0:T(8,128)(2,1)}, u32[]{:S(2)}, u32[]{:S(2)}) collective-permute-start(bf16[384,256]{1,0:T(8,128)(2,1)S(1)} %get-tuple-element.35.refs_3_.refs_1_.refs_2_), channel_id=1, source_target_pairs={{0,1},{1,0},{2,3},{3,2},{4,8},{5,9},{6,10},{7,11},{8,4},{9,5},{10,... | collective-permute-start | bytes 589832 | tf_op jit(solution)/shard_map/ppermute | solution.py:318
  47.3 10.9 %collective-permute-start.8 = (bf16[384,256]{1,0:T(8,128)(2,1)}, bf16[384,256]{1,0:T(8,128)(2,1)}, u32[]{:S(2)}, u32[]{:S(2)}) collective-permute-start(bf16[384,256]{1,0:T(8,128)(2,1)} %get-tuple-element.40.refs_3_.refs_1_), channel_id=1, source_target_pairs={{0,4},{1,5},{2,6},{3,7},{4,0},{5,1},{6,2},{7,3},{8,12},{9,13},{10,... | collective-permute-start | bytes 589832 | tf_op jit(solution)/shard_map/ppermute | solution.py:318
  49.9 0.7 copy-start.18
  50.5 13.4 %all-to-all-start.1 = ((bf16[32,16,256]{2,1,0:T(8,128)(2,1)}), bf16[32,16,256]{2,1,0:T(8,128)(2,1)S(1)}, u32[]{:S(2)}, u32[]{:S(2)}) async-start(bf16[32,16,256]{2,1,0:T(8,128)(2,1)} %copy-done.18), calls=%async_computation.1 | async-start | bytes 524288 | tf_op jit(solution)/shard_map/all_to_all | solution.py:322
  53.4 1.0 %copy-start.19 = (bf16[32,16,256]{2,1,0:T(8,128)(2,1)S(1)}, bf16[32,16,256]{2,1,0:T(8,128)(2,1)}, u32[]{:S(2)}) copy-start(bf16[32,16,256]{2,1,0:T(8,128)(2,1)} %copy-done.18) | copy-start | bytes 786436
  54.4 1.4 %copy-start.4 = (bf16[5,1,384,384]{3,2,1,0:T(8,128)(2,1)S(1)}, bf16[5,1,384,384]{3,2,1,0:T(8,128)(2,1)}, u32[]{:S(2)}) copy-start(bf16[5,1,384,384]{3,2,1,0:T(8,128)(2,1)} %param.11) | copy-start | bytes 4423684
  57.9 6.1 %copy-start.29 = (bf16[16,1536]{1,0:T(8,128)(2,1)S(1)}, bf16[16,1536]{1,0:T(8,128)(2,1)}, u32[]{:S(2)}) copy-start(bf16[16,1536]{1,0:T(8,128)(2,1)} %copy-done.28) | copy-start | bytes 147460
  57.9 6.1 %copy-start.31 = (bf16[192,16]{1,0:T(8,128)(2,1)S(1)}, bf16[192,16]{1,0:T(8,128)(2,1)}, u32[]{:S(2)}) copy-start(bf16[192,16]{1,0:T(8,128)(2,1)} %copy-done.30) | copy-start | bytes 18436
  57.9 12.5 %collective-permute-start.7 = (bf16[384,256]{1,0:T(8,128)(2,1)}, bf16[384,256]{1,0:T(8,128)(2,1)}, u32[]{:S(2)}, u32[]{:S(2)}) collective-permute-start(bf16[384,256]{1,0:T(8,128)(2,1)} %margin_solve.6.refs_4_), channel_id=1, source_target_pairs={{0,1},{1,0},{2,3},{3,2},{4,8},{5,9},{6,10},{7,11},{8,4},{9,5},{10,... | collective-permute-start | bytes 589832 | tf_op jit(solution)/shard_map/ppermute | solution.py:318
  60.4 11.2 %collective-permute-start.10 = (bf16[384,256]{1,0:T(8,128)(2,1)}, bf16[384,256]{1,0:T(8,128)(2,1)}, u32[]{:S(2)}, u32[]{:S(2)}) collective-permute-start(bf16[384,256]{1,0:T(8,128)(2,1)} %margin_solve.7), channel_id=1, source_target_pairs={{0,4},{1,5},{2,6},{3,7},{4,0},{5,1},{6,2},{7,3},{8,12},{9,13},{10,... | collective-permute-start | bytes 589832 | tf_op jit(solution)/shard_map/ppermute | solution.py:318
  64.0 1.4 %copy-start.5 = (bf16[5,1,384,384]{3,2,1,0:T(8,128)(2,1)S(1)}, bf16[5,1,384,384]{3,2,1,0:T(8,128)(2,1)}, u32[]{:S(2)}) copy-start(bf16[5,1,384,384]{3,2,1,0:T(8,128)(2,1)} %param.11) | copy-start | bytes 4423684
  65.4 1.1 %copy-start.14 = (bf16[4,384,256]{2,1,0:T(8,128)(2,1)S(1)}, bf16[4,384,256]{2,1,0:T(8,128)(2,1)}, u32[]{:S(2)}) copy-start(bf16[4,384,256]{2,1,0:T(8,128)(2,1)} %copy-done.13) | copy-start | bytes 2359300
  66.5 0.9 copy-start.25
  70.4 3.7 %copy-start.12 = (bf16[4,1,384,384]{3,2,1,0:T(8,128)(2,1)S(1)}, bf16[4,1,384,384]{3,2,1,0:T(8,128)(2,1)}, u32[]{:S(2)}) copy-start(bf16[4,1,384,384]{3,2,1,0:T(8,128)(2,1)} %param.8) | copy-start | bytes 3538948
  70.4 3.7 %copy-start.15 = (bf16[4,384,256]{2,1,0:T(8,128)(2,1)S(1)}, bf16[4,384,256]{2,1,0:T(8,128)(2,1)}, u32[]{:S(2)}) copy-start(bf16[4,384,256]{2,1,0:T(8,128)(2,1)} %copy-done.13) | copy-start | bytes 2359300
  71.6 2.5 %copy-start.8 = (bf16[4,1,384,256]{3,2,1,0:T(8,128)(2,1)S(1)}, bf16[4,1,384,256]{3,2,1,0:T(8,128)(2,1)}, u32[]{:S(2)}) copy-start(bf16[4,1,384,256]{3,2,1,0:T(8,128)(2,1)} %param.7) | copy-start | bytes 2359300
  71.6 2.5 %copy-start.10 = (f32[4,384,256]{2,1,0:T(8,128)S(1)}, f32[4,384,256]{2,1,0:T(8,128)}, u32[]{:S(2)}) copy-start(f32[4,384,256]{2,1,0:T(8,128)} %copy-done.9) | copy-start | bytes 4718596
  73.1 4.7 %collective-permute-start.11 = (bf16[384,128]{1,0:T(8,128)(2,1)S(1)}, bf16[384,128]{1,0:T(8,128)(2,1)S(1)}, u32[]{:S(2)}, u32[]{:S(2)}) collective-permute-start(bf16[384,128]{1,0:T(8,128)(2,1)S(1)} %get-tuple-element.43), channel_id=1, source_target_pairs={{0,4},{1,5},{2,6},{3,7},{4,0},{5,1},{6,2},{7,3},{8,12},{9,13},{10,... | collective-permute-start | bytes 294920 | tf_op jit(solution)/shard_map/ppermute | solution.py:318
  74.1 3.6 %collective-permute-start.9 = (bf16[384,128]{1,0:T(8,128)(2,1)S(1)}, bf16[384,128]{1,0:T(8,128)(2,1)S(1)}, u32[]{:S(2)}, u32[]{:S(2)}) collective-permute-start(bf16[384,128]{1,0:T(8,128)(2,1)S(1)} %get-tuple-element.42.refs_3_), channel_id=1, source_target_pairs={{0,1},{1,0},{2,3},{3,2},{4,8},{5,9},{6,10},{7,11},{8,4},{9,5},{10,... | collective-permute-start | bytes 294920 | tf_op jit(solution)/shard_map/ppermute | solution.py:318

commit v4 on v3

--- a/solution.py
+++ b/solution.py
@@ -1,3 +1,5 @@
+import math
+
 import jax
 import jax.numpy as jnp
 from jax import lax
@@ -43,6 +45,10 @@
     return jnp.where(low2, from2, from1), jnp.where(low2, from1, from2)
 
 
+def nbytes(shape, dtype):
+    return math.prod(shape) * jnp.dtype(dtype).itemsize
+
+
 def run_copies(pairs, sems):
     copies = [pltpu.make_async_copy(a, b, sems.at[i]) for i, (a, b) in enumerate(pairs)]
     for c in copies:
@@ -51,30 +57,29 @@
         c.wait()
 
 
-def call(body, outs, args, name, flops=0, after=None, scratch=(), hbm=()):
-    shapes = [jax.ShapeDtypeStruct(d, t) for d, t in outs]
-    total = sum(a.size * a.dtype.itemsize for a in list(args) + shapes)
-    count = len(args)
-    late = [] if after is None else list(after)
-    specs = [pl.BlockSpec(memory_space=pltpu.HBM if i in hbm else pltpu.VMEM) for i in range(count)]
+def call(body, outs, args, name, flops=0, after=(), scratch=(), hbm=(), far=()):
+    shapes = [pltpu.HBM(d, t) if i in far else jax.ShapeDtypeStruct(d, t) for i, (d, t) in enumerate(outs)]
+    total = sum(nbytes(a.shape, a.dtype) for a in args)
+    room = sum(nbytes(a.shape, a.dtype) for i, a in enumerate(args) if i not in hbm)
+    room += sum(nbytes(d, t) for i, (d, t) in enumerate(outs) if i not in far)
+    room += sum(nbytes(a.shape, a.dtype) for a in scratch if jnp.issubdtype(a.dtype, jnp.floating))
+    args = [pltpu.with_memory_space_constraint(a, pltpu.HBM) if i in hbm else a for i, a in enumerate(args)]
+    count, late = len(args), len(after)
 
     def kernel(*refs):
-        body(*refs[:count], *refs[count + len(late) :])
-
+        body(*refs[:count], *refs[count + late :])
+
+    space = lambda i, there: pl.BlockSpec(memory_space=pltpu.HBM if i in there else pltpu.VMEM)
     return pl.pallas_call(
         kernel,
         out_shape=shapes,
-        in_specs=specs + [pl.BlockSpec(memory_space=pl.ANY)] * len(late),
-        out_specs=[pl.BlockSpec(memory_space=pltpu.VMEM)] * len(outs),
+        in_specs=[space(i, hbm) for i in range(count)] + [pl.BlockSpec(memory_space=pl.ANY)] * late,
+        out_specs=[space(i, far) for i in range(len(outs))],
         scratch_shapes=list(scratch),
-        compiler_params=pltpu.CompilerParams(vmem_limit_bytes=LIMIT),
+        compiler_params=pltpu.CompilerParams(vmem_limit_bytes=max(LIMIT, room + LIMIT // 2)),
         cost_estimate=pl.CostEstimate(flops=flops, bytes_accessed=total, transcendentals=0),
         name=name,
-    )(*args, *late)
-
-
-def mark(out):
-    out[...] = jnp.zeros(out.shape, F32)
+    )(*args, *after)
 
 
 def load_edge(chain):
@@ -84,11 +89,20 @@
     return body
 
 
-def margin_solve(chain):
-    def body(h, e, ld, lu, s, diag, upper, sems):
+def load_outer(ld, lu, d2, u2, d1, u1, sems):
+    lower = is_lower(2)
+    at = [jnp.where(lower, 0, m.shape[0] - 1) for m in (ld, lu)]
+    to = [m.shape[0] - 1 - i for m, i in zip((ld, lu), at)]
+    blocks = [(ld.at[at[0]], d2), (lu.at[at[1]], u2), (ld.at[to[0]], d1), (lu.at[to[1]], u1)]
+    run_copies(blocks, sems)
+
+
+def margin_solve(chain, fetch):
+    def body(h, e, diag, upper, s, *held):
         lower = is_lower(chain)
-        at = [jnp.where(lower, 0, m.shape[0] - 1) for m in (ld, lu)]
-        run_copies([(ld.at[at[0]], diag), (lu.at[at[1]], upper)], sems)
+        if fetch:
+            run_copies([(h, held[0]), (e, held[1])], held[2])
+            h, e = held[:2]
 
         @pl.when(lower)
         def _():
@@ -101,21 +115,32 @@
     return body
 
 
-def solve_layers(h2, h1, o2, o1, e, ld, lu, gathered, fpad, fown, basis, p):
+def solve_layers(*refs):
+    count = 11
+    far, p, near, sems = refs[:count], refs[count], refs[count + 1 : 2 * count + 1], refs[-1]
+    copies = [pltpu.make_async_copy(a, b, sems.at[i]) for i, (a, b) in enumerate(zip(far, near))]
+    for c in copies:
+        c.start()
+    gathered, fpad, fown, basis, h2, h1, o2, o1, e, ld, lu = near
+    for c in copies[:4]:
+        c.wait()
+    g = gathered[...].reshape(-1, gathered.shape[-1])
+    v = mm(fpad[...], g).astype(BF)
+    u = mmt(fown[...], v).astype(BF)
+    size = p.shape[1]
+    for c in copies[4:10]:
+        c.wait()
     e0, e5 = pick(h2[...], h1[...])
     e0, e5 = kept(e0, True), kept(e5, False)
     e1, e4 = pick(o2[...], o1[...])
     e2, e3 = e[1], e[2]
-    g = gathered[...].reshape(-1, gathered.shape[-1])
-    v = mm(fpad[...], g).astype(BF)
-    u = mmt(fown[...], v).astype(BF)
-    size = p.shape[1]
-    p[0] = mm(ld[1], e1) + mm(lu[1], e2) + mmt(lu[0], e0)
-    p[1] = mm(ld[2], e2) + mm(lu[2], e3) + mmt(lu[1], e1)
-    p[2] = mm(ld[3], e3) + mm(lu[3], e4) + mmt(lu[2], e2)
-    p[3] = mm(ld[4], e4) + mm(lu[4], e5) + mmt(lu[3], e3)
-    for k in range(4):
-        p[k] = p[k] + mmt(basis[:, k * size : (k + 1) * size], u)
+    for k, x in enumerate((e1, e2, e3, e4)):
+        p[k] = mm(ld[k + 1], x) + mmt(basis[:, k * size : (k + 1) * size], u)
+    copies[10].wait()
+    p[0] = p[0] + mm(lu[1], e2) + mmt(lu[0], e0)
+    p[1] = p[1] + mm(lu[2], e3) + mmt(lu[1], e1)
+    p[2] = p[2] + mm(lu[3], e4) + mmt(lu[2], e2)
+    p[3] = p[3] + mm(lu[4], e5) + mmt(lu[3], e3)
 
 
 def join_margin(chain):
@@ -168,18 +193,19 @@
 
 
 def coarse_rhs(ncb):
-    def body(e, basis, g, held, sems):
-        run_copies([(e, held)], sems)
-        out = mm(basis[...], held[...].reshape(-1, e.shape[-1]))
+    def body(e, basis, g, held, rows, block, sems):
+        run_copies([(e, held), (basis, rows)], sems)
+        out = mm(rows[...], held[...].reshape(-1, e.shape[-1]))
         out = jnp.concatenate([out, jnp.zeros((PAD - ncb, out.shape[1]), F32)], axis=0).astype(BF)
         for k in range(g.shape[0]):
-            g[k] = out
+            block[k] = out
+        run_copies([(block, g)], sems)
 
     return body
 
 
 def prepare(ncb):
-    def body(basis, factor, padded, fpad, fown):
+    def body(basis, factor, padded_far, fpad_far, fown_far, padded, fpad, fown, sems):
         rows = basis[...].astype(F32)
         padded[...] = jnp.concatenate([rows, jnp.zeros((PAD - ncb, rows.shape[1]), F32)], axis=0).astype(BF)
         nco = factor.shape[0]
@@ -201,6 +227,7 @@
             return carry
 
         lax.fori_loop(0, fpad.shape[1] // width, step, 0)
+        run_copies([(padded, padded_far), (fpad, fpad_far), (fown, fown_far)], sems)
 
     return body
 
@@ -215,7 +242,7 @@
 
 
 def coarse_rhs_sums(ncb):
-    def body(w2, w1, w, z2, z1, p, rho, basis, g):
+    def body(w2, w1, w, z2, z1, p, rho, basis, g, block, sems):
         ends = [pick(w2[...], w1[...]), pick(z2[...], z1[...])]
         acc = jnp.zeros(rho.shape, F32)
         out = jnp.zeros((ncb, rho.shape[1]), F32)
@@ -227,7 +254,8 @@
         rows = [out, jnp.zeros((8 - ncb, out.shape[1]), F32)] + three(rho[...]) + three(acc)
         out = jnp.concatenate(rows + [jnp.zeros((2, out.shape[1]), F32)], axis=0).astype(BF)
         for k in range(g.shape[0]):
-            g[k] = out
+            block[k] = out
+        run_copies([(block, g)], sems)
 
     return body
 
@@ -253,11 +281,16 @@
     return body
 
 
-def inner_products(q2, q1, o2, o1, p, z, r, w, sd, su, q, sums):
+def inner_products(q2, q1, o2, o1, p, z, r, w, sd, su, early, q, kept_z, first, sums):
     q[0], q[3] = pick(q2[...], q1[...])
     q[1] = p[1]
     q[2] = p[2]
     ends = pick(o2[...], o1[...])
+    kept_z[...] = z[...]
+    total = early[0].astype(F32)
+    for k in range(1, early.shape[0]):
+        total = total + early[k].astype(F32)
+    first[...] = total
     s1 = s2 = s4 = s5 = jnp.zeros((1, q.shape[-1]), F32)
     for k in range(4):
         qk = q[k]
@@ -287,12 +320,10 @@
         out[k] = full
 
 
-def finish(parts, early, z, q, x):
+def finish(parts, first, z, q, x):
     total = parts[0]
-    first = early[0].astype(F32)
     for k in range(1, parts.shape[0]):
         total = total + parts[k]
-        first = first + early[k].astype(F32)
     rho0 = first[8:9] + first[9:10] + first[10:11]
     d0 = first[11:12] + first[12:13] + first[13:14]
     s1, s2, s4, s5 = (total[k : k + 1] for k in range(4))
@@ -334,36 +365,36 @@
     r, sd, su, ld, lu = rhs[:, 0], stiff_diag[:, 0], stiff_upper[:, 0], local_diag[:, 0], local_upper[:, 0]
     raw_basis = coarse_basis[0, 0]
 
-    def margins(h2, h1, o2, o1, order):
-        blocks = [pltpu.VMEM((size, size), BF)] * 2 + [dma(2)]
-        take = lambda chain, h, o, after: call(
-            margin_solve(chain), [(layer, BF)], (h, o, ld, lu), "margin_solve", 2 * block, after, blocks, (2, 3)
+    def margins(h2, h1, o2, o1, g, fetch):
+        g = pltpu.with_memory_space_constraint(g, pltpu.HBM)
+        d2, u2, d1, u1 = call(
+            load_outer, [((size, size), BF)] * 4, (ld, lu), "load_outer", SCHEDULE_COST * block, [g], [dma(4)], (0, 1)
+        )
+        held, far = ([pltpu.VMEM(layer, BF)] * 2 + [dma(2)], (0, 1)) if fetch else ((), ())
+        take = lambda chain, args, after: call(
+            margin_solve(chain, fetch), [(layer, BF)], args, "margin_solve", 2 * block, after, held, far
         )[0]
-        s2 = take(2, h2, o2, order)
-        s1 = take(1, h1, o1, [s2])
-        return swap(2, s2), swap(1, s1)
-
-    def beside(g):
-        return call(mark, [((8, 128), F32)], (), "beside", SCHEDULE_COST * block, [g])[0]
+        s2 = take(2, (h2, o2, d2, u2), ())
+        s1 = take(1, (h1, o1, d1, u1), [s2])
+        return swap(2, s2), swap(1, s1), s1
 
     def solve(h2, h1, o2, o1, e, gathered):
-        args = (h2, h1, o2, o1, e, ld, lu, gathered, fpad, fown, basis)
-        return call(solve_layers, [(whole, F32)], args, "solve_layers", 12 * block)[0]
-
-    (s2,) = call(load_edge(2), [(layer, BF)], (r,), "load_edge", 0, None, [dma(1)], (0,))
+        args = (gathered, fpad, fown, basis, h2, h1, o2, o1, e, ld, lu)
+        held = [pltpu.VMEM(a.shape, a.dtype) for a in args] + [dma(len(args))]
+        return call(solve_layers, [(whole, F32)], args, "solve_layers", 12 * block, (), held, range(len(args)))[0]
+
+    (s2,) = call(load_edge(2), [(layer, BF)], (r,), "load_edge", 0, (), [dma(1)], (0,))
     h2 = swap(2, s2)
     (s1,) = call(load_edge(1), [(layer, BF)], (r,), "load_edge", 0, [s2], [dma(1)], (0,))
     h1 = swap(1, s1)
-    (g,) = call(coarse_rhs(ncb), [copies], (r, raw_basis), "coarse_rhs", block // 32, [s1], [pltpu.VMEM(whole, BF), dma(1)], (0,))
+    held = [pltpu.VMEM(whole, BF), pltpu.VMEM(raw_basis.shape, BF), pltpu.VMEM(*copies), dma(2)]
+    (g,) = call(coarse_rhs(ncb), [copies], (r, raw_basis), "coarse_rhs", block // 32, [s1], held, (0, 1), (0,))
     gathered = gather(g)
-    m2, m1 = margins(h2, h1, s2, s1, [beside(g)])
+    m2, m1, last = margins(h2, h1, s2, s1, g, False)
+    shapes = [((PAD, layers * size), BF), ((nco, devices * PAD), BF), ((nco, PAD), BF)]
+    held = [pltpu.VMEM(*shape) for shape in shapes] + [dma(3)]
     basis, fpad, fown = call(
-        prepare(ncb),
-        [((PAD, layers * size), BF), ((nco, devices * PAD), BF), ((nco, PAD), BF)],
-        (raw_basis, coarse_factor),
-        "prepare",
-        block // 8,
-        [gathered],
+        prepare(ncb), shapes, (raw_basis, coarse_factor), "prepare", block // 8, [last], held, (), (0, 1, 2)
     )
     p = solve(h2, h1, s2, s1, r, gathered)
     z2, s2 = call(join_margin(2), edge, (m2, p, su), "join_margin", block)
@@ -375,23 +406,23 @@
     w2, o2 = call(join_operate(2), edge, (n2, wi, su), "join_operate", block)
     w1, o1 = call(join_operate(1), edge, (n1, wi, su), "join_operate", block, [o2])
     h2, h1 = swap(2, o2), swap(1, o1)
-    (g,) = call(coarse_rhs_sums(ncb), [copies], (w2, w1, wi, z2, z1, p, rho, raw_basis), "coarse_rhs_sums", block // 32)
+    (g,) = call(coarse_rhs_sums(ncb), [copies], (w2, w1, wi, z2, z1, p, rho, raw_basis), "coarse_rhs_sums", block // 32, [o1], [pltpu.VMEM(*copies), dma(1)], (), (0,))
     early = gather(g)
-    m2, m1 = margins(h2, h1, o2, o1, [beside(g)])
+    m2, m1, _ = margins(h2, h1, o2, o1, g, True)
     p = solve(h2, h1, o2, o1, w, early)
     half = [(layer, F32), ((size, cols // 2), BF), (layer, F32)]
     q2, s2, c2 = call(join_second(2), half, (m2, p, su), "join_second", block)
     q1, s1, c1 = call(join_second(1), half, (m1, p, su), "join_second", block, [s2])
     t2, t1 = swap(2, s2), swap(1, s1)
-    q, sums = call(
+    q, z, first, sums = call(
         inner_products,
-        [(whole, F32), ((4, cols), F32)],
-        (q2, q1, o2, o1, p, z, r, w, sd, su),
+        [(whole, F32), (whole, F32), ((PAD, cols), F32), ((4, cols), F32)],
+        (q2, q1, o2, o1, p, z, r, w, sd, su, early),
         "inner_products",
         12 * block,
     )
     (g,) = call(join_sums, [((devices, 4, cols), F32)], (t2, t1, c2, c1, sums), "join_sums")
-    (x,) = call(finish, [(whole, F32)], (gather(g), early, z, q), "finish")
+    (x,) = call(finish, [(whole, F32)], (gather(g), first, z, q), "finish")
     return x[:, None]
 
 

time: 93.8 us -> 86.1 us (0.918)
  local copies, waits for them, and re-layouts: 15 us -> 0.79 us
  Pallas kernels: 24.6 us -> 29.3 us
  starting transfers between devices: 24.6 us -> 26.6 us
  waiting for transfers between devices: 14.6 us -> 16.5 us
  blocking collectives: 13.7 us -> 12 us
    unnamed x66 -> x38, local copies, waits for them, and re-layouts: 15 us -> 0.79 us
    pallas_call x23, Pallas kernels: 24.6 us -> 29.3 us  [call(): pl.pallas_call(kernel, out_shape=shapes, in_specs=[space(i, hbm) for i in...]
    all_to_all x2, waiting for transfers between devices: 4.06 us -> 6.08 us  [gather(): return lax.all_to_all(copies, ALL, 0, 0)]
    all_to_all x1, blocking collectives: 13.7 us -> 12 us  [gather(): return lax.all_to_all(copies, ALL, 0, 0)]
    ppermute x12, starting transfers between devices: 17.1 us -> 18.6 us  [swap(): return lax.ppermute(x, ALL, moves)]
  transfers between devices with their start and end apart: 14 -> 14, of which waited for: 4 -> 4; matrix products, arithmetic and copies ran while one was open for 0% -> 0% of each run, Pallas kernels for 23% -> 31%
where the time goes in v4:
time: 86.1 us; the launch traced here: 85.6 us
  Pallas kernels  29.3 us (34%)
  starting transfers between devices  26.6 us (31%)
  waiting for transfers between devices  16.5 us (19%)
  blocking collectives  12 us (14%)
    pallas_call x23, Pallas kernels, call(): pl.pallas_call(kernel, out_shape=shapes, in_specs=[space(i, hbm) for i in...  29.3 us
    ppermute x12, starting transfers between devices, swap(): return lax.ppermute(x, ALL, moves)  18.6 us
    all_to_all x1, blocking collectives, gather(): return lax.all_to_all(copies, ALL, 0, 0)  12 us
    ppermute x12, waiting for transfers between devices, swap(): return lax.ppermute(x, ALL, moves)  10.4 us
    all_to_all x2, starting transfers between devices, gather(): return lax.all_to_all(copies, ALL, 0, 0)  8.05 us
    all_to_all x2, waiting for transfers between devices, gather(): return lax.all_to_all(copies, ALL, 0, 0)  6.08 us
  transfers between devices with their start and end apart: 14, of which 4 were waited for; matrix products, arithmetic and copies ran while one was open for 0% of the time, Pallas kernels for 31%

profile of v4, /device:TPU:0, one launch (start us, length us, event | category | flops | bytes accessed | tf_op | source)
XLA Modules:
  0.0 85.6 jit_solution(7464056949581074677)
XLA Ops:
  0.0 0.9 %load_edge.2.refs_1_.refs_6_ = bf16[384,256]{1,0:T(8,128)(2,1)S(1)} custom-call(bf16[4,384,256]{2,1,0:T(8,128)(2,1)} %bitcast.17), custom_call_target="tpu_custom_call" | custom-call | bytes 786432 | tf_op jit(solution)/shard_map/load_edge/pallas_call | solution.py:73
  1.0 0.5 collective-permute-start
  1.5 0.9 %load_edge.3.refs_2_.refs_1_.refs_7_ = bf16[384,256]{1,0:T(8,128)(2,1)S(1)} custom-call(bf16[4,384,256]{2,1,0:T(8,128)(2,1)} %bitcast.18, bf16[384,256]{1,0:T(8,128)(2,1)S(1)} %load_edge.2.refs_1_.refs_6_), custom_call_target="tpu_custom_call" | custom-call | bytes 786432 | tf_op jit(solution)/shard_map/load_edge/pallas_call | solution.py:73
  2.4 4.1 %collective-permute-start.2 = (bf16[384,256]{1,0:T(8,128)(2,1)S(1)}, bf16[384,256]{1,0:T(8,128)(2,1)S(1)}, u32[]{:S(2)}, u32[]{:S(2)}) collective-permute-start(bf16[384,256]{1,0:T(8,128)(2,1)S(1)} %load_edge.3.refs_2_.refs_1_.refs_7_), channel_id=1, source_target_pairs={{0,4},{1,5},{2,6},{3,7},{4,0},{5,1},{6,2},{7,3},{8,12},{9,13},{10,... | collective-permute-start | bytes 589832 | tf_op jit(solution)/shard_map/ppermute | solution.py:349
  6.5 2.1 %coarse_rhs.1.refs_2_ = bf16[32,16,256]{2,1,0:T(8,128)(2,1)} custom-call(bf16[4,384,256]{2,1,0:T(8,128)(2,1)} %bitcast.19, bf16[6,1536]{1,0:T(8,128)(2,1)} %bitcast.25, bf16[384,256]{1,0:T(8,128)(2,1)S(1)} %load_edge.3.refs_2_.refs_1_.refs_7_), custom_call_target="tpu_custom_call" | custom-call | flops 2359296 | bytes 804864 | tf_op jit(solution)/shard_map/coarse_rhs/pallas_call | solution.py:73
  8.6 4.7 %all-to-all-start = ((bf16[32,16,256]{2,1,0:T(8,128)(2,1)}), bf16[32,16,256]{2,1,0:T(8,128)(2,1)S(1)}, u32[]{:S(2)}, u32[]{:S(2)}) async-start(bf16[32,16,256]{2,1,0:T(8,128)(2,1)} %coarse_rhs.1.refs_2_), calls=%async_computation | async-start | bytes 524288 | tf_op jit(solution)/shard_map/all_to_all | solution.py:353
  13.3 1.3 %load_outer.2 = (bf16[384,384]{1,0:T(8,128)(2,1)S(1)}, bf16[384,384]{1,0:T(8,128)(2,1)S(1)}, bf16[384,384]{1,0:T(8,128)(2,1)S(1)}, bf16[384,384]{1,0:T(8,128)(2,1)S(1)}) custom-call(bf16[6,384,384]{2,1,0:T(8,128)(2,1)} %bitcast.28, bf16[5,384,384]{2,1,0:T(8,128)(2,1)} %bitcast.32, bf16[32,16,256]{2,1,0:T(8,128)(2,1)} %coarse_rhs.1.refs_2_), custom_call_target="tpu_custom_call" | custom-call | flops 90596966400 | bytes 3244032 | tf_op jit(solution)/shard_map/load_outer/pallas_call | solution.py:73
  14.6 0.0 copy-start.17
  14.7 0.4 margin_solve.4.refs_4_
  15.1 0.3 collective-permute-start.1
  15.4 0.4 margin_solve.5.refs_2_
  15.8 3.0 %collective-permute-start.4 = (bf16[384,256]{1,0:T(8,128)(2,1)S(1)}, bf16[384,256]{1,0:T(8,128)(2,1)S(1)}, u32[]{:S(2)}, u32[]{:S(2)}) collective-permute-start(bf16[384,256]{1,0:T(8,128)(2,1)S(1)} %margin_solve.5.refs_2_), channel_id=1, source_target_pairs={{0,4},{1,5},{2,6},{3,7},{4,0},{5,1},{6,2},{7,3},{8,12},{9,13},{10,... | collective-permute-start | bytes 589832 | tf_op jit(solution)/shard_map/ppermute | solution.py:349
  18.8 1.6 %prepare.1 = (bf16[16,1536]{1,0:T(8,128)(2,1)}, bf16[192,512]{1,0:T(8,128)(2,1)}, bf16[192,16]{1,0:T(8,128)(2,1)}) custom-call(bf16[6,1536]{1,0:T(8,128)(2,1)S(1)} %bitcast.26, bf16[192,192]{1,0:T(8,128)(2,1)S(1)} %copy-done.17, bf16[384,256]{1,0:T(8,128)(2,1)S(1)} %margin_solve.5.refs_2_), custom_call_target="tpu_custom_call" | custom-call | flops 9437184 | bytes 92160 | tf_op jit(solution)/shard_map/prepare/pallas_call | solution.py:73
  20.5 3.5 %all-to-all-done.refs_0_ = bf16[32,16,256]{2,1,0:T(8,128)(2,1)S(1)} async-done(((bf16[32,16,256]{2,1,0:T(8,128)(2,1)}), bf16[32,16,256]{2,1,0:T(8,128)(2,1)S(1)}, u32[]{:S(2)}, u32[]{:S(2)}) %all-to-all-start) | async-done | bytes 262176 | tf_op jit(solution)/shard_map/all_to_all | solution.py:353
  24.0 0.7 copy-done.18
  24.7 4.1 %solve_layers.2.refs_1_.refs_2_.refs_5_ = f32[4,384,256]{2,1,0:T(8,128)S(1)} custom-call(bf16[32,16,256]{2,1,0:T(8,128)(2,1)} %copy-done.18, bf16[192,512]{1,0:T(8,128)(2,1)} %get-tuple-element.42.refs_1_, bf16[192,16]{1,0:T(8,128)(2,1)} %get-tuple-element.43.refs_2_, bf16[16,1536]{1,0:T(8,128)(2,1)} %get-tuple-element.44.refs_3_, ...), custom_call_target="tpu_custom_call" | custom-call | flops 905969664 | bytes 5330944 | tf_op jit(solution)/shard_map/solve_layers/pallas_call | solution.py:73
  28.7 0.1 join_margin.2
  28.8 0.0 copy-start.2
  28.9 0.1 collective-permute-start.3
  28.9 0.4 join_margin.3
  29.3 2.4 %collective-permute-start.6 = (bf16[384,256]{1,0:T(8,128)(2,1)S(1)}, bf16[384,256]{1,0:T(8,128)(2,1)S(1)}, u32[]{:S(2)}, u32[]{:S(2)}) collective-permute-start(bf16[384,256]{1,0:T(8,128)(2,1)S(1)} %get-tuple-element.51), channel_id=1, source_target_pairs={{0,4},{1,5},{2,6},{3,7},{4,0},{5,1},{6,2},{7,3},{8,12},{9,13},{10,... | collective-permute-start | bytes 589832 | tf_op jit(solution)/shard_map/ppermute | solution.py:349
  31.7 1.3 %inner_operate.1 = (f32[4,384,256]{2,1,0:T(8,128)S(1)}, f32[4,384,256]{2,1,0:T(8,128)S(1)}, bf16[4,384,256]{2,1,0:T(8,128)(2,1)S(1)}, f32[1,256]{1,0:T(1,128)S(1)}) custom-call(f32[384,256]{1,0:T(8,128)S(1)} %get-tuple-element.46.refs_0_.refs_3_, f32[384,256]{1,0:T(8,128)S(1)} %get-tuple-element.47.refs_1_.refs_4_, ...), custom_call_target="tpu_custom_call" | custom-call | flops 754974720 | bytes 5505024 | tf_op jit(solution)/shard_map/inner_operate/pallas_call | solution.py:73
  33.0 0.0 copy-start.11
  33.1 0.1 join_operate.2
  33.2 0.0 copy-start.16
  33.2 0.1 collective-permute-start.5
  33.3 10.0 %collective-permute-done.6.refs_0_ = bf16[384,256]{1,0:T(8,128)(2,1)S(1)} collective-permute-done((bf16[384,256]{1,0:T(8,128)(2,1)S(1)}, bf16[384,256]{1,0:T(8,128)(2,1)S(1)}, u32[]{:S(2)}, u32[]{:S(2)}) %collective-permute-start.6) | collective-permute-done | bytes 196640 | tf_op jit(solution)/shard_map/ppermute | solution.py:349
  43.3 0.3 join_operate.3
  43.6 2.3 %collective-permute-start.8 = (bf16[384,256]{1,0:T(8,128)(2,1)S(1)}, bf16[384,256]{1,0:T(8,128)(2,1)}, u32[]{:S(2)}, u32[]{:S(2)}) collective-permute-start(bf16[384,256]{1,0:T(8,128)(2,1)S(1)} %get-tuple-element.54.refs_8_.refs_7_.refs_1_.refs_3_), channel_id=1, source_target_pairs={{0,4},{1,5},{2,6},{3,7},{4,0},{5,1},{6,2},{7,3},{8,12},{9,13},{10,... | collective-permute-start | bytes 589832 | tf_op jit(solution)/shard_map/ppermute | solution.py:349
  45.9 1.1 %coarse_rhs_sums.1.refs_2_ = bf16[32,16,256]{2,1,0:T(8,128)(2,1)} custom-call(f32[384,256]{1,0:T(8,128)S(1)} %get-tuple-element.50.refs_0_, f32[384,256]{1,0:T(8,128)S(1)} %get-tuple-element.52.refs_1_, f32[4,384,256]{2,1,0:T(8,128)S(1)} %get-tuple-element.48.refs_1_.refs_2_, f32[384,256]{1,0:T(8,128)S(1)} %get-tuple-element.46.refs_0_.refs_3_, ...), custom_call_target="tpu_custom_call" | custom-call | flops 2359296 | bytes 4738048 | tf_op jit(solution)/shard_map/coarse_rhs_sums/pallas_call | solution.py:73
  47.1 3.3 %all-to-all-start.1 = ((bf16[32,16,256]{2,1,0:T(8,128)(2,1)}), bf16[32,16,256]{2,1,0:T(8,128)(2,1)}, u32[]{:S(2)}, u32[]{:S(2)}) async-start(bf16[32,16,256]{2,1,0:T(8,128)(2,1)} %coarse_rhs_sums.1.refs_2_), calls=%async_computation.1 | async-start | bytes 524288 | tf_op jit(solution)/shard_map/all_to_all | solution.py:353
  50.4 1.3 %load_outer.3 = (bf16[384,384]{1,0:T(8,128)(2,1)S(1)}, bf16[384,384]{1,0:T(8,128)(2,1)S(1)}, bf16[384,384]{1,0:T(8,128)(2,1)S(1)}, bf16[384,384]{1,0:T(8,128)(2,1)S(1)}) custom-call(bf16[6,384,384]{2,1,0:T(8,128)(2,1)} %bitcast.30, bf16[5,384,384]{2,1,0:T(8,128)(2,1)} %bitcast.34, bf16[32,16,256]{2,1,0:T(8,128)(2,1)} %coarse_rhs_sums.1.refs_2_), custom_call_target="tpu_custom_call" | custom-call | flops 90596966400 | bytes 3244032 | tf_op jit(solution)/shard_map/load_outer/pallas_call | solution.py:73
  51.7 1.4 %margin_solve.6.refs_4_ = bf16[384,256]{1,0:T(8,128)(2,1)S(1)} custom-call(bf16[384,256]{1,0:T(8,128)(2,1)} %collective-permute-done.5.refs_0_.refs_4_, bf16[384,256]{1,0:T(8,128)(2,1)} %copy-done.9, bf16[384,384]{1,0:T(8,128)(2,1)S(1)} %get-tuple-element.55.refs_2_, bf16[384,384]{1,0:T(8,128)(2,1)S(1)} %get-tuple-element.56.refs_3_), custom_call_target="tpu_custom_call" | custom-call | flops 150994944 | bytes 983040 | tf_op jit(solution)/shard_map/margin_solve/pallas_call | solution.py:73
  53.1 0.1 collective-permute-start.7
  53.2 2.1 %margin_solve.7 = bf16[384,256]{1,0:T(8,128)(2,1)} custom-call(bf16[384,256]{1,0:T(8,128)(2,1)} %collective-permute-done.8.refs_5_.refs_0_, bf16[384,256]{1,0:T(8,128)(2,1)} %copy-done.5, bf16[384,384]{1,0:T(8,128)(2,1)S(1)} %get-tuple-element.59.refs_2_, bf16[384,384]{1,0:T(8,128)(2,1)S(1)} %get-tuple-element.60.refs_3_, ...), custom_call_target="tpu_custom_call" | custom-call | flops 150994944 | bytes 983040 | tf_op jit(solution)/shard_map/margin_solve/pallas_call | solution.py:73
  55.4 3.1 %collective-permute-start.10 = (bf16[384,256]{1,0:T(8,128)(2,1)}, bf16[384,256]{1,0:T(8,128)(2,1)S(1)}, u32[]{:S(2)}, u32[]{:S(2)}) collective-permute-start(bf16[384,256]{1,0:T(8,128)(2,1)} %margin_solve.7), channel_id=1, source_target_pairs={{0,4},{1,5},{2,6},{3,7},{4,0},{5,1},{6,2},{7,3},{8,12},{9,13},{10,... | collective-permute-start | bytes 589832 | tf_op jit(solution)/shard_map/ppermute | solution.py:349
  58.4 2.6 %all-to-all-done.1.refs_0_.refs_10_ = bf16[32,16,256]{2,1,0:T(8,128)(2,1)} async-done(((bf16[32,16,256]{2,1,0:T(8,128)(2,1)}), bf16[32,16,256]{2,1,0:T(8,128)(2,1)}, u32[]{:S(2)}, u32[]{:S(2)}) %all-to-all-start.1) | async-done | bytes 262176 | tf_op jit(solution)/shard_map/all_to_all | solution.py:353
  61.0 4.0 %solve_layers.3.refs_1_.refs_4_ = f32[4,384,256]{2,1,0:T(8,128)S(1)} custom-call(bf16[32,16,256]{2,1,0:T(8,128)(2,1)} %all-to-all-done.1.refs_0_.refs_10_, bf16[192,512]{1,0:T(8,128)(2,1)} %get-tuple-element.42.refs_1_, bf16[192,16]{1,0:T(8,128)(2,1)} %get-tuple-element.43.refs_2_, bf16[16,1536]{1,0:T(8,128)(2,1)} %get-tuple-element.44.refs_3_, ...), custom_call_target="tpu_custom_call" | custom-call | flops 905969664 | bytes 5330944 | tf_op jit(solution)/shard_map/solve_layers/pallas_call | solution.py:73
  65.0 1.0 %join_second.2 = (f32[384,256]{1,0:T(8,128)S(1)}, bf16[384,128]{1,0:T(8,128)(2,1)S(1)}, f32[384,256]{1,0:T(8,128)S(1)}) custom-call(bf16[384,256]{1,0:T(8,128)(2,1)} %collective-permute-done.7.refs_0_, f32[4,384,256]{2,1,0:T(8,128)S(1)} %solve_layers.3.refs_1_.refs_4_, bf16[4,384,384]{2,1,0:T(8,128)(2,1)S(1)} %bitcast.14), custom_call_target="tpu_custom_call" | custom-call | flops 75497472 | bytes 2949120 | tf_op jit(solution)/shard_map/join_second/pallas_call | solution.py:73
  66.1 0.0 copy-start.12
  66.1 0.1 collective-permute-start.9
  66.2 0.4 join_second.3
  66.6 2.5 %collective-permute-start.11 = (bf16[384,128]{1,0:T(8,128)(2,1)S(1)}, bf16[384,128]{1,0:T(8,128)(2,1)S(1)}, u32[]{:S(2)}, u32[]{:S(2)}) collective-permute-start(bf16[384,128]{1,0:T(8,128)(2,1)S(1)} %get-tuple-element.61), channel_id=1, source_target_pairs={{0,4},{1,5},{2,6},{3,7},{4,0},{5,1},{6,2},{7,3},{8,12},{9,13},{10,... | collective-permute-start | bytes 294920 | tf_op jit(solution)/shard_map/ppermute | solution.py:349
  69.1 2.6 %inner_products.1 = (f32[4,384,256]{2,1,0:T(8,128)S(1)}, f32[4,384,256]{2,1,0:T(8,128)S(1)}, f32[16,256]{1,0:T(8,128)S(1)}, f32[4,256]{1,0:T(4,128)S(1)}) custom-call(f32[384,256]{1,0:T(8,128)S(1)} %get-tuple-element.64.refs_0_, f32[384,256]{1,0:T(8,128)S(1)} %get-tuple-element.65.refs_1_, bf16[384,256]{1,0:T(8,128)(2,1)S(1)} %copy-done.10, ...), custom_call_target="tpu_custom_call" | custom-call | flops 905969664 | bytes 8519680 | tf_op jit(solution)/shard_map/inner_products/pallas_call | solution.py:73
  71.8 0.3 collective-permute-done.11.refs_1_
  72.1 0.2 join_sums.1
  72.3 12.0 %all_to_all.15.refs_0_ = f32[32,4,256]{2,1,0:T(4,128)S(1)} all-to-all(f32[32,4,256]{2,1,0:T(4,128)S(1)} %join_sums.1), channel_id=1, replica_groups=mesh['row'=8,'col'=4] {'row','col'}, dimensions={0} | all-to-all | bytes 262144 | tf_op jit(solution)/shard_map/all_to_all | solution.py:353
  84.3 1.4 %finish.1 = f32[4,384,256]{2,1,0:T(8,128)} custom-call(f32[32,4,256]{2,1,0:T(4,128)S(1)} %all_to_all.15.refs_0_, f32[16,256]{1,0:T(8,128)S(1)} %get-tuple-element.68.refs_1_, f32[4,384,256]{2,1,0:T(8,128)S(1)} %get-tuple-element.69.refs_2_, f32[4,384,256]{2,1,0:T(8,128)S(1)} %get-tuple-element.70.refs_3_), custom_call_target="tpu_custom_call" | custom-call | bytes 3293184 | tf_op jit(solution)/shard_map/finish/pallas_call | solution.py:73
  (42 shorter events, 0.1 us)
Async XLA Ops:
  0.9 13.7 %copy-start.7 = (bf16[384,256]{1,0:T(8,128)(2,1)}, bf16[384,256]{1,0:T(8,128)(2,1)S(1)}, u32[]{:S(2)}) copy-start(bf16[384,256]{1,0:T(8,128)(2,1)S(1)} %load_edge.2.refs_1_.refs_6_) | copy-start | bytes 589828
  1.0 13.7 %collective-permute-start = (bf16[384,256]{1,0:T(8,128)(2,1)S(1)}, bf16[384,256]{1,0:T(8,128)(2,1)S(1)}, u32[]{:S(2)}, u32[]{:S(2)}) collective-permute-start(bf16[384,256]{1,0:T(8,128)(2,1)S(1)} %load_edge.2.refs_1_.refs_6_), channel_id=1, source_target_pairs={{0,1},{1,0},{2,3},{3,2},{4,8},{5,9},{6,10},{7,11},{8,4},{9,5},{10,... | collective-permute-start | bytes 589832 | tf_op jit(solution)/shard_map/ppermute | solution.py:349
  2.4 13.0 %copy-start.8 = (bf16[384,256]{1,0:T(8,128)(2,1)}, bf16[384,256]{1,0:T(8,128)(2,1)S(1)}, u32[]{:S(2)}) copy-start(bf16[384,256]{1,0:T(8,128)(2,1)S(1)} %load_edge.3.refs_2_.refs_1_.refs_7_) | copy-start | bytes 589828
  2.4 13.0 %collective-permute-start.2 = (bf16[384,256]{1,0:T(8,128)(2,1)S(1)}, bf16[384,256]{1,0:T(8,128)(2,1)S(1)}, u32[]{:S(2)}, u32[]{:S(2)}) collective-permute-start(bf16[384,256]{1,0:T(8,128)(2,1)S(1)} %load_edge.3.refs_2_.refs_1_.refs_7_), channel_id=1, source_target_pairs={{0,4},{1,5},{2,6},{3,7},{4,0},{5,1},{6,2},{7,3},{8,12},{9,13},{10,... | collective-permute-start | bytes 589832 | tf_op jit(solution)/shard_map/ppermute | solution.py:349
  8.6 15.3 %all-to-all-start = ((bf16[32,16,256]{2,1,0:T(8,128)(2,1)}), bf16[32,16,256]{2,1,0:T(8,128)(2,1)S(1)}, u32[]{:S(2)}, u32[]{:S(2)}) async-start(bf16[32,16,256]{2,1,0:T(8,128)(2,1)} %coarse_rhs.1.refs_2_), calls=%async_computation | async-start | bytes 524288 | tf_op jit(solution)/shard_map/all_to_all | solution.py:353
  14.6 4.2 %copy-start.15 = (bf16[1,1,6,1536]{3,2,1,0:T(8,128)(2,1)S(1)}, bf16[1,1,6,1536]{3,2,1,0:T(8,128)(2,1)}, u32[]{:S(2)}) copy-start(bf16[1,1,6,1536]{3,2,1,0:T(8,128)(2,1)} %param.12) | copy-start | bytes 55300
  14.6 4.2 %copy-start.17 = (bf16[192,192]{1,0:T(8,128)(2,1)S(1)}, bf16[192,192]{1,0:T(8,128)(2,1)}, u32[]{:S(2)}) copy-start(bf16[192,192]{1,0:T(8,128)(2,1)} %refs_1_.1) | copy-start | bytes 221188
  14.7 9.3 %copy-start.13 = (bf16[384,256]{1,0:T(8,128)(2,1)}, bf16[384,256]{1,0:T(8,128)(2,1)S(1)}, u32[]{:S(2)}) copy-start(bf16[384,256]{1,0:T(8,128)(2,1)S(1)} %collective-permute-done.refs_0_.refs_4_) | copy-start | bytes 589828
  15.1 13.7 %collective-permute-start.1 = (bf16[384,256]{1,0:T(8,128)(2,1)S(1)}, bf16[384,256]{1,0:T(8,128)(2,1)S(1)}, u32[]{:S(2)}, u32[]{:S(2)}) collective-permute-start(bf16[384,256]{1,0:T(8,128)(2,1)S(1)} %margin_solve.4.refs_4_), channel_id=1, source_target_pairs={{0,1},{1,0},{2,3},{3,2},{4,8},{5,9},{6,10},{7,11},{8,4},{9,5},{10,... | collective-permute-start | bytes 589832 | tf_op jit(solution)/shard_map/ppermute | solution.py:349
  15.4 8.6 %copy-start.14 = (bf16[384,256]{1,0:T(8,128)(2,1)}, bf16[384,256]{1,0:T(8,128)(2,1)S(1)}, u32[]{:S(2)}) copy-start(bf16[384,256]{1,0:T(8,128)(2,1)S(1)} %collective-permute-done.2.refs_0_.refs_5_) | copy-start | bytes 589828
  15.8 13.1 %collective-permute-start.4 = (bf16[384,256]{1,0:T(8,128)(2,1)S(1)}, bf16[384,256]{1,0:T(8,128)(2,1)S(1)}, u32[]{:S(2)}, u32[]{:S(2)}) collective-permute-start(bf16[384,256]{1,0:T(8,128)(2,1)S(1)} %margin_solve.5.refs_2_), channel_id=1, source_target_pairs={{0,4},{1,5},{2,6},{3,7},{4,0},{5,1},{6,2},{7,3},{8,12},{9,13},{10,... | collective-permute-start | bytes 589832 | tf_op jit(solution)/shard_map/ppermute | solution.py:349
  23.9 0.7 copy-start.18
  24.6 4.1 %copy-start = (bf16[4,1,384,384]{3,2,1,0:T(8,128)(2,1)S(1)}, bf16[4,1,384,384]{3,2,1,0:T(8,128)(2,1)}, u32[]{:S(2)}) copy-start(bf16[4,1,384,384]{3,2,1,0:T(8,128)(2,1)} %param.9) | copy-start | bytes 3538948
  28.8 2.9 %copy-start.1 = (bf16[4,1,384,256]{3,2,1,0:T(8,128)(2,1)S(1)}, bf16[4,1,384,256]{3,2,1,0:T(8,128)(2,1)}, u32[]{:S(2)}) copy-start(bf16[4,1,384,256]{3,2,1,0:T(8,128)(2,1)} %param.7) | copy-start | bytes 2359300
  28.8 2.9 %copy-start.2 = (bf16[4,1,384,384]{3,2,1,0:T(8,128)(2,1)S(1)}, bf16[4,1,384,384]{3,2,1,0:T(8,128)(2,1)}, u32[]{:S(2)}) copy-start(bf16[4,1,384,384]{3,2,1,0:T(8,128)(2,1)} %param.8) | copy-start | bytes 3538948
  28.9 4.2 %collective-permute-start.3 = (bf16[384,256]{1,0:T(8,128)(2,1)S(1)}, bf16[384,256]{1,0:T(8,128)(2,1)S(1)}, u32[]{:S(2)}, u32[]{:S(2)}) collective-permute-start(bf16[384,256]{1,0:T(8,128)(2,1)S(1)} %get-tuple-element.45.refs_3_), channel_id=1, source_target_pairs={{0,1},{1,0},{2,3},{3,2},{4,8},{5,9},{6,10},{7,11},{8,4},{9,5},{10,... | collective-permute-start | bytes 589832 | tf_op jit(solution)/shard_map/ppermute | solution.py:349
  29.3 14.0 %collective-permute-start.6 = (bf16[384,256]{1,0:T(8,128)(2,1)S(1)}, bf16[384,256]{1,0:T(8,128)(2,1)S(1)}, u32[]{:S(2)}, u32[]{:S(2)}) collective-permute-start(bf16[384,256]{1,0:T(8,128)(2,1)S(1)} %get-tuple-element.51), channel_id=1, source_target_pairs={{0,4},{1,5},{2,6},{3,7},{4,0},{5,1},{6,2},{7,3},{8,12},{9,13},{10,... | collective-permute-start | bytes 589832 | tf_op jit(solution)/shard_map/ppermute | solution.py:349
  33.0 10.6 %copy-start.3 = (bf16[4,384,256]{2,1,0:T(8,128)(2,1)}, bf16[4,384,256]{2,1,0:T(8,128)(2,1)S(1)}, u32[]{:S(2)}) copy-start(bf16[4,384,256]{2,1,0:T(8,128)(2,1)S(1)} %get-tuple-element.57.refs_8_.refs_7_) | copy-start | bytes 2359300
  33.0 10.6 %copy-start.11 = (f32[4,384,256]{2,1,0:T(8,128)}, f32[4,384,256]{2,1,0:T(8,128)S(1)}, u32[]{:S(2)}) copy-start(f32[4,384,256]{2,1,0:T(8,128)S(1)} %get-tuple-element.66.refs_5_) | copy-start | bytes 4718596
  33.1 10.5 %copy-start.9 = (bf16[384,256]{1,0:T(8,128)(2,1)}, bf16[384,256]{1,0:T(8,128)(2,1)S(1)}, u32[]{:S(2)}) copy-start(bf16[384,256]{1,0:T(8,128)(2,1)S(1)} %get-tuple-element.49.refs_3_.refs_1_.refs_6_.refs_2_) | copy-start | bytes 589828
  33.2 12.8 %copy-start.16 = (bf16[1,1,6,1536]{3,2,1,0:T(8,128)(2,1)S(1)}, bf16[1,1,6,1536]{3,2,1,0:T(8,128)(2,1)}, u32[]{:S(2)}) copy-start(bf16[1,1,6,1536]{3,2,1,0:T(8,128)(2,1)} %param.12) | copy-start | bytes 55300
  33.2 18.5 %collective-permute-start.5 = (bf16[384,256]{1,0:T(8,128)(2,1)S(1)}, bf16[384,256]{1,0:T(8,128)(2,1)}, u32[]{:S(2)}, u32[]{:S(2)}) collective-permute-start(bf16[384,256]{1,0:T(8,128)(2,1)S(1)} %get-tuple-element.49.refs_3_.refs_1_.refs_6_.refs_2_), channel_id=1, source_target_pairs={{0,1},{1,0},{2,3},{3,2},{4,8},{5,9},{6,10},{7,11},{8,4},{9,5},{10,... | collective-permute-start | bytes 589832 | tf_op jit(solution)/shard_map/ppermute | solution.py:349
  43.6 3.5 %copy-start.5 = (bf16[384,256]{1,0:T(8,128)(2,1)}, bf16[384,256]{1,0:T(8,128)(2,1)S(1)}, u32[]{:S(2)}) copy-start(bf16[384,256]{1,0:T(8,128)(2,1)S(1)} %get-tuple-element.54.refs_8_.refs_7_.refs_1_.refs_3_) | copy-start | bytes 589828
  43.6 9.6 %collective-permute-start.8 = (bf16[384,256]{1,0:T(8,128)(2,1)S(1)}, bf16[384,256]{1,0:T(8,128)(2,1)}, u32[]{:S(2)}, u32[]{:S(2)}) collective-permute-start(bf16[384,256]{1,0:T(8,128)(2,1)S(1)} %get-tuple-element.54.refs_8_.refs_7_.refs_1_.refs_3_), channel_id=1, source_target_pairs={{0,4},{1,5},{2,6},{3,7},{4,0},{5,1},{6,2},{7,3},{8,12},{9,13},{10,... | collective-permute-start | bytes 589832 | tf_op jit(solution)/shard_map/ppermute | solution.py:349
  47.1 13.9 %all-to-all-start.1 = ((bf16[32,16,256]{2,1,0:T(8,128)(2,1)}), bf16[32,16,256]{2,1,0:T(8,128)(2,1)}, u32[]{:S(2)}, u32[]{:S(2)}) async-start(bf16[32,16,256]{2,1,0:T(8,128)(2,1)} %coarse_rhs_sums.1.refs_2_), calls=%async_computation.1 | async-start | bytes 524288 | tf_op jit(solution)/shard_map/all_to_all | solution.py:353
  53.1 11.9 %collective-permute-start.7 = (bf16[384,256]{1,0:T(8,128)(2,1)S(1)}, bf16[384,256]{1,0:T(8,128)(2,1)}, u32[]{:S(2)}, u32[]{:S(2)}) collective-permute-start(bf16[384,256]{1,0:T(8,128)(2,1)S(1)} %margin_solve.6.refs_4_), channel_id=1, source_target_pairs={{0,1},{1,0},{2,3},{3,2},{4,8},{5,9},{6,10},{7,11},{8,4},{9,5},{10,... | collective-permute-start | bytes 589832 | tf_op jit(solution)/shard_map/ppermute | solution.py:349
  55.4 10.8 %collective-permute-start.10 = (bf16[384,256]{1,0:T(8,128)(2,1)}, bf16[384,256]{1,0:T(8,128)(2,1)S(1)}, u32[]{:S(2)}, u32[]{:S(2)}) collective-permute-start(bf16[384,256]{1,0:T(8,128)(2,1)} %margin_solve.7), channel_id=1, source_target_pairs={{0,4},{1,5},{2,6},{3,7},{4,0},{5,1},{6,2},{7,3},{8,12},{9,13},{10,... | collective-permute-start | bytes 589832 | tf_op jit(solution)/shard_map/ppermute | solution.py:349
  66.0 3.1 %copy-start.4 = (bf16[4,384,256]{2,1,0:T(8,128)(2,1)S(1)}, bf16[4,384,256]{2,1,0:T(8,128)(2,1)}, u32[]{:S(2)}) copy-start(bf16[4,384,256]{2,1,0:T(8,128)(2,1)} %copy-done.3) | copy-start | bytes 2359300
  66.0 3.0 %copy-start.6 = (bf16[384,256]{1,0:T(8,128)(2,1)S(1)}, bf16[384,256]{1,0:T(8,128)(2,1)}, u32[]{:S(2)}) copy-start(bf16[384,256]{1,0:T(8,128)(2,1)} %copy-done.5) | copy-start | bytes 589828
  66.1 3.0 %copy-start.10 = (bf16[384,256]{1,0:T(8,128)(2,1)S(1)}, bf16[384,256]{1,0:T(8,128)(2,1)}, u32[]{:S(2)}) copy-start(bf16[384,256]{1,0:T(8,128)(2,1)} %copy-done.9) | copy-start | bytes 589828
  66.1 3.0 %copy-start.12 = (f32[4,384,256]{2,1,0:T(8,128)S(1)}, f32[4,384,256]{2,1,0:T(8,128)}, u32[]{:S(2)}) copy-start(f32[4,384,256]{2,1,0:T(8,128)} %copy-done.11) | copy-start | bytes 4718596
  66.1 5.7 %collective-permute-start.9 = (bf16[384,128]{1,0:T(8,128)(2,1)S(1)}, bf16[384,128]{1,0:T(8,128)(2,1)S(1)}, u32[]{:S(2)}, u32[]{:S(2)}) collective-permute-start(bf16[384,128]{1,0:T(8,128)(2,1)S(1)} %get-tuple-element.58.refs_3_), channel_id=1, source_target_pairs={{0,1},{1,0},{2,3},{3,2},{4,8},{5,9},{6,10},{7,11},{8,4},{9,5},{10,... | collective-permute-start | bytes 294920 | tf_op jit(solution)/shard_map/ppermute | solution.py:349
  66.6 5.5 %collective-permute-start.11 = (bf16[384,128]{1,0:T(8,128)(2,1)S(1)}, bf16[384,128]{1,0:T(8,128)(2,1)S(1)}, u32[]{:S(2)}, u32[]{:S(2)}) collective-permute-start(bf16[384,128]{1,0:T(8,128)(2,1)S(1)} %get-tuple-element.61), channel_id=1, source_target_pairs={{0,4},{1,5},{2,6},{3,7},{4,0},{5,1},{6,2},{7,3},{8,12},{9,13},{10,... | collective-permute-start | bytes 294920 | tf_op jit(solution)/shard_map/ppermute | solution.py:349

commit v5 on v4

--- a/solution.py
+++ b/solution.py
@@ -10,7 +10,7 @@
 BF = jnp.bfloat16
 F32 = jnp.float32
 ALL = ("row", "col")
-PAD = 16
+PAD = 8
 LIMIT = 16 * 1024 * 1024
 SCHEDULE_COST = 1200
 
@@ -83,26 +83,27 @@
 
 
 def load_edge(chain):
-    def body(r, s, sems):
-        run_copies([(r.at[jnp.where(is_lower(chain), 0, r.shape[0] - 1)], s)], sems)
-
-    return body
-
-
-def load_outer(ld, lu, d2, u2, d1, u1, sems):
+    def body(r, s, *rest):
+        whole, sems = rest[:-1], rest[-1]
+        edge = (r.at[jnp.where(is_lower(chain), 0, r.shape[0] - 1)], s)
+        run_copies([edge] + [(r, to) for to in whole], sems)
+
+    return body
+
+
+def load_outer(ld, lu, o2, o1, d2, u2, d1, u1, v2, v1, sems):
     lower = is_lower(2)
     at = [jnp.where(lower, 0, m.shape[0] - 1) for m in (ld, lu)]
     to = [m.shape[0] - 1 - i for m, i in zip((ld, lu), at)]
     blocks = [(ld.at[at[0]], d2), (lu.at[at[1]], u2), (ld.at[to[0]], d1), (lu.at[to[1]], u1)]
-    run_copies(blocks, sems)
-
-
-def margin_solve(chain, fetch):
-    def body(h, e, diag, upper, s, *held):
+    run_copies(blocks + [(o2, v2), (o1, v1)], sems)
+
+
+def margin_solve(chain):
+    def body(h, e, diag, upper, s, far, sem):
         lower = is_lower(chain)
-        if fetch:
-            run_copies([(h, held[0]), (e, held[1])], held[2])
-            h, e = held[:2]
+        out = pltpu.make_async_copy(h, far, sem)
+        out.start()
 
         @pl.when(lower)
         def _():
@@ -112,19 +113,20 @@
         def _():
             s[...] = (mm(diag[...], h[...]) + mmt(upper[...], e[...])).astype(BF)
 
+        out.wait()
+
     return body
 
 
 def solve_layers(*refs):
-    count = 11
-    far, p, near, sems = refs[:count], refs[count], refs[count + 1 : 2 * count + 1], refs[-1]
+    far, p, scalars, near, sems = refs[:11], refs[11], refs[12:-12], refs[-12:-1], refs[-1]
     copies = [pltpu.make_async_copy(a, b, sems.at[i]) for i, (a, b) in enumerate(zip(far, near))]
     for c in copies:
         c.start()
     gathered, fpad, fown, basis, h2, h1, o2, o1, e, ld, lu = near
     for c in copies[:4]:
         c.wait()
-    g = gathered[...].reshape(-1, gathered.shape[-1])
+    g = gathered[...].reshape(-1, gathered.shape[-1])[:, : p.shape[2]]
     v = mm(fpad[...], g).astype(BF)
     u = mmt(fown[...], v).astype(BF)
     size = p.shape[1]
@@ -141,6 +143,16 @@
     p[1] = p[1] + mm(lu[2], e3) + mmt(lu[1], e1)
     p[2] = p[2] + mm(lu[3], e4) + mmt(lu[2], e2)
     p[3] = p[3] + mm(lu[4], e5) + mmt(lu[3], e3)
+    for out in scalars:
+        total = gathered[0].astype(F32)
+        for k in range(1, gathered.shape[0]):
+            total = total + gathered[k].astype(F32)
+        beside = total[:, p.shape[2] :]
+        rho, d0 = (
+            jnp.concatenate([beside[k : k + 1] + beside[k + 2 : k + 3], beside[k + 1 : k + 2] + beside[k + 3 : k + 4]], axis=1)
+            for k in (0, 4)
+        )
+        out[...] = jnp.concatenate([rho, d0, rho / d0], axis=0)
 
 
 def join_margin(chain):
@@ -157,45 +169,44 @@
     return body
 
 
-def inner_operate(z2, z1, p, r, sd, su, z, w, wb, rho):
+def inner_operate(z2, z1, p, r, sd, su, z, w, wb, sums):
     z[0], z[3] = pick(z2[...], z1[...])
     z[1] = p[1]
     z[2] = p[2]
-    acc = jnp.zeros(rho.shape, F32)
+    rho = d0 = jnp.zeros((1, p.shape[2]), F32)
     for k in range(4):
         zk = z[k]
-        acc = acc + colsum(r[k].astype(F32) * zk)
+        rho = rho + colsum(r[k].astype(F32) * zk)
         w[k] = mm(sd[k], zk.astype(BF))
         if k < 3:
             w[k] = w[k] + mm(su[k], z[k + 1].astype(BF))
         if k > 0:
             w[k] = w[k] + mmt(su[k - 1], z[k - 1].astype(BF))
         wb[k] = w[k].astype(BF)
-    rho[...] = acc
+        if 0 < k < 3:
+            d0 = d0 + colsum(w[k] * zk)
+    sums[...] = jnp.concatenate([rho, d0], axis=0)
 
 
 def join_operate(chain):
-    def body(n, w, su, edge, s):
+    def body(n, w, su, s):
         lower = is_lower(chain)
         term = kept(n[...], lower)
 
         @pl.when(lower)
         def _():
-            edge[...] = w[0] + term.astype(F32)
+            s[...] = (w[0] + term.astype(F32)).astype(BF)
 
         @pl.when(jnp.logical_not(lower))
         def _():
-            edge[...] = w[3] + mm(su[3], term)
-
-        s[...] = edge[...].astype(BF)
+            s[...] = (w[3] + mm(su[3], term)).astype(BF)
 
     return body
 
 
 def coarse_rhs(ncb):
-    def body(e, basis, g, held, rows, block, sems):
-        run_copies([(e, held), (basis, rows)], sems)
-        out = mm(rows[...], held[...].reshape(-1, e.shape[-1]))
+    def body(e, basis, g, block, sems):
+        out = mm(basis[...], e[...].reshape(-1, e.shape[-1]))
         out = jnp.concatenate([out, jnp.zeros((PAD - ncb, out.shape[1]), F32)], axis=0).astype(BF)
         for k in range(g.shape[0]):
             block[k] = out
@@ -232,27 +243,26 @@
     return body
 
 
-def three(x):
-    parts = []
-    for _ in range(3):
-        top = x.astype(BF).astype(F32)
-        parts.append(top)
-        x = x - top
-    return parts
-
-
-def coarse_rhs_sums(ncb):
-    def body(w2, w1, w, z2, z1, p, rho, basis, g, block, sems):
-        ends = [pick(w2[...], w1[...]), pick(z2[...], z1[...])]
-        acc = jnp.zeros(rho.shape, F32)
-        out = jnp.zeros((ncb, rho.shape[1]), F32)
+def in_two(x):
+    top = x.astype(BF).astype(F32)
+    half = x.shape[1] // 2
+    return [part[:, at : at + half] for part in (top, x - top) for at in (0, half)]
+
+
+def coarse_rhs_joined(ncb):
+    def body(w2, w1, z2, z1, w, sums, basis, g, block, sems):
+        ends, tops = pick(w2[...], w1[...]), pick(z2[...], z1[...])
         size = w.shape[1]
+        out = jnp.zeros((ncb, w.shape[2]), F32)
+        d0 = sums[1:2]
         for k in range(4):
-            wk, zk = (w[k], p[k]) if 0 < k < 3 else (pair[k // 3] for pair in ends)
-            out = out + mm(basis[:, k * size : (k + 1) * size], wk.astype(BF))
-            acc = acc + colsum(wk * zk)
-        rows = [out, jnp.zeros((8 - ncb, out.shape[1]), F32)] + three(rho[...]) + three(acc)
-        out = jnp.concatenate(rows + [jnp.zeros((2, out.shape[1]), F32)], axis=0).astype(BF)
+            wk = w[k].astype(BF) if 0 < k < 3 else ends[k // 3]
+            out = out + mm(basis[:, k * size : (k + 1) * size], wk)
+        for x, y in zip(ends, tops):
+            d0 = d0 + colsum(x.astype(F32) * y)
+        out = jnp.concatenate([out, jnp.zeros((PAD - ncb, out.shape[1]), F32)], axis=0)
+        beside = jnp.concatenate(in_two(sums[0:1]) + in_two(d0), axis=0)
+        out = jnp.concatenate([out, beside], axis=1).astype(BF)
         for k in range(g.shape[0]):
             block[k] = out
         run_copies([(block, g)], sems)
@@ -281,16 +291,13 @@
     return body
 
 
-def inner_products(q2, q1, o2, o1, p, z, r, w, sd, su, early, q, kept_z, first, sums):
+def inner_products(q2, q1, o2, o1, p, z, r, w, sd, su, scalars, q, kept_z, sums):
     q[0], q[3] = pick(q2[...], q1[...])
     q[1] = p[1]
     q[2] = p[2]
     ends = pick(o2[...], o1[...])
     kept_z[...] = z[...]
-    total = early[0].astype(F32)
-    for k in range(1, early.shape[0]):
-        total = total + early[k].astype(F32)
-    first[...] = total
+    a0 = scalars[2:3]
     s1 = s2 = s4 = s5 = jnp.zeros((1, q.shape[-1]), F32)
     for k in range(4):
         qk = q[k]
@@ -305,7 +312,7 @@
             s5 = s5 + 2.0 * colsum(qk * mm(su[k], q[k + 1].astype(BF)))
         s1 = s1 + colsum(r[k].astype(F32) * qk)
         s2 = s2 + colsum(wk * qk)
-    sums[...] = jnp.concatenate([s1, s2, s4, s5], axis=0)
+    sums[...] = jnp.concatenate([a0 * (a0 * s2 - s1), s4, s5], axis=0)
 
 
 def join_sums(t2, t1, c2, c1, sums, out):
@@ -314,21 +321,20 @@
     half = low_in.shape[1]
     above = colsum(high[:, :half] * kept(high_in, False).astype(F32))
     below = colsum(low[:, half:] * kept(low_in, True).astype(F32))
-    s5 = sums[3:4] + jnp.concatenate([above, below], axis=1)
-    full = jnp.concatenate([sums[0:3], s5], axis=0)
+    right = jnp.concatenate([sums[2:3, :half] + above, sums[2:3, half:] + below], axis=0)
+    full = jnp.concatenate([sums[0:2], right], axis=1)
     for k in range(out.shape[0]):
         out[k] = full
 
 
-def finish(parts, first, z, q, x):
+def finish(parts, scalars, z, q, x):
     total = parts[0]
     for k in range(1, parts.shape[0]):
         total = total + parts[k]
-    rho0 = first[8:9] + first[9:10] + first[10:11]
-    d0 = first[11:12] + first[12:13] + first[13:14]
-    s1, s2, s4, s5 = (total[k : k + 1] for k in range(4))
-    a0 = rho0 / d0
-    rho1 = a0 * (a0 * s2 - s1)
+    cols = z.shape[2]
+    rho0, d0, a0 = (scalars[k : k + 1] for k in range(3))
+    rho1, s4 = total[0:1, :cols], total[1:2, :cols]
+    s5 = jnp.concatenate([total[0:1, cols:], total[1:2, cols:]], axis=1)
     grow = 1.0 + rho1 / rho0
     a1 = rho1 / (grow * grow * d0 - grow * a0 * s4 + a0 * a0 * s5)
     cz = a0 + a1 * grow
@@ -357,7 +363,7 @@
     layers, _, size, cols = rhs.shape
     devices = lax.axis_size("row") * lax.axis_size("col")
     ncb, nco = coarse_basis.shape[2], coarse_factor.shape[0]
-    layer, whole, row = (size, cols), (layers, size, cols), (1, cols)
+    layer, whole = (size, cols), (layers, size, cols)
     copies = ((devices, PAD, cols), BF)
     edge = [(layer, F32), (layer, BF)]
     block = 2 * size * size * cols
@@ -365,64 +371,67 @@
     r, sd, su, ld, lu = rhs[:, 0], stiff_diag[:, 0], stiff_upper[:, 0], local_diag[:, 0], local_upper[:, 0]
     raw_basis = coarse_basis[0, 0]
 
-    def margins(h2, h1, o2, o1, g, fetch):
+    def margins(h2, h1, o2, o1, g):
         g = pltpu.with_memory_space_constraint(g, pltpu.HBM)
-        d2, u2, d1, u1 = call(
-            load_outer, [((size, size), BF)] * 4, (ld, lu), "load_outer", SCHEDULE_COST * block, [g], [dma(4)], (0, 1)
+        shapes = [((size, size), BF)] * 4 + [(layer, BF)] * 2
+        d2, u2, d1, u1, v2, v1 = call(
+            load_outer, shapes, (ld, lu, o2, o1), "load_outer", SCHEDULE_COST * block, [g], [dma(6)], range(4)
         )
-        held, far = ([pltpu.VMEM(layer, BF)] * 2 + [dma(2)], (0, 1)) if fetch else ((), ())
         take = lambda chain, args, after: call(
-            margin_solve(chain, fetch), [(layer, BF)], args, "margin_solve", 2 * block, after, held, far
-        )[0]
-        s2 = take(2, (h2, o2, d2, u2), ())
-        s1 = take(1, (h1, o1, d1, u1), [s2])
-        return swap(2, s2), swap(1, s1), s1
-
-    def solve(h2, h1, o2, o1, e, gathered):
+            margin_solve(chain), [(layer, BF)] * 2, args, "margin_solve", 2 * block, after, [pltpu.SemaphoreType.DMA], (), (1,)
+        )
+        s2, h2 = take(2, (h2, v2, d2, u2), [])
+        s1, h1 = take(1, (h1, v1, d1, u1), [s2])
+        return swap(2, s2), swap(1, s1), h2, h1, s1
+
+    def solve(h2, h1, o2, o1, e, gathered, scalars):
         args = (gathered, fpad, fown, basis, h2, h1, o2, o1, e, ld, lu)
         held = [pltpu.VMEM(a.shape, a.dtype) for a in args] + [dma(len(args))]
-        return call(solve_layers, [(whole, F32)], args, "solve_layers", 12 * block, (), held, range(len(args)))[0]
+        outs = [(whole, F32)] + [((3, cols), F32)] * scalars
+        return call(solve_layers, outs, args, "solve_layers", 12 * block, (), held, range(len(args)))
 
     (s2,) = call(load_edge(2), [(layer, BF)], (r,), "load_edge", 0, (), [dma(1)], (0,))
     h2 = swap(2, s2)
-    (s1,) = call(load_edge(1), [(layer, BF)], (r,), "load_edge", 0, [s2], [dma(1)], (0,))
+    s1, near_r = call(load_edge(1), [(layer, BF), (whole, BF)], (r,), "load_edge", 0, [s2], [dma(2)], (0,))
     h1 = swap(1, s1)
-    held = [pltpu.VMEM(whole, BF), pltpu.VMEM(raw_basis.shape, BF), pltpu.VMEM(*copies), dma(2)]
-    (g,) = call(coarse_rhs(ncb), [copies], (r, raw_basis), "coarse_rhs", block // 32, [s1], held, (0, 1), (0,))
+    held = [pltpu.VMEM(*copies), dma(1)]
+    (g,) = call(coarse_rhs(ncb), [copies], (near_r, raw_basis), "coarse_rhs", block // 32, [s1], held, (), (0,))
     gathered = gather(g)
-    m2, m1, last = margins(h2, h1, s2, s1, g, False)
+    m2, m1, h2, h1, last = margins(h2, h1, s2, s1, g)
     shapes = [((PAD, layers * size), BF), ((nco, devices * PAD), BF), ((nco, PAD), BF)]
     held = [pltpu.VMEM(*shape) for shape in shapes] + [dma(3)]
     basis, fpad, fown = call(
         prepare(ncb), shapes, (raw_basis, coarse_factor), "prepare", block // 8, [last], held, (), (0, 1, 2)
     )
-    p = solve(h2, h1, s2, s1, r, gathered)
+    (p,) = solve(h2, h1, s2, s1, r, gathered, 0)
     z2, s2 = call(join_margin(2), edge, (m2, p, su), "join_margin", block)
     z1, s1 = call(join_margin(1), edge, (m1, p, su), "join_margin", block, [s2])
     n2, n1 = swap(2, s2), swap(1, s1)
-    z, wi, w, rho = call(
-        inner_operate, [(whole, F32)] * 2 + [(whole, BF), (row, F32)], (z2, z1, p, r, sd, su), "inner_operate", 10 * block
-    )
-    w2, o2 = call(join_operate(2), edge, (n2, wi, su), "join_operate", block)
-    w1, o1 = call(join_operate(1), edge, (n1, wi, su), "join_operate", block, [o2])
+    outs = [(whole, F32)] * 2 + [(whole, BF), ((2, cols), F32)]
+    z, wi, w, sums = call(inner_operate, outs, (z2, z1, p, r, sd, su), "inner_operate", 10 * block)
+    (o2,) = call(join_operate(2), edge[1:], (n2, wi, su), "join_operate", block, [n1])
+    (o1,) = call(join_operate(1), edge[1:], (n1, wi, su), "join_operate", block, [o2])
     h2, h1 = swap(2, o2), swap(1, o1)
-    (g,) = call(coarse_rhs_sums(ncb), [copies], (w2, w1, wi, z2, z1, p, rho, raw_basis), "coarse_rhs_sums", block // 32, [o1], [pltpu.VMEM(*copies), dma(1)], (), (0,))
+    wider = ((devices, PAD, cols + cols // 2), BF)
+    held = [pltpu.VMEM(*wider), dma(1)]
+    args = (o2, o1, z2, z1, wi, sums, raw_basis)
+    (g,) = call(coarse_rhs_joined(ncb), [wider], args, "coarse_rhs_joined", block // 32, [], held, (), (0,))
     early = gather(g)
-    m2, m1, _ = margins(h2, h1, o2, o1, g, True)
-    p = solve(h2, h1, o2, o1, w, early)
+    m2, m1, h2, h1, _ = margins(h2, h1, o2, o1, g)
+    p, scalars = solve(h2, h1, o2, o1, w, early, 1)
     half = [(layer, F32), ((size, cols // 2), BF), (layer, F32)]
     q2, s2, c2 = call(join_second(2), half, (m2, p, su), "join_second", block)
     q1, s1, c1 = call(join_second(1), half, (m1, p, su), "join_second", block, [s2])
     t2, t1 = swap(2, s2), swap(1, s1)
-    q, z, first, sums = call(
+    q, z, sums = call(
         inner_products,
-        [(whole, F32), (whole, F32), ((PAD, cols), F32), ((4, cols), F32)],
-        (q2, q1, o2, o1, p, z, r, w, sd, su, early),
+        [(whole, F32), (whole, F32), ((3, cols), F32)],
+        (q2, q1, o2, o1, p, z, r, w, sd, su, scalars),
         "inner_products",
         12 * block,
     )
-    (g,) = call(join_sums, [((devices, 4, cols), F32)], (t2, t1, c2, c1, sums), "join_sums")
-    (x,) = call(finish, [(whole, F32)], (gather(g), first, z, q), "finish")
+    (g,) = call(join_sums, [((devices, 2, cols + cols // 2), F32)], (t2, t1, c2, c1, sums), "join_sums")
+    (x,) = call(finish, [(whole, F32)], (gather(g), scalars, z, q), "finish")
     return x[:, None]
 
 

time: 86.1 us -> 80 us (0.929)
  waiting for transfers between devices: 16.5 us -> 9.13 us
  starting transfers between devices: 26.6 us -> 28.8 us
  Pallas kernels: 29.3 us -> 28.1 us
    all_to_all x2, waiting for transfers between devices: 6.08 us -> 0.89 us  [gather(): return lax.all_to_all(copies, ALL, 0, 0)]
    ppermute x12, waiting for transfers between devices: 10.4 us -> 8.24 us  [swap(): return lax.ppermute(x, ALL, moves)]
    pallas_call x23, Pallas kernels: 29.3 us -> 28.1 us  [call(): pl.pallas_call(kernel, out_shape=shapes, in_specs=[space(i, hbm) for i in...]
    all_to_all x2, starting transfers between devices: 8.05 us -> 9.21 us  [gather(): return lax.all_to_all(copies, ALL, 0, 0)]
    ppermute x12, starting transfers between devices: 18.6 us -> 19.6 us  [swap(): return lax.ppermute(x, ALL, moves)]
  transfers between devices with their start and end apart: 14 -> 14, of which waited for: 4 -> 6; matrix products, arithmetic and copies ran while one was open for 0% -> 0% of each run, Pallas kernels for 31% -> 32%
where the time goes in v5:
time: 80 us; the launch traced here: 79.6 us
  starting transfers between devices  28.8 us (36%)
  Pallas kernels  28.1 us (35%)
  blocking collectives  12.4 us (16%)
  waiting for transfers between devices  9.13 us (11%)
    pallas_call x23, Pallas kernels, call(): pl.pallas_call(kernel, out_shape=shapes, in_specs=[space(i, hbm) for i in...  28.1 us
    ppermute x12, starting transfers between devices, swap(): return lax.ppermute(x, ALL, moves)  19.6 us
    all_to_all x1, blocking collectives, gather(): return lax.all_to_all(copies, ALL, 0, 0)  12.4 us
    all_to_all x2, starting transfers between devices, gather(): return lax.all_to_all(copies, ALL, 0, 0)  9.21 us
    ppermute x12, waiting for transfers between devices, swap(): return lax.ppermute(x, ALL, moves)  8.24 us
  transfers between devices with their start and end apart: 14, of which 6 were waited for; matrix products, arithmetic and copies ran while one was open for 0% of the time, Pallas kernels for 32%

profile of v5, /device:TPU:0, one launch (start us, length us, event | category | flops | bytes accessed | tf_op | source)
XLA Modules:
  0.0 79.6 jit_solution(9075876526955861330)
XLA Ops:
  0.0 0.9 %load_edge.2.refs_1_.refs_2_.refs_6_ = bf16[384,256]{1,0:T(8,128)(2,1)S(1)} custom-call(bf16[4,384,256]{2,1,0:T(8,128)(2,1)} %bitcast.17), custom_call_target="tpu_custom_call" | custom-call | bytes 786432 | tf_op jit(solution)/shard_map/load_edge/pallas_call | solution.py:73
  1.0 0.5 collective-permute-start
  1.5 1.3 %load_edge.3 = (bf16[384,256]{1,0:T(8,128)(2,1)S(1)}, bf16[4,384,256]{2,1,0:T(8,128)(2,1)S(1)}) custom-call(bf16[4,384,256]{2,1,0:T(8,128)(2,1)} %bitcast.18, bf16[384,256]{1,0:T(8,128)(2,1)S(1)} %load_edge.2.refs_1_.refs_2_.refs_6_), custom_call_target="tpu_custom_call" | custom-call | bytes 786432 | tf_op jit(solution)/shard_map/load_edge/pallas_call | solution.py:73
  2.8 4.1 %collective-permute-start.2 = (bf16[384,256]{1,0:T(8,128)(2,1)S(1)}, bf16[384,256]{1,0:T(8,128)(2,1)S(1)}, u32[]{:S(2)}, u32[]{:S(2)}) collective-permute-start(bf16[384,256]{1,0:T(8,128)(2,1)S(1)} %get-tuple-element.49.refs_2_.refs_3_.refs_7_), channel_id=1, source_target_pairs={{0,4},{1,5},{2,6},{3,7},{4,0},{5,1},{6,2},{7,3},{8,12},{9,13},{10,... | collective-permute-start | bytes 589832 | tf_op jit(solution)/shard_map/ppermute | solution.py:355
  6.9 0.9 %coarse_rhs.1.refs_4_ = bf16[32,8,256]{2,1,0:T(8,128)(2,1)} custom-call(bf16[4,384,256]{2,1,0:T(8,128)(2,1)S(1)} %get-tuple-element.50.refs_0_, bf16[6,1536]{1,0:T(8,128)(2,1)S(1)} %bitcast.24, bf16[384,256]{1,0:T(8,128)(2,1)S(1)} %get-tuple-element.49.refs_2_.refs_3_.refs_7_), custom_call_target="tpu_custom_call" | custom-call | flops 2359296 | bytes 804864 | tf_op jit(solution)/shard_map/coarse_rhs/pallas_call | solution.py:73
  7.8 4.7 %all-to-all-start = ((bf16[32,8,256]{2,1,0:T(8,128)(2,1)}), bf16[32,8,256]{2,1,0:T(8,128)(2,1)S(1)}, u32[]{:S(2)}, u32[]{:S(2)}) async-start(bf16[32,8,256]{2,1,0:T(8,128)(2,1)} %coarse_rhs.1.refs_4_), calls=%async_computation | async-start | bytes 262144 | tf_op jit(solution)/shard_map/all_to_all | solution.py:359
  12.5 1.4 %load_outer.2 = (bf16[384,384]{1,0:T(8,128)(2,1)S(1)}, bf16[384,384]{1,0:T(8,128)(2,1)S(1)}, bf16[384,384]{1,0:T(8,128)(2,1)S(1)}, bf16[384,384]{1,0:T(8,128)(2,...) custom-call(bf16[6,384,384]{2,1,0:T(8,128)(2,1)} %bitcast.27, bf16[5,384,384]{2,1,0:T(8,128)(2,1)} %bitcast.31, ...), custom_call_target="tpu_custom_call" | custom-call | flops 90596966400 | bytes 3637248 | tf_op jit(solution)/shard_map/load_outer/pallas_call | solution.py:73
  13.9 0.0 copy-start.15
  14.0 0.7 margin_solve.4
  14.6 0.3 collective-permute-start.1
  15.0 0.7 margin_solve.5
  15.7 3.0 %collective-permute-start.4 = (bf16[384,256]{1,0:T(8,128)(2,1)S(1)}, bf16[384,256]{1,0:T(8,128)(2,1)S(1)}, u32[]{:S(2)}, u32[]{:S(2)}) collective-permute-start(bf16[384,256]{1,0:T(8,128)(2,1)S(1)} %get-tuple-element.58.refs_2_), channel_id=1, source_target_pairs={{0,4},{1,5},{2,6},{3,7},{4,0},{5,1},{6,2},{7,3},{8,12},{9,13},{10,... | collective-permute-start | bytes 589832 | tf_op jit(solution)/shard_map/ppermute | solution.py:355
  18.7 1.2 %prepare.1 = (bf16[8,1536]{1,0:T(8,128)(2,1)}, bf16[192,256]{1,0:T(8,128)(2,1)}, bf16[192,8]{1,0:T(8,128)(2,1)}) custom-call(bf16[6,1536]{1,0:T(8,128)(2,1)S(1)} %bitcast.25, bf16[192,192]{1,0:T(8,128)(2,1)S(1)} %copy-done.15, bf16[384,256]{1,0:T(8,128)(2,1)S(1)} %get-tuple-element.58.refs_2_), custom_call_target="tpu_custom_call" | custom-call | flops 9437184 | bytes 92160 | tf_op jit(solution)/shard_map/prepare/pallas_call | solution.py:73
  19.9 0.9 %all-to-all-done.refs_0_ = bf16[32,8,256]{2,1,0:T(8,128)(2,1)S(1)} async-done(((bf16[32,8,256]{2,1,0:T(8,128)(2,1)}), bf16[32,8,256]{2,1,0:T(8,128)(2,1)S(1)}, u32[]{:S(2)}, u32[]{:S(2)}) %all-to-all-start) | async-done | bytes 131104 | tf_op jit(solution)/shard_map/all_to_all | solution.py:359
  20.8 0.7 copy-done.16
  21.5 4.1 %solve_layers.2.refs_1_.refs_2_ = f32[4,384,256]{2,1,0:T(8,128)S(1)} custom-call(bf16[32,8,256]{2,1,0:T(8,128)(2,1)} %copy-done.16, bf16[192,256]{1,0:T(8,128)(2,1)} %get-tuple-element.59.refs_1_, bf16[192,8]{1,0:T(8,128)(2,1)} %get-tuple-element.60.refs_2_, bf16[8,1536]{1,0:T(8,128)(2,1)} %get-tuple-element.61.refs_3_, ...), custom_call_target="tpu_custom_call" | custom-call | flops 905969664 | bytes 5073920 | tf_op jit(solution)/shard_map/solve_layers/pallas_call | solution.py:73
  25.6 0.1 join_margin.2
  25.6 0.0 copy-start.1
  25.7 0.0 copy-start.4
  25.7 0.2 collective-permute-start.3
  25.9 0.4 collective-permute-done.4.refs_0_
  26.3 0.4 join_margin.3
  26.6 2.3 %collective-permute-start.5 = (bf16[384,256]{1,0:T(8,128)(2,1)S(1)}, bf16[384,256]{1,0:T(8,128)(2,1)S(1)}, u32[]{:S(2)}, u32[]{:S(2)}) collective-permute-start(bf16[384,256]{1,0:T(8,128)(2,1)S(1)} %get-tuple-element.68), channel_id=1, source_target_pairs={{0,4},{1,5},{2,6},{3,7},{4,0},{5,1},{6,2},{7,3},{8,12},{9,13},{10,... | collective-permute-start | bytes 589832 | tf_op jit(solution)/shard_map/ppermute | solution.py:355
  28.9 1.3 %inner_operate.1 = (f32[4,384,256]{2,1,0:T(8,128)S(1)}, f32[4,384,256]{2,1,0:T(8,128)S(1)}, bf16[4,384,256]{2,1,0:T(8,128)(2,1)S(1)}, f32[2,256]{1,0:T(2,128)S(1)}) custom-call(f32[384,256]{1,0:T(8,128)S(1)} %get-tuple-element.65.refs_0_.refs_2_, f32[384,256]{1,0:T(8,128)S(1)} %get-tuple-element.66.refs_1_.refs_3_, ...), custom_call_target="tpu_custom_call" | custom-call | flops 754974720 | bytes 5505024 | tf_op jit(solution)/shard_map/inner_operate/pallas_call | solution.py:73
  30.3 5.7 %collective-permute-done.5.refs_3_.refs_0_ = bf16[384,256]{1,0:T(8,128)(2,1)S(1)} collective-permute-done((bf16[384,256]{1,0:T(8,128)(2,1)S(1)}, bf16[384,256]{1,0:T(8,128)(2,1)S(1)}, u32[]{:S(2)}, u32[]{:S(2)}) %collective-permute-start.5) | collective-permute-done | bytes 196640 | tf_op jit(solution)/shard_map/ppermute | solution.py:355
  36.0 0.0 copy-start.14
  36.0 0.1 collective-permute-start.6
  36.1 0.3 join_operate.3.refs_1_.refs_3_.refs_7_
  36.4 3.2 %collective-permute-start.8 = (bf16[384,256]{1,0:T(8,128)(2,1)S(1)}, bf16[384,256]{1,0:T(8,128)(2,1)}, u32[]{:S(2)}, u32[]{:S(2)}) collective-permute-start(bf16[384,256]{1,0:T(8,128)(2,1)S(1)} %join_operate.3.refs_1_.refs_3_.refs_7_), channel_id=1, source_target_pairs={{0,4},{1,5},{2,6},{3,7},{4,0},{5,1},{6,2},{7,3},{8,12},{9,13},{10,... | collective-permute-start | bytes 589832 | tf_op jit(solution)/shard_map/ppermute | solution.py:355
  39.6 1.0 %coarse_rhs_joined.1.refs_4_ = bf16[32,8,384]{2,1,0:T(8,128)(2,1)} custom-call(bf16[384,256]{1,0:T(8,128)(2,1)S(1)} %join_operate.2.refs_3_.refs_0_.refs_2_.refs_6_, bf16[384,256]{1,0:T(8,128)(2,1)S(1)} %join_operate.3.refs_1_.refs_3_.refs_7_, f32[384,256]{1,0:T(8,128)S(1)} %get-tuple-element.65.refs_0_.refs_2_, ...), custom_call_target="tpu_custom_call" | custom-call | flops 2359296 | bytes 2772992 | tf_op jit(solution)/shard_map/coarse_rhs_joined/pallas_call | solution.py:73
  40.6 4.5 %all-to-all-start.1 = ((bf16[32,8,384]{2,1,0:T(8,128)(2,1)}), bf16[32,8,384]{2,1,0:T(8,128)(2,1)}, u32[]{:S(2)}, u32[]{:S(2)}) async-start(bf16[32,8,384]{2,1,0:T(8,128)(2,1)} %coarse_rhs_joined.1.refs_4_), calls=%async_computation.1 | async-start | bytes 393216 | tf_op jit(solution)/shard_map/all_to_all | solution.py:359
  45.1 1.4 %load_outer.3 = (bf16[384,384]{1,0:T(8,128)(2,1)S(1)}, bf16[384,384]{1,0:T(8,128)(2,1)S(1)}, bf16[384,384]{1,0:T(8,128)(2,1)S(1)}, bf16[384,384]{1,0:T(8,128)(2,...) custom-call(bf16[6,384,384]{2,1,0:T(8,128)(2,1)} %bitcast.29, bf16[5,384,384]{2,1,0:T(8,128)(2,1)} %bitcast.33, ...), custom_call_target="tpu_custom_call" | custom-call | flops 90596966400 | bytes 3637248 | tf_op jit(solution)/shard_map/load_outer/pallas_call | solution.py:73
  46.5 1.6 %margin_solve.6 = (bf16[384,256]{1,0:T(8,128)(2,1)S(1)}, bf16[384,256]{1,0:T(8,128)(2,1)}) custom-call(bf16[384,256]{1,0:T(8,128)(2,1)} %collective-permute-done.6.refs_0_, bf16[384,256]{1,0:T(8,128)(2,1)S(1)} %get-tuple-element.70.refs_1_, bf16[384,384]{1,0:T(8,128)(2,1)S(1)} %get-tuple-element.71.refs_2_, bf16[384,384]{1,0:T(8,128)(2,1)S(1)} %get-tuple-element.72.refs_3_), custom_call_target="tpu_custom_call" | custom-call | flops 150994944 | bytes 983040 | tf_op jit(solution)/shard_map/margin_solve/pallas_call | solution.py:73
  48.2 0.3 collective-permute-start.7
  48.4 0.5 collective-permute-done.8.refs_0_
  48.9 2.3 %margin_solve.7 = (bf16[384,256]{1,0:T(8,128)(2,1)}, bf16[384,256]{1,0:T(8,128)(2,1)}) custom-call(bf16[384,256]{1,0:T(8,128)(2,1)} %collective-permute-done.8.refs_0_, bf16[384,256]{1,0:T(8,128)(2,1)S(1)} %get-tuple-element.75.refs_1_, bf16[384,384]{1,0:T(8,128)(2,1)S(1)} %get-tuple-element.76.refs_2_, bf16[384,384]{1,0:T(8,128)(2,1)S(1)} %get-tuple-element.77.refs_3_, ...), custom_call_target="tpu_custom_call" | custom-call | flops 150994944 | bytes 983040 | tf_op jit(solution)/shard_map/margin_solve/pallas_call | solution.py:73
  51.2 2.8 %collective-permute-start.10 = (bf16[384,256]{1,0:T(8,128)(2,1)}, bf16[384,256]{1,0:T(8,128)(2,1)S(1)}, u32[]{:S(2)}, u32[]{:S(2)}) collective-permute-start(bf16[384,256]{1,0:T(8,128)(2,1)} %get-tuple-element.82), channel_id=1, source_target_pairs={{0,4},{1,5},{2,6},{3,7},{4,0},{5,1},{6,2},{7,3},{8,12},{9,13},{10,... | collective-permute-start | bytes 589832 | tf_op jit(solution)/shard_map/ppermute | solution.py:355
  54.0 4.0 %solve_layers.3 = (f32[4,384,256]{2,1,0:T(8,128)S(1)}, f32[3,256]{1,0:T(4,128)S(1)}) custom-call(bf16[32,8,384]{2,1,0:T(8,128)(2,1)} %all-to-all-done.1.refs_0_, bf16[192,256]{1,0:T(8,128)(2,1)} %get-tuple-element.59.refs_1_, bf16[192,8]{1,0:T(8,128)(2,1)} %get-tuple-element.60.refs_2_, bf16[8,1536]{1,0:T(8,128)(2,1)} %get-tuple-element.61.refs_3_, ...), custom_call_target="tpu_custom_call" | custom-call | flops 905969664 | bytes 5139456 | tf_op jit(solution)/shard_map/solve_layers/pallas_call | solution.py:73
  58.0 1.0 %join_second.2 = (f32[384,256]{1,0:T(8,128)S(1)}, bf16[384,128]{1,0:T(8,128)(2,1)S(1)}, f32[384,256]{1,0:T(8,128)S(1)}) custom-call(bf16[384,256]{1,0:T(8,128)(2,1)} %collective-permute-done.7.refs_0_, f32[4,384,256]{2,1,0:T(8,128)S(1)} %get-tuple-element.80.refs_1_.refs_4_, bf16[4,384,384]{2,1,0:T(8,128)(2,1)S(1)} %bitcast.14), custom_call_target="tpu_custom_call" | custom-call | flops 75497472 | bytes 2949120 | tf_op jit(solution)/shard_map/join_second/pallas_call | solution.py:73
  59.0 0.7 collective-permute-start.9
  59.7 0.4 collective-permute-done.10.refs_0_
  60.1 0.4 join_second.3
  60.5 2.1 %collective-permute-start.11 = (bf16[384,128]{1,0:T(8,128)(2,1)S(1)}, bf16[384,128]{1,0:T(8,128)(2,1)S(1)}, u32[]{:S(2)}, u32[]{:S(2)}) collective-permute-start(bf16[384,128]{1,0:T(8,128)(2,1)S(1)} %get-tuple-element.83), channel_id=1, source_target_pairs={{0,4},{1,5},{2,6},{3,7},{4,0},{5,1},{6,2},{7,3},{8,12},{9,13},{10,... | collective-permute-start | bytes 294920 | tf_op jit(solution)/shard_map/ppermute | solution.py:355
  62.6 1.7 %inner_products.1 = (f32[4,384,256]{2,1,0:T(8,128)S(1)}, f32[4,384,256]{2,1,0:T(8,128)S(1)}, f32[3,256]{1,0:T(4,128)S(1)}) custom-call(f32[384,256]{1,0:T(8,128)S(1)} %get-tuple-element.86.refs_0_, f32[384,256]{1,0:T(8,128)S(1)} %get-tuple-element.87.refs_1_, bf16[384,256]{1,0:T(8,128)(2,1)S(1)} %copy-done.3, bf16[384,256]{1,0:T(8,128)(2,1)S(1)} %copy-done.8, ...), custom_call_target="tpu_custom_call" | custom-call | flops 905969664 | bytes 8260608 | tf_op jit(solution)/shard_map/inner_products/pallas_call | solution.py:73
  64.3 1.3 %collective-permute-done.11.refs_1_ = bf16[384,128]{1,0:T(8,128)(2,1)S(1)} collective-permute-done((bf16[384,128]{1,0:T(8,128)(2,1)S(1)}, bf16[384,128]{1,0:T(8,128)(2,1)S(1)}, u32[]{:S(2)}, u32[]{:S(2)}) %collective-permute-start.11) | collective-permute-done | bytes 98336 | tf_op jit(solution)/shard_map/ppermute | solution.py:355
  65.6 0.2 join_sums.1
  65.8 12.4 %all_to_all.15.refs_0_ = f32[32,2,384]{2,1,0:T(2,128)S(1)} all-to-all(f32[32,2,384]{2,1,0:T(2,128)S(1)} %join_sums.1), channel_id=1, replica_groups=mesh['row'=8,'col'=4] {'row','col'}, dimensions={0} | all-to-all | bytes 196608 | tf_op jit(solution)/shard_map/all_to_all | solution.py:359
  78.2 1.4 %finish.1 = f32[4,384,256]{2,1,0:T(8,128)} custom-call(f32[32,2,384]{2,1,0:T(2,128)S(1)} %all_to_all.15.refs_0_, f32[3,256]{1,0:T(4,128)S(1)} %get-tuple-element.89.refs_10_.refs_1_, f32[4,384,256]{2,1,0:T(8,128)S(1)} %get-tuple-element.91.refs_2_, f32[4,384,256]{2,1,0:T(8,128)S(1)} %get-tuple-element.92.refs_3_), custom_call_target="tpu_custom_call" | custom-call | bytes 3247104 | tf_op jit(solution)/shard_map/finish/pallas_call | solution.py:73
  (38 shorter events, 0.1 us)
Async XLA Ops:
  0.0 6.9 %copy-start.13 = (bf16[1,1,6,1536]{3,2,1,0:T(8,128)(2,1)S(1)}, bf16[1,1,6,1536]{3,2,1,0:T(8,128)(2,1)}, u32[]{:S(2)}) copy-start(bf16[1,1,6,1536]{3,2,1,0:T(8,128)(2,1)} %param.12) | copy-start | bytes 55300
  1.0 11.5 %copy-start.9 = (bf16[384,256]{1,0:T(8,128)(2,1)}, bf16[384,256]{1,0:T(8,128)(2,1)S(1)}, u32[]{:S(2)}) copy-start(bf16[384,256]{1,0:T(8,128)(2,1)S(1)} %load_edge.2.refs_1_.refs_2_.refs_6_) | copy-start | bytes 589828
  1.0 13.0 %collective-permute-start = (bf16[384,256]{1,0:T(8,128)(2,1)S(1)}, bf16[384,256]{1,0:T(8,128)(2,1)S(1)}, u32[]{:S(2)}, u32[]{:S(2)}) collective-permute-start(bf16[384,256]{1,0:T(8,128)(2,1)S(1)} %load_edge.2.refs_1_.refs_2_.refs_6_), channel_id=1, source_target_pairs={{0,1},{1,0},{2,3},{3,2},{4,8},{5,9},{6,10},{7,11},{8,4},{9,5},{10,... | collective-permute-start | bytes 589832 | tf_op jit(solution)/shard_map/ppermute | solution.py:355
  2.8 9.8 %copy-start.12 = (bf16[384,256]{1,0:T(8,128)(2,1)}, bf16[384,256]{1,0:T(8,128)(2,1)S(1)}, u32[]{:S(2)}) copy-start(bf16[384,256]{1,0:T(8,128)(2,1)S(1)} %get-tuple-element.49.refs_2_.refs_3_.refs_7_) | copy-start | bytes 589828
  2.8 12.2 %collective-permute-start.2 = (bf16[384,256]{1,0:T(8,128)(2,1)S(1)}, bf16[384,256]{1,0:T(8,128)(2,1)S(1)}, u32[]{:S(2)}, u32[]{:S(2)}) collective-permute-start(bf16[384,256]{1,0:T(8,128)(2,1)S(1)} %get-tuple-element.49.refs_2_.refs_3_.refs_7_), channel_id=1, source_target_pairs={{0,4},{1,5},{2,6},{3,7},{4,0},{5,1},{6,2},{7,3},{8,12},{9,13},{10,... | collective-permute-start | bytes 589832 | tf_op jit(solution)/shard_map/ppermute | solution.py:355
  7.8 13.1 %all-to-all-start = ((bf16[32,8,256]{2,1,0:T(8,128)(2,1)}), bf16[32,8,256]{2,1,0:T(8,128)(2,1)S(1)}, u32[]{:S(2)}, u32[]{:S(2)}) async-start(bf16[32,8,256]{2,1,0:T(8,128)(2,1)} %coarse_rhs.1.refs_4_), calls=%async_computation | async-start | bytes 262144 | tf_op jit(solution)/shard_map/all_to_all | solution.py:359
  13.9 4.8 %copy-start.15 = (bf16[192,192]{1,0:T(8,128)(2,1)S(1)}, bf16[192,192]{1,0:T(8,128)(2,1)}, u32[]{:S(2)}) copy-start(bf16[192,192]{1,0:T(8,128)(2,1)} %refs_1_.1) | copy-start | bytes 221188
  14.6 10.9 %collective-permute-start.1 = (bf16[384,256]{1,0:T(8,128)(2,1)S(1)}, bf16[384,256]{1,0:T(8,128)(2,1)S(1)}, u32[]{:S(2)}, u32[]{:S(2)}) collective-permute-start(bf16[384,256]{1,0:T(8,128)(2,1)S(1)} %get-tuple-element.54.refs_4_), channel_id=1, source_target_pairs={{0,1},{1,0},{2,3},{3,2},{4,8},{5,9},{6,10},{7,11},{8,4},{9,5},{10,... | collective-permute-start | bytes 589832 | tf_op jit(solution)/shard_map/ppermute | solution.py:355
  15.7 10.6 %collective-permute-start.4 = (bf16[384,256]{1,0:T(8,128)(2,1)S(1)}, bf16[384,256]{1,0:T(8,128)(2,1)S(1)}, u32[]{:S(2)}, u32[]{:S(2)}) collective-permute-start(bf16[384,256]{1,0:T(8,128)(2,1)S(1)} %get-tuple-element.58.refs_2_), channel_id=1, source_target_pairs={{0,4},{1,5},{2,6},{3,7},{4,0},{5,1},{6,2},{7,3},{8,12},{9,13},{10,... | collective-permute-start | bytes 589832 | tf_op jit(solution)/shard_map/ppermute | solution.py:355
  20.8 0.7 copy-start.16
  21.5 4.1 %copy-start = (bf16[4,1,384,384]{3,2,1,0:T(8,128)(2,1)S(1)}, bf16[4,1,384,384]{3,2,1,0:T(8,128)(2,1)}, u32[]{:S(2)}) copy-start(bf16[4,1,384,384]{3,2,1,0:T(8,128)(2,1)} %param.9) | copy-start | bytes 3538948
  25.6 3.3 %copy-start.1 = (bf16[4,1,384,256]{3,2,1,0:T(8,128)(2,1)S(1)}, bf16[4,1,384,256]{3,2,1,0:T(8,128)(2,1)}, u32[]{:S(2)}) copy-start(bf16[4,1,384,256]{3,2,1,0:T(8,128)(2,1)} %param.7) | copy-start | bytes 2359300
  25.7 3.2 %copy-start.4 = (bf16[4,1,384,384]{3,2,1,0:T(8,128)(2,1)S(1)}, bf16[4,1,384,384]{3,2,1,0:T(8,128)(2,1)}, u32[]{:S(2)}) copy-start(bf16[4,1,384,384]{3,2,1,0:T(8,128)(2,1)} %param.8) | copy-start | bytes 3538948
  25.7 4.6 %collective-permute-start.3 = (bf16[384,256]{1,0:T(8,128)(2,1)S(1)}, bf16[384,256]{1,0:T(8,128)(2,1)S(1)}, u32[]{:S(2)}, u32[]{:S(2)}) collective-permute-start(bf16[384,256]{1,0:T(8,128)(2,1)S(1)} %get-tuple-element.64.refs_3_), channel_id=1, source_target_pairs={{0,1},{1,0},{2,3},{3,2},{4,8},{5,9},{6,10},{7,11},{8,4},{9,5},{10,... | collective-permute-start | bytes 589832 | tf_op jit(solution)/shard_map/ppermute | solution.py:355
  26.6 9.3 %collective-permute-start.5 = (bf16[384,256]{1,0:T(8,128)(2,1)S(1)}, bf16[384,256]{1,0:T(8,128)(2,1)S(1)}, u32[]{:S(2)}, u32[]{:S(2)}) collective-permute-start(bf16[384,256]{1,0:T(8,128)(2,1)S(1)} %get-tuple-element.68), channel_id=1, source_target_pairs={{0,4},{1,5},{2,6},{3,7},{4,0},{5,1},{6,2},{7,3},{8,12},{9,13},{10,... | collective-permute-start | bytes 589832 | tf_op jit(solution)/shard_map/ppermute | solution.py:355
  30.2 5.7 %copy-start.5 = (bf16[4,384,256]{2,1,0:T(8,128)(2,1)}, bf16[4,384,256]{2,1,0:T(8,128)(2,1)S(1)}, u32[]{:S(2)}) copy-start(bf16[4,384,256]{2,1,0:T(8,128)(2,1)S(1)} %get-tuple-element.79.refs_8_.refs_7_) | copy-start | bytes 2359300
  30.2 5.7 %copy-start.10 = (f32[4,384,256]{2,1,0:T(8,128)}, f32[4,384,256]{2,1,0:T(8,128)S(1)}, u32[]{:S(2)}) copy-start(f32[4,384,256]{2,1,0:T(8,128)S(1)} %get-tuple-element.88.refs_5_) | copy-start | bytes 4718596
  36.0 3.6 %copy-start.2 = (bf16[384,256]{1,0:T(8,128)(2,1)}, bf16[384,256]{1,0:T(8,128)(2,1)S(1)}, u32[]{:S(2)}) copy-start(bf16[384,256]{1,0:T(8,128)(2,1)S(1)} %join_operate.2.refs_3_.refs_0_.refs_2_.refs_6_) | copy-start | bytes 589828
  36.0 3.6 %copy-start.14 = (bf16[1,1,6,1536]{3,2,1,0:T(8,128)(2,1)S(1)}, bf16[1,1,6,1536]{3,2,1,0:T(8,128)(2,1)}, u32[]{:S(2)}) copy-start(bf16[1,1,6,1536]{3,2,1,0:T(8,128)(2,1)} %param.12) | copy-start | bytes 55300
  36.0 10.5 %collective-permute-start.6 = (bf16[384,256]{1,0:T(8,128)(2,1)S(1)}, bf16[384,256]{1,0:T(8,128)(2,1)}, u32[]{:S(2)}, u32[]{:S(2)}) collective-permute-start(bf16[384,256]{1,0:T(8,128)(2,1)S(1)} %join_operate.2.refs_3_.refs_0_.refs_2_.refs_6_), channel_id=1, source_target_pairs={{0,1},{1,0},{2,3},{3,2},{4,8},{5,9},{6,10},{7,11},{8,4},{9,5},{10,... | collective-permute-start | bytes 589832 | tf_op jit(solution)/shard_map/ppermute | solution.py:355
  36.4 4.2 %copy-start.7 = (bf16[384,256]{1,0:T(8,128)(2,1)}, bf16[384,256]{1,0:T(8,128)(2,1)S(1)}, u32[]{:S(2)}) copy-start(bf16[384,256]{1,0:T(8,128)(2,1)S(1)} %join_operate.3.refs_1_.refs_3_.refs_7_) | copy-start | bytes 589828
  36.4 12.5 %collective-permute-start.8 = (bf16[384,256]{1,0:T(8,128)(2,1)S(1)}, bf16[384,256]{1,0:T(8,128)(2,1)}, u32[]{:S(2)}, u32[]{:S(2)}) collective-permute-start(bf16[384,256]{1,0:T(8,128)(2,1)S(1)} %join_operate.3.refs_1_.refs_3_.refs_7_), channel_id=1, source_target_pairs={{0,4},{1,5},{2,6},{3,7},{4,0},{5,1},{6,2},{7,3},{8,12},{9,13},{10,... | collective-permute-start | bytes 589832 | tf_op jit(solution)/shard_map/ppermute | solution.py:355
  40.6 13.4 %all-to-all-start.1 = ((bf16[32,8,384]{2,1,0:T(8,128)(2,1)}), bf16[32,8,384]{2,1,0:T(8,128)(2,1)}, u32[]{:S(2)}, u32[]{:S(2)}) async-start(bf16[32,8,384]{2,1,0:T(8,128)(2,1)} %coarse_rhs_joined.1.refs_4_), calls=%async_computation.1 | async-start | bytes 393216 | tf_op jit(solution)/shard_map/all_to_all | solution.py:359
  48.2 9.8 %collective-permute-start.7 = (bf16[384,256]{1,0:T(8,128)(2,1)S(1)}, bf16[384,256]{1,0:T(8,128)(2,1)}, u32[]{:S(2)}, u32[]{:S(2)}) collective-permute-start(bf16[384,256]{1,0:T(8,128)(2,1)S(1)} %get-tuple-element.73.refs_4_), channel_id=1, source_target_pairs={{0,1},{1,0},{2,3},{3,2},{4,8},{5,9},{6,10},{7,11},{8,4},{9,5},{10,... | collective-permute-start | bytes 589832 | tf_op jit(solution)/shard_map/ppermute | solution.py:355
  51.2 8.9 %collective-permute-start.10 = (bf16[384,256]{1,0:T(8,128)(2,1)}, bf16[384,256]{1,0:T(8,128)(2,1)S(1)}, u32[]{:S(2)}, u32[]{:S(2)}) collective-permute-start(bf16[384,256]{1,0:T(8,128)(2,1)} %get-tuple-element.82), channel_id=1, source_target_pairs={{0,4},{1,5},{2,6},{3,7},{4,0},{5,1},{6,2},{7,3},{8,12},{9,13},{10,... | collective-permute-start | bytes 589832 | tf_op jit(solution)/shard_map/ppermute | solution.py:355
  59.0 3.6 %copy-start.3 = (bf16[384,256]{1,0:T(8,128)(2,1)S(1)}, bf16[384,256]{1,0:T(8,128)(2,1)}, u32[]{:S(2)}) copy-start(bf16[384,256]{1,0:T(8,128)(2,1)} %copy-done.2) | copy-start | bytes 589828
  59.0 3.6 %copy-start.6 = (bf16[4,384,256]{2,1,0:T(8,128)(2,1)S(1)}, bf16[4,384,256]{2,1,0:T(8,128)(2,1)}, u32[]{:S(2)}) copy-start(bf16[4,384,256]{2,1,0:T(8,128)(2,1)} %copy-done.5) | copy-start | bytes 2359300
  59.0 3.6 %copy-start.8 = (bf16[384,256]{1,0:T(8,128)(2,1)S(1)}, bf16[384,256]{1,0:T(8,128)(2,1)}, u32[]{:S(2)}) copy-start(bf16[384,256]{1,0:T(8,128)(2,1)} %copy-done.7) | copy-start | bytes 589828
  59.0 3.6 %copy-start.11 = (f32[4,384,256]{2,1,0:T(8,128)S(1)}, f32[4,384,256]{2,1,0:T(8,128)}, u32[]{:S(2)}) copy-start(f32[4,384,256]{2,1,0:T(8,128)} %copy-done.10) | copy-start | bytes 4718596
  59.0 5.3 %collective-permute-start.9 = (bf16[384,128]{1,0:T(8,128)(2,1)S(1)}, bf16[384,128]{1,0:T(8,128)(2,1)S(1)}, u32[]{:S(2)}, u32[]{:S(2)}) collective-permute-start(bf16[384,128]{1,0:T(8,128)(2,1)S(1)} %get-tuple-element.81.refs_3_), channel_id=1, source_target_pairs={{0,1},{1,0},{2,3},{3,2},{4,8},{5,9},{6,10},{7,11},{8,4},{9,5},{10,... | collective-permute-start | bytes 294920 | tf_op jit(solution)/shard_map/ppermute | solution.py:355
  60.5 5.1 %collective-permute-start.11 = (bf16[384,128]{1,0:T(8,128)(2,1)S(1)}, bf16[384,128]{1,0:T(8,128)(2,1)S(1)}, u32[]{:S(2)}, u32[]{:S(2)}) collective-permute-start(bf16[384,128]{1,0:T(8,128)(2,1)S(1)} %get-tuple-element.83), channel_id=1, source_target_pairs={{0,4},{1,5},{2,6},{3,7},{4,0},{5,1},{6,2},{7,3},{8,12},{9,13},{10,... | collective-permute-start | bytes 294920 | tf_op jit(solution)/shard_map/ppermute | solution.py:355

commit v6 on v5

--- a/solution.py
+++ b/solution.py
@@ -99,11 +99,16 @@
     run_copies(blocks + [(o2, v2), (o1, v1)], sems)
 
 
-def margin_solve(chain):
-    def body(h, e, diag, upper, s, far, sem):
+def margin_solve(chain, fetch):
+    def body(h, e, diag, upper, s, *rest):
         lower = is_lower(chain)
-        out = pltpu.make_async_copy(h, far, sem)
-        out.start()
+        out = None
+        if fetch:
+            run_copies([(h, rest[0])], rest[1])
+            h = rest[0]
+        elif rest:
+            out = pltpu.make_async_copy(h, rest[0], rest[1].at[0])
+            out.start()
 
         @pl.when(lower)
         def _():
@@ -113,9 +118,30 @@
         def _():
             s[...] = (mm(diag[...], h[...]) + mmt(upper[...], e[...])).astype(BF)
 
-        out.wait()
-
-    return body
+        if out is not None:
+            out.wait()
+
+    return body
+
+
+def coarse_values(gathered, factor, compact, ncb):
+    devices, _, width = gathered.shape
+    cols = compact.shape[1]
+    group = math.gcd(devices, 16)
+    target = lax.broadcasted_iota(jnp.int32, (group * ncb, group * PAD), 0)
+    source = lax.broadcasted_iota(jnp.int32, (group * ncb, group * PAD), 1)
+    match = (target // ncb == source // PAD) & (lax.rem(target, ncb) == lax.rem(source, PAD))
+    chosen = jnp.where(match, 1.0, 0.0).astype(BF)
+    for i in range(devices // group):
+        part = gathered[i * group : (i + 1) * group].reshape(group * PAD, width)[:, :cols]
+        compact[i * group * ncb : (i + 1) * group * ncb] = mm(chosen, part).astype(BF)
+    nco = factor.shape[0]
+    own = lax.axis_index("row") * lax.axis_size("col") + lax.axis_index("col")
+    row = lax.broadcasted_iota(jnp.int32, (nco, PAD), 0)
+    at = lax.broadcasted_iota(jnp.int32, (nco, PAD), 1)
+    mine = jnp.where((row == own * ncb + at) & (at < ncb), 1.0, 0.0).astype(BF)
+    v = mm(factor[...], compact[...]).astype(BF)
+    return mmt(mm(factor[...], mine).astype(BF), v).astype(BF)
 
 
 def solve_layers(*refs):
@@ -327,7 +353,7 @@
         out[k] = full
 
 
-def finish(parts, scalars, z, q, x):
+def finish(parts, scalars, z, q, x, held, sems):
     total = parts[0]
     for k in range(1, parts.shape[0]):
         total = total + parts[k]
@@ -340,7 +366,10 @@
     cz = a0 + a1 * grow
     cq = a1 * a0
     for k in range(4):
-        x[k] = cz * z[k] - cq * q[k]
+        held[k] = cz * z[k] - cq * q[k]
+        pltpu.make_async_copy(held.at[k], x.at[k], sems.at[k]).start()
+    for k in range(4):
+        pltpu.make_async_copy(held.at[k], x.at[k], sems.at[k]).wait()
 
 
 def swap(chain, x):
@@ -371,18 +400,21 @@
     r, sd, su, ld, lu = rhs[:, 0], stiff_diag[:, 0], stiff_upper[:, 0], local_diag[:, 0], local_upper[:, 0]
     raw_basis = coarse_basis[0, 0]
 
-    def margins(h2, h1, o2, o1, g):
+    def margins(h2, h1, o2, o1, g, mode, order=()):
         g = pltpu.with_memory_space_constraint(g, pltpu.HBM)
         shapes = [((size, size), BF)] * 4 + [(layer, BF)] * 2
         d2, u2, d1, u1, v2, v1 = call(
             load_outer, shapes, (ld, lu, o2, o1), "load_outer", SCHEDULE_COST * block, [g], [dma(6)], range(4)
         )
+        outs = [(layer, BF)] * (2 if mode == "keep" else 1)
+        held = {"keep": [dma(1)], "fetch": [pltpu.VMEM(layer, BF), dma(1)], "plain": []}[mode]
+        hbm, far = (0,) if mode == "fetch" else (), (1,) if mode == "keep" else ()
         take = lambda chain, args, after: call(
-            margin_solve(chain), [(layer, BF)] * 2, args, "margin_solve", 2 * block, after, [pltpu.SemaphoreType.DMA], (), (1,)
+            margin_solve(chain, mode == "fetch"), outs, args, "margin_solve", 2 * block, after, held, hbm, far
         )
-        s2, h2 = take(2, (h2, v2, d2, u2), [])
-        s1, h1 = take(1, (h1, v1, d1, u1), [s2])
-        return swap(2, s2), swap(1, s1), h2, h1, s1
+        s2, *k2 = take(2, (h2, v2, d2, u2), order)
+        s1, *k1 = take(1, (h1, v1, d1, u1), [s2])
+        return swap(2, s2), swap(1, s1), (k2 or [h2])[0], (k1 or [h1])[0], s1
 
     def solve(h2, h1, o2, o1, e, gathered, scalars):
         args = (gathered, fpad, fown, basis, h2, h1, o2, o1, e, ld, lu)
@@ -397,7 +429,7 @@
     held = [pltpu.VMEM(*copies), dma(1)]
     (g,) = call(coarse_rhs(ncb), [copies], (near_r, raw_basis), "coarse_rhs", block // 32, [s1], held, (), (0,))
     gathered = gather(g)
-    m2, m1, h2, h1, last = margins(h2, h1, s2, s1, g)
+    m2, m1, h2, h1, last = margins(h2, h1, s2, s1, g, "keep")
     shapes = [((PAD, layers * size), BF), ((nco, devices * PAD), BF), ((nco, PAD), BF)]
     held = [pltpu.VMEM(*shape) for shape in shapes] + [dma(3)]
     basis, fpad, fown = call(
@@ -417,7 +449,7 @@
     args = (o2, o1, z2, z1, wi, sums, raw_basis)
     (g,) = call(coarse_rhs_joined(ncb), [wider], args, "coarse_rhs_joined", block // 32, [], held, (), (0,))
     early = gather(g)
-    m2, m1, h2, h1, _ = margins(h2, h1, o2, o1, g)
+    m2, m1, h2, h1, _ = margins(h2, h1, o2, o1, g, "fetch")
     p, scalars = solve(h2, h1, o2, o1, w, early, 1)
     half = [(layer, F32), ((size, cols // 2), BF), (layer, F32)]
     q2, s2, c2 = call(join_second(2), half, (m2, p, su), "join_second", block)
@@ -431,7 +463,7 @@
         12 * block,
     )
     (g,) = call(join_sums, [((devices, 2, cols + cols // 2), F32)], (t2, t1, c2, c1, sums), "join_sums")
-    (x,) = call(finish, [(whole, F32)], (gather(g), scalars, z, q), "finish")
+    (x,) = call(finish, [(whole, F32)], (gather(g), scalars, z, q), "finish", 0, (), [pltpu.VMEM(whole, F32), dma(4)], (), (0,))
     return x[:, None]
 
 

time: 80 us -> 79.6 us (level)
  transfers between devices with their start and end apart: 14 -> 14, of which waited for: 6 -> 7; matrix products, arithmetic and copies ran while one was open for 0% -> 0% of each run, Pallas kernels for 32% -> 32%
where the time goes in v6:
time: 79.6 us; the launch traced here: 79.2 us
  starting transfers between devices  28.9 us (36%)
  Pallas kernels  27.5 us (35%)
  blocking collectives  12.1 us (15%)
  waiting for transfers between devices  9.67 us (12%)
    pallas_call x23, Pallas kernels, call(): pl.pallas_call(kernel, out_shape=shapes, in_specs=[space(i, hbm) for i in...  27.5 us
    ppermute x12, starting transfers between devices, swap(): return lax.ppermute(x, ALL, moves)  19.7 us
    all_to_all x1, blocking collectives, gather(): return lax.all_to_all(copies, ALL, 0, 0)  12.1 us
    all_to_all x2, starting transfers between devices, gather(): return lax.all_to_all(copies, ALL, 0, 0)  9.2 us
    ppermute x12, waiting for transfers between devices, swap(): return lax.ppermute(x, ALL, moves)  8.52 us
  transfers between devices with their start and end apart: 14, of which 7 were waited for; matrix products, arithmetic and copies ran while one was open for 0% of the time, Pallas kernels for 32%

profile of v6, /device:TPU:0, one launch (start us, length us, event | category | flops | bytes accessed | tf_op | source)
XLA Modules:
  0.0 79.2 jit_solution(18418425872480478384)
XLA Ops:
  0.0 0.9 %load_edge.2.refs_1_.refs_2_.refs_6_ = bf16[384,256]{1,0:T(8,128)(2,1)S(1)} custom-call(bf16[4,384,256]{2,1,0:T(8,128)(2,1)} %bitcast.17), custom_call_target="tpu_custom_call" | custom-call | bytes 786432 | tf_op jit(solution)/shard_map/load_edge/pallas_call | solution.py:73
  1.0 0.0 copy-start.9
  1.0 0.5 collective-permute-start
  1.5 1.3 %load_edge.3 = (bf16[384,256]{1,0:T(8,128)(2,1)S(1)}, bf16[4,384,256]{2,1,0:T(8,128)(2,1)S(1)}) custom-call(bf16[4,384,256]{2,1,0:T(8,128)(2,1)} %bitcast.18, bf16[384,256]{1,0:T(8,128)(2,1)S(1)} %load_edge.2.refs_1_.refs_2_.refs_6_), custom_call_target="tpu_custom_call" | custom-call | bytes 786432 | tf_op jit(solution)/shard_map/load_edge/pallas_call | solution.py:73
  2.8 4.1 %collective-permute-start.2 = (bf16[384,256]{1,0:T(8,128)(2,1)S(1)}, bf16[384,256]{1,0:T(8,128)(2,1)S(1)}, u32[]{:S(2)}, u32[]{:S(2)}) collective-permute-start(bf16[384,256]{1,0:T(8,128)(2,1)S(1)} %get-tuple-element.45.refs_2_.refs_3_.refs_7_), channel_id=1, source_target_pairs={{0,4},{1,5},{2,6},{3,7},{4,0},{5,1},{6,2},{7,3},{8,12},{9,13},{10,... | collective-permute-start | bytes 589832 | tf_op jit(solution)/shard_map/ppermute | solution.py:384
  6.9 0.9 %coarse_rhs.1.refs_4_ = bf16[32,8,256]{2,1,0:T(8,128)(2,1)} custom-call(bf16[4,384,256]{2,1,0:T(8,128)(2,1)S(1)} %get-tuple-element.46.refs_0_, bf16[6,1536]{1,0:T(8,128)(2,1)S(1)} %bitcast.24, bf16[384,256]{1,0:T(8,128)(2,1)S(1)} %get-tuple-element.45.refs_2_.refs_3_.refs_7_), custom_call_target="tpu_custom_call" | custom-call | flops 2359296 | bytes 804864 | tf_op jit(solution)/shard_map/coarse_rhs/pallas_call | solution.py:73
  7.8 4.7 %all-to-all-start = ((bf16[32,8,256]{2,1,0:T(8,128)(2,1)}), bf16[32,8,256]{2,1,0:T(8,128)(2,1)S(1)}, u32[]{:S(2)}, u32[]{:S(2)}) async-start(bf16[32,8,256]{2,1,0:T(8,128)(2,1)} %coarse_rhs.1.refs_4_), calls=%async_computation | async-start | bytes 262144 | tf_op jit(solution)/shard_map/all_to_all | solution.py:388
  12.5 1.4 %load_outer.2 = (bf16[384,384]{1,0:T(8,128)(2,1)S(1)}, bf16[384,384]{1,0:T(8,128)(2,1)S(1)}, bf16[384,384]{1,0:T(8,128)(2,1)S(1)}, bf16[384,384]{1,0:T(8,128)(2,...) custom-call(bf16[6,384,384]{2,1,0:T(8,128)(2,1)} %bitcast.27, bf16[5,384,384]{2,1,0:T(8,128)(2,1)} %bitcast.31, ...), custom_call_target="tpu_custom_call" | custom-call | flops 90596966400 | bytes 3637248 | tf_op jit(solution)/shard_map/load_outer/pallas_call | solution.py:73
  13.9 0.0 copy-start.15
  14.0 0.7 margin_solve.4
  14.7 0.3 collective-permute-start.1
  15.0 0.7 margin_solve.5
  15.7 3.0 %collective-permute-start.4 = (bf16[384,256]{1,0:T(8,128)(2,1)S(1)}, bf16[384,256]{1,0:T(8,128)(2,1)S(1)}, u32[]{:S(2)}, u32[]{:S(2)}) collective-permute-start(bf16[384,256]{1,0:T(8,128)(2,1)S(1)} %get-tuple-element.54.refs_2_), channel_id=1, source_target_pairs={{0,4},{1,5},{2,6},{3,7},{4,0},{5,1},{6,2},{7,3},{8,12},{9,13},{10,... | collective-permute-start | bytes 589832 | tf_op jit(solution)/shard_map/ppermute | solution.py:384
  18.7 1.2 %prepare.1 = (bf16[8,1536]{1,0:T(8,128)(2,1)}, bf16[192,256]{1,0:T(8,128)(2,1)}, bf16[192,8]{1,0:T(8,128)(2,1)}) custom-call(bf16[6,1536]{1,0:T(8,128)(2,1)S(1)} %bitcast.25, bf16[192,192]{1,0:T(8,128)(2,1)S(1)} %copy-done.15, bf16[384,256]{1,0:T(8,128)(2,1)S(1)} %get-tuple-element.54.refs_2_), custom_call_target="tpu_custom_call" | custom-call | flops 9437184 | bytes 92160 | tf_op jit(solution)/shard_map/prepare/pallas_call | solution.py:73
  20.0 0.9 %all-to-all-done.refs_0_ = bf16[32,8,256]{2,1,0:T(8,128)(2,1)S(1)} async-done(((bf16[32,8,256]{2,1,0:T(8,128)(2,1)}), bf16[32,8,256]{2,1,0:T(8,128)(2,1)S(1)}, u32[]{:S(2)}, u32[]{:S(2)}) %all-to-all-start) | async-done | bytes 131104 | tf_op jit(solution)/shard_map/all_to_all | solution.py:388
  20.8 0.7 copy-done.16
  21.5 4.1 %solve_layers.2.refs_1_.refs_2_ = f32[4,384,256]{2,1,0:T(8,128)S(1)} custom-call(bf16[32,8,256]{2,1,0:T(8,128)(2,1)} %copy-done.16, bf16[192,256]{1,0:T(8,128)(2,1)} %get-tuple-element.55.refs_1_, bf16[192,8]{1,0:T(8,128)(2,1)} %get-tuple-element.56.refs_2_, bf16[8,1536]{1,0:T(8,128)(2,1)} %get-tuple-element.57.refs_3_, ...), custom_call_target="tpu_custom_call" | custom-call | flops 905969664 | bytes 5073920 | tf_op jit(solution)/shard_map/solve_layers/pallas_call | solution.py:73
  25.6 0.1 join_margin.2
  25.7 0.0 copy-start.4
  25.7 0.2 collective-permute-start.3
  25.8 0.4 collective-permute-done.4.refs_0_
  26.3 0.4 join_margin.3
  26.7 2.2 %collective-permute-start.5 = (bf16[384,256]{1,0:T(8,128)(2,1)S(1)}, bf16[384,256]{1,0:T(8,128)(2,1)S(1)}, u32[]{:S(2)}, u32[]{:S(2)}) collective-permute-start(bf16[384,256]{1,0:T(8,128)(2,1)S(1)} %get-tuple-element.64), channel_id=1, source_target_pairs={{0,4},{1,5},{2,6},{3,7},{4,0},{5,1},{6,2},{7,3},{8,12},{9,13},{10,... | collective-permute-start | bytes 589832 | tf_op jit(solution)/shard_map/ppermute | solution.py:384
  28.9 1.3 %inner_operate.1 = (f32[4,384,256]{2,1,0:T(8,128)S(1)}, f32[4,384,256]{2,1,0:T(8,128)S(1)}, bf16[4,384,256]{2,1,0:T(8,128)(2,1)S(1)}, f32[2,256]{1,0:T(2,128)S(1)}) custom-call(f32[384,256]{1,0:T(8,128)S(1)} %get-tuple-element.61.refs_0_.refs_2_, f32[384,256]{1,0:T(8,128)S(1)} %get-tuple-element.62.refs_1_.refs_3_, ...), custom_call_target="tpu_custom_call" | custom-call | flops 754974720 | bytes 5505024 | tf_op jit(solution)/shard_map/inner_operate/pallas_call | solution.py:73
  30.3 5.6 %collective-permute-done.5.refs_3_.refs_0_ = bf16[384,256]{1,0:T(8,128)(2,1)S(1)} collective-permute-done((bf16[384,256]{1,0:T(8,128)(2,1)S(1)}, bf16[384,256]{1,0:T(8,128)(2,1)S(1)}, u32[]{:S(2)}, u32[]{:S(2)}) %collective-permute-start.5) | collective-permute-done | bytes 196640 | tf_op jit(solution)/shard_map/ppermute | solution.py:384
  36.0 0.1 collective-permute-start.6
  36.1 0.3 join_operate.3.refs_1_.refs_3_.refs_7_
  36.4 3.2 %collective-permute-start.8 = (bf16[384,256]{1,0:T(8,128)(2,1)S(1)}, bf16[384,256]{1,0:T(8,128)(2,1)}, u32[]{:S(2)}, u32[]{:S(2)}) collective-permute-start(bf16[384,256]{1,0:T(8,128)(2,1)S(1)} %join_operate.3.refs_1_.refs_3_.refs_7_), channel_id=1, source_target_pairs={{0,4},{1,5},{2,6},{3,7},{4,0},{5,1},{6,2},{7,3},{8,12},{9,13},{10,... | collective-permute-start | bytes 589832 | tf_op jit(solution)/shard_map/ppermute | solution.py:384
  39.6 1.0 %coarse_rhs_joined.1.refs_4_ = bf16[32,8,384]{2,1,0:T(8,128)(2,1)} custom-call(bf16[384,256]{1,0:T(8,128)(2,1)S(1)} %join_operate.2.refs_3_.refs_0_.refs_2_.refs_6_, bf16[384,256]{1,0:T(8,128)(2,1)S(1)} %join_operate.3.refs_1_.refs_3_.refs_7_, f32[384,256]{1,0:T(8,128)S(1)} %get-tuple-element.61.refs_0_.refs_2_, ...), custom_call_target="tpu_custom_call" | custom-call | flops 2359296 | bytes 2772992 | tf_op jit(solution)/shard_map/coarse_rhs_joined/pallas_call | solution.py:73
  40.6 4.5 %all-to-all-start.1 = ((bf16[32,8,384]{2,1,0:T(8,128)(2,1)}), bf16[32,8,384]{2,1,0:T(8,128)(2,1)}, u32[]{:S(2)}, u32[]{:S(2)}) async-start(bf16[32,8,384]{2,1,0:T(8,128)(2,1)} %coarse_rhs_joined.1.refs_4_), calls=%async_computation.1 | async-start | bytes 393216 | tf_op jit(solution)/shard_map/all_to_all | solution.py:388
  45.1 1.4 %load_outer.3 = (bf16[384,384]{1,0:T(8,128)(2,1)S(1)}, bf16[384,384]{1,0:T(8,128)(2,1)S(1)}, bf16[384,384]{1,0:T(8,128)(2,1)S(1)}, bf16[384,384]{1,0:T(8,128)(2,...) custom-call(bf16[6,384,384]{2,1,0:T(8,128)(2,1)} %bitcast.29, bf16[5,384,384]{2,1,0:T(8,128)(2,1)} %bitcast.33, ...), custom_call_target="tpu_custom_call" | custom-call | flops 90596966400 | bytes 3637248 | tf_op jit(solution)/shard_map/load_outer/pallas_call | solution.py:73
  46.6 1.3 %margin_solve.6.refs_4_ = bf16[384,256]{1,0:T(8,128)(2,1)S(1)} custom-call(bf16[384,256]{1,0:T(8,128)(2,1)} %collective-permute-done.6.refs_0_.refs_4_, bf16[384,256]{1,0:T(8,128)(2,1)S(1)} %get-tuple-element.66.refs_1_, bf16[384,384]{1,0:T(8,128)(2,1)S(1)} %get-tuple-element.67.refs_2_, bf16[384,384]{1,0:T(8,128)(2,1)S(1)} %get-tuple-element.68.refs_3_), custom_call_target="tpu_custom_call" | custom-call | flops 150994944 | bytes 983040 | tf_op jit(solution)/shard_map/margin_solve/pallas_call | solution.py:73
  47.9 0.3 collective-permute-start.7
  48.1 0.8 %collective-permute-done.8.refs_5_.refs_0_ = bf16[384,256]{1,0:T(8,128)(2,1)} collective-permute-done((bf16[384,256]{1,0:T(8,128)(2,1)S(1)}, bf16[384,256]{1,0:T(8,128)(2,1)}, u32[]{:S(2)}, u32[]{:S(2)}) %collective-permute-start.8) | collective-permute-done | bytes 196640 | tf_op jit(solution)/shard_map/ppermute | solution.py:384
  48.9 2.0 %margin_solve.7 = bf16[384,256]{1,0:T(8,128)(2,1)} custom-call(bf16[384,256]{1,0:T(8,128)(2,1)} %collective-permute-done.8.refs_5_.refs_0_, bf16[384,256]{1,0:T(8,128)(2,1)S(1)} %get-tuple-element.72.refs_1_, bf16[384,384]{1,0:T(8,128)(2,1)S(1)} %get-tuple-element.73.refs_2_, bf16[384,384]{1,0:T(8,128)(2,1)S(1)} %get-tuple-element.74.refs_3_, ...), custom_call_target="tpu_custom_call" | custom-call | flops 150994944 | bytes 983040 | tf_op jit(solution)/shard_map/margin_solve/pallas_call | solution.py:73
  50.9 2.8 %collective-permute-start.10 = (bf16[384,256]{1,0:T(8,128)(2,1)}, bf16[384,256]{1,0:T(8,128)(2,1)S(1)}, u32[]{:S(2)}, u32[]{:S(2)}) collective-permute-start(bf16[384,256]{1,0:T(8,128)(2,1)} %margin_solve.7), channel_id=1, source_target_pairs={{0,4},{1,5},{2,6},{3,7},{4,0},{5,1},{6,2},{7,3},{8,12},{9,13},{10,... | collective-permute-start | bytes 589832 | tf_op jit(solution)/shard_map/ppermute | solution.py:384
  53.7 0.3 all-to-all-done.1.refs_0_
  54.0 4.0 %solve_layers.3 = (f32[4,384,256]{2,1,0:T(8,128)S(1)}, f32[3,256]{1,0:T(4,128)S(1)}) custom-call(bf16[32,8,384]{2,1,0:T(8,128)(2,1)} %all-to-all-done.1.refs_0_, bf16[192,256]{1,0:T(8,128)(2,1)} %get-tuple-element.55.refs_1_, bf16[192,8]{1,0:T(8,128)(2,1)} %get-tuple-element.56.refs_2_, bf16[8,1536]{1,0:T(8,128)(2,1)} %get-tuple-element.57.refs_3_, ...), custom_call_target="tpu_custom_call" | custom-call | flops 905969664 | bytes 5139456 | tf_op jit(solution)/shard_map/solve_layers/pallas_call | solution.py:73
  58.0 1.0 %join_second.2 = (f32[384,256]{1,0:T(8,128)S(1)}, bf16[384,128]{1,0:T(8,128)(2,1)S(1)}, f32[384,256]{1,0:T(8,128)S(1)}) custom-call(bf16[384,256]{1,0:T(8,128)(2,1)} %collective-permute-done.7.refs_0_, f32[4,384,256]{2,1,0:T(8,128)S(1)} %get-tuple-element.70.refs_1_.refs_4_, bf16[4,384,384]{2,1,0:T(8,128)(2,1)S(1)} %bitcast.14), custom_call_target="tpu_custom_call" | custom-call | flops 75497472 | bytes 2949120 | tf_op jit(solution)/shard_map/join_second/pallas_call | solution.py:73
  59.1 0.8 collective-permute-start.9
  59.8 0.2 collective-permute-done.10.refs_0_
  60.1 0.4 join_second.3
  60.4 2.1 %collective-permute-start.11 = (bf16[384,128]{1,0:T(8,128)(2,1)S(1)}, bf16[384,128]{1,0:T(8,128)(2,1)S(1)}, u32[]{:S(2)}, u32[]{:S(2)}) collective-permute-start(bf16[384,128]{1,0:T(8,128)(2,1)S(1)} %get-tuple-element.75), channel_id=1, source_target_pairs={{0,4},{1,5},{2,6},{3,7},{4,0},{5,1},{6,2},{7,3},{8,12},{9,13},{10,... | collective-permute-start | bytes 294920 | tf_op jit(solution)/shard_map/ppermute | solution.py:384
  62.6 1.7 %inner_products.1 = (f32[4,384,256]{2,1,0:T(8,128)S(1)}, f32[4,384,256]{2,1,0:T(8,128)S(1)}, f32[3,256]{1,0:T(4,128)S(1)}) custom-call(f32[384,256]{1,0:T(8,128)S(1)} %get-tuple-element.78.refs_0_, f32[384,256]{1,0:T(8,128)S(1)} %get-tuple-element.79.refs_1_, bf16[384,256]{1,0:T(8,128)(2,1)S(1)} %copy-done.3, bf16[384,256]{1,0:T(8,128)(2,1)S(1)} %copy-done.8, ...), custom_call_target="tpu_custom_call" | custom-call | flops 905969664 | bytes 8260608 | tf_op jit(solution)/shard_map/inner_products/pallas_call | solution.py:73
  64.3 1.4 %collective-permute-done.11.refs_1_ = bf16[384,128]{1,0:T(8,128)(2,1)S(1)} collective-permute-done((bf16[384,128]{1,0:T(8,128)(2,1)S(1)}, bf16[384,128]{1,0:T(8,128)(2,1)S(1)}, u32[]{:S(2)}, u32[]{:S(2)}) %collective-permute-start.11) | collective-permute-done | bytes 98336 | tf_op jit(solution)/shard_map/ppermute | solution.py:384
  65.7 0.2 join_sums.1
  65.9 12.1 %all_to_all.15.refs_0_ = f32[32,2,384]{2,1,0:T(2,128)S(1)} all-to-all(f32[32,2,384]{2,1,0:T(2,128)S(1)} %join_sums.1), channel_id=1, replica_groups=mesh['row'=8,'col'=4] {'row','col'}, dimensions={0} | all-to-all | bytes 196608 | tf_op jit(solution)/shard_map/all_to_all | solution.py:388
  77.9 1.3 %finish.1 = f32[4,384,256]{2,1,0:T(8,128)} custom-call(f32[32,2,384]{2,1,0:T(2,128)S(1)} %all_to_all.15.refs_0_, f32[3,256]{1,0:T(4,128)S(1)} %get-tuple-element.81.refs_10_.refs_1_, f32[4,384,256]{2,1,0:T(8,128)S(1)} %get-tuple-element.83.refs_2_, f32[4,384,256]{2,1,0:T(8,128)S(1)} %get-tuple-element.84.refs_3_), custom_call_target="tpu_custom_call" | custom-call | bytes 3247104 | tf_op jit(solution)/shard_map/finish/pallas_call | solution.py:73
  (38 shorter events, 0.1 us)
Async XLA Ops:
  0.0 6.9 %copy-start.13 = (bf16[1,1,6,1536]{3,2,1,0:T(8,128)(2,1)S(1)}, bf16[1,1,6,1536]{3,2,1,0:T(8,128)(2,1)}, u32[]{:S(2)}) copy-start(bf16[1,1,6,1536]{3,2,1,0:T(8,128)(2,1)} %param.12) | copy-start | bytes 55300
  1.0 11.5 %copy-start.9 = (bf16[384,256]{1,0:T(8,128)(2,1)}, bf16[384,256]{1,0:T(8,128)(2,1)S(1)}, u32[]{:S(2)}) copy-start(bf16[384,256]{1,0:T(8,128)(2,1)S(1)} %load_edge.2.refs_1_.refs_2_.refs_6_) | copy-start | bytes 589828
  1.0 13.0 %collective-permute-start = (bf16[384,256]{1,0:T(8,128)(2,1)S(1)}, bf16[384,256]{1,0:T(8,128)(2,1)S(1)}, u32[]{:S(2)}, u32[]{:S(2)}) collective-permute-start(bf16[384,256]{1,0:T(8,128)(2,1)S(1)} %load_edge.2.refs_1_.refs_2_.refs_6_), channel_id=1, source_target_pairs={{0,1},{1,0},{2,3},{3,2},{4,8},{5,9},{6,10},{7,11},{8,4},{9,5},{10,... | collective-permute-start | bytes 589832 | tf_op jit(solution)/shard_map/ppermute | solution.py:384
  2.8 9.8 %copy-start.12 = (bf16[384,256]{1,0:T(8,128)(2,1)}, bf16[384,256]{1,0:T(8,128)(2,1)S(1)}, u32[]{:S(2)}) copy-start(bf16[384,256]{1,0:T(8,128)(2,1)S(1)} %get-tuple-element.45.refs_2_.refs_3_.refs_7_) | copy-start | bytes 589828
  2.8 12.2 %collective-permute-start.2 = (bf16[384,256]{1,0:T(8,128)(2,1)S(1)}, bf16[384,256]{1,0:T(8,128)(2,1)S(1)}, u32[]{:S(2)}, u32[]{:S(2)}) collective-permute-start(bf16[384,256]{1,0:T(8,128)(2,1)S(1)} %get-tuple-element.45.refs_2_.refs_3_.refs_7_), channel_id=1, source_target_pairs={{0,4},{1,5},{2,6},{3,7},{4,0},{5,1},{6,2},{7,3},{8,12},{9,13},{10,... | collective-permute-start | bytes 589832 | tf_op jit(solution)/shard_map/ppermute | solution.py:384
  7.8 13.1 %all-to-all-start = ((bf16[32,8,256]{2,1,0:T(8,128)(2,1)}), bf16[32,8,256]{2,1,0:T(8,128)(2,1)S(1)}, u32[]{:S(2)}, u32[]{:S(2)}) async-start(bf16[32,8,256]{2,1,0:T(8,128)(2,1)} %coarse_rhs.1.refs_4_), calls=%async_computation | async-start | bytes 262144 | tf_op jit(solution)/shard_map/all_to_all | solution.py:388
  13.9 4.8 %copy-start.15 = (bf16[192,192]{1,0:T(8,128)(2,1)S(1)}, bf16[192,192]{1,0:T(8,128)(2,1)}, u32[]{:S(2)}) copy-start(bf16[192,192]{1,0:T(8,128)(2,1)} %refs_1_.1) | copy-start | bytes 221188
  14.7 10.9 %collective-permute-start.1 = (bf16[384,256]{1,0:T(8,128)(2,1)S(1)}, bf16[384,256]{1,0:T(8,128)(2,1)S(1)}, u32[]{:S(2)}, u32[]{:S(2)}) collective-permute-start(bf16[384,256]{1,0:T(8,128)(2,1)S(1)} %get-tuple-element.50.refs_4_), channel_id=1, source_target_pairs={{0,1},{1,0},{2,3},{3,2},{4,8},{5,9},{6,10},{7,11},{8,4},{9,5},{10,... | collective-permute-start | bytes 589832 | tf_op jit(solution)/shard_map/ppermute | solution.py:384
  15.7 10.6 %collective-permute-start.4 = (bf16[384,256]{1,0:T(8,128)(2,1)S(1)}, bf16[384,256]{1,0:T(8,128)(2,1)S(1)}, u32[]{:S(2)}, u32[]{:S(2)}) collective-permute-start(bf16[384,256]{1,0:T(8,128)(2,1)S(1)} %get-tuple-element.54.refs_2_), channel_id=1, source_target_pairs={{0,4},{1,5},{2,6},{3,7},{4,0},{5,1},{6,2},{7,3},{8,12},{9,13},{10,... | collective-permute-start | bytes 589832 | tf_op jit(solution)/shard_map/ppermute | solution.py:384
  20.8 0.7 copy-start.16
  21.5 4.1 %copy-start = (bf16[4,1,384,384]{3,2,1,0:T(8,128)(2,1)S(1)}, bf16[4,1,384,384]{3,2,1,0:T(8,128)(2,1)}, u32[]{:S(2)}) copy-start(bf16[4,1,384,384]{3,2,1,0:T(8,128)(2,1)} %param.9) | copy-start | bytes 3538948
  25.6 3.3 %copy-start.1 = (bf16[4,1,384,256]{3,2,1,0:T(8,128)(2,1)S(1)}, bf16[4,1,384,256]{3,2,1,0:T(8,128)(2,1)}, u32[]{:S(2)}) copy-start(bf16[4,1,384,256]{3,2,1,0:T(8,128)(2,1)} %param.7) | copy-start | bytes 2359300
  25.7 3.2 %copy-start.4 = (bf16[4,1,384,384]{3,2,1,0:T(8,128)(2,1)S(1)}, bf16[4,1,384,384]{3,2,1,0:T(8,128)(2,1)}, u32[]{:S(2)}) copy-start(bf16[4,1,384,384]{3,2,1,0:T(8,128)(2,1)} %param.8) | copy-start | bytes 3538948
  25.7 4.6 %collective-permute-start.3 = (bf16[384,256]{1,0:T(8,128)(2,1)S(1)}, bf16[384,256]{1,0:T(8,128)(2,1)S(1)}, u32[]{:S(2)}, u32[]{:S(2)}) collective-permute-start(bf16[384,256]{1,0:T(8,128)(2,1)S(1)} %get-tuple-element.60.refs_3_), channel_id=1, source_target_pairs={{0,1},{1,0},{2,3},{3,2},{4,8},{5,9},{6,10},{7,11},{8,4},{9,5},{10,... | collective-permute-start | bytes 589832 | tf_op jit(solution)/shard_map/ppermute | solution.py:384
  26.7 9.3 %collective-permute-start.5 = (bf16[384,256]{1,0:T(8,128)(2,1)S(1)}, bf16[384,256]{1,0:T(8,128)(2,1)S(1)}, u32[]{:S(2)}, u32[]{:S(2)}) collective-permute-start(bf16[384,256]{1,0:T(8,128)(2,1)S(1)} %get-tuple-element.64), channel_id=1, source_target_pairs={{0,4},{1,5},{2,6},{3,7},{4,0},{5,1},{6,2},{7,3},{8,12},{9,13},{10,... | collective-permute-start | bytes 589832 | tf_op jit(solution)/shard_map/ppermute | solution.py:384
  30.2 5.7 %copy-start.5 = (bf16[4,384,256]{2,1,0:T(8,128)(2,1)}, bf16[4,384,256]{2,1,0:T(8,128)(2,1)S(1)}, u32[]{:S(2)}) copy-start(bf16[4,384,256]{2,1,0:T(8,128)(2,1)S(1)} %get-tuple-element.69.refs_8_.refs_7_) | copy-start | bytes 2359300
  30.2 5.7 %copy-start.10 = (f32[4,384,256]{2,1,0:T(8,128)}, f32[4,384,256]{2,1,0:T(8,128)S(1)}, u32[]{:S(2)}) copy-start(f32[4,384,256]{2,1,0:T(8,128)S(1)} %get-tuple-element.80.refs_5_) | copy-start | bytes 4718596
  36.0 3.6 %copy-start.2 = (bf16[384,256]{1,0:T(8,128)(2,1)}, bf16[384,256]{1,0:T(8,128)(2,1)S(1)}, u32[]{:S(2)}) copy-start(bf16[384,256]{1,0:T(8,128)(2,1)S(1)} %join_operate.2.refs_3_.refs_0_.refs_2_.refs_6_) | copy-start | bytes 589828
  36.0 3.6 %copy-start.14 = (bf16[1,1,6,1536]{3,2,1,0:T(8,128)(2,1)S(1)}, bf16[1,1,6,1536]{3,2,1,0:T(8,128)(2,1)}, u32[]{:S(2)}) copy-start(bf16[1,1,6,1536]{3,2,1,0:T(8,128)(2,1)} %param.12) | copy-start | bytes 55300
  36.0 10.5 %collective-permute-start.6 = (bf16[384,256]{1,0:T(8,128)(2,1)S(1)}, bf16[384,256]{1,0:T(8,128)(2,1)}, u32[]{:S(2)}, u32[]{:S(2)}) collective-permute-start(bf16[384,256]{1,0:T(8,128)(2,1)S(1)} %join_operate.2.refs_3_.refs_0_.refs_2_.refs_6_), channel_id=1, source_target_pairs={{0,1},{1,0},{2,3},{3,2},{4,8},{5,9},{6,10},{7,11},{8,4},{9,5},{10,... | collective-permute-start | bytes 589832 | tf_op jit(solution)/shard_map/ppermute | solution.py:384
  36.4 4.3 %copy-start.7 = (bf16[384,256]{1,0:T(8,128)(2,1)}, bf16[384,256]{1,0:T(8,128)(2,1)S(1)}, u32[]{:S(2)}) copy-start(bf16[384,256]{1,0:T(8,128)(2,1)S(1)} %join_operate.3.refs_1_.refs_3_.refs_7_) | copy-start | bytes 589828
  36.4 12.5 %collective-permute-start.8 = (bf16[384,256]{1,0:T(8,128)(2,1)S(1)}, bf16[384,256]{1,0:T(8,128)(2,1)}, u32[]{:S(2)}, u32[]{:S(2)}) collective-permute-start(bf16[384,256]{1,0:T(8,128)(2,1)S(1)} %join_operate.3.refs_1_.refs_3_.refs_7_), channel_id=1, source_target_pairs={{0,4},{1,5},{2,6},{3,7},{4,0},{5,1},{6,2},{7,3},{8,12},{9,13},{10,... | collective-permute-start | bytes 589832 | tf_op jit(solution)/shard_map/ppermute | solution.py:384
  40.6 13.4 %all-to-all-start.1 = ((bf16[32,8,384]{2,1,0:T(8,128)(2,1)}), bf16[32,8,384]{2,1,0:T(8,128)(2,1)}, u32[]{:S(2)}, u32[]{:S(2)}) async-start(bf16[32,8,384]{2,1,0:T(8,128)(2,1)} %coarse_rhs_joined.1.refs_4_), calls=%async_computation.1 | async-start | bytes 393216 | tf_op jit(solution)/shard_map/all_to_all | solution.py:388
  47.9 10.1 %collective-permute-start.7 = (bf16[384,256]{1,0:T(8,128)(2,1)S(1)}, bf16[384,256]{1,0:T(8,128)(2,1)}, u32[]{:S(2)}, u32[]{:S(2)}) collective-permute-start(bf16[384,256]{1,0:T(8,128)(2,1)S(1)} %margin_solve.6.refs_4_), channel_id=1, source_target_pairs={{0,1},{1,0},{2,3},{3,2},{4,8},{5,9},{6,10},{7,11},{8,4},{9,5},{10,... | collective-permute-start | bytes 589832 | tf_op jit(solution)/shard_map/ppermute | solution.py:384
  50.9 9.1 %collective-permute-start.10 = (bf16[384,256]{1,0:T(8,128)(2,1)}, bf16[384,256]{1,0:T(8,128)(2,1)S(1)}, u32[]{:S(2)}, u32[]{:S(2)}) collective-permute-start(bf16[384,256]{1,0:T(8,128)(2,1)} %margin_solve.7), channel_id=1, source_target_pairs={{0,4},{1,5},{2,6},{3,7},{4,0},{5,1},{6,2},{7,3},{8,12},{9,13},{10,... | collective-permute-start | bytes 589832 | tf_op jit(solution)/shard_map/ppermute | solution.py:384
  59.0 3.6 %copy-start.3 = (bf16[384,256]{1,0:T(8,128)(2,1)S(1)}, bf16[384,256]{1,0:T(8,128)(2,1)}, u32[]{:S(2)}) copy-start(bf16[384,256]{1,0:T(8,128)(2,1)} %copy-done.2) | copy-start | bytes 589828
  59.0 3.6 %copy-start.6 = (bf16[4,384,256]{2,1,0:T(8,128)(2,1)S(1)}, bf16[4,384,256]{2,1,0:T(8,128)(2,1)}, u32[]{:S(2)}) copy-start(bf16[4,384,256]{2,1,0:T(8,128)(2,1)} %copy-done.5) | copy-start | bytes 2359300
  59.0 3.6 %copy-start.8 = (bf16[384,256]{1,0:T(8,128)(2,1)S(1)}, bf16[384,256]{1,0:T(8,128)(2,1)}, u32[]{:S(2)}) copy-start(bf16[384,256]{1,0:T(8,128)(2,1)} %copy-done.7) | copy-start | bytes 589828
  59.0 3.6 %copy-start.11 = (f32[4,384,256]{2,1,0:T(8,128)S(1)}, f32[4,384,256]{2,1,0:T(8,128)}, u32[]{:S(2)}) copy-start(f32[4,384,256]{2,1,0:T(8,128)} %copy-done.10) | copy-start | bytes 4718596
  59.1 5.3 %collective-permute-start.9 = (bf16[384,128]{1,0:T(8,128)(2,1)S(1)}, bf16[384,128]{1,0:T(8,128)(2,1)S(1)}, u32[]{:S(2)}, u32[]{:S(2)}) collective-permute-start(bf16[384,128]{1,0:T(8,128)(2,1)S(1)} %get-tuple-element.71.refs_3_), channel_id=1, source_target_pairs={{0,1},{1,0},{2,3},{3,2},{4,8},{5,9},{6,10},{7,11},{8,4},{9,5},{10,... | collective-permute-start | bytes 294920 | tf_op jit(solution)/shard_map/ppermute | solution.py:384
  60.4 5.2 %collective-permute-start.11 = (bf16[384,128]{1,0:T(8,128)(2,1)S(1)}, bf16[384,128]{1,0:T(8,128)(2,1)S(1)}, u32[]{:S(2)}, u32[]{:S(2)}) collective-permute-start(bf16[384,128]{1,0:T(8,128)(2,1)S(1)} %get-tuple-element.75), channel_id=1, source_target_pairs={{0,4},{1,5},{2,6},{3,7},{4,0},{5,1},{6,2},{7,3},{8,12},{9,13},{10,... | collective-permute-start | bytes 294920 | tf_op jit(solution)/shard_map/ppermute | solution.py:384

commit v7 on v6

--- a/solution.py
+++ b/solution.py
@@ -124,26 +124,6 @@
     return body
 
 
-def coarse_values(gathered, factor, compact, ncb):
-    devices, _, width = gathered.shape
-    cols = compact.shape[1]
-    group = math.gcd(devices, 16)
-    target = lax.broadcasted_iota(jnp.int32, (group * ncb, group * PAD), 0)
-    source = lax.broadcasted_iota(jnp.int32, (group * ncb, group * PAD), 1)
-    match = (target // ncb == source // PAD) & (lax.rem(target, ncb) == lax.rem(source, PAD))
-    chosen = jnp.where(match, 1.0, 0.0).astype(BF)
-    for i in range(devices // group):
-        part = gathered[i * group : (i + 1) * group].reshape(group * PAD, width)[:, :cols]
-        compact[i * group * ncb : (i + 1) * group * ncb] = mm(chosen, part).astype(BF)
-    nco = factor.shape[0]
-    own = lax.axis_index("row") * lax.axis_size("col") + lax.axis_index("col")
-    row = lax.broadcasted_iota(jnp.int32, (nco, PAD), 0)
-    at = lax.broadcasted_iota(jnp.int32, (nco, PAD), 1)
-    mine = jnp.where((row == own * ncb + at) & (at < ncb), 1.0, 0.0).astype(BF)
-    v = mm(factor[...], compact[...]).astype(BF)
-    return mmt(mm(factor[...], mine).astype(BF), v).astype(BF)
-
-
 def solve_layers(*refs):
     far, p, scalars, near, sems = refs[:11], refs[11], refs[12:-12], refs[-12:-1], refs[-1]
     copies = [pltpu.make_async_copy(a, b, sems.at[i]) for i, (a, b) in enumerate(zip(far, near))]
@@ -152,7 +132,7 @@
     gathered, fpad, fown, basis, h2, h1, o2, o1, e, ld, lu = near
     for c in copies[:4]:
         c.wait()
-    g = gathered[...].reshape(-1, gathered.shape[-1])[:, : p.shape[2]]
+    g = gathered[:, : p.shape[2]]
     v = mm(fpad[...], g).astype(BF)
     u = mmt(fown[...], v).astype(BF)
     size = p.shape[1]
@@ -170,9 +150,7 @@
     p[2] = p[2] + mm(lu[3], e4) + mmt(lu[2], e2)
     p[3] = p[3] + mm(lu[4], e5) + mmt(lu[3], e3)
     for out in scalars:
-        total = gathered[0].astype(F32)
-        for k in range(1, gathered.shape[0]):
-            total = total + gathered[k].astype(F32)
+        total = jnp.sum(gathered[...].astype(F32).reshape(-1, PAD, gathered.shape[1]), axis=0)
         beside = total[:, p.shape[2] :]
         rho, d0 = (
             jnp.concatenate([beside[k : k + 1] + beside[k + 2 : k + 3], beside[k + 1 : k + 2] + beside[k + 3 : k + 4]], axis=1)
@@ -230,12 +208,18 @@
     return body
 
 
+def fill(block, out):
+    twice = jnp.concatenate([out, out], axis=0).astype(BF)
+    rows = twice.shape[0]
+    for k in range(block.shape[0] // rows):
+        block[k * rows : (k + 1) * rows] = twice
+
+
 def coarse_rhs(ncb):
     def body(e, basis, g, block, sems):
         out = mm(basis[...], e[...].reshape(-1, e.shape[-1]))
-        out = jnp.concatenate([out, jnp.zeros((PAD - ncb, out.shape[1]), F32)], axis=0).astype(BF)
-        for k in range(g.shape[0]):
-            block[k] = out
+        out = jnp.concatenate([out, jnp.zeros((PAD - ncb, out.shape[1]), F32)], axis=0)
+        fill(block, out)
         run_copies([(block, g)], sems)
 
     return body
@@ -244,23 +228,23 @@
 def prepare(ncb):
     def body(basis, factor, padded_far, fpad_far, fown_far, padded, fpad, fown, sems):
         rows = basis[...].astype(F32)
-        padded[...] = jnp.concatenate([rows, jnp.zeros((PAD - ncb, rows.shape[1]), F32)], axis=0).astype(BF)
+        padded[...] = jnp.concatenate([rows, jnp.zeros((2 * PAD - ncb, rows.shape[1]), F32)], axis=0).astype(BF)
         nco = factor.shape[0]
         own = lax.axis_index("row") * lax.axis_size("col") + lax.axis_index("col")
 
-        def columns(first, width):
+        def columns(first, width, limit):
             source = lax.broadcasted_iota(jnp.int32, (nco, width), 0)
             target = lax.broadcasted_iota(jnp.int32, (nco, width), 1)
             at = lax.rem(target, PAD)
-            match = (source == (first + target // PAD) * ncb + at) & (at < ncb)
+            match = (source == (first + target // PAD) * ncb + at) & (at < ncb) & (target < limit)
             chosen = jnp.where(match, 1.0, 0.0).astype(BF)
             return mm(factor[...], chosen).astype(BF)
 
-        fown[...] = columns(own, PAD)
+        fown[...] = columns(own, 2 * PAD, ncb)
         width = 128
 
         def step(i, carry):
-            fpad[:, pl.ds(pl.multiple_of(i * width, width), width)] = columns(i * (width // PAD), width)
+            fpad[:, pl.ds(pl.multiple_of(i * width, width), width)] = columns(i * (width // PAD), width, width)
             return carry
 
         lax.fori_loop(0, fpad.shape[1] // width, step, 0)
@@ -288,9 +272,8 @@
             d0 = d0 + colsum(x.astype(F32) * y)
         out = jnp.concatenate([out, jnp.zeros((PAD - ncb, out.shape[1]), F32)], axis=0)
         beside = jnp.concatenate(in_two(sums[0:1]) + in_two(d0), axis=0)
-        out = jnp.concatenate([out, beside], axis=1).astype(BF)
-        for k in range(g.shape[0]):
-            block[k] = out
+        out = jnp.concatenate([out, beside], axis=1)
+        fill(block, out)
         run_copies([(block, g)], sems)
 
     return body
@@ -388,12 +371,17 @@
     return lax.all_to_all(copies, ALL, 0, 0)
 
 
+def gather_rows(copies):
+    rows, width = copies.shape
+    return gather(copies.reshape(rows // PAD, PAD, width)).reshape(rows, width)
+
+
 def on_device(rhs, stiff_diag, stiff_upper, local_diag, local_upper, coarse_basis, coarse_factor):
     layers, _, size, cols = rhs.shape
     devices = lax.axis_size("row") * lax.axis_size("col")
     ncb, nco = coarse_basis.shape[2], coarse_factor.shape[0]
     layer, whole = (size, cols), (layers, size, cols)
-    copies = ((devices, PAD, cols), BF)
+    copies = ((devices * PAD, cols), BF)
     edge = [(layer, F32), (layer, BF)]
     block = 2 * size * size * cols
     dma = lambda n: pltpu.SemaphoreType.DMA((n,))
@@ -428,9 +416,9 @@
     h1 = swap(1, s1)
     held = [pltpu.VMEM(*copies), dma(1)]
     (g,) = call(coarse_rhs(ncb), [copies], (near_r, raw_basis), "coarse_rhs", block // 32, [s1], held, (), (0,))
-    gathered = gather(g)
+    gathered = gather_rows(g)
     m2, m1, h2, h1, last = margins(h2, h1, s2, s1, g, "keep")
-    shapes = [((PAD, layers * size), BF), ((nco, devices * PAD), BF), ((nco, PAD), BF)]
+    shapes = [((2 * PAD, layers * size), BF), ((nco, devices * PAD), BF), ((nco, 2 * PAD), BF)]
     held = [pltpu.VMEM(*shape) for shape in shapes] + [dma(3)]
     basis, fpad, fown = call(
         prepare(ncb), shapes, (raw_basis, coarse_factor), "prepare", block // 8, [last], held, (), (0, 1, 2)
@@ -444,11 +432,11 @@
     (o2,) = call(join_operate(2), edge[1:], (n2, wi, su), "join_operate", block, [n1])
     (o1,) = call(join_operate(1), edge[1:], (n1, wi, su), "join_operate", block, [o2])
     h2, h1 = swap(2, o2), swap(1, o1)
-    wider = ((devices, PAD, cols + cols // 2), BF)
+    wider = ((devices * PAD, cols + cols // 2), BF)
     held = [pltpu.VMEM(*wider), dma(1)]
     args = (o2, o1, z2, z1, wi, sums, raw_basis)
     (g,) = call(coarse_rhs_joined(ncb), [wider], args, "coarse_rhs_joined", block // 32, [], held, (), (0,))
-    early = gather(g)
+    early = gather_rows(g)
     m2, m1, h2, h1, _ = margins(h2, h1, o2, o1, g, "fetch")
     p, scalars = solve(h2, h1, o2, o1, w, early, 1)
     half = [(layer, F32), ((size, cols // 2), BF), (layer, F32)]

time: 79.6 us -> 79.6 us (level)
  no operation moved by 1% of the time
where the time goes in v7:
time: 79.6 us; the launch traced here: 79.2 us
  starting transfers between devices  28.9 us (36%)
  Pallas kernels  27.4 us (34%)
  blocking collectives  12.1 us (15%)
  waiting for transfers between devices  9.67 us (12%)
    pallas_call x23, Pallas kernels, call(): pl.pallas_call(kernel, out_shape=shapes, in_specs=[space(i, hbm) for i in...  27.4 us
    ppermute x12, starting transfers between devices, swap(): return lax.ppermute(x, ALL, moves)  19.7 us
    all_to_all x1, blocking collectives, gather(): return lax.all_to_all(copies, ALL, 0, 0)  12.1 us
    all_to_all x2, starting transfers between devices, gather(): return lax.all_to_all(copies, ALL, 0, 0)  9.2 us
    ppermute x12, waiting for transfers between devices, swap(): return lax.ppermute(x, ALL, moves)  8.52 us
  transfers between devices with their start and end apart: 14, of which 7 were waited for; matrix products, arithmetic and copies ran while one was open for 0% of the time, Pallas kernels for 32%

profile of v7, /device:TPU:0, one launch (start us, length us, event | category | flops | bytes accessed | tf_op | source)
XLA Modules:
  0.0 79.2 jit_solution(6165986332592788776)
XLA Ops:
  0.0 0.9 %load_edge.2.refs_1_.refs_2_.refs_6_ = bf16[384,256]{1,0:T(8,128)(2,1)S(1)} custom-call(bf16[4,384,256]{2,1,0:T(8,128)(2,1)} %bitcast.21), custom_call_target="tpu_custom_call" | custom-call | bytes 786432 | tf_op jit(solution)/shard_map/load_edge/pallas_call | solution.py:73
  1.0 0.0 copy-start.9
  1.0 0.5 collective-permute-start
  1.5 1.3 %load_edge.3 = (bf16[384,256]{1,0:T(8,128)(2,1)S(1)}, bf16[4,384,256]{2,1,0:T(8,128)(2,1)S(1)}) custom-call(bf16[4,384,256]{2,1,0:T(8,128)(2,1)} %bitcast.22, bf16[384,256]{1,0:T(8,128)(2,1)S(1)} %load_edge.2.refs_1_.refs_2_.refs_6_), custom_call_target="tpu_custom_call" | custom-call | bytes 786432 | tf_op jit(solution)/shard_map/load_edge/pallas_call | solution.py:73
  2.8 4.1 %collective-permute-start.2 = (bf16[384,256]{1,0:T(8,128)(2,1)S(1)}, bf16[384,256]{1,0:T(8,128)(2,1)S(1)}, u32[]{:S(2)}, u32[]{:S(2)}) collective-permute-start(bf16[384,256]{1,0:T(8,128)(2,1)S(1)} %get-tuple-element.45.refs_2_.refs_3_.refs_7_), channel_id=1, source_target_pairs={{0,4},{1,5},{2,6},{3,7},{4,0},{5,1},{6,2},{7,3},{8,12},{9,13},{10,... | collective-permute-start | bytes 589832 | tf_op jit(solution)/shard_map/ppermute | solution.py:367
  6.9 0.9 %coarse_rhs.1.refs_4_ = bf16[256,256]{1,0:T(8,128)(2,1)} custom-call(bf16[4,384,256]{2,1,0:T(8,128)(2,1)S(1)} %get-tuple-element.46.refs_0_, bf16[6,1536]{1,0:T(8,128)(2,1)S(1)} %bitcast.28, bf16[384,256]{1,0:T(8,128)(2,1)S(1)} %get-tuple-element.45.refs_2_.refs_3_.refs_7_), custom_call_target="tpu_custom_call" | custom-call | flops 2359296 | bytes 804864 | tf_op jit(solution)/shard_map/coarse_rhs/pallas_call | solution.py:73
  7.8 4.7 %all-to-all-start = ((bf16[32,8,256]{2,1,0:T(8,128)(2,1)}), bf16[32,8,256]{2,1,0:T(8,128)(2,1)S(1)}, u32[]{:S(2)}, u32[]{:S(2)}) async-start(bf16[32,8,256]{2,1,0:T(8,128)(2,1)} %bitcast.41), calls=%async_computation | async-start | bytes 262144 | tf_op jit(solution)/shard_map/all_to_all | solution.py:371
  12.5 1.4 %load_outer.2 = (bf16[384,384]{1,0:T(8,128)(2,1)S(1)}, bf16[384,384]{1,0:T(8,128)(2,1)S(1)}, bf16[384,384]{1,0:T(8,128)(2,1)S(1)}, bf16[384,384]{1,0:T(8,128)(2,...) custom-call(bf16[6,384,384]{2,1,0:T(8,128)(2,1)} %bitcast.31, bf16[5,384,384]{2,1,0:T(8,128)(2,1)} %bitcast.35, ...), custom_call_target="tpu_custom_call" | custom-call | flops 90596966400 | bytes 3637248 | tf_op jit(solution)/shard_map/load_outer/pallas_call | solution.py:73
  13.9 0.0 copy-start.15
  14.0 0.7 margin_solve.4
  14.7 0.3 collective-permute-start.1
  15.0 0.7 margin_solve.5
  15.7 3.0 %collective-permute-start.4 = (bf16[384,256]{1,0:T(8,128)(2,1)S(1)}, bf16[384,256]{1,0:T(8,128)(2,1)S(1)}, u32[]{:S(2)}, u32[]{:S(2)}) collective-permute-start(bf16[384,256]{1,0:T(8,128)(2,1)S(1)} %get-tuple-element.54.refs_2_), channel_id=1, source_target_pairs={{0,4},{1,5},{2,6},{3,7},{4,0},{5,1},{6,2},{7,3},{8,12},{9,13},{10,... | collective-permute-start | bytes 589832 | tf_op jit(solution)/shard_map/ppermute | solution.py:367
  18.7 1.2 %prepare.1 = (bf16[16,1536]{1,0:T(8,128)(2,1)}, bf16[192,256]{1,0:T(8,128)(2,1)}, bf16[192,16]{1,0:T(8,128)(2,1)}) custom-call(bf16[6,1536]{1,0:T(8,128)(2,1)S(1)} %bitcast.29, bf16[192,192]{1,0:T(8,128)(2,1)S(1)} %copy-done.15, bf16[384,256]{1,0:T(8,128)(2,1)S(1)} %get-tuple-element.54.refs_2_), custom_call_target="tpu_custom_call" | custom-call | flops 9437184 | bytes 92160 | tf_op jit(solution)/shard_map/prepare/pallas_call | solution.py:73
  20.0 0.9 %all-to-all-done = bf16[32,8,256]{2,1,0:T(8,128)(2,1)S(1)} async-done(((bf16[32,8,256]{2,1,0:T(8,128)(2,1)}), bf16[32,8,256]{2,1,0:T(8,128)(2,1)S(1)}, u32[]{:S(2)}, u32[]{:S(2)}) %all-to-all-start) | async-done | bytes 131104 | tf_op jit(solution)/shard_map/all_to_all | solution.py:371
  20.8 0.7 copy-done.16
  21.5 4.0 %solve_layers.2.refs_1_.refs_2_ = f32[4,384,256]{2,1,0:T(8,128)S(1)} custom-call(bf16[256,256]{1,0:T(8,128)(2,1)} %bitcast.40, bf16[192,256]{1,0:T(8,128)(2,1)} %get-tuple-element.55.refs_1_, bf16[192,16]{1,0:T(8,128)(2,1)} %get-tuple-element.56.refs_2_, bf16[16,1536]{1,0:T(8,128)(2,1)} %get-tuple-element.57.refs_3_, ...), custom_call_target="tpu_custom_call" | custom-call | flops 905969664 | bytes 5101568 | tf_op jit(solution)/shard_map/solve_layers/pallas_call | solution.py:73
  25.5 0.1 join_margin.2
  25.6 0.0 copy-start.1
  25.6 0.2 collective-permute-start.3
  25.8 0.5 collective-permute-done.4.refs_0_
  26.3 0.4 join_margin.3
  26.7 2.2 %collective-permute-start.5 = (bf16[384,256]{1,0:T(8,128)(2,1)S(1)}, bf16[384,256]{1,0:T(8,128)(2,1)S(1)}, u32[]{:S(2)}, u32[]{:S(2)}) collective-permute-start(bf16[384,256]{1,0:T(8,128)(2,1)S(1)} %get-tuple-element.64), channel_id=1, source_target_pairs={{0,4},{1,5},{2,6},{3,7},{4,0},{5,1},{6,2},{7,3},{8,12},{9,13},{10,... | collective-permute-start | bytes 589832 | tf_op jit(solution)/shard_map/ppermute | solution.py:367
  28.9 1.3 %inner_operate.1 = (f32[4,384,256]{2,1,0:T(8,128)S(1)}, f32[4,384,256]{2,1,0:T(8,128)S(1)}, bf16[4,384,256]{2,1,0:T(8,128)(2,1)S(1)}, f32[2,256]{1,0:T(2,128)S(1)}) custom-call(f32[384,256]{1,0:T(8,128)S(1)} %get-tuple-element.61.refs_0_.refs_2_, f32[384,256]{1,0:T(8,128)S(1)} %get-tuple-element.62.refs_1_.refs_3_, ...), custom_call_target="tpu_custom_call" | custom-call | flops 754974720 | bytes 5505024 | tf_op jit(solution)/shard_map/inner_operate/pallas_call | solution.py:73
  30.3 5.6 %collective-permute-done.5.refs_3_.refs_0_ = bf16[384,256]{1,0:T(8,128)(2,1)S(1)} collective-permute-done((bf16[384,256]{1,0:T(8,128)(2,1)S(1)}, bf16[384,256]{1,0:T(8,128)(2,1)S(1)}, u32[]{:S(2)}, u32[]{:S(2)}) %collective-permute-start.5) | collective-permute-done | bytes 196640 | tf_op jit(solution)/shard_map/ppermute | solution.py:367
  36.0 0.1 collective-permute-start.6
  36.1 0.3 join_operate.3.refs_1_.refs_3_.refs_7_
  36.4 3.2 %collective-permute-start.8 = (bf16[384,256]{1,0:T(8,128)(2,1)S(1)}, bf16[384,256]{1,0:T(8,128)(2,1)}, u32[]{:S(2)}, u32[]{:S(2)}) collective-permute-start(bf16[384,256]{1,0:T(8,128)(2,1)S(1)} %join_operate.3.refs_1_.refs_3_.refs_7_), channel_id=1, source_target_pairs={{0,4},{1,5},{2,6},{3,7},{4,0},{5,1},{6,2},{7,3},{8,12},{9,13},{10,... | collective-permute-start | bytes 589832 | tf_op jit(solution)/shard_map/ppermute | solution.py:367
  39.6 1.0 %coarse_rhs_joined.1.refs_4_ = bf16[256,384]{1,0:T(8,128)(2,1)} custom-call(bf16[384,256]{1,0:T(8,128)(2,1)S(1)} %join_operate.2.refs_3_.refs_0_.refs_2_.refs_6_, bf16[384,256]{1,0:T(8,128)(2,1)S(1)} %join_operate.3.refs_1_.refs_3_.refs_7_, f32[384,256]{1,0:T(8,128)S(1)} %get-tuple-element.61.refs_0_.refs_2_, ...), custom_call_target="tpu_custom_call" | custom-call | flops 2359296 | bytes 2772992 | tf_op jit(solution)/shard_map/coarse_rhs_joined/pallas_call | solution.py:73
  40.6 4.5 %all-to-all-start.1 = ((bf16[32,8,384]{2,1,0:T(8,128)(2,1)}), bf16[32,8,384]{2,1,0:T(8,128)(2,1)}, u32[]{:S(2)}, u32[]{:S(2)}) async-start(bf16[32,8,384]{2,1,0:T(8,128)(2,1)} %bitcast.39), calls=%async_computation.1 | async-start | bytes 393216 | tf_op jit(solution)/shard_map/all_to_all | solution.py:371
  45.1 1.4 %load_outer.3 = (bf16[384,384]{1,0:T(8,128)(2,1)S(1)}, bf16[384,384]{1,0:T(8,128)(2,1)S(1)}, bf16[384,384]{1,0:T(8,128)(2,1)S(1)}, bf16[384,384]{1,0:T(8,128)(2,...) custom-call(bf16[6,384,384]{2,1,0:T(8,128)(2,1)} %bitcast.33, bf16[5,384,384]{2,1,0:T(8,128)(2,1)} %bitcast.37, ...), custom_call_target="tpu_custom_call" | custom-call | flops 90596966400 | bytes 3637248 | tf_op jit(solution)/shard_map/load_outer/pallas_call | solution.py:73
  46.5 1.3 %margin_solve.6.refs_4_ = bf16[384,256]{1,0:T(8,128)(2,1)S(1)} custom-call(bf16[384,256]{1,0:T(8,128)(2,1)} %collective-permute-done.6.refs_0_.refs_4_, bf16[384,256]{1,0:T(8,128)(2,1)S(1)} %get-tuple-element.66.refs_1_, bf16[384,384]{1,0:T(8,128)(2,1)S(1)} %get-tuple-element.67.refs_2_, bf16[384,384]{1,0:T(8,128)(2,1)S(1)} %get-tuple-element.68.refs_3_), custom_call_target="tpu_custom_call" | custom-call | flops 150994944 | bytes 983040 | tf_op jit(solution)/shard_map/margin_solve/pallas_call | solution.py:73
  47.8 0.3 collective-permute-start.7
  48.1 0.8 %collective-permute-done.8.refs_5_.refs_0_ = bf16[384,256]{1,0:T(8,128)(2,1)} collective-permute-done((bf16[384,256]{1,0:T(8,128)(2,1)S(1)}, bf16[384,256]{1,0:T(8,128)(2,1)}, u32[]{:S(2)}, u32[]{:S(2)}) %collective-permute-start.8) | collective-permute-done | bytes 196640 | tf_op jit(solution)/shard_map/ppermute | solution.py:367
  48.9 2.0 %margin_solve.7 = bf16[384,256]{1,0:T(8,128)(2,1)} custom-call(bf16[384,256]{1,0:T(8,128)(2,1)} %collective-permute-done.8.refs_5_.refs_0_, bf16[384,256]{1,0:T(8,128)(2,1)S(1)} %get-tuple-element.72.refs_1_, bf16[384,384]{1,0:T(8,128)(2,1)S(1)} %get-tuple-element.73.refs_2_, bf16[384,384]{1,0:T(8,128)(2,1)S(1)} %get-tuple-element.74.refs_3_, ...), custom_call_target="tpu_custom_call" | custom-call | flops 150994944 | bytes 983040 | tf_op jit(solution)/shard_map/margin_solve/pallas_call | solution.py:73
  50.9 2.8 %collective-permute-start.10 = (bf16[384,256]{1,0:T(8,128)(2,1)}, bf16[384,256]{1,0:T(8,128)(2,1)S(1)}, u32[]{:S(2)}, u32[]{:S(2)}) collective-permute-start(bf16[384,256]{1,0:T(8,128)(2,1)} %margin_solve.7), channel_id=1, source_target_pairs={{0,4},{1,5},{2,6},{3,7},{4,0},{5,1},{6,2},{7,3},{8,12},{9,13},{10,... | collective-permute-start | bytes 589832 | tf_op jit(solution)/shard_map/ppermute | solution.py:367
  53.7 0.3 all-to-all-done.1
  54.0 4.0 %solve_layers.3 = (f32[4,384,256]{2,1,0:T(8,128)S(1)}, f32[3,256]{1,0:T(4,128)S(1)}) custom-call(bf16[256,384]{1,0:T(8,128)(2,1)} %bitcast.9.refs_0_, bf16[192,256]{1,0:T(8,128)(2,1)} %get-tuple-element.55.refs_1_, bf16[192,16]{1,0:T(8,128)(2,1)} %get-tuple-element.56.refs_2_, bf16[16,1536]{1,0:T(8,128)(2,1)} %get-tuple-element.57.refs_3_, ...), custom_call_target="tpu_custom_call" | custom-call | flops 905969664 | bytes 5167104 | tf_op jit(solution)/shard_map/solve_layers/pallas_call | solution.py:73
  58.0 1.0 %join_second.2 = (f32[384,256]{1,0:T(8,128)S(1)}, bf16[384,128]{1,0:T(8,128)(2,1)S(1)}, f32[384,256]{1,0:T(8,128)S(1)}) custom-call(bf16[384,256]{1,0:T(8,128)(2,1)} %collective-permute-done.7.refs_0_, f32[4,384,256]{2,1,0:T(8,128)S(1)} %get-tuple-element.70.refs_1_.refs_4_, bf16[4,384,384]{2,1,0:T(8,128)(2,1)S(1)} %bitcast.18), custom_call_target="tpu_custom_call" | custom-call | flops 75497472 | bytes 2949120 | tf_op jit(solution)/shard_map/join_second/pallas_call | solution.py:73
  59.0 0.8 collective-permute-start.9
  59.8 0.2 collective-permute-done.10.refs_0_
  60.0 0.4 join_second.3
  60.4 2.1 %collective-permute-start.11 = (bf16[384,128]{1,0:T(8,128)(2,1)S(1)}, bf16[384,128]{1,0:T(8,128)(2,1)S(1)}, u32[]{:S(2)}, u32[]{:S(2)}) collective-permute-start(bf16[384,128]{1,0:T(8,128)(2,1)S(1)} %get-tuple-element.75), channel_id=1, source_target_pairs={{0,4},{1,5},{2,6},{3,7},{4,0},{5,1},{6,2},{7,3},{8,12},{9,13},{10,... | collective-permute-start | bytes 294920 | tf_op jit(solution)/shard_map/ppermute | solution.py:367
  62.6 1.7 %inner_products.1 = (f32[4,384,256]{2,1,0:T(8,128)S(1)}, f32[4,384,256]{2,1,0:T(8,128)S(1)}, f32[3,256]{1,0:T(4,128)S(1)}) custom-call(f32[384,256]{1,0:T(8,128)S(1)} %get-tuple-element.78.refs_0_, f32[384,256]{1,0:T(8,128)S(1)} %get-tuple-element.79.refs_1_, bf16[384,256]{1,0:T(8,128)(2,1)S(1)} %copy-done.3, bf16[384,256]{1,0:T(8,128)(2,1)S(1)} %copy-done.8, ...), custom_call_target="tpu_custom_call" | custom-call | flops 905969664 | bytes 8260608 | tf_op jit(solution)/shard_map/inner_products/pallas_call | solution.py:73
  64.3 1.4 %collective-permute-done.11.refs_1_ = bf16[384,128]{1,0:T(8,128)(2,1)S(1)} collective-permute-done((bf16[384,128]{1,0:T(8,128)(2,1)S(1)}, bf16[384,128]{1,0:T(8,128)(2,1)S(1)}, u32[]{:S(2)}, u32[]{:S(2)}) %collective-permute-start.11) | collective-permute-done | bytes 98336 | tf_op jit(solution)/shard_map/ppermute | solution.py:367
  65.6 0.2 join_sums.1
  65.8 12.1 %all_to_all.15.refs_0_ = f32[32,2,384]{2,1,0:T(2,128)S(1)} all-to-all(f32[32,2,384]{2,1,0:T(2,128)S(1)} %join_sums.1), channel_id=1, replica_groups=mesh['row'=8,'col'=4] {'row','col'}, dimensions={0} | all-to-all | bytes 196608 | tf_op jit(solution)/shard_map/all_to_all | solution.py:371
  77.9 1.3 %finish.1 = f32[4,384,256]{2,1,0:T(8,128)} custom-call(f32[32,2,384]{2,1,0:T(2,128)S(1)} %all_to_all.15.refs_0_, f32[3,256]{1,0:T(4,128)S(1)} %get-tuple-element.81.refs_10_.refs_1_, f32[4,384,256]{2,1,0:T(8,128)S(1)} %get-tuple-element.83.refs_2_, f32[4,384,256]{2,1,0:T(8,128)S(1)} %get-tuple-element.84.refs_3_), custom_call_target="tpu_custom_call" | custom-call | bytes 3247104 | tf_op jit(solution)/shard_map/finish/pallas_call | solution.py:73
  (38 shorter events, 0.1 us)
Async XLA Ops:
  0.0 6.9 %copy-start.13 = (bf16[1,1,6,1536]{3,2,1,0:T(8,128)(2,1)S(1)}, bf16[1,1,6,1536]{3,2,1,0:T(8,128)(2,1)}, u32[]{:S(2)}) copy-start(bf16[1,1,6,1536]{3,2,1,0:T(8,128)(2,1)} %param.12) | copy-start | bytes 55300
  1.0 11.5 %copy-start.9 = (bf16[384,256]{1,0:T(8,128)(2,1)}, bf16[384,256]{1,0:T(8,128)(2,1)S(1)}, u32[]{:S(2)}) copy-start(bf16[384,256]{1,0:T(8,128)(2,1)S(1)} %load_edge.2.refs_1_.refs_2_.refs_6_) | copy-start | bytes 589828
  1.0 13.0 %collective-permute-start = (bf16[384,256]{1,0:T(8,128)(2,1)S(1)}, bf16[384,256]{1,0:T(8,128)(2,1)S(1)}, u32[]{:S(2)}, u32[]{:S(2)}) collective-permute-start(bf16[384,256]{1,0:T(8,128)(2,1)S(1)} %load_edge.2.refs_1_.refs_2_.refs_6_), channel_id=1, source_target_pairs={{0,1},{1,0},{2,3},{3,2},{4,8},{5,9},{6,10},{7,11},{8,4},{9,5},{10,... | collective-permute-start | bytes 589832 | tf_op jit(solution)/shard_map/ppermute | solution.py:367
  2.8 9.8 %copy-start.12 = (bf16[384,256]{1,0:T(8,128)(2,1)}, bf16[384,256]{1,0:T(8,128)(2,1)S(1)}, u32[]{:S(2)}) copy-start(bf16[384,256]{1,0:T(8,128)(2,1)S(1)} %get-tuple-element.45.refs_2_.refs_3_.refs_7_) | copy-start | bytes 589828
  2.8 12.2 %collective-permute-start.2 = (bf16[384,256]{1,0:T(8,128)(2,1)S(1)}, bf16[384,256]{1,0:T(8,128)(2,1)S(1)}, u32[]{:S(2)}, u32[]{:S(2)}) collective-permute-start(bf16[384,256]{1,0:T(8,128)(2,1)S(1)} %get-tuple-element.45.refs_2_.refs_3_.refs_7_), channel_id=1, source_target_pairs={{0,4},{1,5},{2,6},{3,7},{4,0},{5,1},{6,2},{7,3},{8,12},{9,13},{10,... | collective-permute-start | bytes 589832 | tf_op jit(solution)/shard_map/ppermute | solution.py:367
  7.8 13.1 %all-to-all-start = ((bf16[32,8,256]{2,1,0:T(8,128)(2,1)}), bf16[32,8,256]{2,1,0:T(8,128)(2,1)S(1)}, u32[]{:S(2)}, u32[]{:S(2)}) async-start(bf16[32,8,256]{2,1,0:T(8,128)(2,1)} %bitcast.41), calls=%async_computation | async-start | bytes 262144 | tf_op jit(solution)/shard_map/all_to_all | solution.py:371
  13.9 4.8 %copy-start.15 = (bf16[192,192]{1,0:T(8,128)(2,1)S(1)}, bf16[192,192]{1,0:T(8,128)(2,1)}, u32[]{:S(2)}) copy-start(bf16[192,192]{1,0:T(8,128)(2,1)} %refs_1_.1) | copy-start | bytes 221188
  14.7 10.9 %collective-permute-start.1 = (bf16[384,256]{1,0:T(8,128)(2,1)S(1)}, bf16[384,256]{1,0:T(8,128)(2,1)S(1)}, u32[]{:S(2)}, u32[]{:S(2)}) collective-permute-start(bf16[384,256]{1,0:T(8,128)(2,1)S(1)} %get-tuple-element.50.refs_4_), channel_id=1, source_target_pairs={{0,1},{1,0},{2,3},{3,2},{4,8},{5,9},{6,10},{7,11},{8,4},{9,5},{10,... | collective-permute-start | bytes 589832 | tf_op jit(solution)/shard_map/ppermute | solution.py:367
  15.7 10.6 %collective-permute-start.4 = (bf16[384,256]{1,0:T(8,128)(2,1)S(1)}, bf16[384,256]{1,0:T(8,128)(2,1)S(1)}, u32[]{:S(2)}, u32[]{:S(2)}) collective-permute-start(bf16[384,256]{1,0:T(8,128)(2,1)S(1)} %get-tuple-element.54.refs_2_), channel_id=1, source_target_pairs={{0,4},{1,5},{2,6},{3,7},{4,0},{5,1},{6,2},{7,3},{8,12},{9,13},{10,... | collective-permute-start | bytes 589832 | tf_op jit(solution)/shard_map/ppermute | solution.py:367
  20.8 0.7 copy-start.16
  21.5 4.0 %copy-start = (bf16[4,1,384,384]{3,2,1,0:T(8,128)(2,1)S(1)}, bf16[4,1,384,384]{3,2,1,0:T(8,128)(2,1)}, u32[]{:S(2)}) copy-start(bf16[4,1,384,384]{3,2,1,0:T(8,128)(2,1)} %param.9) | copy-start | bytes 3538948
  25.6 3.3 %copy-start.1 = (bf16[4,1,384,256]{3,2,1,0:T(8,128)(2,1)S(1)}, bf16[4,1,384,256]{3,2,1,0:T(8,128)(2,1)}, u32[]{:S(2)}) copy-start(bf16[4,1,384,256]{3,2,1,0:T(8,128)(2,1)} %param.7) | copy-start | bytes 2359300
  25.6 3.3 %copy-start.4 = (bf16[4,1,384,384]{3,2,1,0:T(8,128)(2,1)S(1)}, bf16[4,1,384,384]{3,2,1,0:T(8,128)(2,1)}, u32[]{:S(2)}) copy-start(bf16[4,1,384,384]{3,2,1,0:T(8,128)(2,1)} %param.8) | copy-start | bytes 3538948
  25.6 4.6 %collective-permute-start.3 = (bf16[384,256]{1,0:T(8,128)(2,1)S(1)}, bf16[384,256]{1,0:T(8,128)(2,1)S(1)}, u32[]{:S(2)}, u32[]{:S(2)}) collective-permute-start(bf16[384,256]{1,0:T(8,128)(2,1)S(1)} %get-tuple-element.60.refs_3_), channel_id=1, source_target_pairs={{0,1},{1,0},{2,3},{3,2},{4,8},{5,9},{6,10},{7,11},{8,4},{9,5},{10,... | collective-permute-start | bytes 589832 | tf_op jit(solution)/shard_map/ppermute | solution.py:367
  26.7 9.2 %collective-permute-start.5 = (bf16[384,256]{1,0:T(8,128)(2,1)S(1)}, bf16[384,256]{1,0:T(8,128)(2,1)S(1)}, u32[]{:S(2)}, u32[]{:S(2)}) collective-permute-start(bf16[384,256]{1,0:T(8,128)(2,1)S(1)} %get-tuple-element.64), channel_id=1, source_target_pairs={{0,4},{1,5},{2,6},{3,7},{4,0},{5,1},{6,2},{7,3},{8,12},{9,13},{10,... | collective-permute-start | bytes 589832 | tf_op jit(solution)/shard_map/ppermute | solution.py:367
  30.2 5.7 %copy-start.5 = (bf16[4,384,256]{2,1,0:T(8,128)(2,1)}, bf16[4,384,256]{2,1,0:T(8,128)(2,1)S(1)}, u32[]{:S(2)}) copy-start(bf16[4,384,256]{2,1,0:T(8,128)(2,1)S(1)} %get-tuple-element.69.refs_8_.refs_7_) | copy-start | bytes 2359300
  30.2 5.7 %copy-start.10 = (f32[4,384,256]{2,1,0:T(8,128)}, f32[4,384,256]{2,1,0:T(8,128)S(1)}, u32[]{:S(2)}) copy-start(f32[4,384,256]{2,1,0:T(8,128)S(1)} %get-tuple-element.80.refs_5_) | copy-start | bytes 4718596
  35.9 3.6 %copy-start.2 = (bf16[384,256]{1,0:T(8,128)(2,1)}, bf16[384,256]{1,0:T(8,128)(2,1)S(1)}, u32[]{:S(2)}) copy-start(bf16[384,256]{1,0:T(8,128)(2,1)S(1)} %join_operate.2.refs_3_.refs_0_.refs_2_.refs_6_) | copy-start | bytes 589828
  36.0 3.6 %copy-start.14 = (bf16[1,1,6,1536]{3,2,1,0:T(8,128)(2,1)S(1)}, bf16[1,1,6,1536]{3,2,1,0:T(8,128)(2,1)}, u32[]{:S(2)}) copy-start(bf16[1,1,6,1536]{3,2,1,0:T(8,128)(2,1)} %param.12) | copy-start | bytes 55300
  36.0 10.5 %collective-permute-start.6 = (bf16[384,256]{1,0:T(8,128)(2,1)S(1)}, bf16[384,256]{1,0:T(8,128)(2,1)}, u32[]{:S(2)}, u32[]{:S(2)}) collective-permute-start(bf16[384,256]{1,0:T(8,128)(2,1)S(1)} %join_operate.2.refs_3_.refs_0_.refs_2_.refs_6_), channel_id=1, source_target_pairs={{0,1},{1,0},{2,3},{3,2},{4,8},{5,9},{6,10},{7,11},{8,4},{9,5},{10,... | collective-permute-start | bytes 589832 | tf_op jit(solution)/shard_map/ppermute | solution.py:367
  36.3 4.3 %copy-start.7 = (bf16[384,256]{1,0:T(8,128)(2,1)}, bf16[384,256]{1,0:T(8,128)(2,1)S(1)}, u32[]{:S(2)}) copy-start(bf16[384,256]{1,0:T(8,128)(2,1)S(1)} %join_operate.3.refs_1_.refs_3_.refs_7_) | copy-start | bytes 589828
  36.4 12.5 %collective-permute-start.8 = (bf16[384,256]{1,0:T(8,128)(2,1)S(1)}, bf16[384,256]{1,0:T(8,128)(2,1)}, u32[]{:S(2)}, u32[]{:S(2)}) collective-permute-start(bf16[384,256]{1,0:T(8,128)(2,1)S(1)} %join_operate.3.refs_1_.refs_3_.refs_7_), channel_id=1, source_target_pairs={{0,4},{1,5},{2,6},{3,7},{4,0},{5,1},{6,2},{7,3},{8,12},{9,13},{10,... | collective-permute-start | bytes 589832 | tf_op jit(solution)/shard_map/ppermute | solution.py:367
  40.6 13.4 %all-to-all-start.1 = ((bf16[32,8,384]{2,1,0:T(8,128)(2,1)}), bf16[32,8,384]{2,1,0:T(8,128)(2,1)}, u32[]{:S(2)}, u32[]{:S(2)}) async-start(bf16[32,8,384]{2,1,0:T(8,128)(2,1)} %bitcast.39), calls=%async_computation.1 | async-start | bytes 393216 | tf_op jit(solution)/shard_map/all_to_all | solution.py:371
  47.8 10.2 %collective-permute-start.7 = (bf16[384,256]{1,0:T(8,128)(2,1)S(1)}, bf16[384,256]{1,0:T(8,128)(2,1)}, u32[]{:S(2)}, u32[]{:S(2)}) collective-permute-start(bf16[384,256]{1,0:T(8,128)(2,1)S(1)} %margin_solve.6.refs_4_), channel_id=1, source_target_pairs={{0,1},{1,0},{2,3},{3,2},{4,8},{5,9},{6,10},{7,11},{8,4},{9,5},{10,... | collective-permute-start | bytes 589832 | tf_op jit(solution)/shard_map/ppermute | solution.py:367
  50.9 9.1 %collective-permute-start.10 = (bf16[384,256]{1,0:T(8,128)(2,1)}, bf16[384,256]{1,0:T(8,128)(2,1)S(1)}, u32[]{:S(2)}, u32[]{:S(2)}) collective-permute-start(bf16[384,256]{1,0:T(8,128)(2,1)} %margin_solve.7), channel_id=1, source_target_pairs={{0,4},{1,5},{2,6},{3,7},{4,0},{5,1},{6,2},{7,3},{8,12},{9,13},{10,... | collective-permute-start | bytes 589832 | tf_op jit(solution)/shard_map/ppermute | solution.py:367
  59.0 3.6 %copy-start.3 = (bf16[384,256]{1,0:T(8,128)(2,1)S(1)}, bf16[384,256]{1,0:T(8,128)(2,1)}, u32[]{:S(2)}) copy-start(bf16[384,256]{1,0:T(8,128)(2,1)} %copy-done.2) | copy-start | bytes 589828
  59.0 3.6 %copy-start.6 = (bf16[4,384,256]{2,1,0:T(8,128)(2,1)S(1)}, bf16[4,384,256]{2,1,0:T(8,128)(2,1)}, u32[]{:S(2)}) copy-start(bf16[4,384,256]{2,1,0:T(8,128)(2,1)} %copy-done.5) | copy-start | bytes 2359300
  59.0 3.6 %copy-start.8 = (bf16[384,256]{1,0:T(8,128)(2,1)S(1)}, bf16[384,256]{1,0:T(8,128)(2,1)}, u32[]{:S(2)}) copy-start(bf16[384,256]{1,0:T(8,128)(2,1)} %copy-done.7) | copy-start | bytes 589828
  59.0 3.5 %copy-start.11 = (f32[4,384,256]{2,1,0:T(8,128)S(1)}, f32[4,384,256]{2,1,0:T(8,128)}, u32[]{:S(2)}) copy-start(f32[4,384,256]{2,1,0:T(8,128)} %copy-done.10) | copy-start | bytes 4718596
  59.0 5.2 %collective-permute-start.9 = (bf16[384,128]{1,0:T(8,128)(2,1)S(1)}, bf16[384,128]{1,0:T(8,128)(2,1)S(1)}, u32[]{:S(2)}, u32[]{:S(2)}) collective-permute-start(bf16[384,128]{1,0:T(8,128)(2,1)S(1)} %get-tuple-element.71.refs_3_), channel_id=1, source_target_pairs={{0,1},{1,0},{2,3},{3,2},{4,8},{5,9},{6,10},{7,11},{8,4},{9,5},{10,... | collective-permute-start | bytes 294920 | tf_op jit(solution)/shard_map/ppermute | solution.py:367
  60.4 5.2 %collective-permute-start.11 = (bf16[384,128]{1,0:T(8,128)(2,1)S(1)}, bf16[384,128]{1,0:T(8,128)(2,1)S(1)}, u32[]{:S(2)}, u32[]{:S(2)}) collective-permute-start(bf16[384,128]{1,0:T(8,128)(2,1)S(1)} %get-tuple-element.75), channel_id=1, source_target_pairs={{0,4},{1,5},{2,6},{3,7},{4,0},{5,1},{6,2},{7,3},{8,12},{9,13},{10,... | collective-permute-start | bytes 294920 | tf_op jit(solution)/shard_map/ppermute | solution.py:367

commit v8 on v7

--- a/solution.py
+++ b/solution.py
@@ -126,6 +126,11 @@
 
 def solve_layers(*refs):
     far, p, scalars, near, sems = refs[:11], refs[11], refs[12:-12], refs[-12:-1], refs[-1]
+    far = list(far)
+    skip = 0 if scalars else 1
+    if scalars:
+        far[8] = far[8].at[pl.ds(1, 2)]
+        far[9] = far[9].at[pl.ds(1, 4)]
     copies = [pltpu.make_async_copy(a, b, sems.at[i]) for i, (a, b) in enumerate(zip(far, near))]
     for c in copies:
         c.start()
@@ -141,9 +146,9 @@
     e0, e5 = pick(h2[...], h1[...])
     e0, e5 = kept(e0, True), kept(e5, False)
     e1, e4 = pick(o2[...], o1[...])
-    e2, e3 = e[1], e[2]
+    e2, e3 = e[skip], e[skip + 1]
     for k, x in enumerate((e1, e2, e3, e4)):
-        p[k] = mm(ld[k + 1], x) + mmt(basis[:, k * size : (k + 1) * size], u)
+        p[k] = mm(ld[k + skip], x) + mmt(basis[:, k * size : (k + 1) * size], u)
     copies[10].wait()
     p[0] = p[0] + mm(lu[1], e2) + mmt(lu[0], e0)
     p[1] = p[1] + mm(lu[2], e3) + mmt(lu[1], e1)
@@ -406,7 +411,10 @@
 
     def solve(h2, h1, o2, o1, e, gathered, scalars):
         args = (gathered, fpad, fown, basis, h2, h1, o2, o1, e, ld, lu)
-        held = [pltpu.VMEM(a.shape, a.dtype) for a in args] + [dma(len(args))]
+        shapes = [a.shape for a in args]
+        if scalars:
+            shapes = shapes[:8] + [(2,) + layer, (4, size, size), lu.shape]
+        held = [pltpu.VMEM(shape, BF) for shape in shapes] + [dma(len(args))]
         outs = [(whole, F32)] + [((3, cols), F32)] * scalars
         return call(solve_layers, outs, args, "solve_layers", 12 * block, (), held, range(len(args)))
 

time: 79.6 us -> 79.6 us (level)
  transfers between devices with their start and end apart: 14 -> 14, of which waited for: 7 -> 7; matrix products, arithmetic and copies ran while one was open for 0% -> 0% of each run, Pallas kernels for 32% -> 31%
where the time goes in v8:
time: 79.6 us; the launch traced here: 79.2 us
  starting transfers between devices  28.9 us (36%)
  Pallas kernels  27.1 us (34%)
  blocking collectives  12.1 us (15%)
  waiting for transfers between devices  10 us (13%)
    pallas_call x23, Pallas kernels, call(): pl.pallas_call(kernel, out_shape=shapes, in_specs=[space(i, hbm) for i in...  27.1 us
    ppermute x12, starting transfers between devices, swap(): return lax.ppermute(x, ALL, moves)  19.7 us
    all_to_all x1, blocking collectives, gather(): return lax.all_to_all(copies, ALL, 0, 0)  12.1 us
    all_to_all x2, starting transfers between devices, gather(): return lax.all_to_all(copies, ALL, 0, 0)  9.2 us
    ppermute x12, waiting for transfers between devices, swap(): return lax.ppermute(x, ALL, moves)  8.85 us
  transfers between devices with their start and end apart: 14, of which 7 were waited for; matrix products, arithmetic and copies ran while one was open for 0% of the time, Pallas kernels for 31%

profile of v8, /device:TPU:0, one launch (start us, length us, event | category | flops | bytes accessed | tf_op | source)
XLA Modules:
  0.0 79.2 jit_solution(13643319231930174075)
XLA Ops:
  0.0 0.9 %load_edge.2.refs_1_.refs_2_.refs_6_ = bf16[384,256]{1,0:T(8,128)(2,1)S(1)} custom-call(bf16[4,384,256]{2,1,0:T(8,128)(2,1)} %bitcast.21), custom_call_target="tpu_custom_call" | custom-call | bytes 786432 | tf_op jit(solution)/shard_map/load_edge/pallas_call | solution.py:73
  1.0 0.0 copy-start.9
  1.0 0.5 collective-permute-start
  1.5 1.3 %load_edge.3 = (bf16[384,256]{1,0:T(8,128)(2,1)S(1)}, bf16[4,384,256]{2,1,0:T(8,128)(2,1)S(1)}) custom-call(bf16[4,384,256]{2,1,0:T(8,128)(2,1)} %bitcast.22, bf16[384,256]{1,0:T(8,128)(2,1)S(1)} %load_edge.2.refs_1_.refs_2_.refs_6_), custom_call_target="tpu_custom_call" | custom-call | bytes 786432 | tf_op jit(solution)/shard_map/load_edge/pallas_call | solution.py:73
  2.8 4.1 %collective-permute-start.2 = (bf16[384,256]{1,0:T(8,128)(2,1)S(1)}, bf16[384,256]{1,0:T(8,128)(2,1)S(1)}, u32[]{:S(2)}, u32[]{:S(2)}) collective-permute-start(bf16[384,256]{1,0:T(8,128)(2,1)S(1)} %get-tuple-element.45.refs_2_.refs_3_.refs_7_), channel_id=1, source_target_pairs={{0,4},{1,5},{2,6},{3,7},{4,0},{5,1},{6,2},{7,3},{8,12},{9,13},{10,... | collective-permute-start | bytes 589832 | tf_op jit(solution)/shard_map/ppermute | solution.py:372
  6.9 0.9 %coarse_rhs.1.refs_4_ = bf16[256,256]{1,0:T(8,128)(2,1)} custom-call(bf16[4,384,256]{2,1,0:T(8,128)(2,1)S(1)} %get-tuple-element.46.refs_0_, bf16[6,1536]{1,0:T(8,128)(2,1)S(1)} %bitcast.28, bf16[384,256]{1,0:T(8,128)(2,1)S(1)} %get-tuple-element.45.refs_2_.refs_3_.refs_7_), custom_call_target="tpu_custom_call" | custom-call | flops 2359296 | bytes 804864 | tf_op jit(solution)/shard_map/coarse_rhs/pallas_call | solution.py:73
  7.8 4.7 %all-to-all-start = ((bf16[32,8,256]{2,1,0:T(8,128)(2,1)}), bf16[32,8,256]{2,1,0:T(8,128)(2,1)S(1)}, u32[]{:S(2)}, u32[]{:S(2)}) async-start(bf16[32,8,256]{2,1,0:T(8,128)(2,1)} %bitcast.41), calls=%async_computation | async-start | bytes 262144 | tf_op jit(solution)/shard_map/all_to_all | solution.py:376
  12.5 1.4 %load_outer.2 = (bf16[384,384]{1,0:T(8,128)(2,1)S(1)}, bf16[384,384]{1,0:T(8,128)(2,1)S(1)}, bf16[384,384]{1,0:T(8,128)(2,1)S(1)}, bf16[384,384]{1,0:T(8,128)(2,...) custom-call(bf16[6,384,384]{2,1,0:T(8,128)(2,1)} %bitcast.31, bf16[5,384,384]{2,1,0:T(8,128)(2,1)} %bitcast.35, ...), custom_call_target="tpu_custom_call" | custom-call | flops 90596966400 | bytes 3637248 | tf_op jit(solution)/shard_map/load_outer/pallas_call | solution.py:73
  13.9 0.0 copy-start.15
  14.0 0.7 margin_solve.4
  14.7 0.3 collective-permute-start.1
  15.0 0.7 margin_solve.5
  15.7 3.0 %collective-permute-start.4 = (bf16[384,256]{1,0:T(8,128)(2,1)S(1)}, bf16[384,256]{1,0:T(8,128)(2,1)S(1)}, u32[]{:S(2)}, u32[]{:S(2)}) collective-permute-start(bf16[384,256]{1,0:T(8,128)(2,1)S(1)} %get-tuple-element.54.refs_2_), channel_id=1, source_target_pairs={{0,4},{1,5},{2,6},{3,7},{4,0},{5,1},{6,2},{7,3},{8,12},{9,13},{10,... | collective-permute-start | bytes 589832 | tf_op jit(solution)/shard_map/ppermute | solution.py:372
  18.7 1.2 %prepare.1 = (bf16[16,1536]{1,0:T(8,128)(2,1)}, bf16[192,256]{1,0:T(8,128)(2,1)}, bf16[192,16]{1,0:T(8,128)(2,1)}) custom-call(bf16[6,1536]{1,0:T(8,128)(2,1)S(1)} %bitcast.29, bf16[192,192]{1,0:T(8,128)(2,1)S(1)} %copy-done.15, bf16[384,256]{1,0:T(8,128)(2,1)S(1)} %get-tuple-element.54.refs_2_), custom_call_target="tpu_custom_call" | custom-call | flops 9437184 | bytes 92160 | tf_op jit(solution)/shard_map/prepare/pallas_call | solution.py:73
  20.0 0.9 %all-to-all-done = bf16[32,8,256]{2,1,0:T(8,128)(2,1)S(1)} async-done(((bf16[32,8,256]{2,1,0:T(8,128)(2,1)}), bf16[32,8,256]{2,1,0:T(8,128)(2,1)S(1)}, u32[]{:S(2)}, u32[]{:S(2)}) %all-to-all-start) | async-done | bytes 131104 | tf_op jit(solution)/shard_map/all_to_all | solution.py:376
  20.8 0.7 copy-done.16
  21.5 4.0 %solve_layers.2.refs_1_.refs_2_ = f32[4,384,256]{2,1,0:T(8,128)S(1)} custom-call(bf16[256,256]{1,0:T(8,128)(2,1)} %bitcast.40, bf16[192,256]{1,0:T(8,128)(2,1)} %get-tuple-element.55.refs_1_, bf16[192,16]{1,0:T(8,128)(2,1)} %get-tuple-element.56.refs_2_, bf16[16,1536]{1,0:T(8,128)(2,1)} %get-tuple-element.57.refs_3_, ...), custom_call_target="tpu_custom_call" | custom-call | flops 905969664 | bytes 5101568 | tf_op jit(solution)/shard_map/solve_layers/pallas_call | solution.py:73
  25.5 0.1 join_margin.2
  25.6 0.0 copy-start.1
  25.6 0.2 collective-permute-start.3
  25.8 0.5 collective-permute-done.4.refs_0_
  26.3 0.4 join_margin.3
  26.7 2.2 %collective-permute-start.5 = (bf16[384,256]{1,0:T(8,128)(2,1)S(1)}, bf16[384,256]{1,0:T(8,128)(2,1)S(1)}, u32[]{:S(2)}, u32[]{:S(2)}) collective-permute-start(bf16[384,256]{1,0:T(8,128)(2,1)S(1)} %get-tuple-element.64), channel_id=1, source_target_pairs={{0,4},{1,5},{2,6},{3,7},{4,0},{5,1},{6,2},{7,3},{8,12},{9,13},{10,... | collective-permute-start | bytes 589832 | tf_op jit(solution)/shard_map/ppermute | solution.py:372
  28.9 1.3 %inner_operate.1 = (f32[4,384,256]{2,1,0:T(8,128)S(1)}, f32[4,384,256]{2,1,0:T(8,128)S(1)}, bf16[4,384,256]{2,1,0:T(8,128)(2,1)S(1)}, f32[2,256]{1,0:T(2,128)S(1)}) custom-call(f32[384,256]{1,0:T(8,128)S(1)} %get-tuple-element.61.refs_0_.refs_2_, f32[384,256]{1,0:T(8,128)S(1)} %get-tuple-element.62.refs_1_.refs_3_, ...), custom_call_target="tpu_custom_call" | custom-call | flops 754974720 | bytes 5505024 | tf_op jit(solution)/shard_map/inner_operate/pallas_call | solution.py:73
  30.3 5.6 %collective-permute-done.5.refs_3_.refs_0_ = bf16[384,256]{1,0:T(8,128)(2,1)S(1)} collective-permute-done((bf16[384,256]{1,0:T(8,128)(2,1)S(1)}, bf16[384,256]{1,0:T(8,128)(2,1)S(1)}, u32[]{:S(2)}, u32[]{:S(2)}) %collective-permute-start.5) | collective-permute-done | bytes 196640 | tf_op jit(solution)/shard_map/ppermute | solution.py:372
  36.0 0.1 collective-permute-start.6
  36.1 0.3 join_operate.3.refs_1_.refs_3_.refs_7_
  36.4 3.2 %collective-permute-start.8 = (bf16[384,256]{1,0:T(8,128)(2,1)S(1)}, bf16[384,256]{1,0:T(8,128)(2,1)}, u32[]{:S(2)}, u32[]{:S(2)}) collective-permute-start(bf16[384,256]{1,0:T(8,128)(2,1)S(1)} %join_operate.3.refs_1_.refs_3_.refs_7_), channel_id=1, source_target_pairs={{0,4},{1,5},{2,6},{3,7},{4,0},{5,1},{6,2},{7,3},{8,12},{9,13},{10,... | collective-permute-start | bytes 589832 | tf_op jit(solution)/shard_map/ppermute | solution.py:372
  39.6 1.0 %coarse_rhs_joined.1.refs_4_ = bf16[256,384]{1,0:T(8,128)(2,1)} custom-call(bf16[384,256]{1,0:T(8,128)(2,1)S(1)} %join_operate.2.refs_3_.refs_0_.refs_2_.refs_6_, bf16[384,256]{1,0:T(8,128)(2,1)S(1)} %join_operate.3.refs_1_.refs_3_.refs_7_, f32[384,256]{1,0:T(8,128)S(1)} %get-tuple-element.61.refs_0_.refs_2_, ...), custom_call_target="tpu_custom_call" | custom-call | flops 2359296 | bytes 2772992 | tf_op jit(solution)/shard_map/coarse_rhs_joined/pallas_call | solution.py:73
  40.6 4.5 %all-to-all-start.1 = ((bf16[32,8,384]{2,1,0:T(8,128)(2,1)}), bf16[32,8,384]{2,1,0:T(8,128)(2,1)}, u32[]{:S(2)}, u32[]{:S(2)}) async-start(bf16[32,8,384]{2,1,0:T(8,128)(2,1)} %bitcast.39), calls=%async_computation.1 | async-start | bytes 393216 | tf_op jit(solution)/shard_map/all_to_all | solution.py:376
  45.1 1.4 %load_outer.3 = (bf16[384,384]{1,0:T(8,128)(2,1)S(1)}, bf16[384,384]{1,0:T(8,128)(2,1)S(1)}, bf16[384,384]{1,0:T(8,128)(2,1)S(1)}, bf16[384,384]{1,0:T(8,128)(2,...) custom-call(bf16[6,384,384]{2,1,0:T(8,128)(2,1)} %bitcast.33, bf16[5,384,384]{2,1,0:T(8,128)(2,1)} %bitcast.37, ...), custom_call_target="tpu_custom_call" | custom-call | flops 90596966400 | bytes 3637248 | tf_op jit(solution)/shard_map/load_outer/pallas_call | solution.py:73
  46.5 1.3 %margin_solve.6.refs_4_ = bf16[384,256]{1,0:T(8,128)(2,1)S(1)} custom-call(bf16[384,256]{1,0:T(8,128)(2,1)} %collective-permute-done.6.refs_0_.refs_4_, bf16[384,256]{1,0:T(8,128)(2,1)S(1)} %get-tuple-element.66.refs_1_, bf16[384,384]{1,0:T(8,128)(2,1)S(1)} %get-tuple-element.67.refs_2_, bf16[384,384]{1,0:T(8,128)(2,1)S(1)} %get-tuple-element.68.refs_3_), custom_call_target="tpu_custom_call" | custom-call | flops 150994944 | bytes 983040 | tf_op jit(solution)/shard_map/margin_solve/pallas_call | solution.py:73
  47.8 0.3 collective-permute-start.7
  48.1 0.8 %collective-permute-done.8.refs_5_.refs_0_ = bf16[384,256]{1,0:T(8,128)(2,1)} collective-permute-done((bf16[384,256]{1,0:T(8,128)(2,1)S(1)}, bf16[384,256]{1,0:T(8,128)(2,1)}, u32[]{:S(2)}, u32[]{:S(2)}) %collective-permute-start.8) | collective-permute-done | bytes 196640 | tf_op jit(solution)/shard_map/ppermute | solution.py:372
  48.9 2.0 %margin_solve.7 = bf16[384,256]{1,0:T(8,128)(2,1)} custom-call(bf16[384,256]{1,0:T(8,128)(2,1)} %collective-permute-done.8.refs_5_.refs_0_, bf16[384,256]{1,0:T(8,128)(2,1)S(1)} %get-tuple-element.72.refs_1_, bf16[384,384]{1,0:T(8,128)(2,1)S(1)} %get-tuple-element.73.refs_2_, bf16[384,384]{1,0:T(8,128)(2,1)S(1)} %get-tuple-element.74.refs_3_, ...), custom_call_target="tpu_custom_call" | custom-call | flops 150994944 | bytes 983040 | tf_op jit(solution)/shard_map/margin_solve/pallas_call | solution.py:73
  50.9 2.8 %collective-permute-start.10 = (bf16[384,256]{1,0:T(8,128)(2,1)}, bf16[384,256]{1,0:T(8,128)(2,1)S(1)}, u32[]{:S(2)}, u32[]{:S(2)}) collective-permute-start(bf16[384,256]{1,0:T(8,128)(2,1)} %margin_solve.7), channel_id=1, source_target_pairs={{0,4},{1,5},{2,6},{3,7},{4,0},{5,1},{6,2},{7,3},{8,12},{9,13},{10,... | collective-permute-start | bytes 589832 | tf_op jit(solution)/shard_map/ppermute | solution.py:372
  53.7 0.3 all-to-all-done.1
  54.0 3.7 %solve_layers.3 = (f32[4,384,256]{2,1,0:T(8,128)S(1)}, f32[3,256]{1,0:T(4,128)S(1)}) custom-call(bf16[256,384]{1,0:T(8,128)(2,1)} %bitcast.9.refs_0_, bf16[192,256]{1,0:T(8,128)(2,1)} %get-tuple-element.55.refs_1_, bf16[192,16]{1,0:T(8,128)(2,1)} %get-tuple-element.56.refs_2_, bf16[16,1536]{1,0:T(8,128)(2,1)} %get-tuple-element.57.refs_3_, ...), custom_call_target="tpu_custom_call" | custom-call | flops 905969664 | bytes 5167104 | tf_op jit(solution)/shard_map/solve_layers/pallas_call | solution.py:73
  57.6 1.0 %join_second.2 = (f32[384,256]{1,0:T(8,128)S(1)}, bf16[384,128]{1,0:T(8,128)(2,1)S(1)}, f32[384,256]{1,0:T(8,128)S(1)}) custom-call(bf16[384,256]{1,0:T(8,128)(2,1)} %collective-permute-done.7.refs_0_, f32[4,384,256]{2,1,0:T(8,128)S(1)} %get-tuple-element.70.refs_1_.refs_4_, bf16[4,384,384]{2,1,0:T(8,128)(2,1)S(1)} %bitcast.18), custom_call_target="tpu_custom_call" | custom-call | flops 75497472 | bytes 2949120 | tf_op jit(solution)/shard_map/join_second/pallas_call | solution.py:73
  58.7 0.8 collective-permute-start.9
  59.5 0.6 collective-permute-done.10.refs_0_
  60.0 0.4 join_second.3
  60.4 2.1 %collective-permute-start.11 = (bf16[384,128]{1,0:T(8,128)(2,1)S(1)}, bf16[384,128]{1,0:T(8,128)(2,1)S(1)}, u32[]{:S(2)}, u32[]{:S(2)}) collective-permute-start(bf16[384,128]{1,0:T(8,128)(2,1)S(1)} %get-tuple-element.75), channel_id=1, source_target_pairs={{0,4},{1,5},{2,6},{3,7},{4,0},{5,1},{6,2},{7,3},{8,12},{9,13},{10,... | collective-permute-start | bytes 294920 | tf_op jit(solution)/shard_map/ppermute | solution.py:372
  62.6 1.7 %inner_products.1 = (f32[4,384,256]{2,1,0:T(8,128)S(1)}, f32[4,384,256]{2,1,0:T(8,128)S(1)}, f32[3,256]{1,0:T(4,128)S(1)}) custom-call(f32[384,256]{1,0:T(8,128)S(1)} %get-tuple-element.78.refs_0_, f32[384,256]{1,0:T(8,128)S(1)} %get-tuple-element.79.refs_1_, bf16[384,256]{1,0:T(8,128)(2,1)S(1)} %copy-done.3, bf16[384,256]{1,0:T(8,128)(2,1)S(1)} %copy-done.8, ...), custom_call_target="tpu_custom_call" | custom-call | flops 905969664 | bytes 8260608 | tf_op jit(solution)/shard_map/inner_products/pallas_call | solution.py:73
  64.3 1.4 %collective-permute-done.11.refs_1_ = bf16[384,128]{1,0:T(8,128)(2,1)S(1)} collective-permute-done((bf16[384,128]{1,0:T(8,128)(2,1)S(1)}, bf16[384,128]{1,0:T(8,128)(2,1)S(1)}, u32[]{:S(2)}, u32[]{:S(2)}) %collective-permute-start.11) | collective-permute-done | bytes 98336 | tf_op jit(solution)/shard_map/ppermute | solution.py:372
  65.6 0.2 join_sums.1
  65.8 12.1 %all_to_all.15.refs_0_ = f32[32,2,384]{2,1,0:T(2,128)S(1)} all-to-all(f32[32,2,384]{2,1,0:T(2,128)S(1)} %join_sums.1), channel_id=1, replica_groups=mesh['row'=8,'col'=4] {'row','col'}, dimensions={0} | all-to-all | bytes 196608 | tf_op jit(solution)/shard_map/all_to_all | solution.py:376
  77.9 1.3 %finish.1 = f32[4,384,256]{2,1,0:T(8,128)} custom-call(f32[32,2,384]{2,1,0:T(2,128)S(1)} %all_to_all.15.refs_0_, f32[3,256]{1,0:T(4,128)S(1)} %get-tuple-element.81.refs_10_.refs_1_, f32[4,384,256]{2,1,0:T(8,128)S(1)} %get-tuple-element.83.refs_2_, f32[4,384,256]{2,1,0:T(8,128)S(1)} %get-tuple-element.84.refs_3_), custom_call_target="tpu_custom_call" | custom-call | bytes 3247104 | tf_op jit(solution)/shard_map/finish/pallas_call | solution.py:73
  (38 shorter events, 0.1 us)
Async XLA Ops:
  0.0 6.9 %copy-start.13 = (bf16[1,1,6,1536]{3,2,1,0:T(8,128)(2,1)S(1)}, bf16[1,1,6,1536]{3,2,1,0:T(8,128)(2,1)}, u32[]{:S(2)}) copy-start(bf16[1,1,6,1536]{3,2,1,0:T(8,128)(2,1)} %param.12) | copy-start | bytes 55300
  1.0 11.5 %copy-start.9 = (bf16[384,256]{1,0:T(8,128)(2,1)}, bf16[384,256]{1,0:T(8,128)(2,1)S(1)}, u32[]{:S(2)}) copy-start(bf16[384,256]{1,0:T(8,128)(2,1)S(1)} %load_edge.2.refs_1_.refs_2_.refs_6_) | copy-start | bytes 589828
  1.0 13.0 %collective-permute-start = (bf16[384,256]{1,0:T(8,128)(2,1)S(1)}, bf16[384,256]{1,0:T(8,128)(2,1)S(1)}, u32[]{:S(2)}, u32[]{:S(2)}) collective-permute-start(bf16[384,256]{1,0:T(8,128)(2,1)S(1)} %load_edge.2.refs_1_.refs_2_.refs_6_), channel_id=1, source_target_pairs={{0,1},{1,0},{2,3},{3,2},{4,8},{5,9},{6,10},{7,11},{8,4},{9,5},{10,... | collective-permute-start | bytes 589832 | tf_op jit(solution)/shard_map/ppermute | solution.py:372
  2.8 9.8 %copy-start.12 = (bf16[384,256]{1,0:T(8,128)(2,1)}, bf16[384,256]{1,0:T(8,128)(2,1)S(1)}, u32[]{:S(2)}) copy-start(bf16[384,256]{1,0:T(8,128)(2,1)S(1)} %get-tuple-element.45.refs_2_.refs_3_.refs_7_) | copy-start | bytes 589828
  2.8 12.2 %collective-permute-start.2 = (bf16[384,256]{1,0:T(8,128)(2,1)S(1)}, bf16[384,256]{1,0:T(8,128)(2,1)S(1)}, u32[]{:S(2)}, u32[]{:S(2)}) collective-permute-start(bf16[384,256]{1,0:T(8,128)(2,1)S(1)} %get-tuple-element.45.refs_2_.refs_3_.refs_7_), channel_id=1, source_target_pairs={{0,4},{1,5},{2,6},{3,7},{4,0},{5,1},{6,2},{7,3},{8,12},{9,13},{10,... | collective-permute-start | bytes 589832 | tf_op jit(solution)/shard_map/ppermute | solution.py:372
  7.8 13.1 %all-to-all-start = ((bf16[32,8,256]{2,1,0:T(8,128)(2,1)}), bf16[32,8,256]{2,1,0:T(8,128)(2,1)S(1)}, u32[]{:S(2)}, u32[]{:S(2)}) async-start(bf16[32,8,256]{2,1,0:T(8,128)(2,1)} %bitcast.41), calls=%async_computation | async-start | bytes 262144 | tf_op jit(solution)/shard_map/all_to_all | solution.py:376
  13.9 4.8 %copy-start.15 = (bf16[192,192]{1,0:T(8,128)(2,1)S(1)}, bf16[192,192]{1,0:T(8,128)(2,1)}, u32[]{:S(2)}) copy-start(bf16[192,192]{1,0:T(8,128)(2,1)} %refs_1_.1) | copy-start | bytes 221188
  14.7 10.9 %collective-permute-start.1 = (bf16[384,256]{1,0:T(8,128)(2,1)S(1)}, bf16[384,256]{1,0:T(8,128)(2,1)S(1)}, u32[]{:S(2)}, u32[]{:S(2)}) collective-permute-start(bf16[384,256]{1,0:T(8,128)(2,1)S(1)} %get-tuple-element.50.refs_4_), channel_id=1, source_target_pairs={{0,1},{1,0},{2,3},{3,2},{4,8},{5,9},{6,10},{7,11},{8,4},{9,5},{10,... | collective-permute-start | bytes 589832 | tf_op jit(solution)/shard_map/ppermute | solution.py:372
  15.7 10.6 %collective-permute-start.4 = (bf16[384,256]{1,0:T(8,128)(2,1)S(1)}, bf16[384,256]{1,0:T(8,128)(2,1)S(1)}, u32[]{:S(2)}, u32[]{:S(2)}) collective-permute-start(bf16[384,256]{1,0:T(8,128)(2,1)S(1)} %get-tuple-element.54.refs_2_), channel_id=1, source_target_pairs={{0,4},{1,5},{2,6},{3,7},{4,0},{5,1},{6,2},{7,3},{8,12},{9,13},{10,... | collective-permute-start | bytes 589832 | tf_op jit(solution)/shard_map/ppermute | solution.py:372
  20.8 0.7 copy-start.16
  21.5 4.0 %copy-start = (bf16[4,1,384,384]{3,2,1,0:T(8,128)(2,1)S(1)}, bf16[4,1,384,384]{3,2,1,0:T(8,128)(2,1)}, u32[]{:S(2)}) copy-start(bf16[4,1,384,384]{3,2,1,0:T(8,128)(2,1)} %param.9) | copy-start | bytes 3538948
  25.6 3.3 %copy-start.1 = (bf16[4,1,384,256]{3,2,1,0:T(8,128)(2,1)S(1)}, bf16[4,1,384,256]{3,2,1,0:T(8,128)(2,1)}, u32[]{:S(2)}) copy-start(bf16[4,1,384,256]{3,2,1,0:T(8,128)(2,1)} %param.7) | copy-start | bytes 2359300
  25.6 3.3 %copy-start.4 = (bf16[4,1,384,384]{3,2,1,0:T(8,128)(2,1)S(1)}, bf16[4,1,384,384]{3,2,1,0:T(8,128)(2,1)}, u32[]{:S(2)}) copy-start(bf16[4,1,384,384]{3,2,1,0:T(8,128)(2,1)} %param.8) | copy-start | bytes 3538948
  25.6 4.6 %collective-permute-start.3 = (bf16[384,256]{1,0:T(8,128)(2,1)S(1)}, bf16[384,256]{1,0:T(8,128)(2,1)S(1)}, u32[]{:S(2)}, u32[]{:S(2)}) collective-permute-start(bf16[384,256]{1,0:T(8,128)(2,1)S(1)} %get-tuple-element.60.refs_3_), channel_id=1, source_target_pairs={{0,1},{1,0},{2,3},{3,2},{4,8},{5,9},{6,10},{7,11},{8,4},{9,5},{10,... | collective-permute-start | bytes 589832 | tf_op jit(solution)/shard_map/ppermute | solution.py:372
  26.7 9.2 %collective-permute-start.5 = (bf16[384,256]{1,0:T(8,128)(2,1)S(1)}, bf16[384,256]{1,0:T(8,128)(2,1)S(1)}, u32[]{:S(2)}, u32[]{:S(2)}) collective-permute-start(bf16[384,256]{1,0:T(8,128)(2,1)S(1)} %get-tuple-element.64), channel_id=1, source_target_pairs={{0,4},{1,5},{2,6},{3,7},{4,0},{5,1},{6,2},{7,3},{8,12},{9,13},{10,... | collective-permute-start | bytes 589832 | tf_op jit(solution)/shard_map/ppermute | solution.py:372
  30.2 5.7 %copy-start.5 = (bf16[4,384,256]{2,1,0:T(8,128)(2,1)}, bf16[4,384,256]{2,1,0:T(8,128)(2,1)S(1)}, u32[]{:S(2)}) copy-start(bf16[4,384,256]{2,1,0:T(8,128)(2,1)S(1)} %get-tuple-element.69.refs_8_.refs_7_) | copy-start | bytes 2359300
  30.2 5.7 %copy-start.10 = (f32[4,384,256]{2,1,0:T(8,128)}, f32[4,384,256]{2,1,0:T(8,128)S(1)}, u32[]{:S(2)}) copy-start(f32[4,384,256]{2,1,0:T(8,128)S(1)} %get-tuple-element.80.refs_5_) | copy-start | bytes 4718596
  35.9 3.6 %copy-start.2 = (bf16[384,256]{1,0:T(8,128)(2,1)}, bf16[384,256]{1,0:T(8,128)(2,1)S(1)}, u32[]{:S(2)}) copy-start(bf16[384,256]{1,0:T(8,128)(2,1)S(1)} %join_operate.2.refs_3_.refs_0_.refs_2_.refs_6_) | copy-start | bytes 589828
  36.0 3.6 %copy-start.14 = (bf16[1,1,6,1536]{3,2,1,0:T(8,128)(2,1)S(1)}, bf16[1,1,6,1536]{3,2,1,0:T(8,128)(2,1)}, u32[]{:S(2)}) copy-start(bf16[1,1,6,1536]{3,2,1,0:T(8,128)(2,1)} %param.12) | copy-start | bytes 55300
  36.0 10.5 %collective-permute-start.6 = (bf16[384,256]{1,0:T(8,128)(2,1)S(1)}, bf16[384,256]{1,0:T(8,128)(2,1)}, u32[]{:S(2)}, u32[]{:S(2)}) collective-permute-start(bf16[384,256]{1,0:T(8,128)(2,1)S(1)} %join_operate.2.refs_3_.refs_0_.refs_2_.refs_6_), channel_id=1, source_target_pairs={{0,1},{1,0},{2,3},{3,2},{4,8},{5,9},{6,10},{7,11},{8,4},{9,5},{10,... | collective-permute-start | bytes 589832 | tf_op jit(solution)/shard_map/ppermute | solution.py:372
  36.3 4.3 %copy-start.7 = (bf16[384,256]{1,0:T(8,128)(2,1)}, bf16[384,256]{1,0:T(8,128)(2,1)S(1)}, u32[]{:S(2)}) copy-start(bf16[384,256]{1,0:T(8,128)(2,1)S(1)} %join_operate.3.refs_1_.refs_3_.refs_7_) | copy-start | bytes 589828
  36.4 12.5 %collective-permute-start.8 = (bf16[384,256]{1,0:T(8,128)(2,1)S(1)}, bf16[384,256]{1,0:T(8,128)(2,1)}, u32[]{:S(2)}, u32[]{:S(2)}) collective-permute-start(bf16[384,256]{1,0:T(8,128)(2,1)S(1)} %join_operate.3.refs_1_.refs_3_.refs_7_), channel_id=1, source_target_pairs={{0,4},{1,5},{2,6},{3,7},{4,0},{5,1},{6,2},{7,3},{8,12},{9,13},{10,... | collective-permute-start | bytes 589832 | tf_op jit(solution)/shard_map/ppermute | solution.py:372
  40.6 13.4 %all-to-all-start.1 = ((bf16[32,8,384]{2,1,0:T(8,128)(2,1)}), bf16[32,8,384]{2,1,0:T(8,128)(2,1)}, u32[]{:S(2)}, u32[]{:S(2)}) async-start(bf16[32,8,384]{2,1,0:T(8,128)(2,1)} %bitcast.39), calls=%async_computation.1 | async-start | bytes 393216 | tf_op jit(solution)/shard_map/all_to_all | solution.py:376
  47.8 9.8 %collective-permute-start.7 = (bf16[384,256]{1,0:T(8,128)(2,1)S(1)}, bf16[384,256]{1,0:T(8,128)(2,1)}, u32[]{:S(2)}, u32[]{:S(2)}) collective-permute-start(bf16[384,256]{1,0:T(8,128)(2,1)S(1)} %margin_solve.6.refs_4_), channel_id=1, source_target_pairs={{0,1},{1,0},{2,3},{3,2},{4,8},{5,9},{6,10},{7,11},{8,4},{9,5},{10,... | collective-permute-start | bytes 589832 | tf_op jit(solution)/shard_map/ppermute | solution.py:372
  50.9 9.1 %collective-permute-start.10 = (bf16[384,256]{1,0:T(8,128)(2,1)}, bf16[384,256]{1,0:T(8,128)(2,1)S(1)}, u32[]{:S(2)}, u32[]{:S(2)}) collective-permute-start(bf16[384,256]{1,0:T(8,128)(2,1)} %margin_solve.7), channel_id=1, source_target_pairs={{0,4},{1,5},{2,6},{3,7},{4,0},{5,1},{6,2},{7,3},{8,12},{9,13},{10,... | collective-permute-start | bytes 589832 | tf_op jit(solution)/shard_map/ppermute | solution.py:372
  58.7 3.9 %copy-start.3 = (bf16[384,256]{1,0:T(8,128)(2,1)S(1)}, bf16[384,256]{1,0:T(8,128)(2,1)}, u32[]{:S(2)}) copy-start(bf16[384,256]{1,0:T(8,128)(2,1)} %copy-done.2) | copy-start | bytes 589828
  58.7 3.9 %copy-start.6 = (bf16[4,384,256]{2,1,0:T(8,128)(2,1)S(1)}, bf16[4,384,256]{2,1,0:T(8,128)(2,1)}, u32[]{:S(2)}) copy-start(bf16[4,384,256]{2,1,0:T(8,128)(2,1)} %copy-done.5) | copy-start | bytes 2359300
  58.7 3.9 %copy-start.8 = (bf16[384,256]{1,0:T(8,128)(2,1)S(1)}, bf16[384,256]{1,0:T(8,128)(2,1)}, u32[]{:S(2)}) copy-start(bf16[384,256]{1,0:T(8,128)(2,1)} %copy-done.7) | copy-start | bytes 589828
  58.7 3.9 %copy-start.11 = (f32[4,384,256]{2,1,0:T(8,128)S(1)}, f32[4,384,256]{2,1,0:T(8,128)}, u32[]{:S(2)}) copy-start(f32[4,384,256]{2,1,0:T(8,128)} %copy-done.10) | copy-start | bytes 4718596
  58.7 5.6 %collective-permute-start.9 = (bf16[384,128]{1,0:T(8,128)(2,1)S(1)}, bf16[384,128]{1,0:T(8,128)(2,1)S(1)}, u32[]{:S(2)}, u32[]{:S(2)}) collective-permute-start(bf16[384,128]{1,0:T(8,128)(2,1)S(1)} %get-tuple-element.71.refs_3_), channel_id=1, source_target_pairs={{0,1},{1,0},{2,3},{3,2},{4,8},{5,9},{6,10},{7,11},{8,4},{9,5},{10,... | collective-permute-start | bytes 294920 | tf_op jit(solution)/shard_map/ppermute | solution.py:372
  60.4 5.2 %collective-permute-start.11 = (bf16[384,128]{1,0:T(8,128)(2,1)S(1)}, bf16[384,128]{1,0:T(8,128)(2,1)S(1)}, u32[]{:S(2)}, u32[]{:S(2)}) collective-permute-start(bf16[384,128]{1,0:T(8,128)(2,1)S(1)} %get-tuple-element.75), channel_id=1, source_target_pairs={{0,4},{1,5},{2,6},{3,7},{4,0},{5,1},{6,2},{7,3},{8,12},{9,13},{10,... | collective-permute-start | bytes 294920 | tf_op jit(solution)/shard_map/ppermute | solution.py:372
